TPU v7x, 32 devices: a whole 2x2x4 slice. The times are simulated.
32 devices in a mesh: gx: 4 (over x, core), gy: 2 (over y), gz: 4 (over z).
Axes of the slice: x: 2, y: 2, z: 4, core: 2. Of those that a mesh axis runs over, the one named last changes fastest.
Arguments:
- features: bfloat16 [4, 2, 4, 128, 128], P('gx', 'gy', 'gz'), may hold values from -6 to 6
- positions: float32 [4, 2, 4, 3, 128], P('gx', 'gy', 'gz'), may hold values from 0 to 1
- counts: int32 [4, 2, 4], P('gx', 'gy', 'gz'), may hold values from 1 to 128, as said below
- w_proj: bfloat16 [4, 128, 128], replicated, may hold values from -0.5 to 0.5
- w_mix: bfloat16 [128, 128], replicated, may hold values from -0.5 to 0.5
- w_long: bfloat16 [64, 128], replicated, may hold values from -0.75 to 0.75
- w_charge: bfloat16 [64, 128], replicated, may hold values from -0.5 to 0.5
- charge_bias: float32 [64], replicated, may hold values from -4 to 4
- w_energy: float32 [128], replicated, may hold values from -0.5 to 0.5
- k_filter: float32 [64, 2048], replicated, may hold values from 0.1 to 1
- k_index: int32 [3, 2048], replicated, may hold values from -6 to 6
Outputs:
- updated: bfloat16 [4, 2, 4, 128, 128], P('gx', 'gy', 'gz')
- energies: float32 [4, 2, 4, 128], P('gx', 'gy', 'gz')
- forces: float32 [4, 2, 4, 3, 128], P('gx', 'gy', 'gz')
Inputs may be any that keep to these rules, and one draw needn't show every extreme that they name: Slots 0 to counts[x,y,z] - 1 of cell (x,y,z) hold live atoms, the rest are padding; some cell holds 128 live atoms.
All inputs are finite; a program needn't handle non-finite values.
Results may differ from a plain program's by a relative error of at most 0.0068.
Values may be sent and summed in bfloat16 or wider, within the bound.
No kernel may reach another device: no remote copies, remote signals or barrier semaphores. Data moves between devices by JAX's collectives and lax.ppermute only.
A program may use at most 64 MiB of HBM per device.

v0:
```python
import itertools
import math

import jax
import jax.numpy as jnp
import numpy as np
from jax import lax
from jax.experimental import pallas as pl
from jax.experimental.pallas import tpu as pltpu
from jax.sharding import PartitionSpec as P

CUTOFF = 0.9
SCALE = 1.0 / (CUTOFF * CUTOFF)
GAMMAS = (1.0, 3.0, 8.0, 20.0)
AXES = ("gx", "gy", "gz")
ORDERS = 7
NT = (((1,), (1,)), ((), ()))
F32 = jnp.float32
BF16 = jnp.bfloat16
VMEM_BYTES = 56 * 1024 * 1024


def turn_series():
    nodes = np.cos(np.pi * (np.arange(200) + 0.5) / 200)
    r2 = (nodes + 1.0) / 8.0
    r = np.sqrt(r2)
    out = []
    for values in (np.cos(2 * np.pi * r), np.sin(2 * np.pi * r) / r):
        cheb = np.polynomial.chebyshev.Chebyshev.fit(r2, values, 7, domain=[0.0, 0.25])
        out.append([float(c) for c in cheb.convert(kind=np.polynomial.Polynomial).coef])
    return out


COS_SERIES, SIN_SERIES = turn_series()


def dot(a, b):
    return jnp.dot(a, b, preferred_element_type=F32)


def dot_nt(a, b):
    return lax.dot_general(a, b, NT, preferred_element_type=F32)


def sigmoid(v):
    return 1.0 / (1.0 + jnp.exp(-v))


def cos_sin(turns):
    r = turns - jnp.floor(turns + 0.5)
    r2 = r * r
    c = jnp.full_like(r2, COS_SERIES[-1])
    for coef in COS_SERIES[-2::-1]:
        c = c * r2 + coef
    s = jnp.full_like(r2, SIN_SERIES[-1])
    for coef in SIN_SERIES[-2::-1]:
        s = s * r2 + coef
    return c, s * r


def axis_tables(pos, anchor, sizes):
    order = lax.broadcasted_iota(jnp.int32, (8, pos.shape[1]), 0).astype(F32)
    tables = []
    for a in range(3):
        row = (pos[a : a + 1, :] + anchor[a]) * (1.0 / sizes[a])
        tables.append(cos_sin(order * row))
    return tables


def plane_table(first, second):
    rows = []
    for f in first:
        for s in second:
            for a in range(8):
                rows.append(f[a : a + 1, :] * s)
    return jnp.concatenate(rows, axis=0)


def derivative(table, size):
    order = lax.broadcasted_iota(jnp.int32, table[0].shape, 0).astype(F32) * (2.0 * math.pi / size)
    return (-order * table[1], order * table[0])


def spread(weights, third):
    rows = []
    for f in third:
        for c in range(ORDERS):
            rows.append((weights * f[c : c + 1, :]).astype(BF16))
    return jnp.concatenate(rows, axis=0)


def filtered(sums_ref, filt_ref, out_ref, charge_ch):
    for c in range(ORDERS):
        lo, hi = c * charge_ch, (c + 1) * charge_ch
        f0, gfb, fc, gfbc = (filt_ref[c, w * charge_ch : (w + 1) * charge_ch, :] for w in range(4))
        a_c, b_c = sums_ref[lo:hi, 0:128], sums_ref[lo:hi, 128:256]
        shift = ORDERS * charge_ch
        a_s, b_s = (
            sums_ref[shift + lo : shift + hi, 0:128],
            sums_ref[shift + lo : shift + hi, 128:256],
        )
        ra_c, rb_c, ra_s, rb_s = (pltpu.roll(v, 64, 1) for v in (a_c, b_c, a_s, b_s))
        out_ref[lo:hi, 0:128] = (f0 * a_c + gfbc * ra_s - fc * b_s + gfb * rb_c).astype(BF16)
        out_ref[lo:hi, 128:256] = (f0 * b_c - gfb * ra_c + fc * a_s + gfbc * rb_s).astype(BF16)
        out_ref[shift + lo : shift + hi, 0:128] = (
            f0 * a_s + fc * b_c - gfbc * ra_c + gfb * rb_s
        ).astype(BF16)
        out_ref[shift + lo : shift + hi, 128:256] = (
            f0 * b_s - fc * a_c - gfb * ra_s - gfbc * rb_c
        ).astype(BF16)


def field_slope(field, tables, sizes, weights, charge_ch):
    tx, ty, tz = tables
    n = tx[0].shape[1]
    planes = jnp.concatenate(
        [
            plane_table(derivative(tx, sizes[0]), ty).astype(BF16),
            plane_table(tx, derivative(ty, sizes[1])).astype(BF16),
            plane_table(tx, ty).astype(BF16),
        ],
        axis=1,
    )
    spread_field = dot(field, planes)
    slope_z = derivative(tz, sizes[2])
    total = [jnp.zeros((charge_ch, n), F32) for _ in range(3)]
    for kind in range(2):
        for c in range(ORDERS):
            lo = (kind * ORDERS + c) * charge_ch
            part = spread_field[lo : lo + charge_ch, :]
            zrow, drow = tz[kind][c : c + 1, :], slope_z[kind][c : c + 1, :]
            total[0] = total[0] + zrow * part[:, 0:n]
            total[1] = total[1] + zrow * part[:, n : 2 * n]
            total[2] = total[2] + drow * part[:, 2 * n : 3 * n]
    return [jnp.sum(t * weights, axis=0, keepdims=True) for t in total]


def place_of(meta_ref, m, half, sizes):
    nx, ny, nz = sizes
    dz = lax.rem(m, nz)
    dy = lax.rem(m // nz, ny)
    dx = m // (nz * ny)
    start = meta_ref[0] if half == 0 else meta_ref[0] + 1 - 2 * lax.rem(meta_ref[0], 2)
    cx = lax.rem(start - 2 * dx + nx, nx)
    cy = lax.rem(meta_ref[1] - dy + ny, ny)
    cz = lax.rem(meta_ref[2] - dz + nz, nz)
    return (cx.astype(F32), cy.astype(F32), cz.astype(F32))


def blocks_of(sizes):
    options = [((0, False), (1, True)) if n == 2 else ((0, False), (-1, False), (1, False)) for n in sizes]
    return list(itertools.product(*options))


def offsets(own_cols, others, block):
    result = []
    for a, (step, nearest) in enumerate(block):
        if nearest:
            d = others[a] - own_cols[a]
            d = d - jnp.where(d > 0.0, 1.0, -1.0)
        else:
            d = (others[a] + float(step)) - own_cols[a]
        result.append(d)
    return result


def pair_terms(offs, block, first_row):
    s = (offs[0] * offs[0] + offs[1] * offs[1] + offs[2] * offs[2]) * SCALE
    u = jnp.maximum(1.0 - s, 0.0)
    if all(step == 0 for step, _ in block):
        rows = lax.broadcasted_iota(jnp.int32, s.shape, 0) + first_row
        cols = lax.broadcasted_iota(jnp.int32, s.shape, 1)
        u = jnp.where(rows == cols, 0.0, u)
    e1 = jnp.exp(-s)
    e2 = e1 * e1
    e3 = e2 * e1
    e4 = e2 * e2
    e8 = e4 * e4
    e20 = e8 * e8 * e4
    return u, (e1, e3, e8, e20)


def columns(pos, n):
    return [jnp.transpose(jnp.broadcast_to(pos[a : a + 1, :], (n, n))) for a in range(3)]


def pack_kernel(count_ref, features_ref, positions_ref, out_ref):
    n, channels = features_ref.shape
    live_col = lax.broadcasted_iota(jnp.int32, (n, channels), 0) < count_ref[0]
    rows = features_ref[...].astype(F32)
    out_ref[0:n, :] = jnp.where(live_col, rows, 0.0).astype(BF16)
    pos = positions_ref[...]
    coarse = pos.astype(BF16).astype(F32)
    fine = pos - coarse
    living = (lax.broadcasted_iota(jnp.int32, (1, n), 1) < count_ref[0]).astype(F32)
    blank = jnp.zeros((4, n), F32)
    tail = jnp.concatenate([coarse, living, blank, fine, jnp.zeros((5, n), F32)], axis=0)
    out_ref[n : n + 16, :] = tail.astype(BF16)


def fold_kernel(scale, filter_ref, index_ref, out_ref):
    waves = filter_ref.shape[1]
    k = index_ref[...]
    positive = [jnp.where(k[a : a + 1, :] >= 0, 1.0, -1.0) for a in range(3)]
    sign_b = positive[0] * positive[1]
    sign_c = positive[0] * positive[2]
    size = jnp.abs(k)
    plane = size[0:1, :] * 8 + size[1:2, :]
    f = filter_ref[...] * scale
    stacked = jnp.concatenate([f, f * sign_b, f * sign_c, f * (sign_b * sign_c)], axis=0).astype(BF16)
    rows = lax.broadcasted_iota(jnp.int32, (64, waves), 0)
    charge_ch = filter_ref.shape[0]
    turn = jnp.where(lax.broadcasted_iota(jnp.int32, (charge_ch, 128), 1) < 64, -1.0, 1.0)
    for c in range(ORDERS):
        key = jnp.where(size[2:3, :] == c, plane, -1)
        chosen = jnp.where(rows == key, 1.0, 0.0).astype(BF16)
        part = dot_nt(stacked, jnp.concatenate([chosen, chosen], axis=0))
        for w in range(4):
            piece = part[w * charge_ch : (w + 1) * charge_ch, :]
            out_ref[c, w * charge_ch : (w + 1) * charge_ch, :] = piece * turn if w % 2 == 1 else piece


def forward_kernel(
    sizes,
    group,
    count_ref,
    meta_ref,
    near_ref,
    far_ref,
    features_ref,
    w_proj_ref,
    w_mix_ref,
    w_long_ref,
    w_charge_ref,
    bias_ref,
    w_energy_ref,
    filt_ref,
    updated_ref,
    energy_ref,
    grad_ref,
    field_ref,
    neutral_ref,
    places_ref,
    xcat_ref,
    charge_scr,
    sums_scr,
    radial_scr,
):
    n, channels = features_ref.shape
    charge_ch = w_charge_ref.shape[0]
    half_cells = near_ref.shape[0]
    groups = half_cells // group
    halves = (near_ref, far_ref)
    w_charge = w_charge_ref[...]
    bias = bias_ref[...]

    total = jnp.zeros((charge_ch, 1), F32)
    live_total = jnp.zeros((1, 1), F32)
    for half in range(2):
        ref = halves[half]

        def add_charges(g, carry, ref=ref, half=half):
            total, live_total = carry
            for j in range(group):
                m = g * group + j
                tail = ref[m, n : n + 16, :].astype(F32)
                pos = tail[0:8, :] + tail[8:16, :]
                places_ref[half * half_cells + m] = pos
                live = pos[3:4, :]
                v = dot_nt(w_charge, ref[m, 0:n, :]) + bias
                q = v * sigmoid(v) * live
                charge_scr[half * half_cells + m] = q
                total = total + jnp.sum(q, axis=1, keepdims=True)
                live_total = live_total + jnp.sum(live, axis=1, keepdims=True)
            return total, live_total

        total, live_total = lax.fori_loop(0, groups, add_charges, (total, live_total))
    mean = total / live_total

    sums_scr[...] = jnp.zeros_like(sums_scr)
    for half in range(2):

        def add_structure(g, _, half=half):
            left, right = [], []
            for j in range(group):
                m = g * group + j
                pos = places_ref[half * half_cells + m]
                tx, ty, tz = axis_tables(pos, place_of(meta_ref, m, half, sizes), sizes)
                neutral = (charge_scr[half * half_cells + m] - mean) * pos[3:4, :]
                left.append(spread(neutral, tz))
                right.append(plane_table(tx, ty).astype(BF16))
            sums_scr[...] += dot_nt(jnp.concatenate(left, axis=1), jnp.concatenate(right, axis=1))
            return 0

        lax.fori_loop(0, groups, add_structure, 0)

    filtered(sums_scr, filt_ref, field_ref, charge_ch)
    own = places_ref[0]
    live_row = own[3:4, :]
    neutral_ref[...] = (charge_scr[0] - mean) * live_row
    tx, ty, tz = axis_tables(own, place_of(meta_ref, 0, 0, sizes), sizes)
    lifted = dot(field_ref[...], plane_table(tx, ty).astype(BF16))
    potential = jnp.zeros((charge_ch, n), F32)
    for kind in range(2):
        for c in range(ORDERS):
            lo = (kind * ORDERS + c) * charge_ch
            potential = potential + tz[kind][c : c + 1, :] * lifted[lo : lo + charge_ch, :]

    nx, ny, nz = sizes
    odd = lax.rem(meta_ref[0], 2)
    own_cols = columns(own, n)
    for t, block in enumerate(blocks_of(sizes)):
        half = 0 if block[0][0] == 0 else 1
        dy, dz = (-block[1][0]) % ny, (-block[2][0]) % nz
        if half == 0:
            dx = 0
        elif block[0][0] == 1:
            dx = odd * (nx // 2 - 1)
        else:
            dx = (1 - odd) * (1 % (nx // 2))
        m = (dx * ny + dy) * nz + dz
        xcat_ref[t * n : (t + 1) * n, :] = halves[half][m, 0:n, :]
        pos = places_ref[half * half_cells + m]
        others = [pos[a : a + 1, :] for a in range(3)]
        for first in range(0, n, 32):
            cols = [c[first : first + 32, :] for c in own_cols]
            u, decays = pair_terms(offsets(cols, others, block), block, first)
            u2 = u * u
            for b in range(len(GAMMAS)):
                radial_scr[b * n + first : b * n + first + 32, t * n : (t + 1) * n] = (
                    decays[b] * u2
                ).astype(BF16)
    gathered = dot(radial_scr[...], xcat_ref[...]).astype(BF16)
    message = jnp.zeros((n, channels), F32)
    for b in range(len(GAMMAS)):
        message = message + dot(gathered[b * n : (b + 1) * n, :], w_proj_ref[b])

    pre_act = dot(message.astype(BF16), w_mix_ref[...]) + dot(
        jnp.transpose(potential).astype(BF16), w_long_ref[...]
    )
    sig = sigmoid(pre_act)
    refined = features_ref[...].astype(F32) + pre_act * sig
    updated_ref[...] = refined.astype(BF16)
    sig_r = sigmoid(refined)
    w_energy = w_energy_ref[...]
    energy_ref[...] = live_row * jnp.sum(
        jnp.transpose(refined * sig_r * w_energy), axis=0, keepdims=True
    )
    live_rows = lax.broadcasted_iota(jnp.int32, (n, channels), 0) < count_ref[0]
    grad = (
        w_energy
        * (sig_r * (1.0 + refined * (1.0 - sig_r)))
        * (sig * (1.0 + pre_act * (1.0 - sig)))
    )
    grad_ref[...] = jnp.where(live_rows, grad, 0.0).astype(BF16)


def pair_force(sizes, own, neighbour_pos, strengths_ref, n):
    own_cols = columns(own, n)
    blocks = blocks_of(sizes)
    parts = [[], [], []]
    for first in range(0, n, 32):
        cols = [c[first : first + 32, :] for c in own_cols]
        acc = [jnp.zeros((32, n), F32) for _ in range(3)]
        for t, block in enumerate(blocks):
            pos = neighbour_pos(t)
            offs = offsets(cols, [pos[a : a + 1, :] for a in range(3)], block)
            u, decays = pair_terms(offs, block, first)
            strength = jnp.zeros((32, n), F32)
            for b, g in enumerate(GAMMAS):
                part = strengths_ref[b * n + first : b * n + first + 32, t * n : (t + 1) * n]
                strength = strength + decays[b] * (g * u + 2.0) * part
            strength = strength * u
            for a in range(3):
                acc[a] = acc[a] + strength * offs[a]
        for a in range(3):
            parts[a].append(acc[a])
    return [
        (-2.0 * SCALE)
        * jnp.sum(jnp.transpose(jnp.concatenate(parts[a], axis=0)), axis=0, keepdims=True)
        for a in range(3)
    ]


def block_place(sizes, odd, block):
    nx, ny, nz = sizes
    half_cells = nx // 2 * ny * nz
    dy, dz = (-block[1][0]) % ny, (-block[2][0]) % nz
    if block[0][0] == 0:
        return dy * nz + dz
    dx = odd * (nx // 2 - 1) if block[0][0] == 1 else (1 - odd) * (1 % (nx // 2))
    return half_cells + (dx * ny + dy) * nz + dz


def own_kernel(
    sizes,
    meta_ref,
    grad_ref,
    field_ref,
    places_ref,
    xcat_ref,
    w_proj_ref,
    w_mix_ref,
    w_long_ref,
    force_ref,
    lifted_ref,
    strength_scr,
):
    n = grad_ref.shape[0]
    charge_ch = w_long_ref.shape[0]
    grad = grad_ref[...]
    adjoint = dot_nt(grad, w_mix_ref[...]).astype(BF16)
    rows, lifted = [], []
    for b in range(len(GAMMAS)):
        rows.append(dot_nt(adjoint, w_proj_ref[b]).astype(BF16))
        basis = dot(xcat_ref[0:n, :], w_proj_ref[b]).astype(BF16)
        lifted.append(dot(basis, w_mix_ref[...]).astype(BF16))
    lifted_ref[...] = jnp.concatenate(lifted, axis=0)
    strength_scr[...] = dot_nt(jnp.concatenate(rows, axis=0), xcat_ref[...])
    odd = lax.rem(meta_ref[0], 2)
    blocks = blocks_of(sizes)
    own = places_ref[0]
    near = pair_force(
        sizes, own, lambda t: places_ref[block_place(sizes, odd, blocks[t])], strength_scr, n
    )
    pull = dot_nt(w_long_ref[...], grad)
    tables = axis_tables(own, place_of(meta_ref, 0, 0, sizes), sizes)
    slope = field_slope(field_ref[...], tables, sizes, pull, charge_ch)
    force_ref[...] = jnp.concatenate([near[a] - slope[a] for a in range(3)], axis=0)


def backward_kernel(
    sizes,
    group,
    meta_ref,
    near_ref,
    far_ref,
    places_ref,
    neutral_ref,
    lifted_ref,
    force_ref,
    w_long_ref,
    filt_ref,
    out_ref,
    sums_scr,
    field_scr,
    gcat_scr,
    strength_scr,
):
    n = neutral_ref.shape[1]
    charge_ch = w_long_ref.shape[0]
    half_cells = near_ref.shape[0]
    groups = half_cells // group
    halves = (near_ref, far_ref)
    sums_scr[...] = jnp.zeros_like(sums_scr)
    for half in range(2):

        def add_structure(g, _, half=half):
            left, right = [], []
            for j in range(group):
                m = g * group + j
                pos = places_ref[half * half_cells + m]
                tx, ty, tz = axis_tables(pos, place_of(meta_ref, m, half, sizes), sizes)
                left.append(spread(dot_nt(w_long_ref[...], halves[half][m]), tz))
                right.append(plane_table(tx, ty).astype(BF16))
            sums_scr[...] += dot_nt(jnp.concatenate(left, axis=1), jnp.concatenate(right, axis=1))
            return 0

        lax.fori_loop(0, groups, add_structure, 0)
    filtered(sums_scr, filt_ref, field_scr, charge_ch)
    own = places_ref[0]
    tables = axis_tables(own, place_of(meta_ref, 0, 0, sizes), sizes)
    slope = field_slope(field_scr[...], tables, sizes, neutral_ref[...], charge_ch)

    odd = lax.rem(meta_ref[0], 2)
    blocks = blocks_of(sizes)
    for t, block in enumerate(blocks):
        place = block_place(sizes, odd, block)
        half = 0 if block[0][0] == 0 else 1
        gcat_scr[t * n : (t + 1) * n, :] = halves[half][place - half * half_cells]
    strength_scr[...] = dot_nt(lifted_ref[...], gcat_scr[...])
    near = pair_force(
        sizes, own, lambda t: places_ref[block_place(sizes, odd, blocks[t])], strength_scr, n
    )
    out_ref[...] = force_ref[...] + jnp.concatenate([near[a] - slope[a] for a in range(3)], axis=0)


def gather_cells(rows, sizes):
    nx, ny, nz = sizes
    pairs = nx // 2

    def shifted(value, dx, dy):
        moves = []
        for i in range(nx):
            for j in range(ny):
                moves.append((i * ny + j, (i + 2 * dx) % nx * ny + (j + dy) % ny))
        return lax.ppermute(value, ("gx", "gy"), moves)

    value = rows[None]
    value = jnp.concatenate(
        [value]
        + [
            lax.ppermute(value, "gz", [(i, (i + s) % nz) for i in range(nz)])
            for s in range(1, nz)
        ],
        axis=0,
    )
    if pairs * ny <= 4:
        steps = [(dx, dy) for dx in range(pairs) for dy in range(ny)]
        value = jnp.concatenate(
            [value] + [shifted(value, dx, dy) for dx, dy in steps[1:]], axis=0
        )
    else:
        value = jnp.concatenate([value] + [shifted(value, 0, dy) for dy in range(1, ny)], axis=0)
        value = jnp.concatenate([value] + [shifted(value, dx, 0) for dx in range(1, pairs)], axis=0)
    other = lax.ppermute(value, "gx", [(i, i ^ 1) for i in range(nx)])
    return value, other


def call(kernel, name, outs, scratch, smem, operands, flops):
    n_in = len(operands)
    specs = [pl.BlockSpec(memory_space=pltpu.SMEM)] * smem + [
        pl.BlockSpec(memory_space=pltpu.VMEM)
    ] * (n_in - smem)
    return pl.pallas_call(
        kernel,
        name=name,
        out_shape=outs,
        in_specs=specs,
        out_specs=[pl.BlockSpec(memory_space=pltpu.VMEM)] * len(outs),
        scratch_shapes=scratch,
        compiler_params=pltpu.CompilerParams(vmem_limit_bytes=VMEM_BYTES),
        cost_estimate=pl.CostEstimate(flops=flops, bytes_accessed=2_000_000, transcendentals=0),
    )(*operands)


def shards(
    features,
    positions,
    counts,
    w_proj,
    w_mix,
    w_long,
    w_charge,
    charge_bias,
    w_energy,
    k_filter,
    k_index,
):
    own_rows = features[0, 0, 0]
    n, channels = own_rows.shape
    charge_ch = w_charge.shape[0]
    waves = k_index.shape[1]
    bases = w_proj.shape[0]
    sizes = tuple(lax.axis_size(a) for a in AXES)
    cells = sizes[0] * sizes[1] * sizes[2]
    half_cells = cells // 2
    group = max(g for g in (8, 4, 2, 1) if half_cells % g == 0)
    blocks = len(blocks_of(sizes))
    scale_long = 4.0 / math.sqrt(n * cells * waves)
    count = counts.reshape(1)
    meta = jnp.stack([lax.axis_index(a) for a in AXES]).astype(jnp.int32)
    shape = jax.ShapeDtypeStruct
    wide = 2 * ORDERS * charge_ch

    (packed,) = call(
        pack_kernel,
        "pack",
        [shape((n + 16, channels), BF16)],
        [],
        1,
        [count, own_rows, positions[0, 0, 0]],
        1000,
    )
    near, far = gather_cells(packed, sizes)
    (filt,) = call(
        lambda *refs: fold_kernel(scale_long, *refs),
        "fold_filter",
        [shape((ORDERS, 4 * charge_ch, 128), F32)],
        [],
        0,
        [k_filter, k_index],
        1_000_000_000,
    )
    updated, energy, grad, field, neutral, places, xcat = call(
        lambda *refs: forward_kernel(sizes, group, *refs),
        "forward",
        [
            shape((n, channels), BF16),
            shape((1, n), F32),
            shape((n, channels), BF16),
            shape((wide, 256), BF16),
            shape((charge_ch, n), F32),
            shape((cells, 8, n), F32),
            shape((blocks * n, channels), BF16),
        ],
        [
            pltpu.VMEM((cells, charge_ch, n), F32),
            pltpu.VMEM((wide, 256), F32),
            pltpu.VMEM((bases * n, blocks * n), BF16),
        ],
        2,
        [
            count,
            meta,
            near,
            far,
            own_rows,
            w_proj,
            w_mix,
            w_long,
            w_charge,
            charge_bias[:, None],
            w_energy[None, :],
            filt,
        ],
        5_000_000_000,
    )
    grad_near, grad_far = gather_cells(grad, sizes)
    force, lifted = call(
        lambda *refs: own_kernel(sizes, *refs),
        "own_forces",
        [shape((3, n), F32), shape((bases * n, channels), BF16)],
        [pltpu.VMEM((bases * n, blocks * n), F32)],
        1,
        [meta, grad, field, places, xcat, w_proj, w_mix, w_long],
        5_000_000_000,
    )
    (forces,) = call(
        lambda *refs: backward_kernel(sizes, group, *refs),
        "backward",
        [shape((3, n), F32)],
        [
            pltpu.VMEM((wide, 256), F32),
            pltpu.VMEM((wide, 256), BF16),
            pltpu.VMEM((blocks * n, channels), BF16),
            pltpu.VMEM((bases * n, blocks * n), F32),
        ],
        1,
        [meta, grad_near, grad_far, places, neutral, lifted, force, w_long, filt],
        5_000_000_000,
    )
    return (
        updated[None, None, None],
        energy[None, None],
        forces[None, None, None],
    )


def solution(mesh):
    cell = ("gx", "gy", "gz")
    in_specs = (P(*cell, None, None), P(*cell, None, None), P(*cell)) + (P(),) * 8
    out_specs = (P(*cell, None, None), P(*cell, None), P(*cell, None, None))
    return jax.shard_map(shards, mesh=mesh, in_specs=in_specs, out_specs=out_specs, check_vma=False)
```

profile of v0, /device:TPU:0, one launch (start us, length us, event | category | flops | bytes accessed | tf_op | source)
XLA Modules:
  0.0 70.6 jit_solution(11488577956705279798)
XLA Ops:
  1.9 1.4 %pack.1 = bf16[144,128]{1,0:T(8,128)(2,1)} custom-call(s32[1]{0:T(128)} %bitcast.17.count_ref, bf16[128,128]{1,0:T(8,128)(2,1)} %bitcast.27, f32[3,128]{1,0:T(4,128)} %bitcast.29), custom_call_target="tpu_custom_call" | custom-call | flops 1000 | bytes 2000000 | tf_op jit(solution)/shard_map/pack/pallas_call | solution.py:525
  3.3 5.0 %collective-permute-start.2 = (bf16[1,144,128]{2,1,0:T(8,128)(2,1)}, bf16[1,144,128]{2,1,0:T(8,128)(2,1)S(1)}, u32[]{:S(2)}, u32[]{:S(2)}) collective-permute-start(bf16[1,144,128]{2,1,0:T(8,128)(2,1)} %bitcast.19), channel_id=1, source_target_pairs={{0,3},{1,0},{2,1},{3,2},{4,7},{5,4},{6,5},{7,6},{8,11},{9,8},{10,9... | collective-permute-start | bytes 110600 | tf_op jit(solution)/shard_map/ppermute | solution.py:503
  8.3 1.0 %collective-permute-start = (bf16[1,144,128]{2,1,0:T(8,128)(2,1)}, bf16[1,144,128]{2,1,0:T(8,128)(2,1)S(1)}, u32[]{:S(2)}, u32[]{:S(2)}) collective-permute-start(bf16[1,144,128]{2,1,0:T(8,128)(2,1)} %bitcast.21), channel_id=1, source_target_pairs={{0,1},{1,2},{2,3},{3,0},{4,5},{5,6},{6,7},{7,4},{8,9},{9,10},{10,1... | collective-permute-start | bytes 110600 | tf_op jit(solution)/shard_map/ppermute | solution.py:503
  9.3 0.8 %constant_dynamic-update-slice_fusion.6 = bf16[16,144,128]{2,1,0:T(8,128)(2,1)S(1)} fusion(bf16[144,128]{1,0:T(8,128)(2,1)} %pack.1), kind=kLoop, calls=%fused_computation.8 | loop fusion | bytes 73728
  10.3 3.1 %collective-permute-done.1 = bf16[1,144,128]{2,1,0:T(8,128)(2,1)S(1)} collective-permute-done((bf16[1,144,128]{2,1,0:T(8,128)(2,1)}, bf16[1,144,128]{2,1,0:T(8,128)(2,1)S(1)}, u32[]{:S(2)}, u32[]{:S(2)}) %collective-permute-start.1) | collective-permute-done | bytes 36896 | tf_op jit(solution)/shard_map/ppermute | solution.py:503
  13.4 0.9 %collective-permute-done = bf16[1,144,128]{2,1,0:T(8,128)(2,1)S(1)} collective-permute-done((bf16[1,144,128]{2,1,0:T(8,128)(2,1)}, bf16[1,144,128]{2,1,0:T(8,128)(2,1)S(1)}, u32[]{:S(2)}, u32[]{:S(2)}) %collective-permute-start) | collective-permute-done | bytes 36896 | tf_op jit(solution)/shard_map/ppermute | solution.py:503
  14.3 2.5 %collective-permute-start.5 = (bf16[4,144,128]{2,1,0:T(8,128)(2,1)S(1)}, bf16[4,144,128]{2,1,0:T(8,128)(2,1)S(1)}, u32[]{:S(2)}, u32[]{:S(2)}) collective-permute-start(bf16[4,144,128]{2,1,0:T(8,128)(2,1)S(1)} %pad_maximum_fusion), channel_id=1, source_target_pairs={{0,20},{4,16},{8,28},{12,24},{16,4},{20,0},{24,12},{28,8},{1,21},{... | collective-permute-start | bytes 442376 | tf_op jit(solution)/shard_map/ppermute | solution.py:497
  17.9 4.7 %collective-permute-done.3 = bf16[4,144,128]{2,1,0:T(8,128)(2,1)S(1)} collective-permute-done((bf16[4,144,128]{2,1,0:T(8,128)(2,1)S(1)}, bf16[4,144,128]{2,1,0:T(8,128)(2,1)S(1)}, u32[]{:S(2)}, u32[]{:S(2)}) %collective-permute-start.3) | collective-permute-done | bytes 147488 | tf_op jit(solution)/shard_map/ppermute | solution.py:497
  22.8 0.7 copy-done.5
  23.5 0.7 copy.14.refs_9_
  24.2 4.1 %fold_filter.1.refs_11_.refs_8_ = f32[7,256,128]{2,1,0:T(8,128)} custom-call(f32[64,2048]{1,0:T(8,128)} %refs_0_.1, s32[3,2048]{1,0:T(4,128)} %refs_1_.1), custom_call_target="tpu_custom_call" | custom-call | flops 1000000000 | bytes 2000000 | tf_op jit(solution)/shard_map/fold_filter/pallas_call | solution.py:525
  28.8 0.8 %copy-done.6 = bf16[16,144,128]{2,1,0:T(8,128)(2,1)} copy-done((bf16[16,144,128]{2,1,0:T(8,128)(2,1)}, bf16[16,144,128]{2,1,0:T(8,128)(2,1)S(1)}, u32[]{:S(2)}) %copy-start.6) | copy-done | bytes 589848
  29.7 9.6 %forward.1 = (bf16[128,128]{1,0:T(8,128)(2,1)}, f32[1,128]{1,0:T(1,128)}, bf16[128,128]{1,0:T(8,128)(2,1)}, bf16[896,256]{1,0:T(8,128)(2,1)}, f32[64,128]{1,0:T(...) custom-call(s32[1]{0:T(128)} %bitcast.18.refs_0_, s32[3]{0:T(128)} %pad_add_fusion.refs_1_.refs_0_, ...), custom_call_target="tpu_custom_call" | custom-call | flops 5000000000 | bytes 2000000 | tf_op jit(solution)/shard_map/forward/pallas_call | solution.py:525
  39.2 1.0 %collective-permute-start.9 = (bf16[1,128,128]{2,1,0:T(8,128)(2,1)}, bf16[1,128,128]{2,1,0:T(8,128)(2,1)S(1)}, u32[]{:S(2)}, u32[]{:S(2)}) collective-permute-start(bf16[1,128,128]{2,1,0:T(8,128)(2,1)} %bitcast.23), channel_id=1, source_target_pairs={{0,3},{1,0},{2,1},{3,2},{4,7},{5,4},{6,5},{7,6},{8,11},{9,8},{10,9... | collective-permute-start | bytes 98312 | tf_op jit(solution)/shard_map/ppermute | solution.py:503
  40.7 1.9 %collective-permute-start.7 = (bf16[1,128,128]{2,1,0:T(8,128)(2,1)}, bf16[1,128,128]{2,1,0:T(8,128)(2,1)S(1)}, u32[]{:S(2)}, u32[]{:S(2)}) collective-permute-start(bf16[1,128,128]{2,1,0:T(8,128)(2,1)} %bitcast.25), channel_id=1, source_target_pairs={{0,1},{1,2},{2,3},{3,0},{4,5},{5,6},{6,7},{7,4},{8,9},{9,10},{10,1... | collective-permute-start | bytes 98312 | tf_op jit(solution)/shard_map/ppermute | solution.py:503
  42.7 0.8 %constant_dynamic-update-slice_fusion.13 = bf16[16,128,128]{2,1,0:T(8,128)(2,1)S(1)} fusion(bf16[128,128]{1,0:T(8,128)(2,1)} %get-tuple-element.14.refs_1_), kind=kLoop, calls=%fused_computation.15 | loop fusion | bytes 65536
  43.5 1.9 %collective-permute-done.8 = bf16[1,128,128]{2,1,0:T(8,128)(2,1)S(1)} collective-permute-done((bf16[1,128,128]{2,1,0:T(8,128)(2,1)}, bf16[1,128,128]{2,1,0:T(8,128)(2,1)S(1)}, u32[]{:S(2)}, u32[]{:S(2)}) %collective-permute-start.8) | collective-permute-done | bytes 32800 | tf_op jit(solution)/shard_map/ppermute | solution.py:503
  45.3 1.3 %collective-permute-done.7 = bf16[1,128,128]{2,1,0:T(8,128)(2,1)S(1)} collective-permute-done((bf16[1,128,128]{2,1,0:T(8,128)(2,1)}, bf16[1,128,128]{2,1,0:T(8,128)(2,1)S(1)}, u32[]{:S(2)}, u32[]{:S(2)}) %collective-permute-start.7) | collective-permute-done | bytes 32800 | tf_op jit(solution)/shard_map/ppermute | solution.py:503
  46.7 2.5 %collective-permute-start.12 = (bf16[4,128,128]{2,1,0:T(8,128)(2,1)S(1)}, bf16[4,128,128]{2,1,0:T(8,128)(2,1)S(1)}, u32[]{:S(2)}, u32[]{:S(2)}) collective-permute-start(bf16[4,128,128]{2,1,0:T(8,128)(2,1)S(1)} %pad_maximum_fusion.1), channel_id=1, source_target_pairs={{0,20},{4,16},{8,28},{12,24},{16,4},{20,0},{24,12},{28,8},{1,21},{... | collective-permute-start | bytes 393224 | tf_op jit(solution)/shard_map/ppermute | solution.py:497
  50.3 5.0 %collective-permute-done.10 = bf16[4,128,128]{2,1,0:T(8,128)(2,1)S(1)} collective-permute-done((bf16[4,128,128]{2,1,0:T(8,128)(2,1)S(1)}, bf16[4,128,128]{2,1,0:T(8,128)(2,1)S(1)}, u32[]{:S(2)}, u32[]{:S(2)}) %collective-permute-start.10) | collective-permute-done | bytes 131104 | tf_op jit(solution)/shard_map/ppermute | solution.py:497
  55.4 4.5 %own_forces.1 = (f32[3,128]{1,0:T(4,128)}, bf16[512,128]{1,0:T(8,128)(2,1)}) custom-call(s32[3]{0:T(128)} %pad_add_fusion.refs_1_.refs_0_, bf16[128,128]{1,0:T(8,128)(2,1)} %get-tuple-element.14.refs_1_, bf16[896,256]{1,0:T(8,128)(2,1)} %get-tuple-element.17.refs_2_, f32[32,8,128]{2,1,0:T(8,128)} %get-tuple-element.15.refs_3_, ...), custom_call_target="tpu_custom_call" | custom-call | flops 5000000000 | bytes 2000000 | tf_op jit(solution)/shard_map/own_forces/pallas_call | solution.py:525
  60.0 0.8 %copy-done.7 = bf16[16,128,128]{2,1,0:T(8,128)(2,1)} copy-done((bf16[16,128,128]{2,1,0:T(8,128)(2,1)}, bf16[16,128,128]{2,1,0:T(8,128)(2,1)S(1)}, u32[]{:S(2)}) %copy-start.7) | copy-done | bytes 524312
  60.8 8.6 %backward.1 = f32[3,128]{1,0:T(4,128)} custom-call(s32[3]{0:T(128)} %pad_add_fusion.refs_1_.refs_0_, bf16[16,128,128]{2,1,0:T(8,128)(2,1)} %copy-done.3, bf16[16,128,128]{2,1,0:T(8,128)(2,1)} %copy-done.7, f32[32,8,128]{2,1,0:T(8,128)} %get-tuple-element.15.refs_3_, f32[64,128]{1,0:T(8,128)} %get-tuple-element.16.refs_4_, ...), custom_call_target="tpu_custom_call" | custom-call | flops 5000000000 | bytes 2000000 | tf_op jit(solution)/shard_map/backward/pallas_call | solution.py:525
  69.4 1.2 %copy.15 = f32[1,1,1,3,128]{4,2,3,1,0:T(1,128)} copy(f32[1,1,1,3,128]{4,3,2,1,0:T(4,128)} %bitcast.30) | data formatting | bytes 3072
  (45 shorter events, 4.3 us)
Async XLA Ops:
  0.6 0.7 copy-start.4
  3.3 11.0 %copy-start = (bf16[144,128]{1,0:T(8,128)(2,1)S(1)}, bf16[144,128]{1,0:T(8,128)(2,1)}, u32[]{:S(2)}) copy-start(bf16[144,128]{1,0:T(8,128)(2,1)} %pack.1) | copy-start | bytes 110596
  3.3 7.0 %collective-permute-start.2 = (bf16[1,144,128]{2,1,0:T(8,128)(2,1)}, bf16[1,144,128]{2,1,0:T(8,128)(2,1)S(1)}, u32[]{:S(2)}, u32[]{:S(2)}) collective-permute-start(bf16[1,144,128]{2,1,0:T(8,128)(2,1)} %bitcast.19), channel_id=1, source_target_pairs={{0,3},{1,0},{2,1},{3,2},{4,7},{5,4},{6,5},{7,6},{8,11},{9,8},{10,9... | collective-permute-start | bytes 110600 | tf_op jit(solution)/shard_map/ppermute | solution.py:503
  8.3 5.1 %collective-permute-start.1 = (bf16[1,144,128]{2,1,0:T(8,128)(2,1)}, bf16[1,144,128]{2,1,0:T(8,128)(2,1)S(1)}, u32[]{:S(2)}, u32[]{:S(2)}) collective-permute-start(bf16[1,144,128]{2,1,0:T(8,128)(2,1)} %bitcast.20), channel_id=1, source_target_pairs={{0,2},{1,3},{2,0},{3,1},{4,6},{5,7},{6,4},{7,5},{8,10},{9,11},{10,... | collective-permute-start | bytes 110600 | tf_op jit(solution)/shard_map/ppermute | solution.py:503
  8.3 6.0 %collective-permute-start = (bf16[1,144,128]{2,1,0:T(8,128)(2,1)}, bf16[1,144,128]{2,1,0:T(8,128)(2,1)S(1)}, u32[]{:S(2)}, u32[]{:S(2)}) collective-permute-start(bf16[1,144,128]{2,1,0:T(8,128)(2,1)} %bitcast.21), channel_id=1, source_target_pairs={{0,1},{1,2},{2,3},{3,0},{4,5},{5,6},{6,7},{7,4},{8,9},{9,10},{10,1... | collective-permute-start | bytes 110600 | tf_op jit(solution)/shard_map/ppermute | solution.py:503
  14.3 8.4 %collective-permute-start.5 = (bf16[4,144,128]{2,1,0:T(8,128)(2,1)S(1)}, bf16[4,144,128]{2,1,0:T(8,128)(2,1)S(1)}, u32[]{:S(2)}, u32[]{:S(2)}) collective-permute-start(bf16[4,144,128]{2,1,0:T(8,128)(2,1)S(1)} %pad_maximum_fusion), channel_id=1, source_target_pairs={{0,20},{4,16},{8,28},{12,24},{16,4},{20,0},{24,12},{28,8},{1,21},{... | collective-permute-start | bytes 442376 | tf_op jit(solution)/shard_map/ppermute | solution.py:497
  16.8 5.8 %collective-permute-start.4 = (bf16[4,144,128]{2,1,0:T(8,128)(2,1)S(1)}, bf16[4,144,128]{2,1,0:T(8,128)(2,1)S(1)}, u32[]{:S(2)}, u32[]{:S(2)}) collective-permute-start(bf16[4,144,128]{2,1,0:T(8,128)(2,1)S(1)} %pad_maximum_fusion), channel_id=1, source_target_pairs={{0,16},{4,20},{8,24},{12,28},{16,0},{20,4},{24,8},{28,12},{1,17},{... | collective-permute-start | bytes 442376 | tf_op jit(solution)/shard_map/ppermute | solution.py:497
  17.4 5.2 %collective-permute-start.3 = (bf16[4,144,128]{2,1,0:T(8,128)(2,1)S(1)}, bf16[4,144,128]{2,1,0:T(8,128)(2,1)S(1)}, u32[]{:S(2)}, u32[]{:S(2)}) collective-permute-start(bf16[4,144,128]{2,1,0:T(8,128)(2,1)S(1)} %pad_maximum_fusion), channel_id=1, source_target_pairs={{0,4},{4,0},{8,12},{12,8},{16,20},{20,16},{24,28},{28,24},{1,5},{5... | collective-permute-start | bytes 442376 | tf_op jit(solution)/shard_map/ppermute | solution.py:497
  22.7 5.6 %copy-start.2 = (bf16[16,144,128]{2,1,0:T(8,128)(2,1)}, bf16[16,144,128]{2,1,0:T(8,128)(2,1)S(1)}, u32[]{:S(2)}) copy-start(bf16[16,144,128]{2,1,0:T(8,128)(2,1)S(1)} %constant_dynamic-update-slice_fusion.refs_2_) | copy-start | bytes 1769476
  22.7 6.1 %collective-permute-start.6 = (bf16[16,144,128]{2,1,0:T(8,128)(2,1)S(1)}, bf16[16,144,128]{2,1,0:T(8,128)(2,1)S(1)}, u32[]{:S(2)}, u32[]{:S(2)}) collective-permute-start(bf16[16,144,128]{2,1,0:T(8,128)(2,1)S(1)} %constant_dynamic-update-slice_fusion.refs_2_), channel_id=1, source_target_pairs={{0,8},{8,0},{16,24},{24,16},{1,9},{9,1},{17,25},{25,17},{2,10},{10... | collective-permute-start | bytes 1769480 | tf_op jit(solution)/shard_map/ppermute | solution.py:516
  22.8 0.7 copy-start.5
  28.8 0.8 %copy-start.6 = (bf16[16,144,128]{2,1,0:T(8,128)(2,1)}, bf16[16,144,128]{2,1,0:T(8,128)(2,1)S(1)}, u32[]{:S(2)}) copy-start(bf16[16,144,128]{2,1,0:T(8,128)(2,1)S(1)} %collective-permute-done.6.refs_3_) | copy-start | bytes 1769476
  39.2 7.4 %copy-start.1 = (bf16[128,128]{1,0:T(8,128)(2,1)S(1)}, bf16[128,128]{1,0:T(8,128)(2,1)}, u32[]{:S(2)}) copy-start(bf16[128,128]{1,0:T(8,128)(2,1)} %get-tuple-element.14.refs_1_) | copy-start | bytes 98308
  39.2 4.2 %collective-permute-start.9 = (bf16[1,128,128]{2,1,0:T(8,128)(2,1)}, bf16[1,128,128]{2,1,0:T(8,128)(2,1)S(1)}, u32[]{:S(2)}, u32[]{:S(2)}) collective-permute-start(bf16[1,128,128]{2,1,0:T(8,128)(2,1)} %bitcast.23), channel_id=1, source_target_pairs={{0,3},{1,0},{2,1},{3,2},{4,7},{5,4},{6,5},{7,6},{8,11},{9,8},{10,9... | collective-permute-start | bytes 98312 | tf_op jit(solution)/shard_map/ppermute | solution.py:503
  40.3 5.1 %collective-permute-start.8 = (bf16[1,128,128]{2,1,0:T(8,128)(2,1)}, bf16[1,128,128]{2,1,0:T(8,128)(2,1)S(1)}, u32[]{:S(2)}, u32[]{:S(2)}) collective-permute-start(bf16[1,128,128]{2,1,0:T(8,128)(2,1)} %bitcast.24), channel_id=1, source_target_pairs={{0,2},{1,3},{2,0},{3,1},{4,6},{5,7},{6,4},{7,5},{8,10},{9,11},{10,... | collective-permute-start | bytes 98312 | tf_op jit(solution)/shard_map/ppermute | solution.py:503
  40.7 5.9 %collective-permute-start.7 = (bf16[1,128,128]{2,1,0:T(8,128)(2,1)}, bf16[1,128,128]{2,1,0:T(8,128)(2,1)S(1)}, u32[]{:S(2)}, u32[]{:S(2)}) collective-permute-start(bf16[1,128,128]{2,1,0:T(8,128)(2,1)} %bitcast.25), channel_id=1, source_target_pairs={{0,1},{1,2},{2,3},{3,0},{4,5},{5,6},{6,7},{7,4},{8,9},{9,10},{10,1... | collective-permute-start | bytes 98312 | tf_op jit(solution)/shard_map/ppermute | solution.py:503
  46.7 8.6 %collective-permute-start.12 = (bf16[4,128,128]{2,1,0:T(8,128)(2,1)S(1)}, bf16[4,128,128]{2,1,0:T(8,128)(2,1)S(1)}, u32[]{:S(2)}, u32[]{:S(2)}) collective-permute-start(bf16[4,128,128]{2,1,0:T(8,128)(2,1)S(1)} %pad_maximum_fusion.1), channel_id=1, source_target_pairs={{0,20},{4,16},{8,28},{12,24},{16,4},{20,0},{24,12},{28,8},{1,21},{... | collective-permute-start | bytes 393224 | tf_op jit(solution)/shard_map/ppermute | solution.py:497
  49.2 6.1 %collective-permute-start.11 = (bf16[4,128,128]{2,1,0:T(8,128)(2,1)S(1)}, bf16[4,128,128]{2,1,0:T(8,128)(2,1)S(1)}, u32[]{:S(2)}, u32[]{:S(2)}) collective-permute-start(bf16[4,128,128]{2,1,0:T(8,128)(2,1)S(1)} %pad_maximum_fusion.1), channel_id=1, source_target_pairs={{0,16},{4,20},{8,24},{12,28},{16,0},{20,4},{24,8},{28,12},{1,17},{... | collective-permute-start | bytes 393224 | tf_op jit(solution)/shard_map/ppermute | solution.py:497
  49.7 5.6 %collective-permute-start.10 = (bf16[4,128,128]{2,1,0:T(8,128)(2,1)S(1)}, bf16[4,128,128]{2,1,0:T(8,128)(2,1)S(1)}, u32[]{:S(2)}, u32[]{:S(2)}) collective-permute-start(bf16[4,128,128]{2,1,0:T(8,128)(2,1)S(1)} %pad_maximum_fusion.1), channel_id=1, source_target_pairs={{0,4},{4,0},{8,12},{12,8},{16,20},{20,16},{24,28},{28,24},{1,5},{5... | collective-permute-start | bytes 393224 | tf_op jit(solution)/shard_map/ppermute | solution.py:497
  55.3 4.6 %copy-start.3 = (bf16[16,128,128]{2,1,0:T(8,128)(2,1)}, bf16[16,128,128]{2,1,0:T(8,128)(2,1)S(1)}, u32[]{:S(2)}) copy-start(bf16[16,128,128]{2,1,0:T(8,128)(2,1)S(1)} %constant_dynamic-update-slice_fusion.7.refs_1_) | copy-start | bytes 1572868
  55.4 4.6 %collective-permute-start.13 = (bf16[16,128,128]{2,1,0:T(8,128)(2,1)S(1)}, bf16[16,128,128]{2,1,0:T(8,128)(2,1)S(1)}, u32[]{:S(2)}, u32[]{:S(2)}) collective-permute-start(bf16[16,128,128]{2,1,0:T(8,128)(2,1)S(1)} %constant_dynamic-update-slice_fusion.7.refs_1_), channel_id=1, source_target_pairs={{0,8},{8,0},{16,24},{24,16},{1,9},{9,1},{17,25},{25,17},{2,10},{10... | collective-permute-start | bytes 1572872 | tf_op jit(solution)/shard_map/ppermute | solution.py:516
  60.0 0.8 %copy-start.7 = (bf16[16,128,128]{2,1,0:T(8,128)(2,1)}, bf16[16,128,128]{2,1,0:T(8,128)(2,1)S(1)}, u32[]{:S(2)}) copy-start(bf16[16,128,128]{2,1,0:T(8,128)(2,1)S(1)} %collective-permute-done.13.refs_2_) | copy-start | bytes 1572868
where the time goes:
time: 71.1 us; the launch traced here: 70.6 us
  Pallas kernels  28.1 us (40%)
  waiting for transfers between devices  17.1 us (24%)
  starting transfers between devices  16.8 us (24%)
  local copies, waits for them, and re-layouts  6.64 us (9%)
  between operations  1.46 us (2%)
    pallas_call x5, Pallas kernels, call(): pl.pallas_call(kernel, name=name, out_shape=outs, in_specs=specs, out_spe...  28.1 us
    ppermute x6, waiting for transfers between devices, shifted(): return lax.ppermute(value, ('gx', 'gy'), moves)  9.73 us
    ppermute x6, starting transfers between devices, gather_cells(): lax.ppermute(value, 'gz', [(i, (i + s) % nz) for i in range(nz)])  9.5 us
    ppermute x6, waiting for transfers between devices, gather_cells(): lax.ppermute(value, 'gz', [(i, (i + s) % nz) for i in range(nz)])  7.33 us
    ppermute x6, starting transfers between devices, shifted(): return lax.ppermute(value, ('gx', 'gy'), moves)  7.11 us
    unnamed x30, local copies, waits for them, and re-layouts  5.9 us
  transfers between devices with their start and end apart: 14, of which 7 were waited for; matrix products, arithmetic and copies ran while one was open for 4% of the time, Pallas kernels for 12%

commit v1 on v0

--- a/solution.py
+++ b/solution.py
@@ -189,7 +189,7 @@
     live_col = lax.broadcasted_iota(jnp.int32, (n, channels), 0) < count_ref[0]
     rows = features_ref[...].astype(F32)
     out_ref[0:n, :] = jnp.where(live_col, rows, 0.0).astype(BF16)
-    pos = positions_ref[...]
+    pos = jnp.concatenate([positions_ref[a] for a in range(3)], axis=0)
     coarse = pos.astype(BF16).astype(F32)
     fine = pos - coarse
     living = (lax.broadcasted_iota(jnp.int32, (1, n), 1) < count_ref[0]).astype(F32)
@@ -252,7 +252,10 @@
     groups = half_cells // group
     halves = (near_ref, far_ref)
     w_charge = w_charge_ref[...]
-    bias = bias_ref[...]
+    diagonal = lax.broadcasted_iota(jnp.int32, (charge_ch, charge_ch), 0) == (
+        lax.broadcasted_iota(jnp.int32, (charge_ch, charge_ch), 1)
+    )
+    bias = jnp.sum(jnp.where(diagonal, bias_ref[...], 0.0), axis=1, keepdims=True)
 
     total = jnp.zeros((charge_ch, 1), F32)
     live_total = jnp.zeros((1, 1), F32)
@@ -482,10 +485,11 @@
     near = pair_force(
         sizes, own, lambda t: places_ref[block_place(sizes, odd, blocks[t])], strength_scr, n
     )
-    out_ref[...] = force_ref[...] + jnp.concatenate([near[a] - slope[a] for a in range(3)], axis=0)
-
-
-def gather_cells(rows, sizes):
+    for a in range(3):
+        out_ref[a] = force_ref[a : a + 1, :] + near[a] - slope[a]
+
+
+def gather_cells(rows, sizes, beside):
     nx, ny, nz = sizes
     pairs = nx // 2
 
@@ -513,8 +517,9 @@
     else:
         value = jnp.concatenate([value] + [shifted(value, 0, dy) for dy in range(1, ny)], axis=0)
         value = jnp.concatenate([value] + [shifted(value, dx, 0) for dx in range(1, pairs)], axis=0)
+    value, *beside = lax.optimization_barrier((value, *beside))
     other = lax.ppermute(value, "gx", [(i, i ^ 1) for i in range(nx)])
-    return value, other
+    return value, other, *beside
 
 
 def call(kernel, name, outs, scratch, smem, operands, flops):
@@ -569,10 +574,9 @@
         [shape((n + 16, channels), BF16)],
         [],
         1,
-        [count, own_rows, positions[0, 0, 0]],
+        [count, own_rows, positions.reshape(3, 1, n)],
         1000,
     )
-    near, far = gather_cells(packed, sizes)
     (filt,) = call(
         lambda *refs: fold_kernel(scale_long, *refs),
         "fold_filter",
@@ -582,6 +586,7 @@
         [k_filter, k_index],
         1_000_000_000,
     )
+    near, far, filt = gather_cells(packed, sizes, (filt,))
     updated, energy, grad, field, neutral, places, xcat = call(
         lambda *refs: forward_kernel(sizes, group, *refs),
         "forward",
@@ -610,13 +615,12 @@
             w_mix,
             w_long,
             w_charge,
-            charge_bias[:, None],
+            charge_bias[None, :],
             w_energy[None, :],
             filt,
         ],
         5_000_000_000,
     )
-    grad_near, grad_far = gather_cells(grad, sizes)
     force, lifted = call(
         lambda *refs: own_kernel(sizes, *refs),
         "own_forces",
@@ -626,10 +630,11 @@
         [meta, grad, field, places, xcat, w_proj, w_mix, w_long],
         5_000_000_000,
     )
+    grad_near, grad_far, force, lifted = gather_cells(grad, sizes, (force, lifted))
     (forces,) = call(
         lambda *refs: backward_kernel(sizes, group, *refs),
         "backward",
-        [shape((3, n), F32)],
+        [shape((3, 1, n), F32)],
         [
             pltpu.VMEM((wide, 256), F32),
             pltpu.VMEM((wide, 256), BF16),
@@ -643,7 +648,7 @@
     return (
         updated[None, None, None],
         energy[None, None],
-        forces[None, None, None],
+        forces.reshape(positions.shape),
     )
 
 

time: 71.1 us -> 64.9 us (0.913)
  local copies, waits for them, and re-layouts: 6.64 us -> 2.61 us
  waiting for transfers between devices: 17.1 us -> 14.1 us
  starting transfers between devices: 16.8 us -> 17.6 us
    ppermute x6, waiting for transfers between devices: 7.33 us -> 1.23 us  [gather_cells(): lax.ppermute(value, 'gz', [(i, (i + s) % nz) for i in range(nz)])]
    unnamed x30 -> x24, local copies, waits for them, and re-layouts: 5.9 us -> 2.57 us
    ppermute x2, waiting for transfers between devices: 0.01 us -> 3.17 us  [gather_cells(): other = lax.ppermute(value, 'gx', [(i, i ^ 1) for i in range(nx)])]
    ppermute x6, starting transfers between devices: 9.5 us -> 10.4 us  [gather_cells(): lax.ppermute(value, 'gz', [(i, (i + s) % nz) for i in range(nz)])]
  transfers between devices with their start and end apart: 14 -> 14, of which waited for: 7 -> 6; matrix products, arithmetic and copies ran while one was open for 4% -> 3% of each run, Pallas kernels for 12% -> 13%
where the time goes in v1:
time: 64.9 us; the launch traced here: 64.6 us
  Pallas kernels  28.1 us (43%)
  starting transfers between devices  17.6 us (27%)
  waiting for transfers between devices  14.1 us (22%)
  local copies, waits for them, and re-layouts  2.61 us (4%)
  between operations  1.43 us (2%)
  other arithmetic  0.75 us (1%)
    pallas_call x5, Pallas kernels, call(): pl.pallas_call(kernel, name=name, out_shape=outs, in_specs=specs, out_spe...  28.1 us
    ppermute x6, starting transfers between devices, gather_cells(): lax.ppermute(value, 'gz', [(i, (i + s) % nz) for i in range(nz)])  10.4 us
    ppermute x6, waiting for transfers between devices, shifted(): return lax.ppermute(value, ('gx', 'gy'), moves)  9.69 us
    ppermute x6, starting transfers between devices, shifted(): return lax.ppermute(value, ('gx', 'gy'), moves)  7.11 us
    ppermute x2, waiting for transfers between devices, gather_cells(): other = lax.ppermute(value, 'gx', [(i, i ^ 1) for i in range(nx)])  3.17 us
    unnamed x24, local copies, waits for them, and re-layouts  2.57 us
  transfers between devices with their start and end apart: 14, of which 6 were waited for; matrix products, arithmetic and copies ran while one was open for 3% of the time, Pallas kernels for 13%

profile of v1, /device:TPU:0, one launch (start us, length us, event | category | flops | bytes accessed | tf_op | source)
XLA Modules:
  0.0 64.6 jit_solution(6736416972327252925)
XLA Ops:
  1.3 1.4 %pack.1 = bf16[144,128]{1,0:T(8,128)(2,1)} custom-call(s32[1]{0:T(128)} %bitcast.17.count_ref, bf16[128,128]{1,0:T(8,128)(2,1)} %bitcast.27, f32[3,1,128]{2,1,0:T(1,128)} %bitcast.29), custom_call_target="tpu_custom_call" | custom-call | flops 1000 | bytes 2000000 | tf_op jit(solution)/shard_map/pack/pallas_call | solution.py:530
  2.7 5.0 %collective-permute-start.2 = (bf16[1,144,128]{2,1,0:T(8,128)(2,1)}, bf16[1,144,128]{2,1,0:T(8,128)(2,1)S(1)}, u32[]{:S(2)}, u32[]{:S(2)}) collective-permute-start(bf16[1,144,128]{2,1,0:T(8,128)(2,1)} %bitcast.19), channel_id=1, source_target_pairs={{0,3},{1,0},{2,1},{3,2},{4,7},{5,4},{6,5},{7,6},{8,11},{9,8},{10,9... | collective-permute-start | bytes 110600 | tf_op jit(solution)/shard_map/ppermute | solution.py:507
  7.7 1.0 %collective-permute-start = (bf16[1,144,128]{2,1,0:T(8,128)(2,1)}, bf16[1,144,128]{2,1,0:T(8,128)(2,1)S(1)}, u32[]{:S(2)}, u32[]{:S(2)}) collective-permute-start(bf16[1,144,128]{2,1,0:T(8,128)(2,1)} %bitcast.21), channel_id=1, source_target_pairs={{0,1},{1,2},{2,3},{3,0},{4,5},{5,6},{6,7},{7,4},{8,9},{9,10},{10,1... | collective-permute-start | bytes 110600 | tf_op jit(solution)/shard_map/ppermute | solution.py:507
  8.7 0.8 %constant_dynamic-update-slice_fusion.6 = bf16[16,144,128]{2,1,0:T(8,128)(2,1)S(1)} fusion(bf16[144,128]{1,0:T(8,128)(2,1)} %pack.1), kind=kLoop, calls=%fused_computation.8 | loop fusion | bytes 73728
  9.5 4.1 %fold_filter.1.refs_11_.refs_8_ = f32[7,256,128]{2,1,0:T(8,128)} custom-call(f32[64,2048]{1,0:T(8,128)} %refs_0_.1, s32[3,2048]{1,0:T(4,128)} %refs_1_.1), custom_call_target="tpu_custom_call" | custom-call | flops 1000000000 | bytes 2000000 | tf_op jit(solution)/shard_map/fold_filter/pallas_call | solution.py:530
  13.7 2.5 %collective-permute-start.5 = (bf16[4,144,128]{2,1,0:T(8,128)(2,1)S(1)}, bf16[4,144,128]{2,1,0:T(8,128)(2,1)S(1)}, u32[]{:S(2)}, u32[]{:S(2)}) collective-permute-start(bf16[4,144,128]{2,1,0:T(8,128)(2,1)S(1)} %pad_maximum_fusion), channel_id=1, source_target_pairs={{0,20},{4,16},{8,28},{12,24},{16,4},{20,0},{24,12},{28,8},{1,21},{... | collective-permute-start | bytes 442376 | tf_op jit(solution)/shard_map/ppermute | solution.py:501
  16.2 0.5 collective-permute-start.4
  16.8 0.5 collective-permute-start.3
  17.3 5.2 %collective-permute-done.3 = bf16[4,144,128]{2,1,0:T(8,128)(2,1)S(1)} collective-permute-done((bf16[4,144,128]{2,1,0:T(8,128)(2,1)S(1)}, bf16[4,144,128]{2,1,0:T(8,128)(2,1)S(1)}, u32[]{:S(2)}, u32[]{:S(2)}) %collective-permute-start.3) | collective-permute-done | bytes 147488 | tf_op jit(solution)/shard_map/ppermute | solution.py:501
  22.8 0.7 %pad_add_fusion.refs_1_.refs_0_ = s32[3]{0:T(128)} fusion(s32[1]{0:T(128)} %bitcast.3, s32[1]{0:T(128)} %bitcast.2, s32[1]{0:T(128)} %bitcast.1), kind=kLoop, calls=%fused_computation.16 | loop fusion | flops 6 | bytes 24 | tf_op jit(solution)/shard_map/stack | solution.py:567
  23.5 1.3 %collective-permute-done.6.refs_3_ = bf16[16,144,128]{2,1,0:T(8,128)(2,1)S(1)} collective-permute-done((bf16[16,144,128]{2,1,0:T(8,128)(2,1)S(1)}, bf16[16,144,128]{2,1,0:T(8,128)(2,1)S(1)}, u32[]{:S(2)}, u32[]{:S(2)}) %collective-permute-start.6) | collective-permute-done | bytes 589856 | tf_op jit(solution)/shard_map/ppermute | solution.py:521
  24.7 0.8 %copy-done.4 = bf16[16,144,128]{2,1,0:T(8,128)(2,1)} copy-done((bf16[16,144,128]{2,1,0:T(8,128)(2,1)}, bf16[16,144,128]{2,1,0:T(8,128)(2,1)S(1)}, u32[]{:S(2)}) %copy-start.4) | copy-done | bytes 589848
  25.6 9.6 %forward.1 = (bf16[128,128]{1,0:T(8,128)(2,1)}, f32[1,128]{1,0:T(1,128)}, bf16[128,128]{1,0:T(8,128)(2,1)}, bf16[896,256]{1,0:T(8,128)(2,1)}, f32[64,128]{1,0:T(...) custom-call(s32[1]{0:T(128)} %bitcast.18.refs_0_, s32[3]{0:T(128)} %pad_add_fusion.refs_1_.refs_0_, ...), custom_call_target="tpu_custom_call" | custom-call | flops 5000000000 | bytes 2000000 | tf_op jit(solution)/shard_map/forward/pallas_call | solution.py:530
  35.2 3.1 %collective-permute-start.9 = (bf16[1,128,128]{2,1,0:T(8,128)(2,1)}, bf16[1,128,128]{2,1,0:T(8,128)(2,1)S(1)}, u32[]{:S(2)}, u32[]{:S(2)}) collective-permute-start(bf16[1,128,128]{2,1,0:T(8,128)(2,1)} %bitcast.23), channel_id=1, source_target_pairs={{0,3},{1,0},{2,1},{3,2},{4,7},{5,4},{6,5},{7,6},{8,11},{9,8},{10,9... | collective-permute-start | bytes 98312 | tf_op jit(solution)/shard_map/ppermute | solution.py:507
  38.3 0.8 %collective-permute-start.8 = (bf16[1,128,128]{2,1,0:T(8,128)(2,1)}, bf16[1,128,128]{2,1,0:T(8,128)(2,1)S(1)}, u32[]{:S(2)}, u32[]{:S(2)}) collective-permute-start(bf16[1,128,128]{2,1,0:T(8,128)(2,1)} %bitcast.24), channel_id=1, source_target_pairs={{0,2},{1,3},{2,0},{3,1},{4,6},{5,7},{6,4},{7,5},{8,10},{9,11},{10,... | collective-permute-start | bytes 98312 | tf_op jit(solution)/shard_map/ppermute | solution.py:507
  39.5 4.4 %own_forces.1 = (f32[3,128]{1,0:T(4,128)}, bf16[512,128]{1,0:T(8,128)(2,1)}) custom-call(s32[3]{0:T(128)} %pad_add_fusion.refs_1_.refs_0_, bf16[128,128]{1,0:T(8,128)(2,1)} %get-tuple-element.21.refs_1_, bf16[896,256]{1,0:T(8,128)(2,1)} %get-tuple-element.22.refs_2_, f32[32,8,128]{2,1,0:T(8,128)} %get-tuple-element.23.refs_3_, ...), custom_call_target="tpu_custom_call" | custom-call | flops 5000000000 | bytes 2000000 | tf_op jit(solution)/shard_map/own_forces/pallas_call | solution.py:530
  43.9 1.2 %collective-permute-done.7 = bf16[1,128,128]{2,1,0:T(8,128)(2,1)S(1)} collective-permute-done((bf16[1,128,128]{2,1,0:T(8,128)(2,1)}, bf16[1,128,128]{2,1,0:T(8,128)(2,1)S(1)}, u32[]{:S(2)}, u32[]{:S(2)}) %collective-permute-start.7) | collective-permute-done | bytes 32800 | tf_op jit(solution)/shard_map/ppermute | solution.py:507
  45.1 2.5 %collective-permute-start.12 = (bf16[4,128,128]{2,1,0:T(8,128)(2,1)S(1)}, bf16[4,128,128]{2,1,0:T(8,128)(2,1)S(1)}, u32[]{:S(2)}, u32[]{:S(2)}) collective-permute-start(bf16[4,128,128]{2,1,0:T(8,128)(2,1)S(1)} %pad_maximum_fusion.1), channel_id=1, source_target_pairs={{0,20},{4,16},{8,28},{12,24},{16,4},{20,0},{24,12},{28,8},{1,21},{... | collective-permute-start | bytes 393224 | tf_op jit(solution)/shard_map/ppermute | solution.py:501
  47.6 0.5 collective-permute-start.11
  48.1 0.5 collective-permute-start.10
  48.7 4.4 %collective-permute-done.10 = bf16[4,128,128]{2,1,0:T(8,128)(2,1)S(1)} collective-permute-done((bf16[4,128,128]{2,1,0:T(8,128)(2,1)S(1)}, bf16[4,128,128]{2,1,0:T(8,128)(2,1)S(1)}, u32[]{:S(2)}, u32[]{:S(2)}) %collective-permute-start.10) | collective-permute-done | bytes 131104 | tf_op jit(solution)/shard_map/ppermute | solution.py:501
  53.3 1.9 %collective-permute-done.13.refs_2_ = bf16[16,128,128]{2,1,0:T(8,128)(2,1)S(1)} collective-permute-done((bf16[16,128,128]{2,1,0:T(8,128)(2,1)S(1)}, bf16[16,128,128]{2,1,0:T(8,128)(2,1)S(1)}, u32[]{:S(2)}, u32[]{:S(2)}) %collective-permute-start.13) | collective-permute-done | bytes 524320 | tf_op jit(solution)/shard_map/ppermute | solution.py:521
  55.2 0.8 %copy-done.5 = bf16[16,128,128]{2,1,0:T(8,128)(2,1)} copy-done((bf16[16,128,128]{2,1,0:T(8,128)(2,1)}, bf16[16,128,128]{2,1,0:T(8,128)(2,1)S(1)}, u32[]{:S(2)}) %copy-start.5) | copy-done | bytes 524312
  56.0 8.6 %backward.1 = f32[3,1,128]{2,1,0:T(1,128)} custom-call(s32[3]{0:T(128)} %pad_add_fusion.refs_1_.refs_0_, bf16[16,128,128]{2,1,0:T(8,128)(2,1)} %copy-done.3, bf16[16,128,128]{2,1,0:T(8,128)(2,1)} %copy-done.5, f32[32,8,128]{2,1,0:T(8,128)} %get-tuple-element.23.refs_3_, f32[64,128]{1,0:T(8,128)} %get-tuple-element.28.refs_4_, ...), custom_call_target="tpu_custom_call" | custom-call | flops 5000000000 | bytes 2000000 | tf_op jit(solution)/shard_map/backward/pallas_call | solution.py:530
  (38 shorter events, 0.8 us)
Async XLA Ops:
  2.7 11.0 %collective-permute-start.2 = (bf16[1,144,128]{2,1,0:T(8,128)(2,1)}, bf16[1,144,128]{2,1,0:T(8,128)(2,1)S(1)}, u32[]{:S(2)}, u32[]{:S(2)}) collective-permute-start(bf16[1,144,128]{2,1,0:T(8,128)(2,1)} %bitcast.19), channel_id=1, source_target_pairs={{0,3},{1,0},{2,1},{3,2},{4,7},{5,4},{6,5},{7,6},{8,11},{9,8},{10,9... | collective-permute-start | bytes 110600 | tf_op jit(solution)/shard_map/ppermute | solution.py:507
  7.7 5.9 %collective-permute-start.1 = (bf16[1,144,128]{2,1,0:T(8,128)(2,1)}, bf16[1,144,128]{2,1,0:T(8,128)(2,1)S(1)}, u32[]{:S(2)}, u32[]{:S(2)}) collective-permute-start(bf16[1,144,128]{2,1,0:T(8,128)(2,1)} %bitcast.20), channel_id=1, source_target_pairs={{0,2},{1,3},{2,0},{3,1},{4,6},{5,7},{6,4},{7,5},{8,10},{9,11},{10,... | collective-permute-start | bytes 110600 | tf_op jit(solution)/shard_map/ppermute | solution.py:507
  7.7 6.0 %collective-permute-start = (bf16[1,144,128]{2,1,0:T(8,128)(2,1)}, bf16[1,144,128]{2,1,0:T(8,128)(2,1)S(1)}, u32[]{:S(2)}, u32[]{:S(2)}) collective-permute-start(bf16[1,144,128]{2,1,0:T(8,128)(2,1)} %bitcast.21), channel_id=1, source_target_pairs={{0,1},{1,2},{2,3},{3,0},{4,5},{5,6},{6,7},{7,4},{8,9},{9,10},{10,1... | collective-permute-start | bytes 110600 | tf_op jit(solution)/shard_map/ppermute | solution.py:507
  9.5 4.2 %copy-start = (bf16[144,128]{1,0:T(8,128)(2,1)S(1)}, bf16[144,128]{1,0:T(8,128)(2,1)}, u32[]{:S(2)}) copy-start(bf16[144,128]{1,0:T(8,128)(2,1)} %pack.1) | copy-start | bytes 110596
  13.7 8.9 %collective-permute-start.5 = (bf16[4,144,128]{2,1,0:T(8,128)(2,1)S(1)}, bf16[4,144,128]{2,1,0:T(8,128)(2,1)S(1)}, u32[]{:S(2)}, u32[]{:S(2)}) collective-permute-start(bf16[4,144,128]{2,1,0:T(8,128)(2,1)S(1)} %pad_maximum_fusion), channel_id=1, source_target_pairs={{0,20},{4,16},{8,28},{12,24},{16,4},{20,0},{24,12},{28,8},{1,21},{... | collective-permute-start | bytes 442376 | tf_op jit(solution)/shard_map/ppermute | solution.py:501
  16.2 6.4 %collective-permute-start.4 = (bf16[4,144,128]{2,1,0:T(8,128)(2,1)S(1)}, bf16[4,144,128]{2,1,0:T(8,128)(2,1)S(1)}, u32[]{:S(2)}, u32[]{:S(2)}) collective-permute-start(bf16[4,144,128]{2,1,0:T(8,128)(2,1)S(1)} %pad_maximum_fusion), channel_id=1, source_target_pairs={{0,16},{4,20},{8,24},{12,28},{16,0},{20,4},{24,8},{28,12},{1,17},{... | collective-permute-start | bytes 442376 | tf_op jit(solution)/shard_map/ppermute | solution.py:501
  16.8 5.8 %collective-permute-start.3 = (bf16[4,144,128]{2,1,0:T(8,128)(2,1)S(1)}, bf16[4,144,128]{2,1,0:T(8,128)(2,1)S(1)}, u32[]{:S(2)}, u32[]{:S(2)}) collective-permute-start(bf16[4,144,128]{2,1,0:T(8,128)(2,1)S(1)} %pad_maximum_fusion), channel_id=1, source_target_pairs={{0,4},{4,0},{8,12},{12,8},{16,20},{20,16},{24,28},{28,24},{1,5},{5... | collective-permute-start | bytes 442376 | tf_op jit(solution)/shard_map/ppermute | solution.py:501
  22.7 2.1 %copy-start.2 = (bf16[16,144,128]{2,1,0:T(8,128)(2,1)}, bf16[16,144,128]{2,1,0:T(8,128)(2,1)S(1)}, u32[]{:S(2)}) copy-start(bf16[16,144,128]{2,1,0:T(8,128)(2,1)S(1)} %constant_dynamic-update-slice_fusion.refs_2_) | copy-start | bytes 1769476
  22.7 2.1 %collective-permute-start.6 = (bf16[16,144,128]{2,1,0:T(8,128)(2,1)S(1)}, bf16[16,144,128]{2,1,0:T(8,128)(2,1)S(1)}, u32[]{:S(2)}, u32[]{:S(2)}) collective-permute-start(bf16[16,144,128]{2,1,0:T(8,128)(2,1)S(1)} %constant_dynamic-update-slice_fusion.refs_2_), channel_id=1, source_target_pairs={{0,8},{8,0},{16,24},{24,16},{1,9},{9,1},{17,25},{25,17},{2,10},{10... | collective-permute-start | bytes 1769480 | tf_op jit(solution)/shard_map/ppermute | solution.py:521
  24.7 0.8 %copy-start.4 = (bf16[16,144,128]{2,1,0:T(8,128)(2,1)}, bf16[16,144,128]{2,1,0:T(8,128)(2,1)S(1)}, u32[]{:S(2)}) copy-start(bf16[16,144,128]{2,1,0:T(8,128)(2,1)S(1)} %collective-permute-done.6.refs_3_) | copy-start | bytes 1769476
  35.2 8.7 %collective-permute-start.9 = (bf16[1,128,128]{2,1,0:T(8,128)(2,1)}, bf16[1,128,128]{2,1,0:T(8,128)(2,1)S(1)}, u32[]{:S(2)}, u32[]{:S(2)}) collective-permute-start(bf16[1,128,128]{2,1,0:T(8,128)(2,1)} %bitcast.23), channel_id=1, source_target_pairs={{0,3},{1,0},{2,1},{3,2},{4,7},{5,4},{6,5},{7,6},{8,11},{9,8},{10,9... | collective-permute-start | bytes 98312 | tf_op jit(solution)/shard_map/ppermute | solution.py:507
  38.3 5.6 %collective-permute-start.8 = (bf16[1,128,128]{2,1,0:T(8,128)(2,1)}, bf16[1,128,128]{2,1,0:T(8,128)(2,1)S(1)}, u32[]{:S(2)}, u32[]{:S(2)}) collective-permute-start(bf16[1,128,128]{2,1,0:T(8,128)(2,1)} %bitcast.24), channel_id=1, source_target_pairs={{0,2},{1,3},{2,0},{3,1},{4,6},{5,7},{6,4},{7,5},{8,10},{9,11},{10,... | collective-permute-start | bytes 98312 | tf_op jit(solution)/shard_map/ppermute | solution.py:507
  39.2 5.9 %collective-permute-start.7 = (bf16[1,128,128]{2,1,0:T(8,128)(2,1)}, bf16[1,128,128]{2,1,0:T(8,128)(2,1)S(1)}, u32[]{:S(2)}, u32[]{:S(2)}) collective-permute-start(bf16[1,128,128]{2,1,0:T(8,128)(2,1)} %bitcast.25), channel_id=1, source_target_pairs={{0,1},{1,2},{2,3},{3,0},{4,5},{5,6},{6,7},{7,4},{8,9},{9,10},{10,1... | collective-permute-start | bytes 98312 | tf_op jit(solution)/shard_map/ppermute | solution.py:507
  39.5 4.4 %copy-start.1 = (bf16[128,128]{1,0:T(8,128)(2,1)S(1)}, bf16[128,128]{1,0:T(8,128)(2,1)}, u32[]{:S(2)}) copy-start(bf16[128,128]{1,0:T(8,128)(2,1)} %get-tuple-element.21.refs_1_) | copy-start | bytes 98308
  45.1 8.1 %collective-permute-start.12 = (bf16[4,128,128]{2,1,0:T(8,128)(2,1)S(1)}, bf16[4,128,128]{2,1,0:T(8,128)(2,1)S(1)}, u32[]{:S(2)}, u32[]{:S(2)}) collective-permute-start(bf16[4,128,128]{2,1,0:T(8,128)(2,1)S(1)} %pad_maximum_fusion.1), channel_id=1, source_target_pairs={{0,20},{4,16},{8,28},{12,24},{16,4},{20,0},{24,12},{28,8},{1,21},{... | collective-permute-start | bytes 393224 | tf_op jit(solution)/shard_map/ppermute | solution.py:501
  47.6 5.5 %collective-permute-start.11 = (bf16[4,128,128]{2,1,0:T(8,128)(2,1)S(1)}, bf16[4,128,128]{2,1,0:T(8,128)(2,1)S(1)}, u32[]{:S(2)}, u32[]{:S(2)}) collective-permute-start(bf16[4,128,128]{2,1,0:T(8,128)(2,1)S(1)} %pad_maximum_fusion.1), channel_id=1, source_target_pairs={{0,16},{4,20},{8,24},{12,28},{16,0},{20,4},{24,8},{28,12},{1,17},{... | collective-permute-start | bytes 393224 | tf_op jit(solution)/shard_map/ppermute | solution.py:501
  48.1 5.0 %collective-permute-start.10 = (bf16[4,128,128]{2,1,0:T(8,128)(2,1)S(1)}, bf16[4,128,128]{2,1,0:T(8,128)(2,1)S(1)}, u32[]{:S(2)}, u32[]{:S(2)}) collective-permute-start(bf16[4,128,128]{2,1,0:T(8,128)(2,1)S(1)} %pad_maximum_fusion.1), channel_id=1, source_target_pairs={{0,4},{4,0},{8,12},{12,8},{16,20},{20,16},{24,28},{28,24},{1,5},{5... | collective-permute-start | bytes 393224 | tf_op jit(solution)/shard_map/ppermute | solution.py:501
  53.2 2.0 %copy-start.3 = (bf16[16,128,128]{2,1,0:T(8,128)(2,1)}, bf16[16,128,128]{2,1,0:T(8,128)(2,1)S(1)}, u32[]{:S(2)}) copy-start(bf16[16,128,128]{2,1,0:T(8,128)(2,1)S(1)} %constant_dynamic-update-slice_fusion.7.refs_1_) | copy-start | bytes 1572868
  53.2 2.0 %collective-permute-start.13 = (bf16[16,128,128]{2,1,0:T(8,128)(2,1)S(1)}, bf16[16,128,128]{2,1,0:T(8,128)(2,1)S(1)}, u32[]{:S(2)}, u32[]{:S(2)}) collective-permute-start(bf16[16,128,128]{2,1,0:T(8,128)(2,1)S(1)} %constant_dynamic-update-slice_fusion.7.refs_1_), channel_id=1, source_target_pairs={{0,8},{8,0},{16,24},{24,16},{1,9},{9,1},{17,25},{25,17},{2,10},{10... | collective-permute-start | bytes 1572872 | tf_op jit(solution)/shard_map/ppermute | solution.py:521
  55.2 0.8 %copy-start.5 = (bf16[16,128,128]{2,1,0:T(8,128)(2,1)}, bf16[16,128,128]{2,1,0:T(8,128)(2,1)S(1)}, u32[]{:S(2)}) copy-start(bf16[16,128,128]{2,1,0:T(8,128)(2,1)S(1)} %collective-permute-done.13.refs_2_) | copy-start | bytes 1572868

commit v2 on v1

v2 whole, which is shorter than its diff:
```python
import itertools
import math

import jax
import jax.numpy as jnp
import numpy as np
from jax import lax
from jax.experimental import pallas as pl
from jax.experimental.pallas import tpu as pltpu
from jax.sharding import PartitionSpec as P

CUTOFF = 0.9
SCALE = 1.0 / (CUTOFF * CUTOFF)
GAMMAS = (1.0, 3.0, 8.0, 20.0)
AXES = ("gx", "gy", "gz")
ORDERS = 7
NT = (((1,), (1,)), ((), ()))
F32 = jnp.float32
BF16 = jnp.bfloat16


def turn_series():
    nodes = np.cos(np.pi * (np.arange(200) + 0.5) / 200)
    r2 = (nodes + 1.0) / 8.0
    r = np.sqrt(r2)
    out = []
    for values in (np.cos(2 * np.pi * r), np.sin(2 * np.pi * r) / r):
        cheb = np.polynomial.chebyshev.Chebyshev.fit(r2, values, 7, domain=[0.0, 0.25])
        out.append([float(c) for c in cheb.convert(kind=np.polynomial.Polynomial).coef])
    return out


COS_SERIES, SIN_SERIES = turn_series()


def dot(a, b):
    return jnp.dot(a, b, preferred_element_type=F32)


def dot_nt(a, b):
    return lax.dot_general(a, b, NT, preferred_element_type=F32)


def sigmoid(v):
    return 1.0 / (1.0 + jnp.exp(-v))


def cos_sin(turns):
    r = turns - jnp.floor(turns + 0.5)
    r2 = r * r
    c = jnp.full_like(r2, COS_SERIES[-1])
    for coef in COS_SERIES[-2::-1]:
        c = c * r2 + coef
    s = jnp.full_like(r2, SIN_SERIES[-1])
    for coef in SIN_SERIES[-2::-1]:
        s = s * r2 + coef
    return c, s * r


def axis_tables(pos, anchor, sizes):
    order = lax.broadcasted_iota(jnp.int32, (8, pos.shape[1]), 0).astype(F32)
    tables = []
    for a in range(3):
        row = (pos[a : a + 1, :] + anchor[a]) * (1.0 / sizes[a])
        tables.append(cos_sin(order * row))
    return tables


def plane_table(first, second):
    rows = []
    for f in first:
        for s in second:
            for a in range(8):
                rows.append(f[a : a + 1, :] * s)
    return jnp.concatenate(rows, axis=0)


def derivative(table, size):
    order = lax.broadcasted_iota(jnp.int32, table[0].shape, 0).astype(F32) * (2.0 * math.pi / size)
    return (-order * table[1], order * table[0])


def spread(weights, third):
    rows = []
    for f in third:
        for c in range(ORDERS):
            rows.append((weights * f[c : c + 1, :]).astype(BF16))
    return jnp.concatenate(rows, axis=0)


def filtered(load, filt_ref, out_ref, charge_ch):
    shift = ORDERS * charge_ch
    for c in range(ORDERS):
        lo, hi = c * charge_ch, (c + 1) * charge_ch
        f0, gfb, fc, gfbc = (filt_ref[c, w * charge_ch : (w + 1) * charge_ch, :] for w in range(4))
        cos_part, sin_part = load(0, c), load(1, c)
        a_c, b_c = cos_part[:, 0:128], cos_part[:, 128:256]
        a_s, b_s = sin_part[:, 0:128], sin_part[:, 128:256]
        ra_c, rb_c, ra_s, rb_s = (pltpu.roll(v, 64, 1) for v in (a_c, b_c, a_s, b_s))
        out_ref[lo:hi, 0:128] = (f0 * a_c + gfbc * ra_s - fc * b_s + gfb * rb_c).astype(BF16)
        out_ref[lo:hi, 128:256] = (f0 * b_c - gfb * ra_c + fc * a_s + gfbc * rb_s).astype(BF16)
        out_ref[shift + lo : shift + hi, 0:128] = (
            f0 * a_s + fc * b_c - gfbc * ra_c + gfb * rb_s
        ).astype(BF16)
        out_ref[shift + lo : shift + hi, 128:256] = (
            f0 * b_s - fc * a_c - gfb * ra_s - gfbc * rb_c
        ).astype(BF16)


def field_slope(field, tables, sizes, weights, charge_ch):
    tx, ty, tz = tables
    n = tx[0].shape[1]
    planes = jnp.concatenate(
        [
            plane_table(derivative(tx, sizes[0]), ty).astype(BF16),
            plane_table(tx, derivative(ty, sizes[1])).astype(BF16),
            plane_table(tx, ty).astype(BF16),
        ],
        axis=1,
    )
    spread_field = dot(field, planes)
    slope_z = derivative(tz, sizes[2])
    total = [jnp.zeros((charge_ch, n), F32) for _ in range(3)]
    for kind in range(2):
        for c in range(ORDERS):
            lo = (kind * ORDERS + c) * charge_ch
            part = spread_field[lo : lo + charge_ch, :]
            zrow, drow = tz[kind][c : c + 1, :], slope_z[kind][c : c + 1, :]
            total[0] = total[0] + zrow * part[:, 0:n]
            total[1] = total[1] + zrow * part[:, n : 2 * n]
            total[2] = total[2] + drow * part[:, 2 * n : 3 * n]
    return [jnp.sum(t * weights, axis=0, keepdims=True) for t in total]


def place_of(meta_ref, m, half, sizes):
    nx, ny, nz = sizes
    dz = lax.rem(m, nz)
    dy = lax.rem(m // nz, ny)
    dx = m // (nz * ny)
    start = meta_ref[0] if half == 0 else meta_ref[0] + 1 - 2 * lax.rem(meta_ref[0], 2)
    cx = lax.rem(start - 2 * dx + nx, nx)
    cy = lax.rem(meta_ref[1] - dy + ny, ny)
    cz = lax.rem(meta_ref[2] - dz + nz, nz)
    return (cx.astype(F32), cy.astype(F32), cz.astype(F32))


def blocks_of(sizes):
    options = [((0, False), (1, True)) if n == 2 else ((0, False), (-1, False), (1, False)) for n in sizes]
    return list(itertools.product(*options))


def offsets(own_cols, others, block):
    result = []
    for a, (step, nearest) in enumerate(block):
        if nearest:
            d = others[a] - own_cols[a]
            d = d - jnp.where(d > 0.0, 1.0, -1.0)
        else:
            d = (others[a] + float(step)) - own_cols[a]
        result.append(d)
    return result


def pair_terms(offs, block, first_row):
    s = (offs[0] * offs[0] + offs[1] * offs[1] + offs[2] * offs[2]) * SCALE
    u = jnp.maximum(1.0 - s, 0.0)
    if all(step == 0 for step, _ in block):
        rows = lax.broadcasted_iota(jnp.int32, s.shape, 0) + first_row
        cols = lax.broadcasted_iota(jnp.int32, s.shape, 1)
        u = jnp.where(rows == cols, 0.0, u)
    e1 = jnp.exp(-s)
    e2 = e1 * e1
    e3 = e2 * e1
    e4 = e2 * e2
    e8 = e4 * e4
    e20 = e8 * e8 * e4
    return u, (e1, e3, e8, e20)


def columns(pos, n):
    return [jnp.transpose(jnp.broadcast_to(pos[a : a + 1, :], (n, n))) for a in range(3)]


def pack_kernel(count_ref, features_ref, positions_ref, out_ref):
    n, channels = features_ref.shape
    live_col = lax.broadcasted_iota(jnp.int32, (n, channels), 0) < count_ref[0]
    rows = features_ref[...].astype(F32)
    out_ref[0:n, :] = jnp.where(live_col, rows, 0.0).astype(BF16)
    pos = jnp.concatenate([positions_ref[a] for a in range(3)], axis=0)
    coarse = pos.astype(BF16).astype(F32)
    fine = pos - coarse
    living = (lax.broadcasted_iota(jnp.int32, (1, n), 1) < count_ref[0]).astype(F32)
    blank = jnp.zeros((4, n), F32)
    tail = jnp.concatenate([coarse, living, blank, fine, jnp.zeros((5, n), F32)], axis=0)
    out_ref[n : n + 16, :] = tail.astype(BF16)


def fold_kernel(scale, filter_ref, index_ref, bias_ref, energy_ref, out_ref, column_ref, row_ref):
    waves = filter_ref.shape[1]
    k = index_ref[...]
    positive = [jnp.where(k[a : a + 1, :] >= 0, 1.0, -1.0) for a in range(3)]
    sign_b = positive[0] * positive[1]
    sign_c = positive[0] * positive[2]
    size = jnp.abs(k)
    plane = size[0:1, :] * 8 + size[1:2, :]
    f = filter_ref[...] * scale
    stacked = jnp.concatenate([f, f * sign_b, f * sign_c, f * (sign_b * sign_c)], axis=0).astype(BF16)
    rows = lax.broadcasted_iota(jnp.int32, (64, waves), 0)
    charge_ch = filter_ref.shape[0]
    row_ref[...] = energy_ref[...]
    diagonal = lax.broadcasted_iota(jnp.int32, (charge_ch, charge_ch), 0) == (
        lax.broadcasted_iota(jnp.int32, (charge_ch, charge_ch), 1)
    )
    column = jnp.sum(jnp.where(diagonal, bias_ref[...], 0.0), axis=1, keepdims=True)
    column_ref[...] = jnp.broadcast_to(column, column_ref.shape)
    turn = jnp.where(lax.broadcasted_iota(jnp.int32, (charge_ch, 128), 1) < 64, -1.0, 1.0)
    for c in range(ORDERS):
        key = jnp.where(size[2:3, :] == c, plane, -1)
        chosen = jnp.where(rows == key, 1.0, 0.0).astype(BF16)
        part = dot_nt(stacked, jnp.concatenate([chosen, chosen], axis=0))
        for w in range(4):
            piece = part[w * charge_ch : (w + 1) * charge_ch, :]
            out_ref[c, w * charge_ch : (w + 1) * charge_ch, :] = piece * turn if w % 2 == 1 else piece


def block_place(sizes, odd, block):
    nx, ny, nz = sizes
    dy, dz = (-block[1][0]) % ny, (-block[2][0]) % nz
    if block[0][0] == 0:
        return 0, dy * nz + dz
    dx = odd * (nx // 2 - 1) if block[0][0] == 1 else (1 - odd) * (1 % (nx // 2))
    return 1, (dx * ny + dy) * nz + dz


def charge_kernel(
    sizes,
    group,
    meta_ref,
    near_ref,
    w_charge_ref,
    bias_ref,
    sums_ref,
    part_ref,
    places_ref,
    charge_ref,
    charge_scr,
):
    charge_ch, channels = w_charge_ref.shape
    cells = near_ref.shape[0]
    n = near_ref.shape[1] - 16
    wide = 2 * ORDERS * charge_ch
    groups = cells // group
    w_charge = w_charge_ref[...]
    bias = bias_ref[...]

    def add_charges(g, carry):
        total, live_total = carry
        for j in range(group):
            m = g * group + j
            tail = near_ref[m, n : n + 16, :].astype(F32)
            pos = tail[0:8, :] + tail[8:16, :]
            places_ref[m] = pos
            live = pos[3:4, :]
            v = dot_nt(w_charge, near_ref[m, 0:n, :]) + bias
            q = v * sigmoid(v) * live
            charge_scr[m] = q
            total = total + q
            live_total = live_total + live
        return total, live_total

    start = (jnp.zeros((charge_ch, n), F32), jnp.zeros((1, n), F32))
    total, live_total = lax.fori_loop(0, groups, add_charges, start)
    mean = jnp.sum(total, axis=1, keepdims=True) / jnp.sum(live_total, axis=1, keepdims=True)
    mean = mean.astype(BF16).astype(F32)
    charge_ref[...] = charge_scr[0]

    def structure(g):
        left, right = [], []
        for j in range(group):
            m = g * group + j
            pos = places_ref[m]
            tx, ty, tz = axis_tables(pos, place_of(meta_ref, m, 0, sizes), sizes)
            live = pos[3:4, :]
            living = jnp.concatenate([tz[0] * live, tz[1] * live], axis=0).astype(BF16)
            left.append(
                jnp.concatenate([spread((charge_scr[m] - mean) * live, tz), living], axis=0)
            )
            right.append(plane_table(tx, ty).astype(BF16))
        return dot_nt(jnp.concatenate(left, axis=1), jnp.concatenate(right, axis=1))

    sums_ref[...] = structure(0)

    def add_structure(g, _):
        sums_ref[...] += structure(g)
        return 0

    lax.fori_loop(1, groups, add_structure, 0)
    part_ref[0 : wide + 16, :] = sums_ref[...].astype(BF16)
    part_ref[wide + 16 : wide + 16 + charge_ch, :] = jnp.broadcast_to(mean, (charge_ch, 256)).astype(
        BF16
    )


def message_kernel(
    sizes,
    meta_ref,
    near_ref,
    far_ref,
    near_places_ref,
    w_proj_ref,
    w_mix_ref,
    short_ref,
    far_places_ref,
    xcat_ref,
    radial_scr,
):
    channels = near_ref.shape[2]
    n = near_ref.shape[1] - 16
    halves = (near_ref, far_ref)
    places = (near_places_ref, far_places_ref)

    def add_place(m, _):
        tail = far_ref[m, n : n + 16, :].astype(F32)
        far_places_ref[m] = tail[0:8, :] + tail[8:16, :]
        return 0

    lax.fori_loop(0, far_ref.shape[0], add_place, 0, unroll=4)
    odd = lax.rem(meta_ref[0], 2)
    own_cols = columns(near_places_ref[0], n)
    for t, block in enumerate(blocks_of(sizes)):
        half, m = block_place(sizes, odd, block)
        xcat_ref[t * n : (t + 1) * n, :] = halves[half][m, 0:n, :]
        pos = places[half][m]
        others = [pos[a : a + 1, :] for a in range(3)]
        for first in range(0, n, 32):
            cols = [c[first : first + 32, :] for c in own_cols]
            u, decays = pair_terms(offsets(cols, others, block), block, first)
            u2 = u * u
            for b in range(len(GAMMAS)):
                radial_scr[b * n + first : b * n + first + 32, t * n : (t + 1) * n] = (
                    decays[b] * u2
                ).astype(BF16)
    gathered = dot(radial_scr[...], xcat_ref[...]).astype(BF16)
    message = jnp.zeros((n, channels), F32)
    for b in range(len(GAMMAS)):
        message = message + dot(gathered[b * n : (b + 1) * n, :], w_proj_ref[b])
    short_ref[...] = dot(message.astype(BF16), w_mix_ref[...])


def cotangent_kernel(
    sizes,
    count_ref,
    meta_ref,
    sums_ref,
    part_ref,
    far_part_ref,
    places_ref,
    far_places_ref,
    charge_ref,
    short_ref,
    features_ref,
    w_long_ref,
    w_energy_ref,
    filt_ref,
    grad_ref,
    refined_ref,
    field_ref,
    neutral_ref,
):
    n, channels = features_ref.shape
    charge_ch = w_long_ref.shape[0]
    wide = 2 * ORDERS * charge_ch
    own = places_ref[0]
    live_row = own[3:4, :]

    lives = [jnp.sum(r[...], axis=0)[3:4, :] for r in (places_ref, far_places_ref)]
    lives = [jnp.sum(v, axis=1, keepdims=True) for v in lives]
    tail = wide + 16
    bases = [r[tail : tail + charge_ch, 0:1].astype(F32) for r in (part_ref, far_part_ref)]
    rests = [sums_ref[0:charge_ch, 0:1], far_part_ref[0:charge_ch, 0:1].astype(F32)]
    mean = (bases[0] * lives[0] + rests[0] + bases[1] * lives[1] + rests[1]) / (lives[0] + lives[1])
    gaps = [b - mean for b in bases]
    far_living = far_part_ref[wide : wide + 16, :].astype(F32)

    def load(kind, c):
        lo = (kind * ORDERS + c) * charge_ch
        row = kind * 8 + c
        return (
            sums_ref[lo : lo + charge_ch, :]
            + far_part_ref[lo : lo + charge_ch, :].astype(F32)
            + gaps[0] * sums_ref[wide + row : wide + row + 1, :]
            + gaps[1] * far_living[row : row + 1, :]
        )

    filtered(load, filt_ref, field_ref, charge_ch)
    neutral_ref[...] = (charge_ref[...] - mean) * live_row
    tx, ty, tz = axis_tables(own, place_of(meta_ref, 0, 0, sizes), sizes)
    lifted = dot(field_ref[...], plane_table(tx, ty).astype(BF16))
    potential = jnp.zeros((charge_ch, n), F32)
    for kind in range(2):
        for c in range(ORDERS):
            lo = (kind * ORDERS + c) * charge_ch
            potential = potential + tz[kind][c : c + 1, :] * lifted[lo : lo + charge_ch, :]
    pre_act = short_ref[...] + dot(jnp.transpose(potential).astype(BF16), w_long_ref[...])
    sig = sigmoid(pre_act)
    refined = features_ref[...].astype(F32) + pre_act * sig
    refined_ref[...] = refined
    sig_r = sigmoid(refined)
    live_rows = lax.broadcasted_iota(jnp.int32, (n, channels), 0) < count_ref[0]
    grad = (
        w_energy_ref[...]
        * (sig_r * (1.0 + refined * (1.0 - sig_r)))
        * (sig * (1.0 + pre_act * (1.0 - sig)))
    )
    grad_ref[...] = jnp.where(live_rows, grad, 0.0).astype(BF16)


def pair_force(sizes, meta_ref, places, strengths_ref, n):
    own_cols = columns(places[0][0], n)
    odd = lax.rem(meta_ref[0], 2)
    blocks = blocks_of(sizes)
    parts = [[], [], []]
    for first in range(0, n, 32):
        cols = [c[first : first + 32, :] for c in own_cols]
        acc = [jnp.zeros((32, n), F32) for _ in range(3)]
        for t, block in enumerate(blocks):
            half, m = block_place(sizes, odd, block)
            pos = places[half][m]
            offs = offsets(cols, [pos[a : a + 1, :] for a in range(3)], block)
            u, decays = pair_terms(offs, block, first)
            strength = jnp.zeros((32, n), F32)
            for b, g in enumerate(GAMMAS):
                part = strengths_ref[b * n + first : b * n + first + 32, t * n : (t + 1) * n]
                strength = strength + decays[b] * (g * u + 2.0) * part
            strength = strength * u
            for a in range(3):
                acc[a] = acc[a] + strength * offs[a]
        for a in range(3):
            parts[a].append(acc[a])
    return [
        (-2.0 * SCALE)
        * jnp.sum(jnp.transpose(jnp.concatenate(parts[a], axis=0)), axis=0, keepdims=True)
        for a in range(3)
    ]


def own_kernel(
    sizes,
    meta_ref,
    grad_ref,
    field_ref,
    places_ref,
    far_places_ref,
    xcat_ref,
    refined_ref,
    w_proj_ref,
    w_mix_ref,
    w_long_ref,
    w_energy_ref,
    updated_ref,
    energy_ref,
    force_ref,
    lifted_ref,
    strength_scr,
):
    n = grad_ref.shape[0]
    charge_ch = w_long_ref.shape[0]
    own = places_ref[0]
    refined = refined_ref[...]
    updated_ref[...] = refined.astype(BF16)
    energy_ref[...] = own[3:4, :] * jnp.sum(
        jnp.transpose(refined * sigmoid(refined) * w_energy_ref[...]), axis=0, keepdims=True
    )
    grad = grad_ref[...]
    adjoint = dot_nt(grad, w_mix_ref[...]).astype(BF16)
    rows, lifted = [], []
    for b in range(len(GAMMAS)):
        rows.append(dot_nt(adjoint, w_proj_ref[b]).astype(BF16))
        basis = dot(xcat_ref[0:n, :], w_proj_ref[b]).astype(BF16)
        lifted.append(dot(basis, w_mix_ref[...]).astype(BF16))
    lifted_ref[...] = jnp.concatenate(lifted, axis=0)
    strength_scr[...] = dot_nt(jnp.concatenate(rows, axis=0), xcat_ref[...])
    near = pair_force(sizes, meta_ref, (places_ref, far_places_ref), strength_scr, n)
    pull = dot_nt(w_long_ref[...], grad)
    tables = axis_tables(own, place_of(meta_ref, 0, 0, sizes), sizes)
    slope = field_slope(field_ref[...], tables, sizes, pull, charge_ch)
    force_ref[...] = jnp.concatenate([near[a] - slope[a] for a in range(3)], axis=0)


def pull_kernel(sizes, group, meta_ref, near_ref, places_ref, w_long_ref, sums_ref, part_ref):
    groups = near_ref.shape[0] // group

    def structure(g):
        left, right = [], []
        for j in range(group):
            m = g * group + j
            pos = places_ref[m]
            tx, ty, tz = axis_tables(pos, place_of(meta_ref, m, 0, sizes), sizes)
            left.append(spread(dot_nt(w_long_ref[...], near_ref[m]), tz))
            right.append(plane_table(tx, ty).astype(BF16))
        return dot_nt(jnp.concatenate(left, axis=1), jnp.concatenate(right, axis=1))

    sums_ref[...] = structure(0)

    def add_structure(g, _):
        sums_ref[...] += structure(g)
        return 0

    lax.fori_loop(1, groups, add_structure, 0)
    part_ref[...] = sums_ref[...].astype(BF16)


def react_kernel(
    sizes,
    meta_ref,
    near_ref,
    far_ref,
    places_ref,
    far_places_ref,
    lifted_ref,
    force_ref,
    out_ref,
    gcat_scr,
    strength_scr,
):
    n = lifted_ref.shape[1]
    halves = (near_ref, far_ref)
    odd = lax.rem(meta_ref[0], 2)
    for t, block in enumerate(blocks_of(sizes)):
        half, m = block_place(sizes, odd, block)
        gcat_scr[t * n : (t + 1) * n, :] = halves[half][m]
    strength_scr[...] = dot_nt(lifted_ref[...], gcat_scr[...])
    near = pair_force(sizes, meta_ref, (places_ref, far_places_ref), strength_scr, n)
    out_ref[...] = force_ref[...] + jnp.concatenate(near, axis=0)


def finish_kernel(
    sizes,
    meta_ref,
    sums_ref,
    far_part_ref,
    places_ref,
    neutral_ref,
    force_ref,
    filt_ref,
    out_ref,
    field_scr,
):
    charge_ch = neutral_ref.shape[0]

    def load(kind, c):
        lo = (kind * ORDERS + c) * charge_ch
        return sums_ref[lo : lo + charge_ch, :] + far_part_ref[lo : lo + charge_ch, :].astype(F32)

    filtered(load, filt_ref, field_scr, charge_ch)
    tables = axis_tables(places_ref[0], place_of(meta_ref, 0, 0, sizes), sizes)
    slope = field_slope(field_scr[...], tables, sizes, neutral_ref[...], charge_ch)
    for a in range(3):
        out_ref[a] = force_ref[a : a + 1, :] - slope[a]


def gather_cells(rows, sizes, beside):
    nx, ny, nz = sizes
    pairs = nx // 2

    def shifted(value, dx, dy):
        moves = []
        for i in range(nx):
            for j in range(ny):
                moves.append((i * ny + j, (i + 2 * dx) % nx * ny + (j + dy) % ny))
        return lax.ppermute(value, ("gx", "gy"), moves)

    value = rows[None]
    value = jnp.concatenate(
        [value]
        + [
            lax.ppermute(value, "gz", [(i, (i + s) % nz) for i in range(nz)])
            for s in range(1, nz)
        ],
        axis=0,
    )
    if pairs * ny <= 4:
        steps = [(dx, dy) for dx in range(pairs) for dy in range(ny)]
        value = jnp.concatenate(
            [value] + [shifted(value, dx, dy) for dx, dy in steps[1:]], axis=0
        )
    else:
        value = jnp.concatenate([value] + [shifted(value, 0, dy) for dy in range(1, ny)], axis=0)
        value = jnp.concatenate([value] + [shifted(value, dx, 0) for dx in range(1, pairs)], axis=0)
    value, *beside = lax.optimization_barrier((value, *beside))
    return value, *beside


def from_other_core(value):
    return lax.ppermute(value, "gx", [(i, i ^ 1) for i in range(lax.axis_size("gx"))])


def call(kernel, name, outs, scratch, smem, operands, kept, limit, flops):
    n_in = len(operands)
    first = n_in - kept
    operands = [
        pltpu.with_memory_space_constraint(o, pltpu.VMEM) if i >= first else o
        for i, o in enumerate(operands)
    ]
    specs = [pl.BlockSpec(memory_space=pltpu.SMEM)] * smem + [
        pl.BlockSpec(memory_space=pltpu.VMEM)
    ] * (n_in - smem)
    return pl.pallas_call(
        kernel,
        name=name,
        out_shape=outs,
        in_specs=specs,
        out_specs=[pl.BlockSpec(memory_space=pltpu.VMEM)] * len(outs),
        scratch_shapes=scratch,
        compiler_params=pltpu.CompilerParams(vmem_limit_bytes=limit),
        cost_estimate=pl.CostEstimate(flops=flops, bytes_accessed=2_000_000, transcendentals=0),
    )(*operands)


def shards(
    features,
    positions,
    counts,
    w_proj,
    w_mix,
    w_long,
    w_charge,
    charge_bias,
    w_energy,
    k_filter,
    k_index,
):
    own_rows = features[0, 0, 0]
    n, channels = own_rows.shape
    charge_ch = w_charge.shape[0]
    waves = k_index.shape[1]
    bases = w_proj.shape[0]
    sizes = tuple(lax.axis_size(a) for a in AXES)
    cells = sizes[0] * sizes[1] * sizes[2]
    half_cells = cells // 2
    group = max(g for g in (8, 4, 2, 1) if half_cells % g == 0)
    blocks = len(blocks_of(sizes))
    scale_long = 4.0 / math.sqrt(n * cells * waves)
    count = counts.reshape(1)
    meta = jnp.stack([lax.axis_index(a) for a in AXES]).astype(jnp.int32)
    shape = jax.ShapeDtypeStruct
    wide = 2 * ORDERS * charge_ch
    fits = cells <= 64
    limit = (24 if fits else 56) * 1024 * 1024
    held = pltpu.VMEM if fits else shape

    def run(kernel, name, outs, scratch, smem, operands, kept, flops):
        kept = kept if fits else 0
        return call(kernel, name, outs, scratch, smem, operands, kept, limit, flops)

    (packed,) = run(
        pack_kernel,
        "pack",
        [held((n + 16, channels), BF16)],
        [],
        1,
        [count, own_rows, positions.reshape(3, 1, n)],
        0,
        1000,
    )
    filt, bias, energy_row = run(
        lambda *refs: fold_kernel(scale_long, *refs),
        "fold_filter",
        [
            held((ORDERS, 4 * charge_ch, 128), F32),
            held((charge_ch, n), F32),
            held((1, channels), F32),
        ],
        [],
        0,
        [k_filter, k_index, charge_bias[None, :], w_energy[None, :]],
        0,
        1_000_000_000,
    )
    near, filt, bias, energy_row = gather_cells(packed, sizes, (filt, bias, energy_row))
    far = from_other_core(near)
    sums, part, places, charge = run(
        lambda *refs: charge_kernel(sizes, group, *refs),
        "charge_sums",
        [
            held((wide + 16, 256), F32),
            held((wide + 16 + charge_ch, 256), BF16),
            held((half_cells, 8, n), F32),
            held((charge_ch, n), F32),
        ],
        [pltpu.VMEM((half_cells, charge_ch, n), F32)],
        1,
        [meta, near, w_charge, bias],
        3,
        3_000_000_000,
    )
    far_part = from_other_core(part)
    short, far_places, xcat = run(
        lambda *refs: message_kernel(sizes, *refs),
        "message",
        [
            held((n, channels), F32),
            held((half_cells, 8, n), F32),
            held((blocks * n, channels), BF16),
        ],
        [pltpu.VMEM((bases * n, blocks * n), BF16)],
        1,
        [meta, near, far, places, w_proj, w_mix],
        5,
        3_000_000_000,
    )
    grad, refined, field, neutral = run(
        lambda *refs: cotangent_kernel(sizes, *refs),
        "cotangents",
        [
            held((n, channels), BF16),
            held((n, channels), F32),
            held((wide, 256), BF16),
            held((charge_ch, n), F32),
        ],
        [],
        2,
        [
            count,
            meta,
            sums,
            part,
            far_part,
            places,
            far_places,
            charge,
            short,
            own_rows,
            w_long,
            energy_row,
            filt,
        ],
        11,
        3_000_000_000,
    )
    updated, energy, force, lifted = run(
        lambda *refs: own_kernel(sizes, *refs),
        "own_terms",
        [
            shape((n, channels), BF16),
            shape((1, n), F32),
            held((3, n), F32),
            held((bases * n, channels), BF16),
        ],
        [pltpu.VMEM((bases * n, blocks * n), F32)],
        1,
        [
            meta,
            grad,
            field,
            places,
            far_places,
            xcat,
            refined,
            w_proj,
            w_mix,
            w_long,
            energy_row,
        ],
        10,
        4_000_000_000,
    )
    grad_near, force, lifted = gather_cells(grad, sizes, (force, lifted))
    grad_far = from_other_core(grad_near)
    back, back_part = run(
        lambda *refs: pull_kernel(sizes, group, *refs),
        "pull_sums",
        [held((wide, 256), F32), held((wide, 256), BF16)],
        [],
        1,
        [meta, grad_near, places, w_long],
        3,
        3_000_000_000,
    )
    far_back = from_other_core(back_part)
    (force,) = run(
        lambda *refs: react_kernel(sizes, *refs),
        "react",
        [held((3, n), F32)],
        [
            pltpu.VMEM((blocks * n, channels), BF16),
            pltpu.VMEM((bases * n, blocks * n), F32),
        ],
        1,
        [meta, grad_near, grad_far, places, far_places, lifted, force],
        6,
        3_000_000_000,
    )
    (forces,) = run(
        lambda *refs: finish_kernel(sizes, *refs),
        "finish",
        [shape((3, 1, n), F32)],
        [pltpu.VMEM((wide, 256), BF16)],
        1,
        [meta, back, far_back, places, neutral, force, filt],
        6,
        2_000_000_000,
    )
    return (
        updated[None, None, None],
        energy[None, None],
        forces.reshape(positions.shape),
    )


def solution(mesh):
    cell = ("gx", "gy", "gz")
    in_specs = (P(*cell, None, None), P(*cell, None, None), P(*cell)) + (P(),) * 8
    out_specs = (P(*cell, None, None), P(*cell, None), P(*cell, None, None))
    return jax.shard_map(shards, mesh=mesh, in_specs=in_specs, out_specs=out_specs, check_vma=False)
```

time: 64.9 us -> 55.7 us (0.86)
  Pallas kernels: 28.1 us -> 19.9 us
  waiting for transfers between devices: 14.1 us -> 11.9 us
  local copies, waits for them, and re-layouts: 2.61 us -> 3.85 us
    pallas_call x5 -> x9, Pallas kernels: 28.1 us -> 19.9 us  [call(): pl.pallas_call(kernel, name=name, out_shape=outs, in_specs=specs, out_spe...]
    ppermute x2 -> x4, waiting for transfers between devices: 3.17 us -> 0.01 us  [from_other_core(): lax.ppermute(value, 'gx', [(i, i ^ 1) for i in range(lax.axis_size('gx'))])]
    ppermute x6, waiting for transfers between devices: 1.23 us -> 2.72 us  [gather_cells(): lax.ppermute(value, 'gz', [(i, (i + s) % nz) for i in range(nz)])]
    unnamed x24 -> x34, local copies, waits for them, and re-layouts: 2.57 us -> 3.81 us
  transfers between devices with their start and end apart: 14 -> 16, of which waited for: 6 -> 5; matrix products, arithmetic and copies ran while one was open for 3% -> 0% of each run, Pallas kernels for 13% -> 30%
where the time goes in v2:
time: 55.7 us; the launch traced here: 55.4 us
  Pallas kernels  19.9 us (36%)
  starting transfers between devices  18 us (32%)
  waiting for transfers between devices  11.9 us (21%)
  local copies, waits for them, and re-layouts  3.85 us (7%)
  between operations  1.55 us (3%)
    pallas_call x9, Pallas kernels, call(): pl.pallas_call(kernel, name=name, out_shape=outs, in_specs=specs, out_spe...  19.9 us
    ppermute x6, starting transfers between devices, gather_cells(): lax.ppermute(value, 'gz', [(i, (i + s) % nz) for i in range(nz)])  10.1 us
    ppermute x6, waiting for transfers between devices, shifted(): return lax.ppermute(value, ('gx', 'gy'), moves)  9.19 us
    ppermute x6, starting transfers between devices, shifted(): return lax.ppermute(value, ('gx', 'gy'), moves)  7.11 us
    unnamed x34, local copies, waits for them, and re-layouts  3.81 us
    ppermute x6, waiting for transfers between devices, gather_cells(): lax.ppermute(value, 'gz', [(i, (i + s) % nz) for i in range(nz)])  2.72 us
  transfers between devices with their start and end apart: 16, of which 5 were waited for; matrix products, arithmetic and copies ran while one was open for 0% of the time, Pallas kernels for 30%

profile of v2, /device:TPU:0, one launch (start us, length us, event | category | flops | bytes accessed | tf_op | source)
XLA Modules:
  0.0 55.4 jit_solution(11913976521834417786)
XLA Ops:
  1.3 0.7 %copy-done.2 = f32[1,1,1,3,128]{4,2,3,1,0:T(1,128)S(1)} copy-done((f32[1,1,1,3,128]{4,2,3,1,0:T(1,128)S(1)}, f32[1,1,1,3,128]{4,2,3,1,0:T(1,128)}, u32[]{:S(2)}) %copy-start.2) | copy-done | bytes 1560
  2.0 0.8 %copy-done = bf16[1,1,1,128,128]{4,3,2,1,0:T(8,128)(2,1)S(1)} copy-done((bf16[1,1,1,128,128]{4,3,2,1,0:T(8,128)(2,1)S(1)}, bf16[1,1,1,128,128]{4,3,2,1,0:T(8,128)(2,1)}, u32[]{:S(2)}) %copy-start) | copy-done | bytes 32792
  2.7 5.1 %collective-permute-start.2 = (bf16[1,144,128]{2,1,0:T(8,128)(2,1)S(1)}, bf16[1,144,128]{2,1,0:T(8,128)(2,1)S(1)}, u32[]{:S(2)}, u32[]{:S(2)}) collective-permute-start(bf16[1,144,128]{2,1,0:T(8,128)(2,1)S(1)} %bitcast.19), channel_id=1, source_target_pairs={{0,3},{1,0},{2,1},{3,2},{4,7},{5,4},{6,5},{7,6},{8,11},{9,8},{10,9... | collective-permute-start | bytes 110600 | tf_op jit(solution)/shard_map/ppermute | solution.py:577
  7.9 1.0 %collective-permute-start = (bf16[1,144,128]{2,1,0:T(8,128)(2,1)S(1)}, bf16[1,144,128]{2,1,0:T(8,128)(2,1)S(1)}, u32[]{:S(2)}, u32[]{:S(2)}) collective-permute-start(bf16[1,144,128]{2,1,0:T(8,128)(2,1)S(1)} %bitcast.21), channel_id=1, source_target_pairs={{0,1},{1,2},{2,3},{3,0},{4,5},{5,6},{6,7},{7,4},{8,9},{9,10},{10,1... | collective-permute-start | bytes 110600 | tf_op jit(solution)/shard_map/ppermute | solution.py:577
  8.9 0.6 %copy-done.9 = f32[64]{0:T(128)S(1)} copy-done((f32[64]{0:T(128)S(1)}, f32[64]{0:T(128)}, u32[]{:S(2)}) %copy-start.9) | copy-done | bytes 280
  9.5 1.0 %copy-done.3 = f32[64,2048]{1,0:T(8,128)S(1)} copy-done((f32[64,2048]{1,0:T(8,128)S(1)}, f32[64,2048]{1,0:T(8,128)}, u32[]{:S(2)}) %copy-start.3) | copy-done | bytes 524312
  10.6 2.1 %fold_filter.1 = (f32[7,256,128]{2,1,0:T(8,128)S(1)}, f32[64,128]{1,0:T(8,128)S(1)}, f32[1,128]{1,0:T(1,128)S(1)}) custom-call(f32[64,2048]{1,0:T(8,128)S(1)} %copy-done.3, s32[3,2048]{1,0:T(4,128)S(1)} %copy-done.5, f32[1,64]{1,0:T(1,128)S(1)} %bitcast.30, f32[1,128]{1,0:T(1,128)S(1)} %bitcast.31), custom_call_target="tpu_custom_call" | custom-call | flops 1000000000 | bytes 2000000 | tf_op jit(solution)/shard_map/fold_filter/pallas_call | solution.py:608
  12.7 0.9 %collective-permute-done = bf16[1,144,128]{2,1,0:T(8,128)(2,1)S(1)} collective-permute-done((bf16[1,144,128]{2,1,0:T(8,128)(2,1)S(1)}, bf16[1,144,128]{2,1,0:T(8,128)(2,1)S(1)}, u32[]{:S(2)}, u32[]{:S(2)}) %collective-permute-start) | collective-permute-done | bytes 36896 | tf_op jit(solution)/shard_map/ppermute | solution.py:577
  13.6 2.5 %collective-permute-start.5 = (bf16[4,144,128]{2,1,0:T(8,128)(2,1)S(1)}, bf16[4,144,128]{2,1,0:T(8,128)(2,1)S(1)}, u32[]{:S(2)}, u32[]{:S(2)}) collective-permute-start(bf16[4,144,128]{2,1,0:T(8,128)(2,1)S(1)} %pad_maximum_fusion), channel_id=1, source_target_pairs={{0,20},{4,16},{8,28},{12,24},{16,4},{20,0},{24,12},{28,8},{1,21},{... | collective-permute-start | bytes 442376 | tf_op jit(solution)/shard_map/ppermute | solution.py:571
  16.1 0.5 collective-permute-start.4
  17.2 4.7 %collective-permute-done.3 = bf16[4,144,128]{2,1,0:T(8,128)(2,1)S(1)} collective-permute-done((bf16[4,144,128]{2,1,0:T(8,128)(2,1)S(1)}, bf16[4,144,128]{2,1,0:T(8,128)(2,1)S(1)}, u32[]{:S(2)}, u32[]{:S(2)}) %collective-permute-start.3) | collective-permute-done | bytes 147488 | tf_op jit(solution)/shard_map/ppermute | solution.py:571
  22.7 2.4 %charge_sums.1 = (f32[912,256]{1,0:T(8,128)S(1)}, bf16[976,256]{1,0:T(8,128)(2,1)S(1)}, f32[16,8,128]{2,1,0:T(8,128)S(1)}, f32[64,128]{1,0:T(8,128)S(1)}) custom-call(s32[3]{0:T(128)S(1)} %pad_add_fusion.refs_0_.refs_1_, bf16[16,144,128]{2,1,0:T(8,128)(2,1)S(1)} %constant_dynamic-update-slice_fusion.refs_1_, bf16[64,128]{1,0:T(8,128)(2,1)S(1)} %copy-done.7, ...), custom_call_target="tpu_custom_call" | custom-call | flops 3000000000 | bytes 2000000 | tf_op jit(solution)/shard_map/charge_sums/pallas_call | solution.py:608
  25.3 2.6 %message.1 = (f32[128,128]{1,0:T(8,128)S(1)}, f32[16,8,128]{2,1,0:T(8,128)S(1)}, bf16[2304,128]{1,0:T(8,128)(2,1)S(1)}) custom-call(s32[3]{0:T(128)S(1)} %pad_add_fusion.refs_0_.refs_1_, bf16[16,144,128]{2,1,0:T(8,128)(2,1)S(1)} %constant_dynamic-update-slice_fusion.refs_1_, bf16[16,144,128]{2,1,0:T(8,128)(2,1)S(1)} %collective-permute-done.7.refs_2_, ...), custom_call_target="tpu_custom_call" | custom-call | flops 3000000000 | bytes 2000000 | tf_op jit(solution)/shard_map/message/pallas_call | solution.py:608
  28.0 1.7 %cotangents.1 = (bf16[128,128]{1,0:T(8,128)(2,1)S(1)}, f32[128,128]{1,0:T(8,128)S(1)}, bf16[896,256]{1,0:T(8,128)(2,1)S(1)}, f32[64,128]{1,0:T(8,128)S(1)}) custom-call(s32[1]{0:T(128)} %bitcast.18.refs_0_, s32[3]{0:T(128)S(1)} %pad_add_fusion.refs_0_.refs_1_, f32[912,256]{1,0:T(8,128)S(1)} %get-tuple-element.35.refs_2_, ...), custom_call_target="tpu_custom_call" | custom-call | flops 3000000000 | bytes 2000000 | tf_op jit(solution)/shard_map/cotangents/pallas_call | solution.py:608
  29.6 2.8 %collective-permute-start.10 = (bf16[1,128,128]{2,1,0:T(8,128)(2,1)S(1)}, bf16[1,128,128]{2,1,0:T(8,128)(2,1)S(1)}, u32[]{:S(2)}, u32[]{:S(2)}) collective-permute-start(bf16[1,128,128]{2,1,0:T(8,128)(2,1)S(1)} %bitcast.23), channel_id=1, source_target_pairs={{0,3},{1,0},{2,1},{3,2},{4,7},{5,4},{6,5},{7,6},{8,11},{9,8},{10,9... | collective-permute-start | bytes 98312 | tf_op jit(solution)/shard_map/ppermute | solution.py:577
  32.5 0.8 %collective-permute-start.9 = (bf16[1,128,128]{2,1,0:T(8,128)(2,1)S(1)}, bf16[1,128,128]{2,1,0:T(8,128)(2,1)S(1)}, u32[]{:S(2)}, u32[]{:S(2)}) collective-permute-start(bf16[1,128,128]{2,1,0:T(8,128)(2,1)S(1)} %bitcast.24), channel_id=1, source_target_pairs={{0,2},{1,3},{2,0},{3,1},{4,6},{5,7},{6,4},{7,5},{8,10},{9,11},{10,... | collective-permute-start | bytes 98312 | tf_op jit(solution)/shard_map/ppermute | solution.py:577
  33.6 3.6 %own_terms.1 = (bf16[128,128]{1,0:T(8,128)(2,1)}, f32[1,128]{1,0:T(1,128)}, f32[3,128]{1,0:T(4,128)S(1)}, bf16[512,128]{1,0:T(8,128)(2,1)S(1)}) custom-call(s32[3]{0:T(128)S(1)} %pad_add_fusion.refs_0_.refs_1_, bf16[128,128]{1,0:T(8,128)(2,1)S(1)} %get-tuple-element.43.refs_1_, bf16[896,256]{1,0:T(8,128)(2,1)S(1)} %get-tuple-element.44.refs_2_, ...), custom_call_target="tpu_custom_call" | custom-call | flops 4000000000 | bytes 2000000 | tf_op jit(solution)/shard_map/own_terms/pallas_call | solution.py:608
  37.3 1.7 %collective-permute-done.8 = bf16[1,128,128]{2,1,0:T(8,128)(2,1)S(1)} collective-permute-done((bf16[1,128,128]{2,1,0:T(8,128)(2,1)S(1)}, bf16[1,128,128]{2,1,0:T(8,128)(2,1)S(1)}, u32[]{:S(2)}, u32[]{:S(2)}) %collective-permute-start.8) | collective-permute-done | bytes 32800 | tf_op jit(solution)/shard_map/ppermute | solution.py:577
  39.0 2.5 %collective-permute-start.13 = (bf16[4,128,128]{2,1,0:T(8,128)(2,1)S(1)}, bf16[4,128,128]{2,1,0:T(8,128)(2,1)S(1)}, u32[]{:S(2)}, u32[]{:S(2)}) collective-permute-start(bf16[4,128,128]{2,1,0:T(8,128)(2,1)S(1)} %pad_maximum_fusion.1), channel_id=1, source_target_pairs={{0,20},{4,16},{8,28},{12,24},{16,4},{20,0},{24,12},{28,8},{1,21},{... | collective-permute-start | bytes 393224 | tf_op jit(solution)/shard_map/ppermute | solution.py:571
  42.6 4.5 %collective-permute-done.11 = bf16[4,128,128]{2,1,0:T(8,128)(2,1)S(1)} collective-permute-done((bf16[4,128,128]{2,1,0:T(8,128)(2,1)S(1)}, bf16[4,128,128]{2,1,0:T(8,128)(2,1)S(1)}, u32[]{:S(2)}, u32[]{:S(2)}) %collective-permute-start.11) | collective-permute-done | bytes 131104 | tf_op jit(solution)/shard_map/ppermute | solution.py:571
  47.3 2.9 %pull_sums.1 = (f32[896,256]{1,0:T(8,128)S(1)}, bf16[896,256]{1,0:T(8,128)(2,1)S(1)}) custom-call(s32[3]{0:T(128)S(1)} %pad_add_fusion.refs_0_.refs_1_, bf16[16,128,128]{2,1,0:T(8,128)(2,1)S(1)} %constant_dynamic-update-slice_fusion.7.refs_1_, f32[16,8,128]{2,1,0:T(8,128)S(1)} %get-tuple-element.37.refs_3_.refs_5_.refs_2_, bf16[64,128]{1,0:T(8,128)(2,1)S(1)} %copy-done.8), custom_call_target="tpu_custom_call" | custom-call | flops 3000000000 | bytes 2000000 | tf_op jit(solution)/shard_map/pull_sums/pallas_call | solution.py:608
  50.2 0.6 %collective-permute-start.14 = (bf16[896,256]{1,0:T(8,128)(2,1)S(1)}, bf16[896,256]{1,0:T(8,128)(2,1)S(1)}, u32[]{:S(2)}, u32[]{:S(2)}) collective-permute-start(bf16[896,256]{1,0:T(8,128)(2,1)S(1)} %get-tuple-element.53), channel_id=1, source_target_pairs={{0,8},{8,0},{16,24},{24,16},{1,9},{9,1},{17,25},{25,17},{2,10},{10... | collective-permute-start | bytes 1376264 | tf_op jit(solution)/shard_map/ppermute | solution.py:595
  50.7 2.8 %react.1.refs_5_ = f32[3,128]{1,0:T(4,128)S(1)} custom-call(s32[3]{0:T(128)S(1)} %pad_add_fusion.refs_0_.refs_1_, bf16[16,128,128]{2,1,0:T(8,128)(2,1)S(1)} %constant_dynamic-update-slice_fusion.7.refs_1_, bf16[16,128,128]{2,1,0:T(8,128)(2,1)S(1)} %collective-permute-done.15.refs_2_, f32[16,8,128]{2,1,0:T(8,128)S(1)} %get-tuple-element.37.refs_3_.refs_5_.refs_2_, ...), custom_call_target="tpu_custom_call" | custom-call | flops 3000000000 | bytes 2000000 | tf_op jit(solution)/shard_map/react/pallas_call | solution.py:608
  53.5 1.8 %finish.1 = f32[3,1,128]{2,1,0:T(1,128)} custom-call(s32[3]{0:T(128)S(1)} %pad_add_fusion.refs_0_.refs_1_, f32[896,256]{1,0:T(8,128)S(1)} %get-tuple-element.52.refs_1_, bf16[896,256]{1,0:T(8,128)(2,1)S(1)} %collective-permute-done.14.refs_2_, f32[16,8,128]{2,1,0:T(8,128)S(1)} %get-tuple-element.37.refs_3_.refs_5_.refs_2_, ...), custom_call_target="tpu_custom_call" | custom-call | flops 2000000000 | bytes 2000000 | tf_op jit(solution)/shard_map/finish/pallas_call | solution.py:608
  (56 shorter events, 3.1 us)
Async XLA Ops:
  2.0 0.8 %copy-start = (bf16[1,1,1,128,128]{4,3,2,1,0:T(8,128)(2,1)S(1)}, bf16[1,1,1,128,128]{4,3,2,1,0:T(8,128)(2,1)}, u32[]{:S(2)}) copy-start(bf16[1,1,1,128,128]{4,3,2,1,0:T(8,128)(2,1)} %param.11) | copy-start | bytes 98308
  2.7 6.1 %copy-start.5 = (s32[3,2048]{1,0:T(4,128)S(1)}, s32[3,2048]{1,0:T(4,128)}, u32[]{:S(2)}) copy-start(s32[3,2048]{1,0:T(4,128)} %refs_1_.1) | copy-start | bytes 73732
  2.7 9.9 %collective-permute-start.2 = (bf16[1,144,128]{2,1,0:T(8,128)(2,1)S(1)}, bf16[1,144,128]{2,1,0:T(8,128)(2,1)S(1)}, u32[]{:S(2)}, u32[]{:S(2)}) collective-permute-start(bf16[1,144,128]{2,1,0:T(8,128)(2,1)S(1)} %bitcast.19), channel_id=1, source_target_pairs={{0,3},{1,0},{2,1},{3,2},{4,7},{5,4},{6,5},{7,6},{8,11},{9,8},{10,9... | collective-permute-start | bytes 110600 | tf_op jit(solution)/shard_map/ppermute | solution.py:577
  7.9 4.9 %collective-permute-start.1 = (bf16[1,144,128]{2,1,0:T(8,128)(2,1)S(1)}, bf16[1,144,128]{2,1,0:T(8,128)(2,1)S(1)}, u32[]{:S(2)}, u32[]{:S(2)}) collective-permute-start(bf16[1,144,128]{2,1,0:T(8,128)(2,1)S(1)} %bitcast.20), channel_id=1, source_target_pairs={{0,2},{1,3},{2,0},{3,1},{4,6},{5,7},{6,4},{7,5},{8,10},{9,11},{10,... | collective-permute-start | bytes 110600 | tf_op jit(solution)/shard_map/ppermute | solution.py:577
  7.9 5.8 %collective-permute-start = (bf16[1,144,128]{2,1,0:T(8,128)(2,1)S(1)}, bf16[1,144,128]{2,1,0:T(8,128)(2,1)S(1)}, u32[]{:S(2)}, u32[]{:S(2)}) collective-permute-start(bf16[1,144,128]{2,1,0:T(8,128)(2,1)S(1)} %bitcast.21), channel_id=1, source_target_pairs={{0,1},{1,2},{2,3},{3,0},{4,5},{5,6},{6,7},{7,4},{8,9},{9,10},{10,1... | collective-permute-start | bytes 110600 | tf_op jit(solution)/shard_map/ppermute | solution.py:577
  9.5 1.0 %copy-start.3 = (f32[64,2048]{1,0:T(8,128)S(1)}, f32[64,2048]{1,0:T(8,128)}, u32[]{:S(2)}) copy-start(f32[64,2048]{1,0:T(8,128)} %refs_0_.1) | copy-start | bytes 1572868
  13.6 8.4 %collective-permute-start.5 = (bf16[4,144,128]{2,1,0:T(8,128)(2,1)S(1)}, bf16[4,144,128]{2,1,0:T(8,128)(2,1)S(1)}, u32[]{:S(2)}, u32[]{:S(2)}) collective-permute-start(bf16[4,144,128]{2,1,0:T(8,128)(2,1)S(1)} %pad_maximum_fusion), channel_id=1, source_target_pairs={{0,20},{4,16},{8,28},{12,24},{16,4},{20,0},{24,12},{28,8},{1,21},{... | collective-permute-start | bytes 442376 | tf_op jit(solution)/shard_map/ppermute | solution.py:571
  16.1 5.8 %collective-permute-start.4 = (bf16[4,144,128]{2,1,0:T(8,128)(2,1)S(1)}, bf16[4,144,128]{2,1,0:T(8,128)(2,1)S(1)}, u32[]{:S(2)}, u32[]{:S(2)}) collective-permute-start(bf16[4,144,128]{2,1,0:T(8,128)(2,1)S(1)} %pad_maximum_fusion), channel_id=1, source_target_pairs={{0,16},{4,20},{8,24},{12,28},{16,0},{20,4},{24,8},{28,12},{1,17},{... | collective-permute-start | bytes 442376 | tf_op jit(solution)/shard_map/ppermute | solution.py:571
  16.7 5.2 %collective-permute-start.3 = (bf16[4,144,128]{2,1,0:T(8,128)(2,1)S(1)}, bf16[4,144,128]{2,1,0:T(8,128)(2,1)S(1)}, u32[]{:S(2)}, u32[]{:S(2)}) collective-permute-start(bf16[4,144,128]{2,1,0:T(8,128)(2,1)S(1)} %pad_maximum_fusion), channel_id=1, source_target_pairs={{0,4},{4,0},{8,12},{12,8},{16,20},{20,16},{24,28},{28,24},{1,5},{5... | collective-permute-start | bytes 442376 | tf_op jit(solution)/shard_map/ppermute | solution.py:571
  22.0 0.7 %copy-start.7 = (bf16[64,128]{1,0:T(8,128)(2,1)S(1)}, bf16[64,128]{1,0:T(8,128)(2,1)}, u32[]{:S(2)}) copy-start(bf16[64,128]{1,0:T(8,128)(2,1)} %refs_2_.1) | copy-start | bytes 49156
  22.1 3.2 %collective-permute-start.7 = (bf16[16,144,128]{2,1,0:T(8,128)(2,1)S(1)}, bf16[16,144,128]{2,1,0:T(8,128)(2,1)S(1)}, u32[]{:S(2)}, u32[]{:S(2)}) collective-permute-start(bf16[16,144,128]{2,1,0:T(8,128)(2,1)S(1)} %constant_dynamic-update-slice_fusion.refs_1_), channel_id=1, source_target_pairs={{0,8},{8,0},{16,24},{24,16},{1,9},{9,1},{17,25},{25,17},{2,10},{10... | collective-permute-start | bytes 1769480 | tf_op jit(solution)/shard_map/ppermute | solution.py:595
  22.7 2.5 %copy-start.4 = (bf16[4,128,128]{2,1,0:T(8,128)(2,1)S(1)}, bf16[4,128,128]{2,1,0:T(8,128)(2,1)}, u32[]{:S(2)}) copy-start(bf16[4,128,128]{2,1,0:T(8,128)(2,1)} %refs_7_.1) | copy-start | bytes 393220
  22.7 2.5 %copy-start.6 = (bf16[128,128]{1,0:T(8,128)(2,1)S(1)}, bf16[128,128]{1,0:T(8,128)(2,1)}, u32[]{:S(2)}) copy-start(bf16[128,128]{1,0:T(8,128)(2,1)} %refs_8_.1) | copy-start | bytes 98308
  25.2 2.8 %collective-permute-start.6 = (bf16[976,256]{1,0:T(8,128)(2,1)S(1)}, bf16[976,256]{1,0:T(8,128)(2,1)S(1)}, u32[]{:S(2)}, u32[]{:S(2)}) collective-permute-start(bf16[976,256]{1,0:T(8,128)(2,1)S(1)} %get-tuple-element.36.refs_3_), channel_id=1, source_target_pairs={{0,8},{8,0},{16,24},{24,16},{1,9},{9,1},{17,25},{25,17},{2,10},{10... | collective-permute-start | bytes 1499144 | tf_op jit(solution)/shard_map/ppermute | solution.py:595
  25.3 2.7 %copy-start.1 = (bf16[1,1,1,128,128]{4,3,2,1,0:T(8,128)(2,1)S(1)}, bf16[1,1,1,128,128]{4,3,2,1,0:T(8,128)(2,1)}, u32[]{:S(2)}) copy-start(bf16[1,1,1,128,128]{4,3,2,1,0:T(8,128)(2,1)} %param.11) | copy-start | bytes 98308
  25.3 2.7 %copy-start.8 = (bf16[64,128]{1,0:T(8,128)(2,1)S(1)}, bf16[64,128]{1,0:T(8,128)(2,1)}, u32[]{:S(2)}) copy-start(bf16[64,128]{1,0:T(8,128)(2,1)} %refs_3_.1) | copy-start | bytes 49156
  29.6 7.6 %collective-permute-start.10 = (bf16[1,128,128]{2,1,0:T(8,128)(2,1)S(1)}, bf16[1,128,128]{2,1,0:T(8,128)(2,1)S(1)}, u32[]{:S(2)}, u32[]{:S(2)}) collective-permute-start(bf16[1,128,128]{2,1,0:T(8,128)(2,1)S(1)} %bitcast.23), channel_id=1, source_target_pairs={{0,3},{1,0},{2,1},{3,2},{4,7},{5,4},{6,5},{7,6},{8,11},{9,8},{10,9... | collective-permute-start | bytes 98312 | tf_op jit(solution)/shard_map/ppermute | solution.py:577
  32.5 4.8 %collective-permute-start.9 = (bf16[1,128,128]{2,1,0:T(8,128)(2,1)S(1)}, bf16[1,128,128]{2,1,0:T(8,128)(2,1)S(1)}, u32[]{:S(2)}, u32[]{:S(2)}) collective-permute-start(bf16[1,128,128]{2,1,0:T(8,128)(2,1)S(1)} %bitcast.24), channel_id=1, source_target_pairs={{0,2},{1,3},{2,0},{3,1},{4,6},{5,7},{6,4},{7,5},{8,10},{9,11},{10,... | collective-permute-start | bytes 98312 | tf_op jit(solution)/shard_map/ppermute | solution.py:577
  33.3 5.7 %collective-permute-start.8 = (bf16[1,128,128]{2,1,0:T(8,128)(2,1)S(1)}, bf16[1,128,128]{2,1,0:T(8,128)(2,1)S(1)}, u32[]{:S(2)}, u32[]{:S(2)}) collective-permute-start(bf16[1,128,128]{2,1,0:T(8,128)(2,1)S(1)} %bitcast.25), channel_id=1, source_target_pairs={{0,1},{1,2},{2,3},{3,0},{4,5},{5,6},{6,7},{7,4},{8,9},{9,10},{10,1... | collective-permute-start | bytes 98312 | tf_op jit(solution)/shard_map/ppermute | solution.py:577
  39.0 8.1 %collective-permute-start.13 = (bf16[4,128,128]{2,1,0:T(8,128)(2,1)S(1)}, bf16[4,128,128]{2,1,0:T(8,128)(2,1)S(1)}, u32[]{:S(2)}, u32[]{:S(2)}) collective-permute-start(bf16[4,128,128]{2,1,0:T(8,128)(2,1)S(1)} %pad_maximum_fusion.1), channel_id=1, source_target_pairs={{0,20},{4,16},{8,28},{12,24},{16,4},{20,0},{24,12},{28,8},{1,21},{... | collective-permute-start | bytes 393224 | tf_op jit(solution)/shard_map/ppermute | solution.py:571
  41.5 5.6 %collective-permute-start.12 = (bf16[4,128,128]{2,1,0:T(8,128)(2,1)S(1)}, bf16[4,128,128]{2,1,0:T(8,128)(2,1)S(1)}, u32[]{:S(2)}, u32[]{:S(2)}) collective-permute-start(bf16[4,128,128]{2,1,0:T(8,128)(2,1)S(1)} %pad_maximum_fusion.1), channel_id=1, source_target_pairs={{0,16},{4,20},{8,24},{12,28},{16,0},{20,4},{24,8},{28,12},{1,17},{... | collective-permute-start | bytes 393224 | tf_op jit(solution)/shard_map/ppermute | solution.py:571
  42.1 5.0 %collective-permute-start.11 = (bf16[4,128,128]{2,1,0:T(8,128)(2,1)S(1)}, bf16[4,128,128]{2,1,0:T(8,128)(2,1)S(1)}, u32[]{:S(2)}, u32[]{:S(2)}) collective-permute-start(bf16[4,128,128]{2,1,0:T(8,128)(2,1)S(1)} %pad_maximum_fusion.1), channel_id=1, source_target_pairs={{0,4},{4,0},{8,12},{12,8},{16,20},{20,16},{24,28},{28,24},{1,5},{5... | collective-permute-start | bytes 393224 | tf_op jit(solution)/shard_map/ppermute | solution.py:571
  47.2 3.5 %collective-permute-start.15 = (bf16[16,128,128]{2,1,0:T(8,128)(2,1)S(1)}, bf16[16,128,128]{2,1,0:T(8,128)(2,1)S(1)}, u32[]{:S(2)}, u32[]{:S(2)}) collective-permute-start(bf16[16,128,128]{2,1,0:T(8,128)(2,1)S(1)} %constant_dynamic-update-slice_fusion.7.refs_1_), channel_id=1, source_target_pairs={{0,8},{8,0},{16,24},{24,16},{1,9},{9,1},{17,25},{25,17},{2,10},{10... | collective-permute-start | bytes 1572872 | tf_op jit(solution)/shard_map/ppermute | solution.py:595
  50.2 3.3 %collective-permute-start.14 = (bf16[896,256]{1,0:T(8,128)(2,1)S(1)}, bf16[896,256]{1,0:T(8,128)(2,1)S(1)}, u32[]{:S(2)}, u32[]{:S(2)}) collective-permute-start(bf16[896,256]{1,0:T(8,128)(2,1)S(1)} %get-tuple-element.53), channel_id=1, source_target_pairs={{0,8},{8,0},{16,24},{24,16},{1,9},{9,1},{17,25},{25,17},{2,10},{10... | collective-permute-start | bytes 1376264 | tf_op jit(solution)/shard_map/ppermute | solution.py:595
  (3 other events, 2.0 us)

commit v3 on v2

--- a/solution.py
+++ b/solution.py
@@ -25,7 +25,7 @@
     r = np.sqrt(r2)
     out = []
     for values in (np.cos(2 * np.pi * r), np.sin(2 * np.pi * r) / r):
-        cheb = np.polynomial.chebyshev.Chebyshev.fit(r2, values, 7, domain=[0.0, 0.25])
+        cheb = np.polynomial.chebyshev.Chebyshev.fit(r2, values, 6, domain=[0.0, 0.25])
         out.append([float(c) for c in cheb.convert(kind=np.polynomial.Polynomial).coef])
     return out
 
@@ -232,6 +232,22 @@
     return 1, (dx * ny + dy) * nz + dz
 
 
+def add_groups(structure, groups, sums_ref):
+    if groups <= 4:
+        total = structure(0)
+        for g in range(1, groups):
+            total = total + structure(g)
+        sums_ref[...] = total
+        return
+    sums_ref[...] = structure(0)
+
+    def add_structure(g, _):
+        sums_ref[...] += structure(g)
+        return 0
+
+    lax.fori_loop(1, groups, add_structure, 0)
+
+
 def charge_kernel(
     sizes,
     group,
@@ -243,8 +259,9 @@
     part_ref,
     places_ref,
     charge_ref,
-    charge_scr,
+    *rest,
 ):
+    *kept, charge_scr = rest
     charge_ch, channels = w_charge_ref.shape
     cells = near_ref.shape[0]
     n = near_ref.shape[1] - 16
@@ -269,7 +286,12 @@
         return total, live_total
 
     start = (jnp.zeros((charge_ch, n), F32), jnp.zeros((1, n), F32))
-    total, live_total = lax.fori_loop(0, groups, add_charges, start)
+    if groups <= 4:
+        for g in range(groups):
+            start = add_charges(g, start)
+        total, live_total = start
+    else:
+        total, live_total = lax.fori_loop(0, groups, add_charges, start)
     mean = jnp.sum(total, axis=1, keepdims=True) / jnp.sum(live_total, axis=1, keepdims=True)
     mean = mean.astype(BF16).astype(F32)
     charge_ref[...] = charge_scr[0]
@@ -282,19 +304,17 @@
             tx, ty, tz = axis_tables(pos, place_of(meta_ref, m, 0, sizes), sizes)
             live = pos[3:4, :]
             living = jnp.concatenate([tz[0] * live, tz[1] * live], axis=0).astype(BF16)
+            plane = plane_table(tx, ty).astype(BF16)
+            if kept:
+                kept[0][m] = plane
+                kept[1][m] = jnp.concatenate(tz, axis=0)
             left.append(
                 jnp.concatenate([spread((charge_scr[m] - mean) * live, tz), living], axis=0)
             )
-            right.append(plane_table(tx, ty).astype(BF16))
+            right.append(plane)
         return dot_nt(jnp.concatenate(left, axis=1), jnp.concatenate(right, axis=1))
 
-    sums_ref[...] = structure(0)
-
-    def add_structure(g, _):
-        sums_ref[...] += structure(g)
-        return 0
-
-    lax.fori_loop(1, groups, add_structure, 0)
+    add_groups(structure, groups, sums_ref)
     part_ref[0 : wide + 16, :] = sums_ref[...].astype(BF16)
     part_ref[wide + 16 : wide + 16 + charge_ch, :] = jnp.broadcast_to(mean, (charge_ch, 256)).astype(
         BF16
@@ -415,7 +435,7 @@
     grad_ref[...] = jnp.where(live_rows, grad, 0.0).astype(BF16)
 
 
-def pair_force(sizes, meta_ref, places, strengths_ref, n):
+def pair_force(sizes, meta_ref, places, strengths_ref, n, slopes_to=None, slopes_from=None):
     own_cols = columns(places[0][0], n)
     odd = lax.rem(meta_ref[0], 2)
     blocks = blocks_of(sizes)
@@ -427,12 +447,19 @@
             half, m = block_place(sizes, odd, block)
             pos = places[half][m]
             offs = offsets(cols, [pos[a : a + 1, :] for a in range(3)], block)
-            u, decays = pair_terms(offs, block, first)
+            if slopes_from is None:
+                u, decays = pair_terms(offs, block, first)
             strength = jnp.zeros((32, n), F32)
             for b, g in enumerate(GAMMAS):
-                part = strengths_ref[b * n + first : b * n + first + 32, t * n : (t + 1) * n]
-                strength = strength + decays[b] * (g * u + 2.0) * part
-            strength = strength * u
+                lo = b * n + first
+                part = strengths_ref[lo : lo + 32, t * n : (t + 1) * n]
+                if slopes_from is None:
+                    slope = decays[b] * (g * u + 2.0) * u
+                else:
+                    slope = slopes_from[lo : lo + 32, t * n : (t + 1) * n]
+                if slopes_to is not None:
+                    slopes_to[lo : lo + 32, t * n : (t + 1) * n] = slope
+                strength = strength + slope * part
             for a in range(3):
                 acc[a] = acc[a] + strength * offs[a]
         for a in range(3):
@@ -461,8 +488,9 @@
     energy_ref,
     force_ref,
     lifted_ref,
-    strength_scr,
+    *rest,
 ):
+    *slopes, strength_scr = rest
     n = grad_ref.shape[0]
     charge_ch = w_long_ref.shape[0]
     own = places_ref[0]
@@ -480,33 +508,36 @@
         lifted.append(dot(basis, w_mix_ref[...]).astype(BF16))
     lifted_ref[...] = jnp.concatenate(lifted, axis=0)
     strength_scr[...] = dot_nt(jnp.concatenate(rows, axis=0), xcat_ref[...])
-    near = pair_force(sizes, meta_ref, (places_ref, far_places_ref), strength_scr, n)
+    places = (places_ref, far_places_ref)
+    near = pair_force(sizes, meta_ref, places, strength_scr, n, slopes[0] if slopes else None)
     pull = dot_nt(w_long_ref[...], grad)
     tables = axis_tables(own, place_of(meta_ref, 0, 0, sizes), sizes)
     slope = field_slope(field_ref[...], tables, sizes, pull, charge_ch)
     force_ref[...] = jnp.concatenate([near[a] - slope[a] for a in range(3)], axis=0)
 
 
-def pull_kernel(sizes, group, meta_ref, near_ref, places_ref, w_long_ref, sums_ref, part_ref):
+def pull_kernel(sizes, group, meta_ref, near_ref, places_ref, w_long_ref, *rest):
+    *kept, sums_ref, part_ref = rest
+    n = near_ref.shape[1]
     groups = near_ref.shape[0] // group
 
     def structure(g):
         left, right = [], []
+        rows = jnp.concatenate([near_ref[g * group + j] for j in range(group)], axis=0)
+        pulls = dot_nt(w_long_ref[...], rows)
         for j in range(group):
             m = g * group + j
-            pos = places_ref[m]
-            tx, ty, tz = axis_tables(pos, place_of(meta_ref, m, 0, sizes), sizes)
-            left.append(spread(dot_nt(w_long_ref[...], near_ref[m]), tz))
-            right.append(plane_table(tx, ty).astype(BF16))
+            if kept:
+                tz = (kept[1][m, 0:8, :], kept[1][m, 8:16, :])
+                right.append(kept[0][m])
+            else:
+                pos = places_ref[m]
+                tx, ty, tz = axis_tables(pos, place_of(meta_ref, m, 0, sizes), sizes)
+                right.append(plane_table(tx, ty).astype(BF16))
+            left.append(spread(pulls[:, j * n : (j + 1) * n], tz))
         return dot_nt(jnp.concatenate(left, axis=1), jnp.concatenate(right, axis=1))
 
-    sums_ref[...] = structure(0)
-
-    def add_structure(g, _):
-        sums_ref[...] += structure(g)
-        return 0
-
-    lax.fori_loop(1, groups, add_structure, 0)
+    add_groups(structure, groups, sums_ref)
     part_ref[...] = sums_ref[...].astype(BF16)
 
 
@@ -519,10 +550,9 @@
     far_places_ref,
     lifted_ref,
     force_ref,
-    out_ref,
-    gcat_scr,
-    strength_scr,
+    *rest,
 ):
+    *slopes, out_ref, gcat_scr, strength_scr = rest
     n = lifted_ref.shape[1]
     halves = (near_ref, far_ref)
     odd = lax.rem(meta_ref[0], 2)
@@ -530,7 +560,8 @@
         half, m = block_place(sizes, odd, block)
         gcat_scr[t * n : (t + 1) * n, :] = halves[half][m]
     strength_scr[...] = dot_nt(lifted_ref[...], gcat_scr[...])
-    near = pair_force(sizes, meta_ref, (places_ref, far_places_ref), strength_scr, n)
+    places = (places_ref, far_places_ref)
+    near = pair_force(sizes, meta_ref, places, strength_scr, n, None, slopes[0] if slopes else None)
     out_ref[...] = force_ref[...] + jnp.concatenate(near, axis=0)
 
 
@@ -559,7 +590,19 @@
         out_ref[a] = force_ref[a : a + 1, :] - slope[a]
 
 
-def gather_cells(rows, sizes, beside):
+def gather_line(rows, nz):
+    value = rows[None]
+    return jnp.concatenate(
+        [value]
+        + [
+            lax.ppermute(value, "gz", [(i, (i + s) % nz) for i in range(nz)])
+            for s in range(1, nz)
+        ],
+        axis=0,
+    )
+
+
+def gather_cells(value, sizes, beside):
     nx, ny, nz = sizes
     pairs = nx // 2
 
@@ -570,15 +613,6 @@
                 moves.append((i * ny + j, (i + 2 * dx) % nx * ny + (j + dy) % ny))
         return lax.ppermute(value, ("gx", "gy"), moves)
 
-    value = rows[None]
-    value = jnp.concatenate(
-        [value]
-        + [
-            lax.ppermute(value, "gz", [(i, (i + s) % nz) for i in range(nz)])
-            for s in range(1, nz)
-        ],
-        axis=0,
-    )
     if pairs * ny <= 4:
         steps = [(dx, dy) for dx in range(pairs) for dy in range(ny)]
         value = jnp.concatenate(
@@ -663,6 +697,7 @@
         0,
         1000,
     )
+    line, k_filter, k_index = lax.optimization_barrier((gather_line(packed, sizes[2]), k_filter, k_index))
     filt, bias, energy_row = run(
         lambda *refs: fold_kernel(scale_long, *refs),
         "fold_filter",
@@ -677,9 +712,9 @@
         0,
         1_000_000_000,
     )
-    near, filt, bias, energy_row = gather_cells(packed, sizes, (filt, bias, energy_row))
+    near, filt, bias, energy_row = gather_cells(line, sizes, (filt, bias, energy_row))
     far = from_other_core(near)
-    sums, part, places, charge = run(
+    sums, part, places, charge, *kept = run(
         lambda *refs: charge_kernel(sizes, group, *refs),
         "charge_sums",
         [
@@ -687,7 +722,8 @@
             held((wide + 16 + charge_ch, 256), BF16),
             held((half_cells, 8, n), F32),
             held((charge_ch, n), F32),
-        ],
+        ]
+        + ([held((half_cells, 256, n), BF16), held((half_cells, 16, n), F32)] if fits else []),
         [pltpu.VMEM((half_cells, charge_ch, n), F32)],
         1,
         [meta, near, w_charge, bias],
@@ -738,7 +774,8 @@
         11,
         3_000_000_000,
     )
-    updated, energy, force, lifted = run(
+    grad_line, grad = lax.optimization_barrier((gather_line(grad, sizes[2]), grad))
+    updated, energy, force, lifted, *slopes = run(
         lambda *refs: own_kernel(sizes, *refs),
         "own_terms",
         [
@@ -746,7 +783,8 @@
             shape((1, n), F32),
             held((3, n), F32),
             held((bases * n, channels), BF16),
-        ],
+        ]
+        + ([held((bases * n, blocks * n), F32)] if fits else []),
         [pltpu.VMEM((bases * n, blocks * n), F32)],
         1,
         [
@@ -765,7 +803,7 @@
         10,
         4_000_000_000,
     )
-    grad_near, force, lifted = gather_cells(grad, sizes, (force, lifted))
+    grad_near, force, lifted = gather_cells(grad_line, sizes, (force, lifted))
     grad_far = from_other_core(grad_near)
     back, back_part = run(
         lambda *refs: pull_kernel(sizes, group, *refs),
@@ -773,8 +811,8 @@
         [held((wide, 256), F32), held((wide, 256), BF16)],
         [],
         1,
-        [meta, grad_near, places, w_long],
-        3,
+        [meta, grad_near, places, w_long, *kept],
+        3 + len(kept),
         3_000_000_000,
     )
     far_back = from_other_core(back_part)
@@ -787,8 +825,8 @@
             pltpu.VMEM((bases * n, blocks * n), F32),
         ],
         1,
-        [meta, grad_near, grad_far, places, far_places, lifted, force],
-        6,
+        [meta, grad_near, grad_far, places, far_places, lifted, force, *slopes],
+        6 + len(slopes),
         3_000_000_000,
     )
     (forces,) = run(

time: 55.7 us -> 53.2 us (0.955)
  waiting for transfers between devices: 11.9 us -> 9.43 us
  Pallas kernels: 19.9 us -> 18 us
  starting transfers between devices: 18 us -> 19.1 us
  local copies, waits for them, and re-layouts: 3.85 us -> 4.56 us
    ppermute x6, waiting for transfers between devices: 9.19 us -> 1.9 us  [shifted(): return lax.ppermute(value, ('gx', 'gy'), moves)]
    ppermute x6, waiting for transfers between devices: 2.72 us -> 7.51 us  [gather_line(): lax.ppermute(value, 'gz', [(i, (i + s) % nz) for i in range(nz)])]
    pallas_call x9, Pallas kernels: 19.9 us -> 18 us  [call(): pl.pallas_call(kernel, name=name, out_shape=outs, in_specs=specs, out_spe...]
    unnamed x34 -> x22, local copies, waits for them, and re-layouts: 3.81 us -> 4.56 us
    ppermute x6, starting transfers between devices: 10.1 us -> 10.7 us  [gather_line(): lax.ppermute(value, 'gz', [(i, (i + s) % nz) for i in range(nz)])]
  transfers between devices with their start and end apart: 16 -> 16, of which waited for: 5 -> 6; matrix products, arithmetic and copies ran while one was open for 0% -> 0% of each run, Pallas kernels for 30% -> 28%
where the time goes in v3:
time: 53.2 us; the launch traced here: 52.8 us
  starting transfers between devices  19.1 us (36%)
  Pallas kernels  18 us (34%)
  waiting for transfers between devices  9.43 us (18%)
  local copies, waits for them, and re-layouts  4.56 us (9%)
  between operations  1.44 us (3%)
    pallas_call x9, Pallas kernels, call(): pl.pallas_call(kernel, name=name, out_shape=outs, in_specs=specs, out_spe...  18 us
    ppermute x6, starting transfers between devices, gather_line(): lax.ppermute(value, 'gz', [(i, (i + s) % nz) for i in range(nz)])  10.7 us
    ppermute x6, waiting for transfers between devices, gather_line(): lax.ppermute(value, 'gz', [(i, (i + s) % nz) for i in range(nz)])  7.51 us
    ppermute x6, starting transfers between devices, shifted(): return lax.ppermute(value, ('gx', 'gy'), moves)  7.11 us
    unnamed x22, local copies, waits for them, and re-layouts  4.56 us
    ppermute x6, waiting for transfers between devices, shifted(): return lax.ppermute(value, ('gx', 'gy'), moves)  1.9 us
    ppermute x4, starting transfers between devices, from_other_core(): lax.ppermute(value, 'gx', [(i, i ^ 1) for i in range(lax.axis_size('gx'))])  1.26 us
  transfers between devices with their start and end apart: 16, of which 6 were waited for; matrix products, arithmetic and copies ran while one was open for 0% of the time, Pallas kernels for 28%

profile of v3, /device:TPU:0, one launch (start us, length us, event | category | flops | bytes accessed | tf_op | source)
XLA Modules:
  0.0 52.8 jit_solution(5576430630225665423)
XLA Ops:
  2.7 3.1 %collective-permute-start = (bf16[1,144,128]{2,1,0:T(8,128)(2,1)S(1)}, bf16[1,144,128]{2,1,0:T(8,128)(2,1)S(1)}, u32[]{:S(2)}, u32[]{:S(2)}) collective-permute-start(bf16[1,144,128]{2,1,0:T(8,128)(2,1)S(1)} %bitcast.17), channel_id=1, source_target_pairs={{0,1},{1,2},{2,3},{3,0},{4,5},{5,6},{6,7},{7,4},{8,9},{9,10},{10,1... | collective-permute-start | bytes 110600 | tf_op jit(solution)/shard_map/ppermute | solution.py:598
  5.8 2.6 %collective-permute-start.1 = (bf16[1,144,128]{2,1,0:T(8,128)(2,1)S(1)}, bf16[1,144,128]{2,1,0:T(8,128)(2,1)S(1)}, u32[]{:S(2)}, u32[]{:S(2)}) collective-permute-start(bf16[1,144,128]{2,1,0:T(8,128)(2,1)S(1)} %bitcast.18), channel_id=1, source_target_pairs={{0,2},{1,3},{2,0},{3,1},{4,6},{5,7},{6,4},{7,5},{8,10},{9,11},{10,... | collective-permute-start | bytes 110600 | tf_op jit(solution)/shard_map/ppermute | solution.py:598
  8.4 1.3 %collective-permute-start.2 = (bf16[1,144,128]{2,1,0:T(8,128)(2,1)S(1)}, bf16[1,144,128]{2,1,0:T(8,128)(2,1)S(1)}, u32[]{:S(2)}, u32[]{:S(2)}) collective-permute-start(bf16[1,144,128]{2,1,0:T(8,128)(2,1)S(1)} %bitcast.19), channel_id=1, source_target_pairs={{0,3},{1,0},{2,1},{3,2},{4,7},{5,4},{6,5},{7,6},{8,11},{9,8},{10,9... | collective-permute-start | bytes 110600 | tf_op jit(solution)/shard_map/ppermute | solution.py:598
  9.8 1.3 %collective-permute-done.1 = bf16[1,144,128]{2,1,0:T(8,128)(2,1)S(1)} collective-permute-done((bf16[1,144,128]{2,1,0:T(8,128)(2,1)S(1)}, bf16[1,144,128]{2,1,0:T(8,128)(2,1)S(1)}, u32[]{:S(2)}, u32[]{:S(2)}) %collective-permute-start.1) | collective-permute-done | bytes 36896 | tf_op jit(solution)/shard_map/ppermute | solution.py:598
  11.1 1.3 %collective-permute-done.2 = bf16[1,144,128]{2,1,0:T(8,128)(2,1)S(1)} collective-permute-done((bf16[1,144,128]{2,1,0:T(8,128)(2,1)S(1)}, bf16[1,144,128]{2,1,0:T(8,128)(2,1)S(1)}, u32[]{:S(2)}, u32[]{:S(2)}) %collective-permute-start.2) | collective-permute-done | bytes 36896 | tf_op jit(solution)/shard_map/ppermute | solution.py:598
  12.4 1.6 %collective-permute-start.3 = (bf16[4,144,128]{2,1,0:T(8,128)(2,1)S(1)}, bf16[4,144,128]{2,1,0:T(8,128)(2,1)S(1)}, u32[]{:S(2)}, u32[]{:S(2)}) collective-permute-start(bf16[4,144,128]{2,1,0:T(8,128)(2,1)S(1)} %pad_maximum_fusion.2), channel_id=1, source_target_pairs={{0,4},{4,0},{8,12},{12,8},{16,20},{20,16},{24,28},{28,24},{1,5},{5... | collective-permute-start | bytes 442376 | tf_op jit(solution)/shard_map/ppermute | solution.py:614
  14.0 1.5 %collective-permute-start.4 = (bf16[4,144,128]{2,1,0:T(8,128)(2,1)S(1)}, bf16[4,144,128]{2,1,0:T(8,128)(2,1)S(1)}, u32[]{:S(2)}, u32[]{:S(2)}) collective-permute-start(bf16[4,144,128]{2,1,0:T(8,128)(2,1)S(1)} %pad_maximum_fusion.2), channel_id=1, source_target_pairs={{0,16},{4,20},{8,24},{12,28},{16,0},{20,4},{24,8},{28,12},{1,17},{... | collective-permute-start | bytes 442376 | tf_op jit(solution)/shard_map/ppermute | solution.py:614
  15.9 1.0 %copy-done.3 = f32[64,2048]{1,0:T(8,128)S(1)} copy-done((f32[64,2048]{1,0:T(8,128)S(1)}, f32[64,2048]{1,0:T(8,128)}, u32[]{:S(2)}) %copy-start.3) | copy-done | bytes 524312
  19.1 2.1 %fold_filter.1 = (f32[7,256,128]{2,1,0:T(8,128)S(1)}, f32[64,128]{1,0:T(8,128)S(1)}, f32[1,128]{1,0:T(1,128)S(1)}) custom-call(f32[64,2048]{1,0:T(8,128)S(1)} %copy-done.3, s32[3,2048]{1,0:T(4,128)S(1)} %copy-done.5, f32[1,64]{1,0:T(1,128)S(1)} %bitcast.28, f32[1,128]{1,0:T(1,128)S(1)} %bitcast.29), custom_call_target="tpu_custom_call" | custom-call | flops 1000000000 | bytes 2000000 | tf_op jit(solution)/shard_map/fold_filter/pallas_call | solution.py:642
  22.1 2.3 %charge_sums.1 = (f32[912,256]{1,0:T(8,128)S(1)}, bf16[976,256]{1,0:T(8,128)(2,1)S(1)}, f32[16,8,128]{2,1,0:T(8,128)S(1)}, f32[64,128]{1,0:T(8,128)S(1)}, bf16[1...) custom-call(s32[3]{0:T(128)S(1)} %pad_add_fusion.refs_0_.refs_1_, ...), custom_call_target="tpu_custom_call" | custom-call | flops 3000000000 | bytes 2000000 | tf_op jit(solution)/shard_map/charge_sums/pallas_call | solution.py:642
  24.9 2.6 %message.1 = (f32[128,128]{1,0:T(8,128)S(1)}, f32[16,8,128]{2,1,0:T(8,128)S(1)}, bf16[2304,128]{1,0:T(8,128)(2,1)S(1)}) custom-call(s32[3]{0:T(128)S(1)} %pad_add_fusion.refs_0_.refs_1_, bf16[16,144,128]{2,1,0:T(8,128)(2,1)S(1)} %pad_maximum_fusion.refs_1_, bf16[16,144,128]{2,1,0:T(8,128)(2,1)S(1)} %collective-permute-done.7.refs_2_, ...), custom_call_target="tpu_custom_call" | custom-call | flops 3000000000 | bytes 2000000 | tf_op jit(solution)/shard_map/message/pallas_call | solution.py:642
  27.6 1.6 %cotangents.1 = (bf16[128,128]{1,0:T(8,128)(2,1)S(1)}, f32[128,128]{1,0:T(8,128)S(1)}, bf16[896,256]{1,0:T(8,128)(2,1)S(1)}, f32[64,128]{1,0:T(8,128)S(1)}) custom-call(s32[1]{0:T(128)} %bitcast.16.refs_0_, s32[3]{0:T(128)S(1)} %pad_add_fusion.refs_0_.refs_1_, f32[912,256]{1,0:T(8,128)S(1)} %get-tuple-element.46.refs_2_, ...), custom_call_target="tpu_custom_call" | custom-call | flops 3000000000 | bytes 2000000 | tf_op jit(solution)/shard_map/cotangents/pallas_call | solution.py:642
  29.3 2.9 %collective-permute-start.10 = (bf16[1,128,128]{2,1,0:T(8,128)(2,1)S(1)}, bf16[1,128,128]{2,1,0:T(8,128)(2,1)S(1)}, u32[]{:S(2)}, u32[]{:S(2)}) collective-permute-start(bf16[1,128,128]{2,1,0:T(8,128)(2,1)S(1)} %bitcast.23), channel_id=1, source_target_pairs={{0,3},{1,0},{2,1},{3,2},{4,7},{5,4},{6,5},{7,6},{8,11},{9,8},{10,9... | collective-permute-start | bytes 98312 | tf_op jit(solution)/shard_map/ppermute | solution.py:598
  32.1 0.8 %collective-permute-start.9 = (bf16[1,128,128]{2,1,0:T(8,128)(2,1)S(1)}, bf16[1,128,128]{2,1,0:T(8,128)(2,1)S(1)}, u32[]{:S(2)}, u32[]{:S(2)}) collective-permute-start(bf16[1,128,128]{2,1,0:T(8,128)(2,1)S(1)} %bitcast.25), channel_id=1, source_target_pairs={{0,2},{1,3},{2,0},{3,1},{4,6},{5,7},{6,4},{7,5},{8,10},{9,11},{10,... | collective-permute-start | bytes 98312 | tf_op jit(solution)/shard_map/ppermute | solution.py:598
  33.0 0.8 %collective-permute-done.10 = bf16[1,128,128]{2,1,0:T(8,128)(2,1)S(1)} collective-permute-done((bf16[1,128,128]{2,1,0:T(8,128)(2,1)S(1)}, bf16[1,128,128]{2,1,0:T(8,128)(2,1)S(1)}, u32[]{:S(2)}, u32[]{:S(2)}) %collective-permute-start.10) | collective-permute-done | bytes 32800 | tf_op jit(solution)/shard_map/ppermute | solution.py:598
  33.7 4.1 %collective-permute-done.8 = bf16[1,128,128]{2,1,0:T(8,128)(2,1)S(1)} collective-permute-done((bf16[1,128,128]{2,1,0:T(8,128)(2,1)S(1)}, bf16[1,128,128]{2,1,0:T(8,128)(2,1)S(1)}, u32[]{:S(2)}, u32[]{:S(2)}) %collective-permute-start.8) | collective-permute-done | bytes 32800 | tf_op jit(solution)/shard_map/ppermute | solution.py:598
  37.9 1.3 %collective-permute-start.11 = (bf16[4,128,128]{2,1,0:T(8,128)(2,1)S(1)}, bf16[4,128,128]{2,1,0:T(8,128)(2,1)S(1)}, u32[]{:S(2)}, u32[]{:S(2)}) collective-permute-start(bf16[4,128,128]{2,1,0:T(8,128)(2,1)S(1)} %pad_maximum_fusion.3), channel_id=1, source_target_pairs={{0,4},{4,0},{8,12},{12,8},{16,20},{20,16},{24,28},{28,24},{1,5},{5... | collective-permute-start | bytes 393224 | tf_op jit(solution)/shard_map/ppermute | solution.py:614
  39.2 1.5 %collective-permute-start.12 = (bf16[4,128,128]{2,1,0:T(8,128)(2,1)S(1)}, bf16[4,128,128]{2,1,0:T(8,128)(2,1)S(1)}, u32[]{:S(2)}, u32[]{:S(2)}) collective-permute-start(bf16[4,128,128]{2,1,0:T(8,128)(2,1)S(1)} %pad_maximum_fusion.3), channel_id=1, source_target_pairs={{0,16},{4,20},{8,24},{12,28},{16,0},{20,4},{24,8},{28,12},{1,17},{... | collective-permute-start | bytes 393224 | tf_op jit(solution)/shard_map/ppermute | solution.py:614
  40.6 0.8 %collective-permute-start.13 = (bf16[4,128,128]{2,1,0:T(8,128)(2,1)S(1)}, bf16[4,128,128]{2,1,0:T(8,128)(2,1)S(1)}, u32[]{:S(2)}, u32[]{:S(2)}) collective-permute-start(bf16[4,128,128]{2,1,0:T(8,128)(2,1)S(1)} %pad_maximum_fusion.3), channel_id=1, source_target_pairs={{0,20},{4,16},{8,28},{12,24},{16,4},{20,0},{24,12},{28,8},{1,21},{... | collective-permute-start | bytes 393224 | tf_op jit(solution)/shard_map/ppermute | solution.py:614
  41.4 3.8 %own_terms.1 = (bf16[128,128]{1,0:T(8,128)(2,1)}, f32[1,128]{1,0:T(1,128)}, f32[3,128]{1,0:T(4,128)S(1)}, bf16[512,128]{1,0:T(8,128)(2,1)S(1)}, f32[512,2304]{1,0:T(8,128)S(1)}) custom-call(s32[3]{0:T(128)S(1)} %pad_add_fusion.refs_0_.refs_1_, bf16[128,128]{1,0:T(8,128)(2,1)S(1)} %get-tuple-element.55.refs_1_, ...), custom_call_target="tpu_custom_call" | custom-call | flops 4000000000 | bytes 2000000 | tf_op jit(solution)/shard_map/own_terms/pallas_call | solution.py:642
  45.3 1.2 %collective-permute-done.13 = bf16[4,128,128]{2,1,0:T(8,128)(2,1)S(1)} collective-permute-done((bf16[4,128,128]{2,1,0:T(8,128)(2,1)S(1)}, bf16[4,128,128]{2,1,0:T(8,128)(2,1)S(1)}, u32[]{:S(2)}, u32[]{:S(2)}) %collective-permute-start.13) | collective-permute-done | bytes 131104 | tf_op jit(solution)/shard_map/ppermute | solution.py:614
  46.7 2.0 %pull_sums.1 = (f32[896,256]{1,0:T(8,128)S(1)}, bf16[896,256]{1,0:T(8,128)(2,1)S(1)}) custom-call(s32[3]{0:T(128)S(1)} %pad_add_fusion.refs_0_.refs_1_, bf16[16,128,128]{2,1,0:T(8,128)(2,1)S(1)} %pad_maximum_fusion.1.refs_1_, f32[16,8,128]{2,1,0:T(8,128)S(1)} %get-tuple-element.48.refs_3_.refs_5_.refs_2_, bf16[64,128]{1,0:T(8,128)(2,1)S(1)} %copy-done.8, ...), custom_call_target="tpu_custom_call" | custom-call | flops 3000000000 | bytes 2000000 | tf_op jit(solution)/shard_map/pull_sums/pallas_call | solution.py:642
  49.2 1.8 %react.1.refs_5_ = f32[3,128]{1,0:T(4,128)S(1)} custom-call(s32[3]{0:T(128)S(1)} %pad_add_fusion.refs_0_.refs_1_, bf16[16,128,128]{2,1,0:T(8,128)(2,1)S(1)} %pad_maximum_fusion.1.refs_1_, bf16[16,128,128]{2,1,0:T(8,128)(2,1)S(1)} %collective-permute-done.15.refs_2_, f32[16,8,128]{2,1,0:T(8,128)S(1)} %get-tuple-element.48.refs_3_.refs_5_.refs_2_, ...), custom_call_target="tpu_custom_call" | custom-call | flops 3000000000 | bytes 2000000 | tf_op jit(solution)/shard_map/react/pallas_call | solution.py:642
  51.0 1.8 %finish.1 = f32[3,1,128]{2,1,0:T(1,128)} custom-call(s32[3]{0:T(128)S(1)} %pad_add_fusion.refs_0_.refs_1_, f32[896,256]{1,0:T(8,128)S(1)} %get-tuple-element.67.refs_1_, bf16[896,256]{1,0:T(8,128)(2,1)S(1)} %collective-permute-done.14.refs_2_, f32[16,8,128]{2,1,0:T(8,128)S(1)} %get-tuple-element.48.refs_3_.refs_5_.refs_2_, ...), custom_call_target="tpu_custom_call" | custom-call | flops 2000000000 | bytes 2000000 | tf_op jit(solution)/shard_map/finish/pallas_call | solution.py:642
  (44 shorter events, 6.2 us)
Async XLA Ops:
  1.3 0.8 %copy-start = (bf16[1,1,1,128,128]{4,3,2,1,0:T(8,128)(2,1)S(1)}, bf16[1,1,1,128,128]{4,3,2,1,0:T(8,128)(2,1)}, u32[]{:S(2)}) copy-start(bf16[1,1,1,128,128]{4,3,2,1,0:T(8,128)(2,1)} %param.11) | copy-start | bytes 98308
  2.7 19.3 %copy-start.7 = (bf16[64,128]{1,0:T(8,128)(2,1)S(1)}, bf16[64,128]{1,0:T(8,128)(2,1)}, u32[]{:S(2)}) copy-start(bf16[64,128]{1,0:T(8,128)(2,1)} %refs_2_.1) | copy-start | bytes 49156
  2.7 7.0 %collective-permute-start = (bf16[1,144,128]{2,1,0:T(8,128)(2,1)S(1)}, bf16[1,144,128]{2,1,0:T(8,128)(2,1)S(1)}, u32[]{:S(2)}, u32[]{:S(2)}) collective-permute-start(bf16[1,144,128]{2,1,0:T(8,128)(2,1)S(1)} %bitcast.17), channel_id=1, source_target_pairs={{0,1},{1,2},{2,3},{3,0},{4,5},{5,6},{6,7},{7,4},{8,9},{9,10},{10,1... | collective-permute-start | bytes 110600 | tf_op jit(solution)/shard_map/ppermute | solution.py:598
  5.8 5.2 %collective-permute-start.1 = (bf16[1,144,128]{2,1,0:T(8,128)(2,1)S(1)}, bf16[1,144,128]{2,1,0:T(8,128)(2,1)S(1)}, u32[]{:S(2)}, u32[]{:S(2)}) collective-permute-start(bf16[1,144,128]{2,1,0:T(8,128)(2,1)S(1)} %bitcast.18), channel_id=1, source_target_pairs={{0,2},{1,3},{2,0},{3,1},{4,6},{5,7},{6,4},{7,5},{8,10},{9,11},{10,... | collective-permute-start | bytes 110600 | tf_op jit(solution)/shard_map/ppermute | solution.py:598
  8.4 4.0 %collective-permute-start.2 = (bf16[1,144,128]{2,1,0:T(8,128)(2,1)S(1)}, bf16[1,144,128]{2,1,0:T(8,128)(2,1)S(1)}, u32[]{:S(2)}, u32[]{:S(2)}) collective-permute-start(bf16[1,144,128]{2,1,0:T(8,128)(2,1)S(1)} %bitcast.19), channel_id=1, source_target_pairs={{0,3},{1,0},{2,1},{3,2},{4,7},{5,4},{6,5},{7,6},{8,11},{9,8},{10,9... | collective-permute-start | bytes 110600 | tf_op jit(solution)/shard_map/ppermute | solution.py:598
  12.4 8.8 %collective-permute-start.3 = (bf16[4,144,128]{2,1,0:T(8,128)(2,1)S(1)}, bf16[4,144,128]{2,1,0:T(8,128)(2,1)S(1)}, u32[]{:S(2)}, u32[]{:S(2)}) collective-permute-start(bf16[4,144,128]{2,1,0:T(8,128)(2,1)S(1)} %pad_maximum_fusion.2), channel_id=1, source_target_pairs={{0,4},{4,0},{8,12},{12,8},{16,20},{20,16},{24,28},{28,24},{1,5},{5... | collective-permute-start | bytes 442376 | tf_op jit(solution)/shard_map/ppermute | solution.py:614
  14.0 7.2 %collective-permute-start.4 = (bf16[4,144,128]{2,1,0:T(8,128)(2,1)S(1)}, bf16[4,144,128]{2,1,0:T(8,128)(2,1)S(1)}, u32[]{:S(2)}, u32[]{:S(2)}) collective-permute-start(bf16[4,144,128]{2,1,0:T(8,128)(2,1)S(1)} %pad_maximum_fusion.2), channel_id=1, source_target_pairs={{0,16},{4,20},{8,24},{12,28},{16,0},{20,4},{24,8},{28,12},{1,17},{... | collective-permute-start | bytes 442376 | tf_op jit(solution)/shard_map/ppermute | solution.py:614
  15.5 6.3 %collective-permute-start.5 = (bf16[4,144,128]{2,1,0:T(8,128)(2,1)S(1)}, bf16[4,144,128]{2,1,0:T(8,128)(2,1)S(1)}, u32[]{:S(2)}, u32[]{:S(2)}) collective-permute-start(bf16[4,144,128]{2,1,0:T(8,128)(2,1)S(1)} %pad_maximum_fusion.2), channel_id=1, source_target_pairs={{0,20},{4,16},{8,28},{12,24},{16,4},{20,0},{24,12},{28,8},{1,21},{... | collective-permute-start | bytes 442376 | tf_op jit(solution)/shard_map/ppermute | solution.py:614
  15.9 1.0 %copy-start.3 = (f32[64,2048]{1,0:T(8,128)S(1)}, f32[64,2048]{1,0:T(8,128)}, u32[]{:S(2)}) copy-start(f32[64,2048]{1,0:T(8,128)} %refs_0_) | copy-start | bytes 1572868
  17.0 0.8 %copy-start.5 = (s32[3,2048]{1,0:T(4,128)S(1)}, s32[3,2048]{1,0:T(4,128)}, u32[]{:S(2)}) copy-start(s32[3,2048]{1,0:T(4,128)} %refs_1_) | copy-start | bytes 73732
  21.9 3.0 %collective-permute-start.7 = (bf16[16,144,128]{2,1,0:T(8,128)(2,1)S(1)}, bf16[16,144,128]{2,1,0:T(8,128)(2,1)S(1)}, u32[]{:S(2)}, u32[]{:S(2)}) collective-permute-start(bf16[16,144,128]{2,1,0:T(8,128)(2,1)S(1)} %pad_maximum_fusion.refs_1_), channel_id=1, source_target_pairs={{0,8},{8,0},{16,24},{24,16},{1,9},{9,1},{17,25},{25,17},{2,10},{10... | collective-permute-start | bytes 1769480 | tf_op jit(solution)/shard_map/ppermute | solution.py:629
  22.1 2.9 %copy-start.4 = (bf16[4,128,128]{2,1,0:T(8,128)(2,1)S(1)}, bf16[4,128,128]{2,1,0:T(8,128)(2,1)}, u32[]{:S(2)}) copy-start(bf16[4,128,128]{2,1,0:T(8,128)(2,1)} %refs_7_.1) | copy-start | bytes 393220
  22.1 2.9 %copy-start.6 = (bf16[128,128]{1,0:T(8,128)(2,1)S(1)}, bf16[128,128]{1,0:T(8,128)(2,1)}, u32[]{:S(2)}) copy-start(bf16[128,128]{1,0:T(8,128)(2,1)} %refs_8_.1) | copy-start | bytes 98308
  24.4 3.2 %collective-permute-start.6 = (bf16[976,256]{1,0:T(8,128)(2,1)S(1)}, bf16[976,256]{1,0:T(8,128)(2,1)S(1)}, u32[]{:S(2)}, u32[]{:S(2)}) collective-permute-start(bf16[976,256]{1,0:T(8,128)(2,1)S(1)} %get-tuple-element.47.refs_3_), channel_id=1, source_target_pairs={{0,8},{8,0},{16,24},{24,16},{1,9},{9,1},{17,25},{25,17},{2,10},{10... | collective-permute-start | bytes 1499144 | tf_op jit(solution)/shard_map/ppermute | solution.py:629
  24.9 2.7 %copy-start.1 = (bf16[1,1,1,128,128]{4,3,2,1,0:T(8,128)(2,1)S(1)}, bf16[1,1,1,128,128]{4,3,2,1,0:T(8,128)(2,1)}, u32[]{:S(2)}) copy-start(bf16[1,1,1,128,128]{4,3,2,1,0:T(8,128)(2,1)} %param.11) | copy-start | bytes 98308
  24.9 2.7 %copy-start.8 = (bf16[64,128]{1,0:T(8,128)(2,1)S(1)}, bf16[64,128]{1,0:T(8,128)(2,1)}, u32[]{:S(2)}) copy-start(bf16[64,128]{1,0:T(8,128)(2,1)} %refs_3_.1) | copy-start | bytes 49156
  29.3 4.5 %collective-permute-start.10 = (bf16[1,128,128]{2,1,0:T(8,128)(2,1)S(1)}, bf16[1,128,128]{2,1,0:T(8,128)(2,1)S(1)}, u32[]{:S(2)}, u32[]{:S(2)}) collective-permute-start(bf16[1,128,128]{2,1,0:T(8,128)(2,1)S(1)} %bitcast.23), channel_id=1, source_target_pairs={{0,3},{1,0},{2,1},{3,2},{4,7},{5,4},{6,5},{7,6},{8,11},{9,8},{10,9... | collective-permute-start | bytes 98312 | tf_op jit(solution)/shard_map/ppermute | solution.py:598
  32.1 5.7 %collective-permute-start.8 = (bf16[1,128,128]{2,1,0:T(8,128)(2,1)S(1)}, bf16[1,128,128]{2,1,0:T(8,128)(2,1)S(1)}, u32[]{:S(2)}, u32[]{:S(2)}) collective-permute-start(bf16[1,128,128]{2,1,0:T(8,128)(2,1)S(1)} %bitcast.24), channel_id=1, source_target_pairs={{0,1},{1,2},{2,3},{3,0},{4,5},{5,6},{6,7},{7,4},{8,9},{9,10},{10,1... | collective-permute-start | bytes 98312 | tf_op jit(solution)/shard_map/ppermute | solution.py:598
  32.1 5.7 %collective-permute-start.9 = (bf16[1,128,128]{2,1,0:T(8,128)(2,1)S(1)}, bf16[1,128,128]{2,1,0:T(8,128)(2,1)S(1)}, u32[]{:S(2)}, u32[]{:S(2)}) collective-permute-start(bf16[1,128,128]{2,1,0:T(8,128)(2,1)S(1)} %bitcast.25), channel_id=1, source_target_pairs={{0,2},{1,3},{2,0},{3,1},{4,6},{5,7},{6,4},{7,5},{8,10},{9,11},{10,... | collective-permute-start | bytes 98312 | tf_op jit(solution)/shard_map/ppermute | solution.py:598
  37.9 7.4 %collective-permute-start.11 = (bf16[4,128,128]{2,1,0:T(8,128)(2,1)S(1)}, bf16[4,128,128]{2,1,0:T(8,128)(2,1)S(1)}, u32[]{:S(2)}, u32[]{:S(2)}) collective-permute-start(bf16[4,128,128]{2,1,0:T(8,128)(2,1)S(1)} %pad_maximum_fusion.3), channel_id=1, source_target_pairs={{0,4},{4,0},{8,12},{12,8},{16,20},{20,16},{24,28},{28,24},{1,5},{5... | collective-permute-start | bytes 393224 | tf_op jit(solution)/shard_map/ppermute | solution.py:614
  39.2 6.1 %collective-permute-start.12 = (bf16[4,128,128]{2,1,0:T(8,128)(2,1)S(1)}, bf16[4,128,128]{2,1,0:T(8,128)(2,1)S(1)}, u32[]{:S(2)}, u32[]{:S(2)}) collective-permute-start(bf16[4,128,128]{2,1,0:T(8,128)(2,1)S(1)} %pad_maximum_fusion.3), channel_id=1, source_target_pairs={{0,16},{4,20},{8,24},{12,28},{16,0},{20,4},{24,8},{28,12},{1,17},{... | collective-permute-start | bytes 393224 | tf_op jit(solution)/shard_map/ppermute | solution.py:614
  40.6 5.9 %collective-permute-start.13 = (bf16[4,128,128]{2,1,0:T(8,128)(2,1)S(1)}, bf16[4,128,128]{2,1,0:T(8,128)(2,1)S(1)}, u32[]{:S(2)}, u32[]{:S(2)}) collective-permute-start(bf16[4,128,128]{2,1,0:T(8,128)(2,1)S(1)} %pad_maximum_fusion.3), channel_id=1, source_target_pairs={{0,20},{4,16},{8,28},{12,24},{16,4},{20,0},{24,12},{28,8},{1,21},{... | collective-permute-start | bytes 393224 | tf_op jit(solution)/shard_map/ppermute | solution.py:614
  46.6 2.6 %collective-permute-start.15 = (bf16[16,128,128]{2,1,0:T(8,128)(2,1)S(1)}, bf16[16,128,128]{2,1,0:T(8,128)(2,1)S(1)}, u32[]{:S(2)}, u32[]{:S(2)}) collective-permute-start(bf16[16,128,128]{2,1,0:T(8,128)(2,1)S(1)} %pad_maximum_fusion.1.refs_1_), channel_id=1, source_target_pairs={{0,8},{8,0},{16,24},{24,16},{1,9},{9,1},{17,25},{25,17},{2,10},{10... | collective-permute-start | bytes 1572872 | tf_op jit(solution)/shard_map/ppermute | solution.py:629
  48.7 2.3 %collective-permute-start.14 = (bf16[896,256]{1,0:T(8,128)(2,1)S(1)}, bf16[896,256]{1,0:T(8,128)(2,1)S(1)}, u32[]{:S(2)}, u32[]{:S(2)}) collective-permute-start(bf16[896,256]{1,0:T(8,128)(2,1)S(1)} %get-tuple-element.68), channel_id=1, source_target_pairs={{0,8},{8,0},{16,24},{24,16},{1,9},{9,1},{17,25},{25,17},{2,10},{10... | collective-permute-start | bytes 1376264 | tf_op jit(solution)/shard_map/ppermute | solution.py:629
  (3 other events, 2.0 us)

commit v4 on v3

--- a/solution.py
+++ b/solution.py
@@ -107,10 +107,9 @@
         ).astype(BF16)
 
 
-def field_slope(field, tables, sizes, weights, charge_ch):
-    tx, ty, tz = tables
-    n = tx[0].shape[1]
-    planes = jnp.concatenate(
+def slope_planes(tables, sizes):
+    tx, ty, _ = tables
+    return jnp.concatenate(
         [
             plane_table(derivative(tx, sizes[0]), ty).astype(BF16),
             plane_table(tx, derivative(ty, sizes[1])).astype(BF16),
@@ -118,6 +117,10 @@
         ],
         axis=1,
     )
+
+
+def field_slope(field, planes, tz, sizes, weights, charge_ch):
+    n = tz[0].shape[1]
     spread_field = dot(field, planes)
     slope_z = derivative(tz, sizes[2])
     total = [jnp.zeros((charge_ch, n), F32) for _ in range(3)]
@@ -181,7 +184,16 @@
     return [jnp.transpose(jnp.broadcast_to(pos[a : a + 1, :], (n, n))) for a in range(3)]
 
 
-def pack_kernel(count_ref, features_ref, positions_ref, out_ref):
+def fetch(sources, places, sems):
+    copies = [pltpu.make_async_copy(s, p, sems.at[i]) for i, (s, p) in enumerate(zip(sources, places))]
+    for c in copies:
+        c.start()
+    for c in copies:
+        c.wait()
+
+
+def pack_kernel(count_ref, features_hbm, positions_hbm, out_ref, features_ref, positions_ref, sems):
+    fetch((features_hbm, positions_hbm), (features_ref, positions_ref), sems)
     n, channels = features_ref.shape
     live_col = lax.broadcasted_iota(jnp.int32, (n, channels), 0) < count_ref[0]
     rows = features_ref[...].astype(F32)
@@ -195,29 +207,54 @@
     out_ref[n : n + 16, :] = tail.astype(BF16)
 
 
-def fold_kernel(scale, filter_ref, index_ref, bias_ref, energy_ref, out_ref, column_ref, row_ref):
+def fold_kernel(
+    scale,
+    filter_hbm,
+    index_hbm,
+    bias_hbm,
+    energy_hbm,
+    proj_hbm,
+    mix_hbm,
+    out_ref,
+    column_ref,
+    row_ref,
+    mixed_ref,
+    filter_ref,
+    index_ref,
+    bias_ref,
+    energy_ref,
+    proj_ref,
+    mix_ref,
+    sems,
+):
+    fetch(
+        (filter_hbm, index_hbm, bias_hbm, energy_hbm, proj_hbm, mix_hbm),
+        (filter_ref, index_ref, bias_ref, energy_ref, proj_ref, mix_ref),
+        sems,
+    )
     waves = filter_ref.shape[1]
+    charge_ch = filter_ref.shape[0]
+    row_ref[...] = energy_ref[...]
+    diagonal = lax.broadcasted_iota(jnp.int32, (charge_ch, charge_ch), 0) == (
+        lax.broadcasted_iota(jnp.int32, (charge_ch, charge_ch), 1)
+    )
+    column = jnp.sum(jnp.where(diagonal, bias_ref[...], 0.0), axis=1, keepdims=True)
+    column_ref[...] = jnp.broadcast_to(column, column_ref.shape)
+    mixed_ref[...] = dot(proj_ref[...], mix_ref[...]).astype(BF16)
     k = index_ref[...]
     positive = [jnp.where(k[a : a + 1, :] >= 0, 1.0, -1.0) for a in range(3)]
     sign_b = positive[0] * positive[1]
     sign_c = positive[0] * positive[2]
     size = jnp.abs(k)
-    plane = size[0:1, :] * 8 + size[1:2, :]
+    key = size[2:3, :] * 64 + size[0:1, :] * 8 + size[1:2, :]
     f = filter_ref[...] * scale
     stacked = jnp.concatenate([f, f * sign_b, f * sign_c, f * (sign_b * sign_c)], axis=0).astype(BF16)
-    rows = lax.broadcasted_iota(jnp.int32, (64, waves), 0)
-    charge_ch = filter_ref.shape[0]
-    row_ref[...] = energy_ref[...]
-    diagonal = lax.broadcasted_iota(jnp.int32, (charge_ch, charge_ch), 0) == (
-        lax.broadcasted_iota(jnp.int32, (charge_ch, charge_ch), 1)
-    )
-    column = jnp.sum(jnp.where(diagonal, bias_ref[...], 0.0), axis=1, keepdims=True)
-    column_ref[...] = jnp.broadcast_to(column, column_ref.shape)
+    rows = lax.broadcasted_iota(jnp.int32, (ORDERS * 64, waves), 0)
+    parts = dot_nt(stacked, jnp.where(rows == key, 1.0, 0.0).astype(BF16))
     turn = jnp.where(lax.broadcasted_iota(jnp.int32, (charge_ch, 128), 1) < 64, -1.0, 1.0)
     for c in range(ORDERS):
-        key = jnp.where(size[2:3, :] == c, plane, -1)
-        chosen = jnp.where(rows == key, 1.0, 0.0).astype(BF16)
-        part = dot_nt(stacked, jnp.concatenate([chosen, chosen], axis=0))
+        part = parts[:, c * 64 : (c + 1) * 64]
+        part = jnp.concatenate([part, part], axis=1)
         for w in range(4):
             piece = part[w * charge_ch : (w + 1) * charge_ch, :]
             out_ref[c, w * charge_ch : (w + 1) * charge_ch, :] = piece * turn if w % 2 == 1 else piece
@@ -327,14 +364,12 @@
     near_ref,
     far_ref,
     near_places_ref,
-    w_proj_ref,
-    w_mix_ref,
+    mixed_ref,
     short_ref,
     far_places_ref,
     xcat_ref,
     radial_scr,
 ):
-    channels = near_ref.shape[2]
     n = near_ref.shape[1] - 16
     halves = (near_ref, far_ref)
     places = (near_places_ref, far_places_ref)
@@ -361,10 +396,8 @@
                     decays[b] * u2
                 ).astype(BF16)
     gathered = dot(radial_scr[...], xcat_ref[...]).astype(BF16)
-    message = jnp.zeros((n, channels), F32)
-    for b in range(len(GAMMAS)):
-        message = message + dot(gathered[b * n : (b + 1) * n, :], w_proj_ref[b])
-    short_ref[...] = dot(message.astype(BF16), w_mix_ref[...])
+    gathered = jnp.concatenate([gathered[b * n : (b + 1) * n, :] for b in range(len(GAMMAS))], axis=1)
+    short_ref[...] = dot(gathered, mixed_ref[...])
 
 
 def cotangent_kernel(
@@ -382,11 +415,9 @@
     w_long_ref,
     w_energy_ref,
     filt_ref,
-    grad_ref,
-    refined_ref,
-    field_ref,
-    neutral_ref,
+    *rest,
 ):
+    *kept, grad_ref, refined_ref, field_ref, neutral_ref = rest
     n, channels = features_ref.shape
     charge_ch = w_long_ref.shape[0]
     wide = 2 * ORDERS * charge_ch
@@ -414,8 +445,13 @@
 
     filtered(load, filt_ref, field_ref, charge_ch)
     neutral_ref[...] = (charge_ref[...] - mean) * live_row
-    tx, ty, tz = axis_tables(own, place_of(meta_ref, 0, 0, sizes), sizes)
-    lifted = dot(field_ref[...], plane_table(tx, ty).astype(BF16))
+    if kept:
+        plane = kept[0][0]
+        tz = (kept[1][0, 0:8, :], kept[1][0, 8:16, :])
+    else:
+        tx, ty, tz = axis_tables(own, place_of(meta_ref, 0, 0, sizes), sizes)
+        plane = plane_table(tx, ty).astype(BF16)
+    lifted = dot(field_ref[...], plane)
     potential = jnp.zeros((charge_ch, n), F32)
     for kind in range(2):
         for c in range(ORDERS):
@@ -480,14 +516,15 @@
     far_places_ref,
     xcat_ref,
     refined_ref,
-    w_proj_ref,
-    w_mix_ref,
+    mixed_ref,
     w_long_ref,
     w_energy_ref,
     updated_ref,
     energy_ref,
     force_ref,
     lifted_ref,
+    planes_ref,
+    levels_ref,
     *rest,
 ):
     *slopes, strength_scr = rest
@@ -500,19 +537,22 @@
         jnp.transpose(refined * sigmoid(refined) * w_energy_ref[...]), axis=0, keepdims=True
     )
     grad = grad_ref[...]
-    adjoint = dot_nt(grad, w_mix_ref[...]).astype(BF16)
+    channels = grad.shape[1]
     rows, lifted = [], []
     for b in range(len(GAMMAS)):
-        rows.append(dot_nt(adjoint, w_proj_ref[b]).astype(BF16))
-        basis = dot(xcat_ref[0:n, :], w_proj_ref[b]).astype(BF16)
-        lifted.append(dot(basis, w_mix_ref[...]).astype(BF16))
+        mixed = mixed_ref[b * channels : (b + 1) * channels, :]
+        rows.append(dot_nt(grad, mixed).astype(BF16))
+        lifted.append(dot(xcat_ref[0:n, :], mixed).astype(BF16))
     lifted_ref[...] = jnp.concatenate(lifted, axis=0)
     strength_scr[...] = dot_nt(jnp.concatenate(rows, axis=0), xcat_ref[...])
     places = (places_ref, far_places_ref)
     near = pair_force(sizes, meta_ref, places, strength_scr, n, slopes[0] if slopes else None)
     pull = dot_nt(w_long_ref[...], grad)
     tables = axis_tables(own, place_of(meta_ref, 0, 0, sizes), sizes)
-    slope = field_slope(field_ref[...], tables, sizes, pull, charge_ch)
+    planes = slope_planes(tables, sizes)
+    planes_ref[...] = planes
+    levels_ref[...] = jnp.concatenate(tables[2], axis=0)
+    slope = field_slope(field_ref[...], planes, tables[2], sizes, pull, charge_ch)
     force_ref[...] = jnp.concatenate([near[a] - slope[a] for a in range(3)], axis=0)
 
 
@@ -567,10 +607,10 @@
 
 def finish_kernel(
     sizes,
-    meta_ref,
     sums_ref,
     far_part_ref,
-    places_ref,
+    planes_ref,
+    levels_ref,
     neutral_ref,
     force_ref,
     filt_ref,
@@ -584,8 +624,8 @@
         return sums_ref[lo : lo + charge_ch, :] + far_part_ref[lo : lo + charge_ch, :].astype(F32)
 
     filtered(load, filt_ref, field_scr, charge_ch)
-    tables = axis_tables(places_ref[0], place_of(meta_ref, 0, 0, sizes), sizes)
-    slope = field_slope(field_scr[...], tables, sizes, neutral_ref[...], charge_ch)
+    tz = (levels_ref[0:8, :], levels_ref[8:16, :])
+    slope = field_slope(field_scr[...], planes_ref[...], tz, sizes, neutral_ref[...], charge_ch)
     for a in range(3):
         out_ref[a] = force_ref[a : a + 1, :] - slope[a]
 
@@ -629,15 +669,17 @@
     return lax.ppermute(value, "gx", [(i, i ^ 1) for i in range(lax.axis_size("gx"))])
 
 
-def call(kernel, name, outs, scratch, smem, operands, kept, limit, flops):
+def call(kernel, name, outs, scratch, smem, operands, kept, limit, flops, fetched):
     n_in = len(operands)
     first = n_in - kept
     operands = [
-        pltpu.with_memory_space_constraint(o, pltpu.VMEM) if i >= first else o
+        pltpu.with_memory_space_constraint(o, pltpu.HBM if fetched else pltpu.VMEM)
+        if i >= (smem if fetched else first)
+        else o
         for i, o in enumerate(operands)
     ]
     specs = [pl.BlockSpec(memory_space=pltpu.SMEM)] * smem + [
-        pl.BlockSpec(memory_space=pltpu.VMEM)
+        pl.BlockSpec(memory_space=pltpu.HBM if fetched else pltpu.VMEM)
     ] * (n_in - smem)
     return pl.pallas_call(
         kernel,
@@ -683,9 +725,12 @@
     limit = (24 if fits else 56) * 1024 * 1024
     held = pltpu.VMEM if fits else shape
 
-    def run(kernel, name, outs, scratch, smem, operands, kept, flops):
+    def run(kernel, name, outs, scratch, smem, operands, kept, flops, fetched=False):
         kept = kept if fits else 0
-        return call(kernel, name, outs, scratch, smem, operands, kept, limit, flops)
+        if fetched:
+            places = [pltpu.VMEM(o.shape, o.dtype) for o in operands[smem:]]
+            scratch = [*places, pltpu.SemaphoreType.DMA((len(places),))]
+        return call(kernel, name, outs, scratch, smem, operands, kept, limit, flops, fetched)
 
     (packed,) = run(
         pack_kernel,
@@ -696,23 +741,34 @@
         [count, own_rows, positions.reshape(3, 1, n)],
         0,
         1000,
-    )
-    line, k_filter, k_index = lax.optimization_barrier((gather_line(packed, sizes[2]), k_filter, k_index))
-    filt, bias, energy_row = run(
+        fetched=True,
+    )
+    filt, bias, energy_row, mixed = run(
         lambda *refs: fold_kernel(scale_long, *refs),
         "fold_filter",
         [
             held((ORDERS, 4 * charge_ch, 128), F32),
             held((charge_ch, n), F32),
             held((1, channels), F32),
+            held((bases * channels, channels), BF16),
         ],
         [],
         0,
-        [k_filter, k_index, charge_bias[None, :], w_energy[None, :]],
+        [
+            k_filter,
+            k_index,
+            charge_bias[None, :],
+            w_energy[None, :],
+            w_proj.reshape(bases * channels, channels),
+            w_mix,
+        ],
         0,
         1_000_000_000,
-    )
-    near, filt, bias, energy_row = gather_cells(line, sizes, (filt, bias, energy_row))
+        fetched=True,
+    )
+    line = gather_line(packed, sizes[2])
+    line, filt, bias, energy_row, mixed = lax.optimization_barrier((line, filt, bias, energy_row, mixed))
+    (near,) = gather_cells(line, sizes, ())
     far = from_other_core(near)
     sums, part, places, charge, *kept = run(
         lambda *refs: charge_kernel(sizes, group, *refs),
@@ -741,8 +797,8 @@
         ],
         [pltpu.VMEM((bases * n, blocks * n), BF16)],
         1,
-        [meta, near, far, places, w_proj, w_mix],
-        5,
+        [meta, near, far, places, mixed],
+        4,
         3_000_000_000,
     )
     grad, refined, field, neutral = run(
@@ -770,12 +826,13 @@
             w_long,
             energy_row,
             filt,
+            *kept,
         ],
-        11,
+        11 + len(kept),
         3_000_000_000,
     )
     grad_line, grad = lax.optimization_barrier((gather_line(grad, sizes[2]), grad))
-    updated, energy, force, lifted, *slopes = run(
+    updated, energy, force, lifted, planes, levels, *slopes = run(
         lambda *refs: own_kernel(sizes, *refs),
         "own_terms",
         [
@@ -783,6 +840,8 @@
             shape((1, n), F32),
             held((3, n), F32),
             held((bases * n, channels), BF16),
+            held((256, 3 * n), BF16),
+            held((16, n), F32),
         ]
         + ([held((bases * n, blocks * n), F32)] if fits else []),
         [pltpu.VMEM((bases * n, blocks * n), F32)],
@@ -795,12 +854,11 @@
             far_places,
             xcat,
             refined,
-            w_proj,
-            w_mix,
+            mixed,
             w_long,
             energy_row,
         ],
-        10,
+        9,
         4_000_000_000,
     )
     grad_near, force, lifted = gather_cells(grad_line, sizes, (force, lifted))
@@ -834,9 +892,9 @@
         "finish",
         [shape((3, 1, n), F32)],
         [pltpu.VMEM((wide, 256), BF16)],
-        1,
-        [meta, back, far_back, places, neutral, force, filt],
-        6,
+        0,
+        [back, far_back, planes, levels, neutral, force, filt],
+        7,
         2_000_000_000,
     )
     return (

time: 53.2 us -> 51.4 us (0.966)
  local copies, waits for them, and re-layouts: 4.56 us -> 0.01 us
  waiting for transfers between devices: 9.43 us -> 12.4 us
    ppermute x6, waiting for transfers between devices: 1.9 us -> 6.96 us  [shifted(): return lax.ppermute(value, ('gx', 'gy'), moves)]
    unnamed x22 -> x6, local copies, waits for them, and re-layouts: 4.56 us -> 0.01 us
    ppermute x6, waiting for transfers between devices: 7.51 us -> 5.45 us  [gather_line(): lax.ppermute(value, 'gz', [(i, (i + s) % nz) for i in range(nz)])]
  transfers between devices with their start and end apart: 16 -> 16, of which waited for: 6 -> 7; matrix products, arithmetic and copies ran while one was open for 0% -> 0% of each run, Pallas kernels for 28% -> 28%
where the time goes in v4:
time: 51.4 us; the launch traced here: 51.1 us
  starting transfers between devices  19.1 us (37%)
  Pallas kernels  17.9 us (35%)
  waiting for transfers between devices  12.4 us (24%)
  between operations  1.44 us (3%)
    pallas_call x9, Pallas kernels, call(): pl.pallas_call(kernel, name=name, out_shape=outs, in_specs=specs, out_spe...  17.9 us
    ppermute x6, starting transfers between devices, gather_line(): lax.ppermute(value, 'gz', [(i, (i + s) % nz) for i in range(nz)])  10.7 us
    ppermute x6, starting transfers between devices, shifted(): return lax.ppermute(value, ('gx', 'gy'), moves)  7.11 us
    ppermute x6, waiting for transfers between devices, shifted(): return lax.ppermute(value, ('gx', 'gy'), moves)  6.96 us
    ppermute x6, waiting for transfers between devices, gather_line(): lax.ppermute(value, 'gz', [(i, (i + s) % nz) for i in range(nz)])  5.45 us
    ppermute x4, starting transfers between devices, from_other_core(): lax.ppermute(value, 'gx', [(i, i ^ 1) for i in range(lax.axis_size('gx'))])  1.26 us
  transfers between devices with their start and end apart: 16, of which 7 were waited for; matrix products, arithmetic and copies ran while one was open for 0% of the time, Pallas kernels for 28%

profile of v4, /device:TPU:0, one launch (start us, length us, event | category | flops | bytes accessed | tf_op | source)
XLA Modules:
  0.0 51.1 jit_solution(10315720404033493216)
XLA Ops:
  1.3 0.8 %pack.1 = bf16[144,128]{1,0:T(8,128)(2,1)S(1)} custom-call(s32[1]{0:T(128)} %bitcast.16.count_ref, bf16[128,128]{1,0:T(8,128)(2,1)} %bitcast.22, f32[3,1,128]{2,1,0:T(1,128)} %bitcast.28), custom_call_target="tpu_custom_call" | custom-call | flops 1000 | bytes 2000000 | tf_op jit(solution)/shard_map/pack/pallas_call | solution.py:684
  2.1 3.1 %collective-permute-start = (bf16[1,144,128]{2,1,0:T(8,128)(2,1)S(1)}, bf16[1,144,128]{2,1,0:T(8,128)(2,1)S(1)}, u32[]{:S(2)}, u32[]{:S(2)}) collective-permute-start(bf16[1,144,128]{2,1,0:T(8,128)(2,1)S(1)} %bitcast.18), channel_id=1, source_target_pairs={{0,1},{1,2},{2,3},{3,0},{4,5},{5,6},{6,7},{7,4},{8,9},{9,10},{10,1... | collective-permute-start | bytes 110600 | tf_op jit(solution)/shard_map/ppermute | solution.py:638
  5.2 2.6 %collective-permute-start.1 = (bf16[1,144,128]{2,1,0:T(8,128)(2,1)S(1)}, bf16[1,144,128]{2,1,0:T(8,128)(2,1)S(1)}, u32[]{:S(2)}, u32[]{:S(2)}) collective-permute-start(bf16[1,144,128]{2,1,0:T(8,128)(2,1)S(1)} %bitcast.19), channel_id=1, source_target_pairs={{0,2},{1,3},{2,0},{3,1},{4,6},{5,7},{6,4},{7,5},{8,10},{9,11},{10,... | collective-permute-start | bytes 110600 | tf_op jit(solution)/shard_map/ppermute | solution.py:638
  7.8 1.3 %collective-permute-start.2 = (bf16[1,144,128]{2,1,0:T(8,128)(2,1)S(1)}, bf16[1,144,128]{2,1,0:T(8,128)(2,1)S(1)}, u32[]{:S(2)}, u32[]{:S(2)}) collective-permute-start(bf16[1,144,128]{2,1,0:T(8,128)(2,1)S(1)} %bitcast.20), channel_id=1, source_target_pairs={{0,3},{1,0},{2,1},{3,2},{4,7},{5,4},{6,5},{7,6},{8,11},{9,8},{10,9... | collective-permute-start | bytes 110600 | tf_op jit(solution)/shard_map/ppermute | solution.py:638
  9.1 2.0 %fold_filter.1 = (f32[7,256,128]{2,1,0:T(8,128)S(1)}, f32[64,128]{1,0:T(8,128)S(1)}, f32[1,128]{1,0:T(1,128)S(1)}, bf16[512,128]{1,0:T(8,128)(2,1)S(1)}) custom-call(f32[64,2048]{1,0:T(8,128)} %refs_0_.1, s32[3,2048]{1,0:T(4,128)} %refs_1_.1, f32[1,64]{1,0:T(1,128)} %bitcast.30, f32[1,128]{1,0:T(1,128)} %bitcast.31, bf16[512,128]{1,0:T(8,128)(2,1)} %bitcast.29, ...), custom_call_target="tpu_custom_call" | custom-call | flops 1000000000 | bytes 2000000 | tf_op jit(solution)/shard_map/fold_filter/pallas_call | solution.py:684
  11.8 1.6 %collective-permute-start.3 = (bf16[4,144,128]{2,1,0:T(8,128)(2,1)S(1)}, bf16[4,144,128]{2,1,0:T(8,128)(2,1)S(1)}, u32[]{:S(2)}, u32[]{:S(2)}) collective-permute-start(bf16[4,144,128]{2,1,0:T(8,128)(2,1)S(1)} %pad_maximum_fusion.2), channel_id=1, source_target_pairs={{0,4},{4,0},{8,12},{12,8},{16,20},{20,16},{24,28},{28,24},{1,5},{5... | collective-permute-start | bytes 442376 | tf_op jit(solution)/shard_map/ppermute | solution.py:654
  13.3 1.5 %collective-permute-start.4 = (bf16[4,144,128]{2,1,0:T(8,128)(2,1)S(1)}, bf16[4,144,128]{2,1,0:T(8,128)(2,1)S(1)}, u32[]{:S(2)}, u32[]{:S(2)}) collective-permute-start(bf16[4,144,128]{2,1,0:T(8,128)(2,1)S(1)} %pad_maximum_fusion.2), channel_id=1, source_target_pairs={{0,16},{4,20},{8,24},{12,28},{16,0},{20,4},{24,8},{28,12},{1,17},{... | collective-permute-start | bytes 442376 | tf_op jit(solution)/shard_map/ppermute | solution.py:654
  15.3 2.5 %collective-permute-done.3 = bf16[4,144,128]{2,1,0:T(8,128)(2,1)S(1)} collective-permute-done((bf16[4,144,128]{2,1,0:T(8,128)(2,1)S(1)}, bf16[4,144,128]{2,1,0:T(8,128)(2,1)S(1)}, u32[]{:S(2)}, u32[]{:S(2)}) %collective-permute-start.3) | collective-permute-done | bytes 147488 | tf_op jit(solution)/shard_map/ppermute | solution.py:654
  17.8 1.3 %collective-permute-done.4 = bf16[4,144,128]{2,1,0:T(8,128)(2,1)S(1)} collective-permute-done((bf16[4,144,128]{2,1,0:T(8,128)(2,1)S(1)}, bf16[4,144,128]{2,1,0:T(8,128)(2,1)S(1)}, u32[]{:S(2)}, u32[]{:S(2)}) %collective-permute-start.4) | collective-permute-done | bytes 147488 | tf_op jit(solution)/shard_map/ppermute | solution.py:654
  19.1 2.1 %collective-permute-done.5 = bf16[4,144,128]{2,1,0:T(8,128)(2,1)S(1)} collective-permute-done((bf16[4,144,128]{2,1,0:T(8,128)(2,1)S(1)}, bf16[4,144,128]{2,1,0:T(8,128)(2,1)S(1)}, u32[]{:S(2)}, u32[]{:S(2)}) %collective-permute-start.5) | collective-permute-done | bytes 147488 | tf_op jit(solution)/shard_map/ppermute | solution.py:654
  21.4 2.3 %charge_sums.1 = (f32[912,256]{1,0:T(8,128)S(1)}, bf16[976,256]{1,0:T(8,128)(2,1)S(1)}, f32[16,8,128]{2,1,0:T(8,128)S(1)}, f32[64,128]{1,0:T(8,128)S(1)}, bf16[1...) custom-call(s32[3]{0:T(128)S(1)} %pad_add_fusion.refs_0_.refs_1_, ...), custom_call_target="tpu_custom_call" | custom-call | flops 3000000000 | bytes 2000000 | tf_op jit(solution)/shard_map/charge_sums/pallas_call | solution.py:684
  24.3 2.5 %message.1 = (f32[128,128]{1,0:T(8,128)S(1)}, f32[16,8,128]{2,1,0:T(8,128)S(1)}, bf16[2304,128]{1,0:T(8,128)(2,1)S(1)}) custom-call(s32[3]{0:T(128)S(1)} %pad_add_fusion.refs_0_.refs_1_, bf16[16,144,128]{2,1,0:T(8,128)(2,1)S(1)} %pad_maximum_fusion.refs_1_, bf16[16,144,128]{2,1,0:T(8,128)(2,1)S(1)} %collective-permute-done.7.refs_2_, ...), custom_call_target="tpu_custom_call" | custom-call | flops 3000000000 | bytes 2000000 | tf_op jit(solution)/shard_map/message/pallas_call | solution.py:684
  26.8 1.6 %cotangents.1 = (bf16[128,128]{1,0:T(8,128)(2,1)S(1)}, f32[128,128]{1,0:T(8,128)S(1)}, bf16[896,256]{1,0:T(8,128)(2,1)S(1)}, f32[64,128]{1,0:T(8,128)S(1)}) custom-call(s32[1]{0:T(128)} %bitcast.17.refs_0_, s32[3]{0:T(128)S(1)} %pad_add_fusion.refs_0_.refs_1_, f32[912,256]{1,0:T(8,128)S(1)} %get-tuple-element.45.refs_2_, ...), custom_call_target="tpu_custom_call" | custom-call | flops 3000000000 | bytes 2000000 | tf_op jit(solution)/shard_map/cotangents/pallas_call | solution.py:684
  28.5 2.9 %collective-permute-start.10 = (bf16[1,128,128]{2,1,0:T(8,128)(2,1)S(1)}, bf16[1,128,128]{2,1,0:T(8,128)(2,1)S(1)}, u32[]{:S(2)}, u32[]{:S(2)}) collective-permute-start(bf16[1,128,128]{2,1,0:T(8,128)(2,1)S(1)} %bitcast.24), channel_id=1, source_target_pairs={{0,3},{1,0},{2,1},{3,2},{4,7},{5,4},{6,5},{7,6},{8,11},{9,8},{10,9... | collective-permute-start | bytes 98312 | tf_op jit(solution)/shard_map/ppermute | solution.py:638
  31.3 0.8 %collective-permute-start.9 = (bf16[1,128,128]{2,1,0:T(8,128)(2,1)S(1)}, bf16[1,128,128]{2,1,0:T(8,128)(2,1)S(1)}, u32[]{:S(2)}, u32[]{:S(2)}) collective-permute-start(bf16[1,128,128]{2,1,0:T(8,128)(2,1)S(1)} %bitcast.26), channel_id=1, source_target_pairs={{0,2},{1,3},{2,0},{3,1},{4,6},{5,7},{6,4},{7,5},{8,10},{9,11},{10,... | collective-permute-start | bytes 98312 | tf_op jit(solution)/shard_map/ppermute | solution.py:638
  32.9 4.1 %collective-permute-done.8 = bf16[1,128,128]{2,1,0:T(8,128)(2,1)S(1)} collective-permute-done((bf16[1,128,128]{2,1,0:T(8,128)(2,1)S(1)}, bf16[1,128,128]{2,1,0:T(8,128)(2,1)S(1)}, u32[]{:S(2)}, u32[]{:S(2)}) %collective-permute-start.8) | collective-permute-done | bytes 32800 | tf_op jit(solution)/shard_map/ppermute | solution.py:638
  37.1 0.9 %collective-permute-start.11 = (bf16[4,128,128]{2,1,0:T(8,128)(2,1)S(1)}, bf16[4,128,128]{2,1,0:T(8,128)(2,1)S(1)}, u32[]{:S(2)}, u32[]{:S(2)}) collective-permute-start(bf16[4,128,128]{2,1,0:T(8,128)(2,1)S(1)} %pad_maximum_fusion.3), channel_id=1, source_target_pairs={{0,4},{4,0},{8,12},{12,8},{16,20},{20,16},{24,28},{28,24},{1,5},{5... | collective-permute-start | bytes 393224 | tf_op jit(solution)/shard_map/ppermute | solution.py:654
  38.0 1.5 %collective-permute-start.12 = (bf16[4,128,128]{2,1,0:T(8,128)(2,1)S(1)}, bf16[4,128,128]{2,1,0:T(8,128)(2,1)S(1)}, u32[]{:S(2)}, u32[]{:S(2)}) collective-permute-start(bf16[4,128,128]{2,1,0:T(8,128)(2,1)S(1)} %pad_maximum_fusion.3), channel_id=1, source_target_pairs={{0,16},{4,20},{8,24},{12,28},{16,0},{20,4},{24,8},{28,12},{1,17},{... | collective-permute-start | bytes 393224 | tf_op jit(solution)/shard_map/ppermute | solution.py:654
  39.5 1.1 %collective-permute-start.13 = (bf16[4,128,128]{2,1,0:T(8,128)(2,1)S(1)}, bf16[4,128,128]{2,1,0:T(8,128)(2,1)S(1)}, u32[]{:S(2)}, u32[]{:S(2)}) collective-permute-start(bf16[4,128,128]{2,1,0:T(8,128)(2,1)S(1)} %pad_maximum_fusion.3), channel_id=1, source_target_pairs={{0,20},{4,16},{8,28},{12,24},{16,4},{20,0},{24,12},{28,8},{1,21},{... | collective-permute-start | bytes 393224 | tf_op jit(solution)/shard_map/ppermute | solution.py:654
  40.6 3.6 %own_terms.1 = (bf16[128,128]{1,0:T(8,128)(2,1)}, f32[1,128]{1,0:T(1,128)}, f32[3,128]{1,0:T(4,128)S(1)}, bf16[512,128]{1,0:T(8,128)(2,1)S(1)}, bf16[256,384]{1,...) custom-call(s32[3]{0:T(128)S(1)} %pad_add_fusion.refs_0_.refs_1_, ...), custom_call_target="tpu_custom_call" | custom-call | flops 4000000000 | bytes 2000000 | tf_op jit(solution)/shard_map/own_terms/pallas_call | solution.py:684
  44.3 1.1 %collective-permute-done.13 = bf16[4,128,128]{2,1,0:T(8,128)(2,1)S(1)} collective-permute-done((bf16[4,128,128]{2,1,0:T(8,128)(2,1)S(1)}, bf16[4,128,128]{2,1,0:T(8,128)(2,1)S(1)}, u32[]{:S(2)}, u32[]{:S(2)}) %collective-permute-start.13) | collective-permute-done | bytes 131104 | tf_op jit(solution)/shard_map/ppermute | solution.py:654
  45.5 2.0 %pull_sums.1 = (f32[896,256]{1,0:T(8,128)S(1)}, bf16[896,256]{1,0:T(8,128)(2,1)S(1)}) custom-call(s32[3]{0:T(128)S(1)} %pad_add_fusion.refs_0_.refs_1_, bf16[16,128,128]{2,1,0:T(8,128)(2,1)S(1)} %pad_maximum_fusion.1.refs_1_, f32[16,8,128]{2,1,0:T(8,128)S(1)} %get-tuple-element.47.refs_3_.refs_5_.refs_2_, bf16[64,128]{1,0:T(8,128)(2,1)S(1)} %copy-done.2, ...), custom_call_target="tpu_custom_call" | custom-call | flops 3000000000 | bytes 2000000 | tf_op jit(solution)/shard_map/pull_sums/pallas_call | solution.py:684
  48.1 1.8 %react.1.refs_5_ = f32[3,128]{1,0:T(4,128)S(1)} custom-call(s32[3]{0:T(128)S(1)} %pad_add_fusion.refs_0_.refs_1_, bf16[16,128,128]{2,1,0:T(8,128)(2,1)S(1)} %pad_maximum_fusion.1.refs_1_, bf16[16,128,128]{2,1,0:T(8,128)(2,1)S(1)} %collective-permute-done.15.refs_2_, f32[16,8,128]{2,1,0:T(8,128)S(1)} %get-tuple-element.47.refs_3_.refs_5_.refs_2_, ...), custom_call_target="tpu_custom_call" | custom-call | flops 3000000000 | bytes 2000000 | tf_op jit(solution)/shard_map/react/pallas_call | solution.py:684
  49.9 1.3 %finish.1 = f32[3,1,128]{2,1,0:T(1,128)} custom-call(f32[896,256]{1,0:T(8,128)S(1)} %get-tuple-element.67.refs_0_, bf16[896,256]{1,0:T(8,128)(2,1)S(1)} %collective-permute-done.14.refs_1_, bf16[256,384]{1,0:T(8,128)(2,1)S(1)} %get-tuple-element.69.refs_2_, f32[16,128]{1,0:T(8,128)S(1)} %get-tuple-element.70.refs_3_, ...), custom_call_target="tpu_custom_call" | custom-call | flops 2000000000 | bytes 2000000 | tf_op jit(solution)/shard_map/finish/pallas_call | solution.py:684
  (28 shorter events, 3.4 us)
Async XLA Ops:
  0.6 20.8 %copy-start.1 = (bf16[64,128]{1,0:T(8,128)(2,1)S(1)}, bf16[64,128]{1,0:T(8,128)(2,1)}, u32[]{:S(2)}) copy-start(bf16[64,128]{1,0:T(8,128)(2,1)} %refs_2_.1) | copy-start | bytes 49156
  2.1 9.1 %collective-permute-start = (bf16[1,144,128]{2,1,0:T(8,128)(2,1)S(1)}, bf16[1,144,128]{2,1,0:T(8,128)(2,1)S(1)}, u32[]{:S(2)}, u32[]{:S(2)}) collective-permute-start(bf16[1,144,128]{2,1,0:T(8,128)(2,1)S(1)} %bitcast.18), channel_id=1, source_target_pairs={{0,1},{1,2},{2,3},{3,0},{4,5},{5,6},{6,7},{7,4},{8,9},{9,10},{10,1... | collective-permute-start | bytes 110600 | tf_op jit(solution)/shard_map/ppermute | solution.py:638
  5.2 6.0 %collective-permute-start.1 = (bf16[1,144,128]{2,1,0:T(8,128)(2,1)S(1)}, bf16[1,144,128]{2,1,0:T(8,128)(2,1)S(1)}, u32[]{:S(2)}, u32[]{:S(2)}) collective-permute-start(bf16[1,144,128]{2,1,0:T(8,128)(2,1)S(1)} %bitcast.19), channel_id=1, source_target_pairs={{0,2},{1,3},{2,0},{3,1},{4,6},{5,7},{6,4},{7,5},{8,10},{9,11},{10,... | collective-permute-start | bytes 110600 | tf_op jit(solution)/shard_map/ppermute | solution.py:638
  7.8 4.0 %collective-permute-start.2 = (bf16[1,144,128]{2,1,0:T(8,128)(2,1)S(1)}, bf16[1,144,128]{2,1,0:T(8,128)(2,1)S(1)}, u32[]{:S(2)}, u32[]{:S(2)}) collective-permute-start(bf16[1,144,128]{2,1,0:T(8,128)(2,1)S(1)} %bitcast.20), channel_id=1, source_target_pairs={{0,3},{1,0},{2,1},{3,2},{4,7},{5,4},{6,5},{7,6},{8,11},{9,8},{10,9... | collective-permute-start | bytes 110600 | tf_op jit(solution)/shard_map/ppermute | solution.py:638
  11.8 6.0 %collective-permute-start.3 = (bf16[4,144,128]{2,1,0:T(8,128)(2,1)S(1)}, bf16[4,144,128]{2,1,0:T(8,128)(2,1)S(1)}, u32[]{:S(2)}, u32[]{:S(2)}) collective-permute-start(bf16[4,144,128]{2,1,0:T(8,128)(2,1)S(1)} %pad_maximum_fusion.2), channel_id=1, source_target_pairs={{0,4},{4,0},{8,12},{12,8},{16,20},{20,16},{24,28},{28,24},{1,5},{5... | collective-permute-start | bytes 442376 | tf_op jit(solution)/shard_map/ppermute | solution.py:654
  13.3 5.8 %collective-permute-start.4 = (bf16[4,144,128]{2,1,0:T(8,128)(2,1)S(1)}, bf16[4,144,128]{2,1,0:T(8,128)(2,1)S(1)}, u32[]{:S(2)}, u32[]{:S(2)}) collective-permute-start(bf16[4,144,128]{2,1,0:T(8,128)(2,1)S(1)} %pad_maximum_fusion.2), channel_id=1, source_target_pairs={{0,16},{4,20},{8,24},{12,28},{16,0},{20,4},{24,8},{28,12},{1,17},{... | collective-permute-start | bytes 442376 | tf_op jit(solution)/shard_map/ppermute | solution.py:654
  14.8 6.3 %collective-permute-start.5 = (bf16[4,144,128]{2,1,0:T(8,128)(2,1)S(1)}, bf16[4,144,128]{2,1,0:T(8,128)(2,1)S(1)}, u32[]{:S(2)}, u32[]{:S(2)}) collective-permute-start(bf16[4,144,128]{2,1,0:T(8,128)(2,1)S(1)} %pad_maximum_fusion.2), channel_id=1, source_target_pairs={{0,20},{4,16},{8,28},{12,24},{16,4},{20,0},{24,12},{28,8},{1,21},{... | collective-permute-start | bytes 442376 | tf_op jit(solution)/shard_map/ppermute | solution.py:654
  21.3 3.0 %collective-permute-start.7 = (bf16[16,144,128]{2,1,0:T(8,128)(2,1)S(1)}, bf16[16,144,128]{2,1,0:T(8,128)(2,1)S(1)}, u32[]{:S(2)}, u32[]{:S(2)}) collective-permute-start(bf16[16,144,128]{2,1,0:T(8,128)(2,1)S(1)} %pad_maximum_fusion.refs_1_), channel_id=1, source_target_pairs={{0,8},{8,0},{16,24},{24,16},{1,9},{9,1},{17,25},{25,17},{2,10},{10... | collective-permute-start | bytes 1769480 | tf_op jit(solution)/shard_map/ppermute | solution.py:669
  23.7 3.1 %collective-permute-start.6 = (bf16[976,256]{1,0:T(8,128)(2,1)S(1)}, bf16[976,256]{1,0:T(8,128)(2,1)S(1)}, u32[]{:S(2)}, u32[]{:S(2)}) collective-permute-start(bf16[976,256]{1,0:T(8,128)(2,1)S(1)} %get-tuple-element.46.refs_3_), channel_id=1, source_target_pairs={{0,8},{8,0},{16,24},{24,16},{1,9},{9,1},{17,25},{25,17},{2,10},{10... | collective-permute-start | bytes 1499144 | tf_op jit(solution)/shard_map/ppermute | solution.py:669
  24.3 2.5 %copy-start = (bf16[1,1,1,128,128]{4,3,2,1,0:T(8,128)(2,1)S(1)}, bf16[1,1,1,128,128]{4,3,2,1,0:T(8,128)(2,1)}, u32[]{:S(2)}) copy-start(bf16[1,1,1,128,128]{4,3,2,1,0:T(8,128)(2,1)} %param.11) | copy-start | bytes 98308
  24.3 2.6 %copy-start.2 = (bf16[64,128]{1,0:T(8,128)(2,1)S(1)}, bf16[64,128]{1,0:T(8,128)(2,1)}, u32[]{:S(2)}) copy-start(bf16[64,128]{1,0:T(8,128)(2,1)} %refs_3_.1) | copy-start | bytes 49156
  28.5 4.5 %collective-permute-start.10 = (bf16[1,128,128]{2,1,0:T(8,128)(2,1)S(1)}, bf16[1,128,128]{2,1,0:T(8,128)(2,1)S(1)}, u32[]{:S(2)}, u32[]{:S(2)}) collective-permute-start(bf16[1,128,128]{2,1,0:T(8,128)(2,1)S(1)} %bitcast.24), channel_id=1, source_target_pairs={{0,3},{1,0},{2,1},{3,2},{4,7},{5,4},{6,5},{7,6},{8,11},{9,8},{10,9... | collective-permute-start | bytes 98312 | tf_op jit(solution)/shard_map/ppermute | solution.py:638
  31.3 5.7 %collective-permute-start.8 = (bf16[1,128,128]{2,1,0:T(8,128)(2,1)S(1)}, bf16[1,128,128]{2,1,0:T(8,128)(2,1)S(1)}, u32[]{:S(2)}, u32[]{:S(2)}) collective-permute-start(bf16[1,128,128]{2,1,0:T(8,128)(2,1)S(1)} %bitcast.25), channel_id=1, source_target_pairs={{0,1},{1,2},{2,3},{3,0},{4,5},{5,6},{6,7},{7,4},{8,9},{9,10},{10,1... | collective-permute-start | bytes 98312 | tf_op jit(solution)/shard_map/ppermute | solution.py:638
  31.3 5.7 %collective-permute-start.9 = (bf16[1,128,128]{2,1,0:T(8,128)(2,1)S(1)}, bf16[1,128,128]{2,1,0:T(8,128)(2,1)S(1)}, u32[]{:S(2)}, u32[]{:S(2)}) collective-permute-start(bf16[1,128,128]{2,1,0:T(8,128)(2,1)S(1)} %bitcast.26), channel_id=1, source_target_pairs={{0,2},{1,3},{2,0},{3,1},{4,6},{5,7},{6,4},{7,5},{8,10},{9,11},{10,... | collective-permute-start | bytes 98312 | tf_op jit(solution)/shard_map/ppermute | solution.py:638
  37.1 7.2 %collective-permute-start.11 = (bf16[4,128,128]{2,1,0:T(8,128)(2,1)S(1)}, bf16[4,128,128]{2,1,0:T(8,128)(2,1)S(1)}, u32[]{:S(2)}, u32[]{:S(2)}) collective-permute-start(bf16[4,128,128]{2,1,0:T(8,128)(2,1)S(1)} %pad_maximum_fusion.3), channel_id=1, source_target_pairs={{0,4},{4,0},{8,12},{12,8},{16,20},{20,16},{24,28},{28,24},{1,5},{5... | collective-permute-start | bytes 393224 | tf_op jit(solution)/shard_map/ppermute | solution.py:654
  38.0 6.3 %collective-permute-start.12 = (bf16[4,128,128]{2,1,0:T(8,128)(2,1)S(1)}, bf16[4,128,128]{2,1,0:T(8,128)(2,1)S(1)}, u32[]{:S(2)}, u32[]{:S(2)}) collective-permute-start(bf16[4,128,128]{2,1,0:T(8,128)(2,1)S(1)} %pad_maximum_fusion.3), channel_id=1, source_target_pairs={{0,16},{4,20},{8,24},{12,28},{16,0},{20,4},{24,8},{28,12},{1,17},{... | collective-permute-start | bytes 393224 | tf_op jit(solution)/shard_map/ppermute | solution.py:654
  39.5 5.9 %collective-permute-start.13 = (bf16[4,128,128]{2,1,0:T(8,128)(2,1)S(1)}, bf16[4,128,128]{2,1,0:T(8,128)(2,1)S(1)}, u32[]{:S(2)}, u32[]{:S(2)}) collective-permute-start(bf16[4,128,128]{2,1,0:T(8,128)(2,1)S(1)} %pad_maximum_fusion.3), channel_id=1, source_target_pairs={{0,20},{4,16},{8,28},{12,24},{16,4},{20,0},{24,12},{28,8},{1,21},{... | collective-permute-start | bytes 393224 | tf_op jit(solution)/shard_map/ppermute | solution.py:654
  45.5 2.6 %collective-permute-start.15 = (bf16[16,128,128]{2,1,0:T(8,128)(2,1)S(1)}, bf16[16,128,128]{2,1,0:T(8,128)(2,1)S(1)}, u32[]{:S(2)}, u32[]{:S(2)}) collective-permute-start(bf16[16,128,128]{2,1,0:T(8,128)(2,1)S(1)} %pad_maximum_fusion.1.refs_1_), channel_id=1, source_target_pairs={{0,8},{8,0},{16,24},{24,16},{1,9},{9,1},{17,25},{25,17},{2,10},{10... | collective-permute-start | bytes 1572872 | tf_op jit(solution)/shard_map/ppermute | solution.py:669
  47.5 2.3 %collective-permute-start.14 = (bf16[896,256]{1,0:T(8,128)(2,1)S(1)}, bf16[896,256]{1,0:T(8,128)(2,1)S(1)}, u32[]{:S(2)}, u32[]{:S(2)}) collective-permute-start(bf16[896,256]{1,0:T(8,128)(2,1)S(1)} %get-tuple-element.68), channel_id=1, source_target_pairs={{0,8},{8,0},{16,24},{24,16},{1,9},{9,1},{17,25},{25,17},{2,10},{10... | collective-permute-start | bytes 1376264 | tf_op jit(solution)/shard_map/ppermute | solution.py:669

commit v5 on v4

--- a/solution.py
+++ b/solution.py
@@ -135,15 +135,15 @@
     return [jnp.sum(t * weights, axis=0, keepdims=True) for t in total]
 
 
-def place_of(meta_ref, m, half, sizes):
+def place_of(m, half, sizes):
     nx, ny, nz = sizes
     dz = lax.rem(m, nz)
     dy = lax.rem(m // nz, ny)
     dx = m // (nz * ny)
-    start = meta_ref[0] if half == 0 else meta_ref[0] + 1 - 2 * lax.rem(meta_ref[0], 2)
+    start = lax.axis_index(AXES[0]) if half == 0 else lax.axis_index(AXES[0]) + 1 - 2 * lax.rem(lax.axis_index(AXES[0]), 2)
     cx = lax.rem(start - 2 * dx + nx, nx)
-    cy = lax.rem(meta_ref[1] - dy + ny, ny)
-    cz = lax.rem(meta_ref[2] - dz + nz, nz)
+    cy = lax.rem(lax.axis_index(AXES[1]) - dy + ny, ny)
+    cz = lax.rem(lax.axis_index(AXES[2]) - dz + nz, nz)
     return (cx.astype(F32), cy.astype(F32), cz.astype(F32))
 
 
@@ -192,10 +192,20 @@
         c.wait()
 
 
-def pack_kernel(count_ref, features_hbm, positions_hbm, out_ref, features_ref, positions_ref, sems):
+def pack_kernel(
+    count_ref,
+    features_hbm,
+    positions_hbm,
+    out_ref,
+    live_ref,
+    features_ref,
+    positions_ref,
+    sems,
+):
     fetch((features_hbm, positions_hbm), (features_ref, positions_ref), sems)
     n, channels = features_ref.shape
     live_col = lax.broadcasted_iota(jnp.int32, (n, channels), 0) < count_ref[0]
+    live_ref[...] = live_col.astype(F32)
     rows = features_ref[...].astype(F32)
     out_ref[0:n, :] = jnp.where(live_col, rows, 0.0).astype(BF16)
     pos = jnp.concatenate([positions_ref[a] for a in range(3)], axis=0)
@@ -288,7 +298,6 @@
 def charge_kernel(
     sizes,
     group,
-    meta_ref,
     near_ref,
     w_charge_ref,
     bias_ref,
@@ -338,7 +347,7 @@
         for j in range(group):
             m = g * group + j
             pos = places_ref[m]
-            tx, ty, tz = axis_tables(pos, place_of(meta_ref, m, 0, sizes), sizes)
+            tx, ty, tz = axis_tables(pos, place_of(m, 0, sizes), sizes)
             live = pos[3:4, :]
             living = jnp.concatenate([tz[0] * live, tz[1] * live], axis=0).astype(BF16)
             plane = plane_table(tx, ty).astype(BF16)
@@ -360,7 +369,6 @@
 
 def message_kernel(
     sizes,
-    meta_ref,
     near_ref,
     far_ref,
     near_places_ref,
@@ -380,7 +388,7 @@
         return 0
 
     lax.fori_loop(0, far_ref.shape[0], add_place, 0, unroll=4)
-    odd = lax.rem(meta_ref[0], 2)
+    odd = lax.rem(lax.axis_index(AXES[0]), 2)
     own_cols = columns(near_places_ref[0], n)
     for t, block in enumerate(blocks_of(sizes)):
         half, m = block_place(sizes, odd, block)
@@ -402,8 +410,7 @@
 
 def cotangent_kernel(
     sizes,
-    count_ref,
-    meta_ref,
+    live_ref,
     sums_ref,
     part_ref,
     far_part_ref,
@@ -449,7 +456,7 @@
         plane = kept[0][0]
         tz = (kept[1][0, 0:8, :], kept[1][0, 8:16, :])
     else:
-        tx, ty, tz = axis_tables(own, place_of(meta_ref, 0, 0, sizes), sizes)
+        tx, ty, tz = axis_tables(own, place_of(0, 0, sizes), sizes)
         plane = plane_table(tx, ty).astype(BF16)
     lifted = dot(field_ref[...], plane)
     potential = jnp.zeros((charge_ch, n), F32)
@@ -462,18 +469,17 @@
     refined = features_ref[...].astype(F32) + pre_act * sig
     refined_ref[...] = refined
     sig_r = sigmoid(refined)
-    live_rows = lax.broadcasted_iota(jnp.int32, (n, channels), 0) < count_ref[0]
     grad = (
         w_energy_ref[...]
         * (sig_r * (1.0 + refined * (1.0 - sig_r)))
         * (sig * (1.0 + pre_act * (1.0 - sig)))
     )
-    grad_ref[...] = jnp.where(live_rows, grad, 0.0).astype(BF16)
-
-
-def pair_force(sizes, meta_ref, places, strengths_ref, n, slopes_to=None, slopes_from=None):
+    grad_ref[...] = (grad * live_ref[...]).astype(BF16)
+
+
+def pair_force(sizes, places, strengths_ref, n, slopes_to=None, slopes_from=None):
     own_cols = columns(places[0][0], n)
-    odd = lax.rem(meta_ref[0], 2)
+    odd = lax.rem(lax.axis_index(AXES[0]), 2)
     blocks = blocks_of(sizes)
     parts = [[], [], []]
     for first in range(0, n, 32):
@@ -509,7 +515,6 @@
 
 def own_kernel(
     sizes,
-    meta_ref,
     grad_ref,
     field_ref,
     places_ref,
@@ -546,9 +551,9 @@
     lifted_ref[...] = jnp.concatenate(lifted, axis=0)
     strength_scr[...] = dot_nt(jnp.concatenate(rows, axis=0), xcat_ref[...])
     places = (places_ref, far_places_ref)
-    near = pair_force(sizes, meta_ref, places, strength_scr, n, slopes[0] if slopes else None)
+    near = pair_force(sizes, places, strength_scr, n, slopes[0] if slopes else None)
     pull = dot_nt(w_long_ref[...], grad)
-    tables = axis_tables(own, place_of(meta_ref, 0, 0, sizes), sizes)
+    tables = axis_tables(own, place_of(0, 0, sizes), sizes)
     planes = slope_planes(tables, sizes)
     planes_ref[...] = planes
     levels_ref[...] = jnp.concatenate(tables[2], axis=0)
@@ -556,7 +561,7 @@
     force_ref[...] = jnp.concatenate([near[a] - slope[a] for a in range(3)], axis=0)
 
 
-def pull_kernel(sizes, group, meta_ref, near_ref, places_ref, w_long_ref, *rest):
+def pull_kernel(sizes, group, near_ref, places_ref, w_long_ref, *rest):
     *kept, sums_ref, part_ref = rest
     n = near_ref.shape[1]
     groups = near_ref.shape[0] // group
@@ -572,7 +577,7 @@
                 right.append(kept[0][m])
             else:
                 pos = places_ref[m]
-                tx, ty, tz = axis_tables(pos, place_of(meta_ref, m, 0, sizes), sizes)
+                tx, ty, tz = axis_tables(pos, place_of(m, 0, sizes), sizes)
                 right.append(plane_table(tx, ty).astype(BF16))
             left.append(spread(pulls[:, j * n : (j + 1) * n], tz))
         return dot_nt(jnp.concatenate(left, axis=1), jnp.concatenate(right, axis=1))
@@ -583,7 +588,6 @@
 
 def react_kernel(
     sizes,
-    meta_ref,
     near_ref,
     far_ref,
     places_ref,
@@ -595,13 +599,13 @@
     *slopes, out_ref, gcat_scr, strength_scr = rest
     n = lifted_ref.shape[1]
     halves = (near_ref, far_ref)
-    odd = lax.rem(meta_ref[0], 2)
+    odd = lax.rem(lax.axis_index(AXES[0]), 2)
     for t, block in enumerate(blocks_of(sizes)):
         half, m = block_place(sizes, odd, block)
         gcat_scr[t * n : (t + 1) * n, :] = halves[half][m]
     strength_scr[...] = dot_nt(lifted_ref[...], gcat_scr[...])
     places = (places_ref, far_places_ref)
-    near = pair_force(sizes, meta_ref, places, strength_scr, n, None, slopes[0] if slopes else None)
+    near = pair_force(sizes, places, strength_scr, n, None, slopes[0] if slopes else None)
     out_ref[...] = force_ref[...] + jnp.concatenate(near, axis=0)
 
 
@@ -669,18 +673,21 @@
     return lax.ppermute(value, "gx", [(i, i ^ 1) for i in range(lax.axis_size("gx"))])
 
 
-def call(kernel, name, outs, scratch, smem, operands, kept, limit, flops, fetched):
+def call(kernel, name, outs, scratch, operands, kept, limit, flops, fetched):
     n_in = len(operands)
     first = n_in - kept
     operands = [
         pltpu.with_memory_space_constraint(o, pltpu.HBM if fetched else pltpu.VMEM)
-        if i >= (smem if fetched else first)
+        if (fetched and o.size > 1) or i >= first
         else o
         for i, o in enumerate(operands)
     ]
-    specs = [pl.BlockSpec(memory_space=pltpu.SMEM)] * smem + [
-        pl.BlockSpec(memory_space=pltpu.HBM if fetched else pltpu.VMEM)
-    ] * (n_in - smem)
+    specs = [
+        pl.BlockSpec(
+            memory_space=pltpu.SMEM if o.size == 1 else pltpu.HBM if fetched else pltpu.VMEM
+        )
+        for o in operands
+    ]
     return pl.pallas_call(
         kernel,
         name=name,
@@ -718,26 +725,24 @@
     blocks = len(blocks_of(sizes))
     scale_long = 4.0 / math.sqrt(n * cells * waves)
     count = counts.reshape(1)
-    meta = jnp.stack([lax.axis_index(a) for a in AXES]).astype(jnp.int32)
     shape = jax.ShapeDtypeStruct
     wide = 2 * ORDERS * charge_ch
     fits = cells <= 64
     limit = (24 if fits else 56) * 1024 * 1024
     held = pltpu.VMEM if fits else shape
 
-    def run(kernel, name, outs, scratch, smem, operands, kept, flops, fetched=False):
+    def run(kernel, name, outs, scratch, operands, kept, flops, fetched=False):
         kept = kept if fits else 0
         if fetched:
-            places = [pltpu.VMEM(o.shape, o.dtype) for o in operands[smem:]]
+            places = [pltpu.VMEM(o.shape, o.dtype) for o in operands if o.size > 1]
             scratch = [*places, pltpu.SemaphoreType.DMA((len(places),))]
-        return call(kernel, name, outs, scratch, smem, operands, kept, limit, flops, fetched)
-
-    (packed,) = run(
+        return call(kernel, name, outs, scratch, operands, kept, limit, flops, fetched)
+
+    packed, live = run(
         pack_kernel,
         "pack",
-        [held((n + 16, channels), BF16)],
+        [held((n + 16, channels), BF16), held((n, channels), F32)],
         [],
-        1,
         [count, own_rows, positions.reshape(3, 1, n)],
         0,
         1000,
@@ -753,7 +758,6 @@
             held((bases * channels, channels), BF16),
         ],
         [],
-        0,
         [
             k_filter,
             k_index,
@@ -781,8 +785,7 @@
         ]
         + ([held((half_cells, 256, n), BF16), held((half_cells, 16, n), F32)] if fits else []),
         [pltpu.VMEM((half_cells, charge_ch, n), F32)],
-        1,
-        [meta, near, w_charge, bias],
+        [near, w_charge, bias],
         3,
         3_000_000_000,
     )
@@ -796,8 +799,7 @@
             held((blocks * n, channels), BF16),
         ],
         [pltpu.VMEM((bases * n, blocks * n), BF16)],
-        1,
-        [meta, near, far, places, mixed],
+        [near, far, places, mixed],
         4,
         3_000_000_000,
     )
@@ -811,10 +813,8 @@
             held((charge_ch, n), F32),
         ],
         [],
-        2,
         [
-            count,
-            meta,
+            live,
             sums,
             part,
             far_part,
@@ -828,7 +828,7 @@
             filt,
             *kept,
         ],
-        11 + len(kept),
+        12 + len(kept),
         3_000_000_000,
     )
     grad_line, grad = lax.optimization_barrier((gather_line(grad, sizes[2]), grad))
@@ -845,9 +845,7 @@
         ]
         + ([held((bases * n, blocks * n), F32)] if fits else []),
         [pltpu.VMEM((bases * n, blocks * n), F32)],
-        1,
         [
-            meta,
             grad,
             field,
             places,
@@ -868,8 +866,7 @@
         "pull_sums",
         [held((wide, 256), F32), held((wide, 256), BF16)],
         [],
-        1,
-        [meta, grad_near, places, w_long, *kept],
+        [grad_near, places, w_long, *kept],
         3 + len(kept),
         3_000_000_000,
     )
@@ -882,8 +879,7 @@
             pltpu.VMEM((blocks * n, channels), BF16),
             pltpu.VMEM((bases * n, blocks * n), F32),
         ],
-        1,
-        [meta, grad_near, grad_far, places, far_places, lifted, force, *slopes],
+        [grad_near, grad_far, places, far_places, lifted, force, *slopes],
         6 + len(slopes),
         3_000_000_000,
     )
@@ -892,7 +888,6 @@
         "finish",
         [shape((3, 1, n), F32)],
         [pltpu.VMEM((wide, 256), BF16)],
-        0,
         [back, far_back, planes, levels, neutral, force, filt],
         7,
         2_000_000_000,

time: 51.4 us -> 48.9 us (0.951)
  Pallas kernels: 17.9 us -> 14.9 us
  waiting for transfers between devices: 12.4 us -> 13.3 us
    pallas_call x9, Pallas kernels: 17.9 us -> 14.9 us  [call(): pl.pallas_call(kernel, name=name, out_shape=outs, in_specs=specs, out_spe...]
    ppermute x6, waiting for transfers between devices: 6.96 us -> 7.52 us  [shifted(): return lax.ppermute(value, ('gx', 'gy'), moves)]
  transfers between devices with their start and end apart: 16 -> 16, of which waited for: 7 -> 8; matrix products, arithmetic and copies ran while one was open for 0% -> 0% of each run, Pallas kernels for 28% -> 24%
where the time goes in v5:
time: 48.9 us; the launch traced here: 48.7 us
  starting transfers between devices  18.9 us (39%)
  Pallas kernels  14.9 us (30%)
  waiting for transfers between devices  13.3 us (27%)
  between operations  1.44 us (3%)
    pallas_call x9, Pallas kernels, call(): pl.pallas_call(kernel, name=name, out_shape=outs, in_specs=specs, out_spe...  14.9 us
    ppermute x6, starting transfers between devices, gather_line(): lax.ppermute(value, 'gz', [(i, (i + s) % nz) for i in range(nz)])  10.5 us
    ppermute x6, waiting for transfers between devices, shifted(): return lax.ppermute(value, ('gx', 'gy'), moves)  7.52 us
    ppermute x6, starting transfers between devices, shifted(): return lax.ppermute(value, ('gx', 'gy'), moves)  7.11 us
    ppermute x6, waiting for transfers between devices, gather_line(): lax.ppermute(value, 'gz', [(i, (i + s) % nz) for i in range(nz)])  5.63 us
    ppermute x4, starting transfers between devices, from_other_core(): lax.ppermute(value, 'gx', [(i, i ^ 1) for i in range(lax.axis_size('gx'))])  1.25 us
  transfers between devices with their start and end apart: 16, of which 8 were waited for; matrix products, arithmetic and copies ran while one was open for 0% of the time, Pallas kernels for 24%

profile of v5, /device:TPU:0, one launch (start us, length us, event | category | flops | bytes accessed | tf_op | source)
XLA Modules:
  0.0 48.7 jit_solution(15842378821623324514)
XLA Ops:
  1.3 0.8 %pack.1 = (bf16[144,128]{1,0:T(8,128)(2,1)S(1)}, f32[128,128]{1,0:T(8,128)S(1)}) custom-call(s32[1]{0:T(128)} %bitcast.13.count_ref, bf16[128,128]{1,0:T(8,128)(2,1)} %bitcast.18, f32[3,1,128]{2,1,0:T(1,128)} %bitcast.24), custom_call_target="tpu_custom_call" | custom-call | flops 1000 | bytes 2000000 | tf_op jit(solution)/shard_map/pack/pallas_call | solution.py:691
  2.1 3.1 %collective-permute-start = (bf16[1,144,128]{2,1,0:T(8,128)(2,1)S(1)}, bf16[1,144,128]{2,1,0:T(8,128)(2,1)S(1)}, u32[]{:S(2)}, u32[]{:S(2)}) collective-permute-start(bf16[1,144,128]{2,1,0:T(8,128)(2,1)S(1)} %bitcast.14), channel_id=1, source_target_pairs={{0,1},{1,2},{2,3},{3,0},{4,5},{5,6},{6,7},{7,4},{8,9},{9,10},{10,1... | collective-permute-start | bytes 110600 | tf_op jit(solution)/shard_map/ppermute | solution.py:642
  5.2 2.6 %collective-permute-start.1 = (bf16[1,144,128]{2,1,0:T(8,128)(2,1)S(1)}, bf16[1,144,128]{2,1,0:T(8,128)(2,1)S(1)}, u32[]{:S(2)}, u32[]{:S(2)}) collective-permute-start(bf16[1,144,128]{2,1,0:T(8,128)(2,1)S(1)} %bitcast.15), channel_id=1, source_target_pairs={{0,2},{1,3},{2,0},{3,1},{4,6},{5,7},{6,4},{7,5},{8,10},{9,11},{10,... | collective-permute-start | bytes 110600 | tf_op jit(solution)/shard_map/ppermute | solution.py:642
  7.8 1.3 %collective-permute-start.2 = (bf16[1,144,128]{2,1,0:T(8,128)(2,1)S(1)}, bf16[1,144,128]{2,1,0:T(8,128)(2,1)S(1)}, u32[]{:S(2)}, u32[]{:S(2)}) collective-permute-start(bf16[1,144,128]{2,1,0:T(8,128)(2,1)S(1)} %bitcast.16), channel_id=1, source_target_pairs={{0,3},{1,0},{2,1},{3,2},{4,7},{5,4},{6,5},{7,6},{8,11},{9,8},{10,9... | collective-permute-start | bytes 110600 | tf_op jit(solution)/shard_map/ppermute | solution.py:642
  9.1 2.0 %fold_filter.1 = (f32[7,256,128]{2,1,0:T(8,128)S(1)}, f32[64,128]{1,0:T(8,128)S(1)}, f32[1,128]{1,0:T(1,128)S(1)}, bf16[512,128]{1,0:T(8,128)(2,1)S(1)}) custom-call(f32[64,2048]{1,0:T(8,128)} %refs_0_.1, s32[3,2048]{1,0:T(4,128)} %refs_1_.2, f32[1,64]{1,0:T(1,128)} %bitcast.26, f32[1,128]{1,0:T(1,128)} %bitcast.27, bf16[512,128]{1,0:T(8,128)(2,1)} %bitcast.25, ...), custom_call_target="tpu_custom_call" | custom-call | flops 1000000000 | bytes 2000000 | tf_op jit(solution)/shard_map/fold_filter/pallas_call | solution.py:691
  11.8 1.6 %collective-permute-start.3 = (bf16[4,144,128]{2,1,0:T(8,128)(2,1)S(1)}, bf16[4,144,128]{2,1,0:T(8,128)(2,1)S(1)}, u32[]{:S(2)}, u32[]{:S(2)}) collective-permute-start(bf16[4,144,128]{2,1,0:T(8,128)(2,1)S(1)} %pad_maximum_fusion.2), channel_id=1, source_target_pairs={{0,4},{4,0},{8,12},{12,8},{16,20},{20,16},{24,28},{28,24},{1,5},{5... | collective-permute-start | bytes 442376 | tf_op jit(solution)/shard_map/ppermute | solution.py:658
  13.3 1.5 %collective-permute-start.4 = (bf16[4,144,128]{2,1,0:T(8,128)(2,1)S(1)}, bf16[4,144,128]{2,1,0:T(8,128)(2,1)S(1)}, u32[]{:S(2)}, u32[]{:S(2)}) collective-permute-start(bf16[4,144,128]{2,1,0:T(8,128)(2,1)S(1)} %pad_maximum_fusion.2), channel_id=1, source_target_pairs={{0,16},{4,20},{8,24},{12,28},{16,0},{20,4},{24,8},{28,12},{1,17},{... | collective-permute-start | bytes 442376 | tf_op jit(solution)/shard_map/ppermute | solution.py:658
  15.3 2.5 %collective-permute-done.3 = bf16[4,144,128]{2,1,0:T(8,128)(2,1)S(1)} collective-permute-done((bf16[4,144,128]{2,1,0:T(8,128)(2,1)S(1)}, bf16[4,144,128]{2,1,0:T(8,128)(2,1)S(1)}, u32[]{:S(2)}, u32[]{:S(2)}) %collective-permute-start.3) | collective-permute-done | bytes 147488 | tf_op jit(solution)/shard_map/ppermute | solution.py:658
  17.8 1.3 %collective-permute-done.4 = bf16[4,144,128]{2,1,0:T(8,128)(2,1)S(1)} collective-permute-done((bf16[4,144,128]{2,1,0:T(8,128)(2,1)S(1)}, bf16[4,144,128]{2,1,0:T(8,128)(2,1)S(1)}, u32[]{:S(2)}, u32[]{:S(2)}) %collective-permute-start.4) | collective-permute-done | bytes 147488 | tf_op jit(solution)/shard_map/ppermute | solution.py:658
  19.1 2.1 %collective-permute-done.5 = bf16[4,144,128]{2,1,0:T(8,128)(2,1)S(1)} collective-permute-done((bf16[4,144,128]{2,1,0:T(8,128)(2,1)S(1)}, bf16[4,144,128]{2,1,0:T(8,128)(2,1)S(1)}, u32[]{:S(2)}, u32[]{:S(2)}) %collective-permute-start.5) | collective-permute-done | bytes 147488 | tf_op jit(solution)/shard_map/ppermute | solution.py:658
  21.4 1.8 %charge_sums.1 = (f32[912,256]{1,0:T(8,128)S(1)}, bf16[976,256]{1,0:T(8,128)(2,1)S(1)}, f32[16,8,128]{2,1,0:T(8,128)S(1)}, f32[64,128]{1,0:T(8,128)S(1)}, bf16[1...) custom-call(bf16[16,144,128]{2,1,0:T(8,128)(2,1)S(1)} %pad_maximum_fusion.refs_0_, bf16[64,128]{1,0:T(8,128)(2,1)S(1)} %copy-done.1, ...), custom_call_target="tpu_custom_call" | custom-call | flops 3000000000 | bytes 2000000 | tf_op jit(solution)/shard_map/charge_sums/pallas_call | solution.py:691
  23.7 2.0 %message.1 = (f32[128,128]{1,0:T(8,128)S(1)}, f32[16,8,128]{2,1,0:T(8,128)S(1)}, bf16[2304,128]{1,0:T(8,128)(2,1)S(1)}) custom-call(bf16[16,144,128]{2,1,0:T(8,128)(2,1)S(1)} %pad_maximum_fusion.refs_0_, bf16[16,144,128]{2,1,0:T(8,128)(2,1)S(1)} %collective-permute-done.7.refs_1_, f32[16,8,128]{2,1,0:T(8,128)S(1)} %get-tuple-element.51.refs_2_.refs_4_.refs_1_, ...), custom_call_target="tpu_custom_call" | custom-call | flops 3000000000 | bytes 2000000 | tf_op jit(solution)/shard_map/message/pallas_call | solution.py:691
  25.7 1.1 %cotangents.1 = (bf16[128,128]{1,0:T(8,128)(2,1)S(1)}, f32[128,128]{1,0:T(8,128)S(1)}, bf16[896,256]{1,0:T(8,128)(2,1)S(1)}, f32[64,128]{1,0:T(8,128)S(1)}) custom-call(f32[128,128]{1,0:T(8,128)S(1)} %get-tuple-element.41.refs_0_, f32[912,256]{1,0:T(8,128)S(1)} %get-tuple-element.49.refs_1_, bf16[976,256]{1,0:T(8,128)(2,1)S(1)} %get-tuple-element.50.refs_2_, ...), custom_call_target="tpu_custom_call" | custom-call | flops 3000000000 | bytes 2000000 | tf_op jit(solution)/shard_map/cotangents/pallas_call | solution.py:691
  26.8 2.9 %collective-permute-start.10 = (bf16[1,128,128]{2,1,0:T(8,128)(2,1)S(1)}, bf16[1,128,128]{2,1,0:T(8,128)(2,1)S(1)}, u32[]{:S(2)}, u32[]{:S(2)}) collective-permute-start(bf16[1,128,128]{2,1,0:T(8,128)(2,1)S(1)} %bitcast.20), channel_id=1, source_target_pairs={{0,3},{1,0},{2,1},{3,2},{4,7},{5,4},{6,5},{7,6},{8,11},{9,8},{10,9... | collective-permute-start | bytes 98312 | tf_op jit(solution)/shard_map/ppermute | solution.py:642
  30.4 1.0 %collective-permute-done.10 = bf16[1,128,128]{2,1,0:T(8,128)(2,1)S(1)} collective-permute-done((bf16[1,128,128]{2,1,0:T(8,128)(2,1)S(1)}, bf16[1,128,128]{2,1,0:T(8,128)(2,1)S(1)}, u32[]{:S(2)}, u32[]{:S(2)}) %collective-permute-start.10) | collective-permute-done | bytes 32800 | tf_op jit(solution)/shard_map/ppermute | solution.py:642
  31.3 4.1 %collective-permute-done.8 = bf16[1,128,128]{2,1,0:T(8,128)(2,1)S(1)} collective-permute-done((bf16[1,128,128]{2,1,0:T(8,128)(2,1)S(1)}, bf16[1,128,128]{2,1,0:T(8,128)(2,1)S(1)}, u32[]{:S(2)}, u32[]{:S(2)}) %collective-permute-start.8) | collective-permute-done | bytes 32800 | tf_op jit(solution)/shard_map/ppermute | solution.py:642
  35.5 0.9 %collective-permute-start.11 = (bf16[4,128,128]{2,1,0:T(8,128)(2,1)S(1)}, bf16[4,128,128]{2,1,0:T(8,128)(2,1)S(1)}, u32[]{:S(2)}, u32[]{:S(2)}) collective-permute-start(bf16[4,128,128]{2,1,0:T(8,128)(2,1)S(1)} %pad_maximum_fusion.3), channel_id=1, source_target_pairs={{0,4},{4,0},{8,12},{12,8},{16,20},{20,16},{24,28},{28,24},{1,5},{5... | collective-permute-start | bytes 393224 | tf_op jit(solution)/shard_map/ppermute | solution.py:658
  36.4 1.5 %collective-permute-start.12 = (bf16[4,128,128]{2,1,0:T(8,128)(2,1)S(1)}, bf16[4,128,128]{2,1,0:T(8,128)(2,1)S(1)}, u32[]{:S(2)}, u32[]{:S(2)}) collective-permute-start(bf16[4,128,128]{2,1,0:T(8,128)(2,1)S(1)} %pad_maximum_fusion.3), channel_id=1, source_target_pairs={{0,16},{4,20},{8,24},{12,28},{16,0},{20,4},{24,8},{28,12},{1,17},{... | collective-permute-start | bytes 393224 | tf_op jit(solution)/shard_map/ppermute | solution.py:658
  37.9 1.1 %collective-permute-start.13 = (bf16[4,128,128]{2,1,0:T(8,128)(2,1)S(1)}, bf16[4,128,128]{2,1,0:T(8,128)(2,1)S(1)}, u32[]{:S(2)}, u32[]{:S(2)}) collective-permute-start(bf16[4,128,128]{2,1,0:T(8,128)(2,1)S(1)} %pad_maximum_fusion.3), channel_id=1, source_target_pairs={{0,20},{4,16},{8,28},{12,24},{16,4},{20,0},{24,12},{28,8},{1,21},{... | collective-permute-start | bytes 393224 | tf_op jit(solution)/shard_map/ppermute | solution.py:658
  39.0 3.1 %own_terms.1 = (bf16[128,128]{1,0:T(8,128)(2,1)}, f32[1,128]{1,0:T(1,128)}, f32[3,128]{1,0:T(4,128)S(1)}, bf16[512,128]{1,0:T(8,128)(2,1)S(1)}, bf16[256,384]{1,...) custom-call(bf16[128,128]{1,0:T(8,128)(2,1)S(1)} %get-tuple-element.61.refs_0_, ...), custom_call_target="tpu_custom_call" | custom-call | flops 4000000000 | bytes 2000000 | tf_op jit(solution)/shard_map/own_terms/pallas_call | solution.py:691
  42.1 1.6 %collective-permute-done.13 = bf16[4,128,128]{2,1,0:T(8,128)(2,1)S(1)} collective-permute-done((bf16[4,128,128]{2,1,0:T(8,128)(2,1)S(1)}, bf16[4,128,128]{2,1,0:T(8,128)(2,1)S(1)}, u32[]{:S(2)}, u32[]{:S(2)}) %collective-permute-start.13) | collective-permute-done | bytes 131104 | tf_op jit(solution)/shard_map/ppermute | solution.py:658
  43.9 1.5 %pull_sums.1 = (f32[896,256]{1,0:T(8,128)S(1)}, bf16[896,256]{1,0:T(8,128)(2,1)S(1)}) custom-call(bf16[16,128,128]{2,1,0:T(8,128)(2,1)S(1)} %pad_maximum_fusion.1.refs_0_, f32[16,8,128]{2,1,0:T(8,128)S(1)} %get-tuple-element.51.refs_2_.refs_4_.refs_1_, bf16[64,128]{1,0:T(8,128)(2,1)S(1)} %copy-done.2, ...), custom_call_target="tpu_custom_call" | custom-call | flops 3000000000 | bytes 2000000 | tf_op jit(solution)/shard_map/pull_sums/pallas_call | solution.py:691
  45.9 1.3 %react.1.refs_5_ = f32[3,128]{1,0:T(4,128)S(1)} custom-call(bf16[16,128,128]{2,1,0:T(8,128)(2,1)S(1)} %pad_maximum_fusion.1.refs_0_, bf16[16,128,128]{2,1,0:T(8,128)(2,1)S(1)} %collective-permute-done.15.refs_1_, f32[16,8,128]{2,1,0:T(8,128)S(1)} %get-tuple-element.51.refs_2_.refs_4_.refs_1_, f32[16,8,128]{2,1,0:T(8,128)S(1)} %get-tuple-element.53.refs_5_.refs_3_, ...), custom_call_target="tpu_custom_call" | custom-call | flops 3000000000 | bytes 2000000 | tf_op jit(solution)/shard_map/react/pallas_call | solution.py:691
  47.4 1.3 %finish.1 = f32[3,1,128]{2,1,0:T(1,128)} custom-call(f32[896,256]{1,0:T(8,128)S(1)} %get-tuple-element.71.refs_0_, bf16[896,256]{1,0:T(8,128)(2,1)S(1)} %collective-permute-done.14.refs_1_, bf16[256,384]{1,0:T(8,128)(2,1)S(1)} %get-tuple-element.73.refs_2_, f32[16,128]{1,0:T(8,128)S(1)} %get-tuple-element.74.refs_3_, ...), custom_call_target="tpu_custom_call" | custom-call | flops 2000000000 | bytes 2000000 | tf_op jit(solution)/shard_map/finish/pallas_call | solution.py:691
  (27 shorter events, 3.2 us)
Async XLA Ops:
  0.6 20.7 %copy-start.1 = (bf16[64,128]{1,0:T(8,128)(2,1)S(1)}, bf16[64,128]{1,0:T(8,128)(2,1)}, u32[]{:S(2)}) copy-start(bf16[64,128]{1,0:T(8,128)(2,1)} %refs_1_.3) | copy-start | bytes 49156
  2.1 9.1 %collective-permute-start = (bf16[1,144,128]{2,1,0:T(8,128)(2,1)S(1)}, bf16[1,144,128]{2,1,0:T(8,128)(2,1)S(1)}, u32[]{:S(2)}, u32[]{:S(2)}) collective-permute-start(bf16[1,144,128]{2,1,0:T(8,128)(2,1)S(1)} %bitcast.14), channel_id=1, source_target_pairs={{0,1},{1,2},{2,3},{3,0},{4,5},{5,6},{6,7},{7,4},{8,9},{9,10},{10,1... | collective-permute-start | bytes 110600 | tf_op jit(solution)/shard_map/ppermute | solution.py:642
  5.2 6.0 %collective-permute-start.1 = (bf16[1,144,128]{2,1,0:T(8,128)(2,1)S(1)}, bf16[1,144,128]{2,1,0:T(8,128)(2,1)S(1)}, u32[]{:S(2)}, u32[]{:S(2)}) collective-permute-start(bf16[1,144,128]{2,1,0:T(8,128)(2,1)S(1)} %bitcast.15), channel_id=1, source_target_pairs={{0,2},{1,3},{2,0},{3,1},{4,6},{5,7},{6,4},{7,5},{8,10},{9,11},{10,... | collective-permute-start | bytes 110600 | tf_op jit(solution)/shard_map/ppermute | solution.py:642
  7.8 4.0 %collective-permute-start.2 = (bf16[1,144,128]{2,1,0:T(8,128)(2,1)S(1)}, bf16[1,144,128]{2,1,0:T(8,128)(2,1)S(1)}, u32[]{:S(2)}, u32[]{:S(2)}) collective-permute-start(bf16[1,144,128]{2,1,0:T(8,128)(2,1)S(1)} %bitcast.16), channel_id=1, source_target_pairs={{0,3},{1,0},{2,1},{3,2},{4,7},{5,4},{6,5},{7,6},{8,11},{9,8},{10,9... | collective-permute-start | bytes 110600 | tf_op jit(solution)/shard_map/ppermute | solution.py:642
  11.8 6.0 %collective-permute-start.3 = (bf16[4,144,128]{2,1,0:T(8,128)(2,1)S(1)}, bf16[4,144,128]{2,1,0:T(8,128)(2,1)S(1)}, u32[]{:S(2)}, u32[]{:S(2)}) collective-permute-start(bf16[4,144,128]{2,1,0:T(8,128)(2,1)S(1)} %pad_maximum_fusion.2), channel_id=1, source_target_pairs={{0,4},{4,0},{8,12},{12,8},{16,20},{20,16},{24,28},{28,24},{1,5},{5... | collective-permute-start | bytes 442376 | tf_op jit(solution)/shard_map/ppermute | solution.py:658
  13.3 5.8 %collective-permute-start.4 = (bf16[4,144,128]{2,1,0:T(8,128)(2,1)S(1)}, bf16[4,144,128]{2,1,0:T(8,128)(2,1)S(1)}, u32[]{:S(2)}, u32[]{:S(2)}) collective-permute-start(bf16[4,144,128]{2,1,0:T(8,128)(2,1)S(1)} %pad_maximum_fusion.2), channel_id=1, source_target_pairs={{0,16},{4,20},{8,24},{12,28},{16,0},{20,4},{24,8},{28,12},{1,17},{... | collective-permute-start | bytes 442376 | tf_op jit(solution)/shard_map/ppermute | solution.py:658
  14.8 6.3 %collective-permute-start.5 = (bf16[4,144,128]{2,1,0:T(8,128)(2,1)S(1)}, bf16[4,144,128]{2,1,0:T(8,128)(2,1)S(1)}, u32[]{:S(2)}, u32[]{:S(2)}) collective-permute-start(bf16[4,144,128]{2,1,0:T(8,128)(2,1)S(1)} %pad_maximum_fusion.2), channel_id=1, source_target_pairs={{0,20},{4,16},{8,28},{12,24},{16,4},{20,0},{24,12},{28,8},{1,21},{... | collective-permute-start | bytes 442376 | tf_op jit(solution)/shard_map/ppermute | solution.py:658
  21.3 2.4 %collective-permute-start.7 = (bf16[16,144,128]{2,1,0:T(8,128)(2,1)S(1)}, bf16[16,144,128]{2,1,0:T(8,128)(2,1)S(1)}, u32[]{:S(2)}, u32[]{:S(2)}) collective-permute-start(bf16[16,144,128]{2,1,0:T(8,128)(2,1)S(1)} %pad_maximum_fusion.refs_0_), channel_id=1, source_target_pairs={{0,8},{8,0},{16,24},{24,16},{1,9},{9,1},{17,25},{25,17},{2,10},{10... | collective-permute-start | bytes 1769480 | tf_op jit(solution)/shard_map/ppermute | solution.py:673
  23.1 2.5 %collective-permute-start.6 = (bf16[976,256]{1,0:T(8,128)(2,1)S(1)}, bf16[976,256]{1,0:T(8,128)(2,1)S(1)}, u32[]{:S(2)}, u32[]{:S(2)}) collective-permute-start(bf16[976,256]{1,0:T(8,128)(2,1)S(1)} %get-tuple-element.50.refs_2_), channel_id=1, source_target_pairs={{0,8},{8,0},{16,24},{24,16},{1,9},{9,1},{17,25},{25,17},{2,10},{10... | collective-permute-start | bytes 1499144 | tf_op jit(solution)/shard_map/ppermute | solution.py:673
  23.7 2.0 %copy-start = (bf16[1,1,1,128,128]{4,3,2,1,0:T(8,128)(2,1)S(1)}, bf16[1,1,1,128,128]{4,3,2,1,0:T(8,128)(2,1)}, u32[]{:S(2)}) copy-start(bf16[1,1,1,128,128]{4,3,2,1,0:T(8,128)(2,1)} %param.11) | copy-start | bytes 98308
  23.7 2.0 %copy-start.2 = (bf16[64,128]{1,0:T(8,128)(2,1)S(1)}, bf16[64,128]{1,0:T(8,128)(2,1)}, u32[]{:S(2)}) copy-start(bf16[64,128]{1,0:T(8,128)(2,1)} %refs_2_.1) | copy-start | bytes 49156
  26.8 4.5 %collective-permute-start.10 = (bf16[1,128,128]{2,1,0:T(8,128)(2,1)S(1)}, bf16[1,128,128]{2,1,0:T(8,128)(2,1)S(1)}, u32[]{:S(2)}, u32[]{:S(2)}) collective-permute-start(bf16[1,128,128]{2,1,0:T(8,128)(2,1)S(1)} %bitcast.20), channel_id=1, source_target_pairs={{0,3},{1,0},{2,1},{3,2},{4,7},{5,4},{6,5},{7,6},{8,11},{9,8},{10,9... | collective-permute-start | bytes 98312 | tf_op jit(solution)/shard_map/ppermute | solution.py:642
  29.7 5.7 %collective-permute-start.8 = (bf16[1,128,128]{2,1,0:T(8,128)(2,1)S(1)}, bf16[1,128,128]{2,1,0:T(8,128)(2,1)S(1)}, u32[]{:S(2)}, u32[]{:S(2)}) collective-permute-start(bf16[1,128,128]{2,1,0:T(8,128)(2,1)S(1)} %bitcast.21), channel_id=1, source_target_pairs={{0,1},{1,2},{2,3},{3,0},{4,5},{5,6},{6,7},{7,4},{8,9},{9,10},{10,1... | collective-permute-start | bytes 98312 | tf_op jit(solution)/shard_map/ppermute | solution.py:642
  29.7 5.7 %collective-permute-start.9 = (bf16[1,128,128]{2,1,0:T(8,128)(2,1)S(1)}, bf16[1,128,128]{2,1,0:T(8,128)(2,1)S(1)}, u32[]{:S(2)}, u32[]{:S(2)}) collective-permute-start(bf16[1,128,128]{2,1,0:T(8,128)(2,1)S(1)} %bitcast.22), channel_id=1, source_target_pairs={{0,2},{1,3},{2,0},{3,1},{4,6},{5,7},{6,4},{7,5},{8,10},{9,11},{10,... | collective-permute-start | bytes 98312 | tf_op jit(solution)/shard_map/ppermute | solution.py:642
  35.5 6.6 %collective-permute-start.11 = (bf16[4,128,128]{2,1,0:T(8,128)(2,1)S(1)}, bf16[4,128,128]{2,1,0:T(8,128)(2,1)S(1)}, u32[]{:S(2)}, u32[]{:S(2)}) collective-permute-start(bf16[4,128,128]{2,1,0:T(8,128)(2,1)S(1)} %pad_maximum_fusion.3), channel_id=1, source_target_pairs={{0,4},{4,0},{8,12},{12,8},{16,20},{20,16},{24,28},{28,24},{1,5},{5... | collective-permute-start | bytes 393224 | tf_op jit(solution)/shard_map/ppermute | solution.py:658
  36.4 5.7 %collective-permute-start.12 = (bf16[4,128,128]{2,1,0:T(8,128)(2,1)S(1)}, bf16[4,128,128]{2,1,0:T(8,128)(2,1)S(1)}, u32[]{:S(2)}, u32[]{:S(2)}) collective-permute-start(bf16[4,128,128]{2,1,0:T(8,128)(2,1)S(1)} %pad_maximum_fusion.3), channel_id=1, source_target_pairs={{0,16},{4,20},{8,24},{12,28},{16,0},{20,4},{24,8},{28,12},{1,17},{... | collective-permute-start | bytes 393224 | tf_op jit(solution)/shard_map/ppermute | solution.py:658
  37.9 5.9 %collective-permute-start.13 = (bf16[4,128,128]{2,1,0:T(8,128)(2,1)S(1)}, bf16[4,128,128]{2,1,0:T(8,128)(2,1)S(1)}, u32[]{:S(2)}, u32[]{:S(2)}) collective-permute-start(bf16[4,128,128]{2,1,0:T(8,128)(2,1)S(1)} %pad_maximum_fusion.3), channel_id=1, source_target_pairs={{0,20},{4,16},{8,28},{12,24},{16,4},{20,0},{24,12},{28,8},{1,21},{... | collective-permute-start | bytes 393224 | tf_op jit(solution)/shard_map/ppermute | solution.py:658
  43.8 2.1 %collective-permute-start.15 = (bf16[16,128,128]{2,1,0:T(8,128)(2,1)S(1)}, bf16[16,128,128]{2,1,0:T(8,128)(2,1)S(1)}, u32[]{:S(2)}, u32[]{:S(2)}) collective-permute-start(bf16[16,128,128]{2,1,0:T(8,128)(2,1)S(1)} %pad_maximum_fusion.1.refs_0_), channel_id=1, source_target_pairs={{0,8},{8,0},{16,24},{24,16},{1,9},{9,1},{17,25},{25,17},{2,10},{10... | collective-permute-start | bytes 1572872 | tf_op jit(solution)/shard_map/ppermute | solution.py:673
  45.4 2.0 %collective-permute-start.14 = (bf16[896,256]{1,0:T(8,128)(2,1)S(1)}, bf16[896,256]{1,0:T(8,128)(2,1)S(1)}, u32[]{:S(2)}, u32[]{:S(2)}) collective-permute-start(bf16[896,256]{1,0:T(8,128)(2,1)S(1)} %get-tuple-element.72), channel_id=1, source_target_pairs={{0,8},{8,0},{16,24},{24,16},{1,9},{9,1},{17,25},{25,17},{2,10},{10... | collective-permute-start | bytes 1376264 | tf_op jit(solution)/shard_map/ppermute | solution.py:673

commit v6 on v5

--- a/solution.py
+++ b/solution.py
@@ -196,13 +196,23 @@
     count_ref,
     features_hbm,
     positions_hbm,
+    w_charge_hbm,
+    bias_hbm,
     out_ref,
+    slim_ref,
     live_ref,
+    column_ref,
     features_ref,
     positions_ref,
+    w_charge_ref,
+    bias_ref,
     sems,
 ):
-    fetch((features_hbm, positions_hbm), (features_ref, positions_ref), sems)
+    fetch(
+        (features_hbm, positions_hbm, w_charge_hbm, bias_hbm),
+        (features_ref, positions_ref, w_charge_ref, bias_ref),
+        sems,
+    )
     n, channels = features_ref.shape
     live_col = lax.broadcasted_iota(jnp.int32, (n, channels), 0) < count_ref[0]
     live_ref[...] = live_col.astype(F32)
@@ -215,41 +225,42 @@
     blank = jnp.zeros((4, n), F32)
     tail = jnp.concatenate([coarse, living, blank, fine, jnp.zeros((5, n), F32)], axis=0)
     out_ref[n : n + 16, :] = tail.astype(BF16)
+    charge_ch = w_charge_ref.shape[0]
+    diagonal = lax.broadcasted_iota(jnp.int32, (charge_ch, charge_ch), 0) == (
+        lax.broadcasted_iota(jnp.int32, (charge_ch, charge_ch), 1)
+    )
+    column = jnp.sum(jnp.where(diagonal, bias_ref[...], 0.0), axis=1, keepdims=True)
+    column_ref[...] = jnp.broadcast_to(column, column_ref.shape)
+    v = dot_nt(w_charge_ref[...], out_ref[0:n, :]) + column
+    slim_ref[0:charge_ch, :] = (v * sigmoid(v) * living).astype(BF16)
+    slim_ref[charge_ch : charge_ch + 16, :] = tail.astype(BF16)
 
 
 def fold_kernel(
     scale,
     filter_hbm,
     index_hbm,
-    bias_hbm,
     energy_hbm,
     proj_hbm,
     mix_hbm,
     out_ref,
-    column_ref,
     row_ref,
     mixed_ref,
     filter_ref,
     index_ref,
-    bias_ref,
     energy_ref,
     proj_ref,
     mix_ref,
     sems,
 ):
     fetch(
-        (filter_hbm, index_hbm, bias_hbm, energy_hbm, proj_hbm, mix_hbm),
-        (filter_ref, index_ref, bias_ref, energy_ref, proj_ref, mix_ref),
+        (filter_hbm, index_hbm, energy_hbm, proj_hbm, mix_hbm),
+        (filter_ref, index_ref, energy_ref, proj_ref, mix_ref),
         sems,
     )
     waves = filter_ref.shape[1]
     charge_ch = filter_ref.shape[0]
     row_ref[...] = energy_ref[...]
-    diagonal = lax.broadcasted_iota(jnp.int32, (charge_ch, charge_ch), 0) == (
-        lax.broadcasted_iota(jnp.int32, (charge_ch, charge_ch), 1)
-    )
-    column = jnp.sum(jnp.where(diagonal, bias_ref[...], 0.0), axis=1, keepdims=True)
-    column_ref[...] = jnp.broadcast_to(column, column_ref.shape)
     mixed_ref[...] = dot(proj_ref[...], mix_ref[...]).astype(BF16)
     k = index_ref[...]
     positive = [jnp.where(k[a : a + 1, :] >= 0, 1.0, -1.0) for a in range(3)]
@@ -270,13 +281,30 @@
             out_ref[c, w * charge_ch : (w + 1) * charge_ch, :] = piece * turn if w % 2 == 1 else piece
 
 
+def full_steps(nz):
+    return sorted({0, 1 % nz, nz - 1})
+
+
+def row_of(step, nz, full_rows, slim_rows):
+    full = full_steps(nz)
+    if step in full:
+        return full.index(step) * full_rows
+    return len(full) * full_rows + (step - 2) * slim_rows
+
+
+def place_rows(ref, q, step, nz, n, charge_ch):
+    lo = row_of(step, nz, n + 16, charge_ch + 16) + (n if step in full_steps(nz) else charge_ch)
+    tail = ref[q, lo : lo + 16, :].astype(F32)
+    return tail[0:8, :] + tail[8:16, :]
+
+
 def block_place(sizes, odd, block):
     nx, ny, nz = sizes
     dy, dz = (-block[1][0]) % ny, (-block[2][0]) % nz
     if block[0][0] == 0:
-        return 0, dy * nz + dz
+        return 0, dy, dz
     dx = odd * (nx // 2 - 1) if block[0][0] == 1 else (1 - odd) * (1 % (nx // 2))
-    return 1, (dx * ny + dy) * nz + dz
+    return 1, dx * ny + dy, dz
 
 
 def add_groups(structure, groups, sums_ref):
@@ -309,23 +337,28 @@
 ):
     *kept, charge_scr = rest
     charge_ch, channels = w_charge_ref.shape
-    cells = near_ref.shape[0]
-    n = near_ref.shape[1] - 16
+    nz = sizes[2]
+    n = places_ref.shape[2]
     wide = 2 * ORDERS * charge_ch
-    groups = cells // group
+    groups = near_ref.shape[0] // group
+    members = [(r, step) for r in range(group) for step in range(nz)]
     w_charge = w_charge_ref[...]
     bias = bias_ref[...]
 
     def add_charges(g, carry):
         total, live_total = carry
-        for j in range(group):
-            m = g * group + j
-            tail = near_ref[m, n : n + 16, :].astype(F32)
-            pos = tail[0:8, :] + tail[8:16, :]
+        for r, step in members:
+            row = g * group + r
+            m = row * nz + step
+            pos = place_rows(near_ref, row, step, nz, n, charge_ch)
             places_ref[m] = pos
             live = pos[3:4, :]
-            v = dot_nt(w_charge, near_ref[m, 0:n, :]) + bias
-            q = v * sigmoid(v) * live
+            lo = row_of(step, nz, n + 16, charge_ch + 16)
+            if step in full_steps(nz):
+                v = dot_nt(w_charge, near_ref[row, lo : lo + n, :]) + bias
+                q = v * sigmoid(v) * live
+            else:
+                q = near_ref[row, lo : lo + charge_ch, :].astype(F32)
             charge_scr[m] = q
             total = total + q
             live_total = live_total + live
@@ -344,8 +377,8 @@
 
     def structure(g):
         left, right = [], []
-        for j in range(group):
-            m = g * group + j
+        for r, step in members:
+            m = (g * group + r) * nz + step
             pos = places_ref[m]
             tx, ty, tz = axis_tables(pos, place_of(m, 0, sizes), sizes)
             live = pos[3:4, :]
@@ -369,6 +402,7 @@
 
 def message_kernel(
     sizes,
+    charge_ch,
     near_ref,
     far_ref,
     near_places_ref,
@@ -378,22 +412,24 @@
     xcat_ref,
     radial_scr,
 ):
-    n = near_ref.shape[1] - 16
+    n = short_ref.shape[0]
+    nz = sizes[2]
     halves = (near_ref, far_ref)
     places = (near_places_ref, far_places_ref)
 
-    def add_place(m, _):
-        tail = far_ref[m, n : n + 16, :].astype(F32)
-        far_places_ref[m] = tail[0:8, :] + tail[8:16, :]
+    def add_place(row, _):
+        for step in range(nz):
+            far_places_ref[row * nz + step] = place_rows(far_ref, row, step, nz, n, charge_ch)
         return 0
 
-    lax.fori_loop(0, far_ref.shape[0], add_place, 0, unroll=4)
+    lax.fori_loop(0, far_ref.shape[0], add_place, 0, unroll=min(4, far_ref.shape[0]))
     odd = lax.rem(lax.axis_index(AXES[0]), 2)
     own_cols = columns(near_places_ref[0], n)
     for t, block in enumerate(blocks_of(sizes)):
-        half, m = block_place(sizes, odd, block)
-        xcat_ref[t * n : (t + 1) * n, :] = halves[half][m, 0:n, :]
-        pos = places[half][m]
+        half, row, step = block_place(sizes, odd, block)
+        lo = row_of(step, nz, n + 16, 0)
+        xcat_ref[t * n : (t + 1) * n, :] = halves[half][row, lo : lo + n, :]
+        pos = places[half][row * nz + step]
         others = [pos[a : a + 1, :] for a in range(3)]
         for first in range(0, n, 32):
             cols = [c[first : first + 32, :] for c in own_cols]
@@ -424,7 +460,7 @@
     filt_ref,
     *rest,
 ):
-    *kept, grad_ref, refined_ref, field_ref, neutral_ref = rest
+    *kept, grad_ref, pull_ref, refined_ref, field_ref, neutral_ref = rest
     n, channels = features_ref.shape
     charge_ch = w_long_ref.shape[0]
     wide = 2 * ORDERS * charge_ch
@@ -474,7 +510,9 @@
         * (sig_r * (1.0 + refined * (1.0 - sig_r)))
         * (sig * (1.0 + pre_act * (1.0 - sig)))
     )
-    grad_ref[...] = (grad * live_ref[...]).astype(BF16)
+    grad = (grad * live_ref[...]).astype(BF16)
+    grad_ref[...] = grad
+    pull_ref[...] = dot_nt(w_long_ref[...], grad).astype(BF16)
 
 
 def pair_force(sizes, places, strengths_ref, n, slopes_to=None, slopes_from=None):
@@ -486,8 +524,8 @@
         cols = [c[first : first + 32, :] for c in own_cols]
         acc = [jnp.zeros((32, n), F32) for _ in range(3)]
         for t, block in enumerate(blocks):
-            half, m = block_place(sizes, odd, block)
-            pos = places[half][m]
+            half, row, step = block_place(sizes, odd, block)
+            pos = places[half][row * sizes[2] + step]
             offs = offsets(cols, [pos[a : a + 1, :] for a in range(3)], block)
             if slopes_from is None:
                 u, decays = pair_terms(offs, block, first)
@@ -563,23 +601,31 @@
 
 def pull_kernel(sizes, group, near_ref, places_ref, w_long_ref, *rest):
     *kept, sums_ref, part_ref = rest
-    n = near_ref.shape[1]
+    charge_ch = w_long_ref.shape[0]
+    n = places_ref.shape[2]
+    nz = sizes[2]
+    whole = len(full_steps(nz)) * n
     groups = near_ref.shape[0] // group
 
     def structure(g):
         left, right = [], []
-        rows = jnp.concatenate([near_ref[g * group + j] for j in range(group)], axis=0)
+        rows = jnp.concatenate([near_ref[g * group + r, 0:whole, :] for r in range(group)], axis=0)
         pulls = dot_nt(w_long_ref[...], rows)
-        for j in range(group):
-            m = g * group + j
-            if kept:
-                tz = (kept[1][m, 0:8, :], kept[1][m, 8:16, :])
-                right.append(kept[0][m])
-            else:
-                pos = places_ref[m]
-                tx, ty, tz = axis_tables(pos, place_of(m, 0, sizes), sizes)
-                right.append(plane_table(tx, ty).astype(BF16))
-            left.append(spread(pulls[:, j * n : (j + 1) * n], tz))
+        for r in range(group):
+            for step in range(nz):
+                m = (g * group + r) * nz + step
+                lo = row_of(step, nz, n, charge_ch)
+                if step in full_steps(nz):
+                    pull = pulls[:, r * whole + lo : r * whole + lo + n]
+                else:
+                    pull = near_ref[g * group + r, lo : lo + charge_ch, :].astype(F32)
+                if kept:
+                    tz = (kept[1][m, 0:8, :], kept[1][m, 8:16, :])
+                    right.append(kept[0][m])
+                else:
+                    tx, ty, tz = axis_tables(places_ref[m], place_of(m, 0, sizes), sizes)
+                    right.append(plane_table(tx, ty).astype(BF16))
+                left.append(spread(pull, tz))
         return dot_nt(jnp.concatenate(left, axis=1), jnp.concatenate(right, axis=1))
 
     add_groups(structure, groups, sums_ref)
@@ -597,12 +643,13 @@
     *rest,
 ):
     *slopes, out_ref, gcat_scr, strength_scr = rest
-    n = lifted_ref.shape[1]
+    n = force_ref.shape[1]
     halves = (near_ref, far_ref)
     odd = lax.rem(lax.axis_index(AXES[0]), 2)
     for t, block in enumerate(blocks_of(sizes)):
-        half, m = block_place(sizes, odd, block)
-        gcat_scr[t * n : (t + 1) * n, :] = halves[half][m]
+        half, row, step = block_place(sizes, odd, block)
+        lo = row_of(step, sizes[2], n, 0)
+        gcat_scr[t * n : (t + 1) * n, :] = halves[half][row, lo : lo + n, :]
     strength_scr[...] = dot_nt(lifted_ref[...], gcat_scr[...])
     places = (places_ref, far_places_ref)
     near = pair_force(sizes, places, strength_scr, n, None, slopes[0] if slopes else None)
@@ -634,16 +681,13 @@
         out_ref[a] = force_ref[a : a + 1, :] - slope[a]
 
 
-def gather_line(rows, nz):
-    value = rows[None]
-    return jnp.concatenate(
-        [value]
-        + [
-            lax.ppermute(value, "gz", [(i, (i + s) % nz) for i in range(nz)])
-            for s in range(1, nz)
-        ],
-        axis=0,
-    )
+def gather_line(full, slim, nz):
+    def moved(step):
+        rows = full if step in full_steps(nz) else slim
+        return lax.ppermute(rows, "gz", [(i, (i + step) % nz) for i in range(nz)])
+
+    steps = sorted(range(1, nz), key=lambda step: step not in full_steps(nz))
+    return jnp.concatenate([full] + [moved(step) for step in steps], axis=0)[None]
 
 
 def gather_cells(value, sizes, beside):
@@ -721,7 +765,8 @@
     sizes = tuple(lax.axis_size(a) for a in AXES)
     cells = sizes[0] * sizes[1] * sizes[2]
     half_cells = cells // 2
-    group = max(g for g in (8, 4, 2, 1) if half_cells % g == 0)
+    lines = half_cells // sizes[2]
+    group = 2 if sizes[2] <= 4 and lines % 2 == 0 else 1
     blocks = len(blocks_of(sizes))
     scale_long = 4.0 / math.sqrt(n * cells * waves)
     count = counts.reshape(1)
@@ -738,22 +783,26 @@
             scratch = [*places, pltpu.SemaphoreType.DMA((len(places),))]
         return call(kernel, name, outs, scratch, operands, kept, limit, flops, fetched)
 
-    packed, live = run(
+    packed, slim, live, bias = run(
         pack_kernel,
         "pack",
-        [held((n + 16, channels), BF16), held((n, channels), F32)],
+        [
+            held((n + 16, channels), BF16),
+            held((charge_ch + 16, n), BF16),
+            held((n, channels), F32),
+            held((charge_ch, n), F32),
+        ],
         [],
-        [count, own_rows, positions.reshape(3, 1, n)],
+        [count, own_rows, positions.reshape(3, 1, n), w_charge, charge_bias[None, :]],
         0,
         1000,
         fetched=True,
     )
-    filt, bias, energy_row, mixed = run(
+    filt, energy_row, mixed = run(
         lambda *refs: fold_kernel(scale_long, *refs),
         "fold_filter",
         [
             held((ORDERS, 4 * charge_ch, 128), F32),
-            held((charge_ch, n), F32),
             held((1, channels), F32),
             held((bases * channels, channels), BF16),
         ],
@@ -761,7 +810,6 @@
         [
             k_filter,
             k_index,
-            charge_bias[None, :],
             w_energy[None, :],
             w_proj.reshape(bases * channels, channels),
             w_mix,
@@ -770,8 +818,8 @@
         1_000_000_000,
         fetched=True,
     )
-    line = gather_line(packed, sizes[2])
-    line, filt, bias, energy_row, mixed = lax.optimization_barrier((line, filt, bias, energy_row, mixed))
+    line = gather_line(packed, slim, sizes[2])
+    line, filt, energy_row, mixed = lax.optimization_barrier((line, filt, energy_row, mixed))
     (near,) = gather_cells(line, sizes, ())
     far = from_other_core(near)
     sums, part, places, charge, *kept = run(
@@ -791,7 +839,7 @@
     )
     far_part = from_other_core(part)
     short, far_places, xcat = run(
-        lambda *refs: message_kernel(sizes, *refs),
+        lambda *refs: message_kernel(sizes, charge_ch, *refs),
         "message",
         [
             held((n, channels), F32),
@@ -803,11 +851,12 @@
         4,
         3_000_000_000,
     )
-    grad, refined, field, neutral = run(
+    grad, pull, refined, field, neutral = run(
         lambda *refs: cotangent_kernel(sizes, *refs),
         "cotangents",
         [
             held((n, channels), BF16),
+            held((charge_ch, n), BF16),
             held((n, channels), F32),
             held((wide, 256), BF16),
             held((charge_ch, n), F32),
@@ -831,7 +880,7 @@
         12 + len(kept),
         3_000_000_000,
     )
-    grad_line, grad = lax.optimization_barrier((gather_line(grad, sizes[2]), grad))
+    grad_line, grad = lax.optimization_barrier((gather_line(grad, pull, sizes[2]), grad))
     updated, energy, force, lifted, planes, levels, *slopes = run(
         lambda *refs: own_kernel(sizes, *refs),
         "own_terms",

time: 48.9 us -> 48.2 us (0.986)
  starting transfers between devices: 18.9 us -> 18.3 us
    ppermute x6, waiting for transfers between devices: 7.52 us -> 6.63 us  [shifted(): return lax.ppermute(value, ('gx', 'gy'), moves)]
    ppermute x6, waiting for transfers between devices: 5.63 us -> 6.36 us  [moved(): return lax.ppermute(rows, 'gz', [(i, (i + step) % nz) for i in range(nz)])]
    ppermute x6, starting transfers between devices: 10.5 us -> 9.96 us  [moved(): return lax.ppermute(rows, 'gz', [(i, (i + step) % nz) for i in range(nz)])]
  transfers between devices with their start and end apart: 16 -> 16, of which waited for: 8 -> 7; matrix products, arithmetic and copies ran while one was open for 0% -> 0% of each run, Pallas kernels for 24% -> 24%
where the time goes in v6:
time: 48.2 us; the launch traced here: 47.9 us
  starting transfers between devices  18.3 us (38%)
  Pallas kernels  14.9 us (31%)
  waiting for transfers between devices  13.1 us (27%)
  between operations  1.42 us (3%)
    pallas_call x9, Pallas kernels, call(): pl.pallas_call(kernel, name=name, out_shape=outs, in_specs=specs, out_spe...  14.9 us
    ppermute x6, starting transfers between devices, moved(): return lax.ppermute(rows, 'gz', [(i, (i + step) % nz) for i in range(nz)])  9.96 us
    ppermute x6, starting transfers between devices, shifted(): return lax.ppermute(value, ('gx', 'gy'), moves)  7.11 us
    ppermute x6, waiting for transfers between devices, shifted(): return lax.ppermute(value, ('gx', 'gy'), moves)  6.63 us
    ppermute x6, waiting for transfers between devices, moved(): return lax.ppermute(rows, 'gz', [(i, (i + step) % nz) for i in range(nz)])  6.36 us
    ppermute x4, starting transfers between devices, from_other_core(): lax.ppermute(value, 'gx', [(i, i ^ 1) for i in range(lax.axis_size('gx'))])  1.26 us
  transfers between devices with their start and end apart: 16, of which 7 were waited for; matrix products, arithmetic and copies ran while one was open for 0% of the time, Pallas kernels for 24%

profile of v6, /device:TPU:0, one launch (start us, length us, event | category | flops | bytes accessed | tf_op | source)
XLA Modules:
  0.0 47.9 jit_solution(5782726766416714161)
XLA Ops:
  1.3 1.0 %pack.1 = (bf16[144,128]{1,0:T(8,128)(2,1)S(1)}, bf16[80,128]{1,0:T(8,128)(2,1)S(1)}, f32[128,128]{1,0:T(8,128)S(1)}, f32[64,128]{1,0:T(8,128)S(1)}) custom-call(s32[1]{0:T(128)} %bitcast.15.count_ref, bf16[128,128]{1,0:T(8,128)(2,1)} %bitcast.16, f32[3,1,128]{2,1,0:T(1,128)} %bitcast.18, bf16[64,128]{1,0:T(8,128)(2,1)} %refs_1_.3, f32[1,64]{1,0:T(1,128)} %bitcast.19), custom_call_target="tpu_custom_call" | custom-call | flops 1000 | bytes 2000000 | tf_op jit(solution)/shard_map/pack/pallas_call | solution.py:735
  2.3 3.1 %collective-permute-start = (bf16[144,128]{1,0:T(8,128)(2,1)S(1)}, bf16[144,128]{1,0:T(8,128)(2,1)S(1)}, u32[]{:S(2)}, u32[]{:S(2)}) collective-permute-start(bf16[144,128]{1,0:T(8,128)(2,1)S(1)} %get-tuple-element.43), channel_id=1, source_target_pairs={{0,1},{1,2},{2,3},{3,0},{4,5},{5,6},{6,7},{7,4},{8,9},{9,10},{10,1... | collective-permute-start | bytes 110600 | tf_op jit(solution)/shard_map/ppermute | solution.py:687
  5.4 2.1 %collective-permute-start.1 = (bf16[144,128]{1,0:T(8,128)(2,1)S(1)}, bf16[144,128]{1,0:T(8,128)(2,1)S(1)}, u32[]{:S(2)}, u32[]{:S(2)}) collective-permute-start(bf16[144,128]{1,0:T(8,128)(2,1)S(1)} %get-tuple-element.43), channel_id=1, source_target_pairs={{0,3},{1,0},{2,1},{3,2},{4,7},{5,4},{6,5},{7,6},{8,11},{9,8},{10,9... | collective-permute-start | bytes 110600 | tf_op jit(solution)/shard_map/ppermute | solution.py:687
  7.5 0.9 %collective-permute-start.2 = (bf16[80,128]{1,0:T(8,128)(2,1)S(1)}, bf16[80,128]{1,0:T(8,128)(2,1)S(1)}, u32[]{:S(2)}, u32[]{:S(2)}) collective-permute-start(bf16[80,128]{1,0:T(8,128)(2,1)S(1)} %get-tuple-element.44), channel_id=1, source_target_pairs={{0,2},{1,3},{2,0},{3,1},{4,6},{5,7},{6,4},{7,5},{8,10},{9,11},{10,... | collective-permute-start | bytes 61448 | tf_op jit(solution)/shard_map/ppermute | solution.py:687
  8.4 2.0 %fold_filter.1 = (f32[7,256,128]{2,1,0:T(8,128)S(1)}, f32[1,128]{1,0:T(1,128)S(1)}, bf16[512,128]{1,0:T(8,128)(2,1)S(1)}) custom-call(f32[64,2048]{1,0:T(8,128)} %refs_0_.1, s32[3,2048]{1,0:T(4,128)} %refs_1_.2, f32[1,128]{1,0:T(1,128)} %bitcast.21, bf16[512,128]{1,0:T(8,128)(2,1)} %bitcast.20, bf16[128,128]{1,0:T(8,128)(2,1)} %refs_4_.1), custom_call_target="tpu_custom_call" | custom-call | flops 1000000000 | bytes 2000000 | tf_op jit(solution)/shard_map/fold_filter/pallas_call | solution.py:735
  10.4 1.7 %collective-permute-done.2 = bf16[80,128]{1,0:T(8,128)(2,1)S(1)} collective-permute-done((bf16[80,128]{1,0:T(8,128)(2,1)S(1)}, bf16[80,128]{1,0:T(8,128)(2,1)S(1)}, u32[]{:S(2)}, u32[]{:S(2)}) %collective-permute-start.2) | collective-permute-done | bytes 20512 | tf_op jit(solution)/shard_map/ppermute | solution.py:687
  12.2 1.7 %collective-permute-start.3 = (bf16[1,512,128]{2,1,0:T(8,128)(2,1)S(1)}, bf16[1,512,128]{2,1,0:T(8,128)(2,1)S(1)}, u32[]{:S(2)}, u32[]{:S(2)}) collective-permute-start(bf16[1,512,128]{2,1,0:T(8,128)(2,1)S(1)} %maximum_bitcast_fusion), channel_id=1, source_target_pairs={{0,4},{4,0},{8,12},{12,8},{16,20},{20,16},{24,28},{28,24},{1,5},{5... | collective-permute-start | bytes 393224 | tf_op jit(solution)/shard_map/ppermute | solution.py:702
  13.9 1.5 %collective-permute-start.4 = (bf16[1,512,128]{2,1,0:T(8,128)(2,1)S(1)}, bf16[1,512,128]{2,1,0:T(8,128)(2,1)S(1)}, u32[]{:S(2)}, u32[]{:S(2)}) collective-permute-start(bf16[1,512,128]{2,1,0:T(8,128)(2,1)S(1)} %maximum_bitcast_fusion), channel_id=1, source_target_pairs={{0,16},{4,20},{8,24},{12,28},{16,0},{20,4},{24,8},{28,12},{1,17},{... | collective-permute-start | bytes 393224 | tf_op jit(solution)/shard_map/ppermute | solution.py:702
  15.7 2.6 %collective-permute-done.3 = bf16[1,512,128]{2,1,0:T(8,128)(2,1)S(1)} collective-permute-done((bf16[1,512,128]{2,1,0:T(8,128)(2,1)S(1)}, bf16[1,512,128]{2,1,0:T(8,128)(2,1)S(1)}, u32[]{:S(2)}, u32[]{:S(2)}) %collective-permute-start.3) | collective-permute-done | bytes 131104 | tf_op jit(solution)/shard_map/ppermute | solution.py:702
  18.9 2.4 %collective-permute-done.5 = bf16[1,512,128]{2,1,0:T(8,128)(2,1)S(1)} collective-permute-done((bf16[1,512,128]{2,1,0:T(8,128)(2,1)S(1)}, bf16[1,512,128]{2,1,0:T(8,128)(2,1)S(1)}, u32[]{:S(2)}, u32[]{:S(2)}) %collective-permute-start.5) | collective-permute-done | bytes 131104 | tf_op jit(solution)/shard_map/ppermute | solution.py:702
  21.4 1.7 %charge_sums.1 = (f32[912,256]{1,0:T(8,128)S(1)}, bf16[976,256]{1,0:T(8,128)(2,1)S(1)}, f32[16,8,128]{2,1,0:T(8,128)S(1)}, f32[64,128]{1,0:T(8,128)S(1)}, bf16[1...) custom-call(bf16[4,512,128]{2,1,0:T(8,128)(2,1)S(1)} %pad_maximum_fusion.refs_0_, bf16[64,128]{1,0:T(8,128)(2,1)S(1)} %copy-done.1, ...), custom_call_target="tpu_custom_call" | custom-call | flops 3000000000 | bytes 2000000 | tf_op jit(solution)/shard_map/charge_sums/pallas_call | solution.py:735
  23.1 0.6 %collective-permute-start.6 = (bf16[976,256]{1,0:T(8,128)(2,1)S(1)}, bf16[976,256]{1,0:T(8,128)(2,1)S(1)}, u32[]{:S(2)}, u32[]{:S(2)}) collective-permute-start(bf16[976,256]{1,0:T(8,128)(2,1)S(1)} %get-tuple-element.51.refs_2_), channel_id=1, source_target_pairs={{0,8},{8,0},{16,24},{24,16},{1,9},{9,1},{17,25},{25,17},{2,10},{10... | collective-permute-start | bytes 1499144 | tf_op jit(solution)/shard_map/ppermute | solution.py:717
  23.7 1.9 %message.1 = (f32[128,128]{1,0:T(8,128)S(1)}, f32[16,8,128]{2,1,0:T(8,128)S(1)}, bf16[2304,128]{1,0:T(8,128)(2,1)S(1)}) custom-call(bf16[4,512,128]{2,1,0:T(8,128)(2,1)S(1)} %pad_maximum_fusion.refs_0_, bf16[4,512,128]{2,1,0:T(8,128)(2,1)S(1)} %collective-permute-done.7.refs_1_, f32[16,8,128]{2,1,0:T(8,128)S(1)} %get-tuple-element.52.refs_2_.refs_4_.refs_1_, ...), custom_call_target="tpu_custom_call" | custom-call | flops 3000000000 | bytes 2000000 | tf_op jit(solution)/shard_map/message/pallas_call | solution.py:735
  25.7 1.2 %cotangents.1 = (bf16[128,128]{1,0:T(8,128)(2,1)S(1)}, bf16[64,128]{1,0:T(8,128)(2,1)S(1)}, f32[128,128]{1,0:T(8,128)S(1)}, bf16[896,256]{1,0:T(8,128)(2,1)S(1)}, f32[64,128]{1,0:T(8,128)S(1)}) custom-call(f32[128,128]{1,0:T(8,128)S(1)} %get-tuple-element.42.refs_0_, f32[912,256]{1,0:T(8,128)S(1)} %get-tuple-element.50.refs_1_, ...), custom_call_target="tpu_custom_call" | custom-call | flops 3000000000 | bytes 2000000 | tf_op jit(solution)/shard_map/cotangents/pallas_call | solution.py:735
  26.9 3.8 %collective-permute-start.9 = (bf16[128,128]{1,0:T(8,128)(2,1)S(1)}, bf16[128,128]{1,0:T(8,128)(2,1)S(1)}, u32[]{:S(2)}, u32[]{:S(2)}) collective-permute-start(bf16[128,128]{1,0:T(8,128)(2,1)S(1)} %get-tuple-element.63.refs_0_), channel_id=1, source_target_pairs={{0,3},{1,0},{2,1},{3,2},{4,7},{5,4},{6,5},{7,6},{8,11},{9,8},{10,9... | collective-permute-start | bytes 98312 | tf_op jit(solution)/shard_map/ppermute | solution.py:687
  30.8 4.6 %collective-permute-done.10 = bf16[64,128]{1,0:T(8,128)(2,1)S(1)} collective-permute-done((bf16[64,128]{1,0:T(8,128)(2,1)S(1)}, bf16[64,128]{1,0:T(8,128)(2,1)S(1)}, u32[]{:S(2)}, u32[]{:S(2)}) %collective-permute-start.10) | collective-permute-done | bytes 16416 | tf_op jit(solution)/shard_map/ppermute | solution.py:687
  35.4 0.6 %collective-permute-start.11 = (bf16[1,448,128]{2,1,0:T(8,128)(2,1)S(1)}, bf16[1,448,128]{2,1,0:T(8,128)(2,1)S(1)}, u32[]{:S(2)}, u32[]{:S(2)}) collective-permute-start(bf16[1,448,128]{2,1,0:T(8,128)(2,1)S(1)} %maximum_bitcast_fusion.1), channel_id=1, source_target_pairs={{0,4},{4,0},{8,12},{12,8},{16,20},{20,16},{24,28},{28,24},{1,5},{5... | collective-permute-start | bytes 344072 | tf_op jit(solution)/shard_map/ppermute | solution.py:702
  36.0 1.5 %collective-permute-start.12 = (bf16[1,448,128]{2,1,0:T(8,128)(2,1)S(1)}, bf16[1,448,128]{2,1,0:T(8,128)(2,1)S(1)}, u32[]{:S(2)}, u32[]{:S(2)}) collective-permute-start(bf16[1,448,128]{2,1,0:T(8,128)(2,1)S(1)} %maximum_bitcast_fusion.1), channel_id=1, source_target_pairs={{0,16},{4,20},{8,24},{12,28},{16,0},{20,4},{24,8},{28,12},{1,17},{... | collective-permute-start | bytes 344072 | tf_op jit(solution)/shard_map/ppermute | solution.py:702
  37.4 1.5 %collective-permute-start.13 = (bf16[1,448,128]{2,1,0:T(8,128)(2,1)S(1)}, bf16[1,448,128]{2,1,0:T(8,128)(2,1)S(1)}, u32[]{:S(2)}, u32[]{:S(2)}) collective-permute-start(bf16[1,448,128]{2,1,0:T(8,128)(2,1)S(1)} %maximum_bitcast_fusion.1), channel_id=1, source_target_pairs={{0,20},{4,16},{8,28},{12,24},{16,4},{20,0},{24,12},{28,8},{1,21},{... | collective-permute-start | bytes 344072 | tf_op jit(solution)/shard_map/ppermute | solution.py:702
  39.0 3.1 %own_terms.1 = (bf16[128,128]{1,0:T(8,128)(2,1)}, f32[1,128]{1,0:T(1,128)}, f32[3,128]{1,0:T(4,128)S(1)}, bf16[512,128]{1,0:T(8,128)(2,1)S(1)}, bf16[256,384]{1,...) custom-call(bf16[128,128]{1,0:T(8,128)(2,1)S(1)} %get-tuple-element.63.refs_0_, ...), custom_call_target="tpu_custom_call" | custom-call | flops 4000000000 | bytes 2000000 | tf_op jit(solution)/shard_map/own_terms/pallas_call | solution.py:735
  42.1 1.1 %collective-permute-done.13 = bf16[1,448,128]{2,1,0:T(8,128)(2,1)S(1)} collective-permute-done((bf16[1,448,128]{2,1,0:T(8,128)(2,1)S(1)}, bf16[1,448,128]{2,1,0:T(8,128)(2,1)S(1)}, u32[]{:S(2)}, u32[]{:S(2)}) %collective-permute-start.13) | collective-permute-done | bytes 114720 | tf_op jit(solution)/shard_map/ppermute | solution.py:702
  43.3 1.4 %pull_sums.1 = (f32[896,256]{1,0:T(8,128)S(1)}, bf16[896,256]{1,0:T(8,128)(2,1)S(1)}) custom-call(bf16[4,448,128]{2,1,0:T(8,128)(2,1)S(1)} %pad_maximum_fusion.1.refs_0_, f32[16,8,128]{2,1,0:T(8,128)S(1)} %get-tuple-element.52.refs_2_.refs_4_.refs_1_, bf16[64,128]{1,0:T(8,128)(2,1)S(1)} %copy-done.2, ...), custom_call_target="tpu_custom_call" | custom-call | flops 3000000000 | bytes 2000000 | tf_op jit(solution)/shard_map/pull_sums/pallas_call | solution.py:735
  45.2 1.3 %react.1.refs_5_ = f32[3,128]{1,0:T(4,128)S(1)} custom-call(bf16[4,448,128]{2,1,0:T(8,128)(2,1)S(1)} %pad_maximum_fusion.1.refs_0_, bf16[4,448,128]{2,1,0:T(8,128)(2,1)S(1)} %collective-permute-done.15.refs_1_, f32[16,8,128]{2,1,0:T(8,128)S(1)} %get-tuple-element.52.refs_2_.refs_4_.refs_1_, f32[16,8,128]{2,1,0:T(8,128)S(1)} %get-tuple-element.54.refs_5_.refs_3_, ...), custom_call_target="tpu_custom_call" | custom-call | flops 3000000000 | bytes 2000000 | tf_op jit(solution)/shard_map/react/pallas_call | solution.py:735
  46.7 1.3 %finish.1 = f32[3,1,128]{2,1,0:T(1,128)} custom-call(f32[896,256]{1,0:T(8,128)S(1)} %get-tuple-element.73.refs_0_, bf16[896,256]{1,0:T(8,128)(2,1)S(1)} %collective-permute-done.14.refs_1_, bf16[256,384]{1,0:T(8,128)(2,1)S(1)} %get-tuple-element.75.refs_2_, f32[16,128]{1,0:T(8,128)S(1)} %get-tuple-element.76.refs_3_, ...), custom_call_target="tpu_custom_call" | custom-call | flops 2000000000 | bytes 2000000 | tf_op jit(solution)/shard_map/finish/pallas_call | solution.py:735
  (27 shorter events, 1.9 us)
Async XLA Ops:
  0.6 20.8 %copy-start.1 = (bf16[64,128]{1,0:T(8,128)(2,1)S(1)}, bf16[64,128]{1,0:T(8,128)(2,1)}, u32[]{:S(2)}) copy-start(bf16[64,128]{1,0:T(8,128)(2,1)} %refs_1_.3) | copy-start | bytes 49156
  2.3 9.9 %collective-permute-start = (bf16[144,128]{1,0:T(8,128)(2,1)S(1)}, bf16[144,128]{1,0:T(8,128)(2,1)S(1)}, u32[]{:S(2)}, u32[]{:S(2)}) collective-permute-start(bf16[144,128]{1,0:T(8,128)(2,1)S(1)} %get-tuple-element.43), channel_id=1, source_target_pairs={{0,1},{1,2},{2,3},{3,0},{4,5},{5,6},{6,7},{7,4},{8,9},{9,10},{10,1... | collective-permute-start | bytes 110600 | tf_op jit(solution)/shard_map/ppermute | solution.py:687
  5.4 6.8 %collective-permute-start.1 = (bf16[144,128]{1,0:T(8,128)(2,1)S(1)}, bf16[144,128]{1,0:T(8,128)(2,1)S(1)}, u32[]{:S(2)}, u32[]{:S(2)}) collective-permute-start(bf16[144,128]{1,0:T(8,128)(2,1)S(1)} %get-tuple-element.43), channel_id=1, source_target_pairs={{0,3},{1,0},{2,1},{3,2},{4,7},{5,4},{6,5},{7,6},{8,11},{9,8},{10,9... | collective-permute-start | bytes 110600 | tf_op jit(solution)/shard_map/ppermute | solution.py:687
  7.5 4.7 %collective-permute-start.2 = (bf16[80,128]{1,0:T(8,128)(2,1)S(1)}, bf16[80,128]{1,0:T(8,128)(2,1)S(1)}, u32[]{:S(2)}, u32[]{:S(2)}) collective-permute-start(bf16[80,128]{1,0:T(8,128)(2,1)S(1)} %get-tuple-element.44), channel_id=1, source_target_pairs={{0,2},{1,3},{2,0},{3,1},{4,6},{5,7},{6,4},{7,5},{8,10},{9,11},{10,... | collective-permute-start | bytes 61448 | tf_op jit(solution)/shard_map/ppermute | solution.py:687
  12.2 6.2 %collective-permute-start.3 = (bf16[1,512,128]{2,1,0:T(8,128)(2,1)S(1)}, bf16[1,512,128]{2,1,0:T(8,128)(2,1)S(1)}, u32[]{:S(2)}, u32[]{:S(2)}) collective-permute-start(bf16[1,512,128]{2,1,0:T(8,128)(2,1)S(1)} %maximum_bitcast_fusion), channel_id=1, source_target_pairs={{0,4},{4,0},{8,12},{12,8},{16,20},{20,16},{24,28},{28,24},{1,5},{5... | collective-permute-start | bytes 393224 | tf_op jit(solution)/shard_map/ppermute | solution.py:702
  13.9 5.0 %collective-permute-start.4 = (bf16[1,512,128]{2,1,0:T(8,128)(2,1)S(1)}, bf16[1,512,128]{2,1,0:T(8,128)(2,1)S(1)}, u32[]{:S(2)}, u32[]{:S(2)}) collective-permute-start(bf16[1,512,128]{2,1,0:T(8,128)(2,1)S(1)} %maximum_bitcast_fusion), channel_id=1, source_target_pairs={{0,16},{4,20},{8,24},{12,28},{16,0},{20,4},{24,8},{28,12},{1,17},{... | collective-permute-start | bytes 393224 | tf_op jit(solution)/shard_map/ppermute | solution.py:702
  15.4 5.9 %collective-permute-start.5 = (bf16[1,512,128]{2,1,0:T(8,128)(2,1)S(1)}, bf16[1,512,128]{2,1,0:T(8,128)(2,1)S(1)}, u32[]{:S(2)}, u32[]{:S(2)}) collective-permute-start(bf16[1,512,128]{2,1,0:T(8,128)(2,1)S(1)} %maximum_bitcast_fusion), channel_id=1, source_target_pairs={{0,20},{4,16},{8,28},{12,24},{16,4},{20,0},{24,12},{28,8},{1,21},{... | collective-permute-start | bytes 393224 | tf_op jit(solution)/shard_map/ppermute | solution.py:702
  21.3 2.3 %collective-permute-start.7 = (bf16[4,512,128]{2,1,0:T(8,128)(2,1)S(1)}, bf16[4,512,128]{2,1,0:T(8,128)(2,1)S(1)}, u32[]{:S(2)}, u32[]{:S(2)}) collective-permute-start(bf16[4,512,128]{2,1,0:T(8,128)(2,1)S(1)} %pad_maximum_fusion.refs_0_), channel_id=1, source_target_pairs={{0,8},{8,0},{16,24},{24,16},{1,9},{9,1},{17,25},{25,17},{2,10},{10... | collective-permute-start | bytes 1572872 | tf_op jit(solution)/shard_map/ppermute | solution.py:717
  23.1 2.5 %collective-permute-start.6 = (bf16[976,256]{1,0:T(8,128)(2,1)S(1)}, bf16[976,256]{1,0:T(8,128)(2,1)S(1)}, u32[]{:S(2)}, u32[]{:S(2)}) collective-permute-start(bf16[976,256]{1,0:T(8,128)(2,1)S(1)} %get-tuple-element.51.refs_2_), channel_id=1, source_target_pairs={{0,8},{8,0},{16,24},{24,16},{1,9},{9,1},{17,25},{25,17},{2,10},{10... | collective-permute-start | bytes 1499144 | tf_op jit(solution)/shard_map/ppermute | solution.py:717
  23.7 2.0 %copy-start = (bf16[1,1,1,128,128]{4,3,2,1,0:T(8,128)(2,1)S(1)}, bf16[1,1,1,128,128]{4,3,2,1,0:T(8,128)(2,1)}, u32[]{:S(2)}) copy-start(bf16[1,1,1,128,128]{4,3,2,1,0:T(8,128)(2,1)} %param.11) | copy-start | bytes 98308
  23.7 2.0 %copy-start.2 = (bf16[64,128]{1,0:T(8,128)(2,1)S(1)}, bf16[64,128]{1,0:T(8,128)(2,1)}, u32[]{:S(2)}) copy-start(bf16[64,128]{1,0:T(8,128)(2,1)} %refs_2_.1) | copy-start | bytes 49156
  26.9 8.5 %collective-permute-start.8 = (bf16[128,128]{1,0:T(8,128)(2,1)S(1)}, bf16[128,128]{1,0:T(8,128)(2,1)S(1)}, u32[]{:S(2)}, u32[]{:S(2)}) collective-permute-start(bf16[128,128]{1,0:T(8,128)(2,1)S(1)} %get-tuple-element.63.refs_0_), channel_id=1, source_target_pairs={{0,1},{1,2},{2,3},{3,0},{4,5},{5,6},{6,7},{7,4},{8,9},{9,10},{10,1... | collective-permute-start | bytes 98312 | tf_op jit(solution)/shard_map/ppermute | solution.py:687
  26.9 8.5 %collective-permute-start.9 = (bf16[128,128]{1,0:T(8,128)(2,1)S(1)}, bf16[128,128]{1,0:T(8,128)(2,1)S(1)}, u32[]{:S(2)}, u32[]{:S(2)}) collective-permute-start(bf16[128,128]{1,0:T(8,128)(2,1)S(1)} %get-tuple-element.63.refs_0_), channel_id=1, source_target_pairs={{0,3},{1,0},{2,1},{3,2},{4,7},{5,4},{6,5},{7,6},{8,11},{9,8},{10,9... | collective-permute-start | bytes 98312 | tf_op jit(solution)/shard_map/ppermute | solution.py:687
  30.8 4.6 %collective-permute-start.10 = (bf16[64,128]{1,0:T(8,128)(2,1)S(1)}, bf16[64,128]{1,0:T(8,128)(2,1)S(1)}, u32[]{:S(2)}, u32[]{:S(2)}) collective-permute-start(bf16[64,128]{1,0:T(8,128)(2,1)S(1)} %get-tuple-element.62), channel_id=1, source_target_pairs={{0,2},{1,3},{2,0},{3,1},{4,6},{5,7},{6,4},{7,5},{8,10},{9,11},{10,... | collective-permute-start | bytes 49160 | tf_op jit(solution)/shard_map/ppermute | solution.py:687
  35.4 6.6 %collective-permute-start.11 = (bf16[1,448,128]{2,1,0:T(8,128)(2,1)S(1)}, bf16[1,448,128]{2,1,0:T(8,128)(2,1)S(1)}, u32[]{:S(2)}, u32[]{:S(2)}) collective-permute-start(bf16[1,448,128]{2,1,0:T(8,128)(2,1)S(1)} %maximum_bitcast_fusion.1), channel_id=1, source_target_pairs={{0,4},{4,0},{8,12},{12,8},{16,20},{20,16},{24,28},{28,24},{1,5},{5... | collective-permute-start | bytes 344072 | tf_op jit(solution)/shard_map/ppermute | solution.py:702
  36.0 6.1 %collective-permute-start.12 = (bf16[1,448,128]{2,1,0:T(8,128)(2,1)S(1)}, bf16[1,448,128]{2,1,0:T(8,128)(2,1)S(1)}, u32[]{:S(2)}, u32[]{:S(2)}) collective-permute-start(bf16[1,448,128]{2,1,0:T(8,128)(2,1)S(1)} %maximum_bitcast_fusion.1), channel_id=1, source_target_pairs={{0,16},{4,20},{8,24},{12,28},{16,0},{20,4},{24,8},{28,12},{1,17},{... | collective-permute-start | bytes 344072 | tf_op jit(solution)/shard_map/ppermute | solution.py:702
  37.4 5.7 %collective-permute-start.13 = (bf16[1,448,128]{2,1,0:T(8,128)(2,1)S(1)}, bf16[1,448,128]{2,1,0:T(8,128)(2,1)S(1)}, u32[]{:S(2)}, u32[]{:S(2)}) collective-permute-start(bf16[1,448,128]{2,1,0:T(8,128)(2,1)S(1)} %maximum_bitcast_fusion.1), channel_id=1, source_target_pairs={{0,20},{4,16},{8,28},{12,24},{16,4},{20,0},{24,12},{28,8},{1,21},{... | collective-permute-start | bytes 344072 | tf_op jit(solution)/shard_map/ppermute | solution.py:702
  43.2 2.0 %collective-permute-start.15 = (bf16[4,448,128]{2,1,0:T(8,128)(2,1)S(1)}, bf16[4,448,128]{2,1,0:T(8,128)(2,1)S(1)}, u32[]{:S(2)}, u32[]{:S(2)}) collective-permute-start(bf16[4,448,128]{2,1,0:T(8,128)(2,1)S(1)} %pad_maximum_fusion.1.refs_0_), channel_id=1, source_target_pairs={{0,8},{8,0},{16,24},{24,16},{1,9},{9,1},{17,25},{25,17},{2,10},{10... | collective-permute-start | bytes 1376264 | tf_op jit(solution)/shard_map/ppermute | solution.py:717
  44.7 2.0 %collective-permute-start.14 = (bf16[896,256]{1,0:T(8,128)(2,1)S(1)}, bf16[896,256]{1,0:T(8,128)(2,1)S(1)}, u32[]{:S(2)}, u32[]{:S(2)}) collective-permute-start(bf16[896,256]{1,0:T(8,128)(2,1)S(1)} %get-tuple-element.74), channel_id=1, source_target_pairs={{0,8},{8,0},{16,24},{24,16},{1,9},{9,1},{17,25},{25,17},{2,10},{10... | collective-permute-start | bytes 1376264 | tf_op jit(solution)/shard_map/ppermute | solution.py:717

commit v7 on v6

--- a/solution.py
+++ b/solution.py
@@ -149,7 +149,8 @@
 
 def blocks_of(sizes):
     options = [((0, False), (1, True)) if n == 2 else ((0, False), (-1, False), (1, False)) for n in sizes]
-    return list(itertools.product(*options))
+    blocks = itertools.product(*options)
+    return sorted(blocks, key=lambda block: block[0][0] != 0 or block[1][0] != 0)
 
 
 def offsets(own_cols, others, block):
@@ -307,97 +308,145 @@
     return 1, dx * ny + dy, dz
 
 
-def add_groups(structure, groups, sums_ref):
-    if groups <= 4:
-        total = structure(0)
-        for g in range(1, groups):
-            total = total + structure(g)
+def add_groups(structure, rows, group, sums_ref, first_ref):
+    steps = (rows - 1) // group
+    if steps <= 4:
+        total = first_ref[...]
+        for g in range(steps):
+            total = total + structure(1 + g * group)
         sums_ref[...] = total
         return
-    sums_ref[...] = structure(0)
+    sums_ref[...] = first_ref[...]
 
     def add_structure(g, _):
-        sums_ref[...] += structure(g)
+        sums_ref[...] += structure(1 + g * group)
         return 0
 
-    lax.fori_loop(1, groups, add_structure, 0)
+    lax.fori_loop(0, steps, add_structure, 0)
+
+
+def cell_charges(ref, row, step, sizes, w_charge, bias, n):
+    charge_ch = w_charge.shape[0]
+    nz = sizes[2]
+    pos = place_rows(ref, row, step, nz, n, charge_ch)
+    lo = row_of(step, nz, n + 16, charge_ch + 16)
+    if step in full_steps(nz):
+        v = dot_nt(w_charge, ref[row, lo : lo + n, :]) + bias
+        return pos, v * sigmoid(v) * pos[3:4, :]
+    return pos, ref[row, lo : lo + charge_ch, :].astype(F32)
+
+
+def charge_sides(pos, charge, m, sizes, base):
+    tx, ty, tz = axis_tables(pos, place_of(m, 0, sizes), sizes)
+    live = pos[3:4, :]
+    living = jnp.concatenate([tz[0] * live, tz[1] * live], axis=0).astype(BF16)
+    left = jnp.concatenate([spread((charge - base) * live, tz), living], axis=0)
+    return left, plane_table(tx, ty).astype(BF16), jnp.concatenate(tz, axis=0)
+
+
+def block_radials(pos, block, own_cols, store, n):
+    others = [pos[a : a + 1, :] for a in range(3)]
+    for first in range(0, n, 32):
+        cols = [c[first : first + 32, :] for c in own_cols]
+        u, decays = pair_terms(offsets(cols, others, block), block, first)
+        u2 = u * u
+        for b in range(len(GAMMAS)):
+            store(b * n + first, (decays[b] * u2).astype(BF16))
+
+
+def line_blocks(sizes):
+    return [b for b in blocks_of(sizes) if b[0][0] == 0 and b[1][0] == 0]
+
+
+def line_kernel(
+    sizes,
+    line_ref,
+    w_charge_ref,
+    bias_ref,
+    sums_ref,
+    base_ref,
+    places_ref,
+    charge_ref,
+    gathered_ref,
+    planes_ref,
+    levels_ref,
+    radial_scr,
+    xcat_scr,
+):
+    nz = sizes[2]
+    n = places_ref.shape[2]
+    w_charge = w_charge_ref[...]
+    bias = bias_ref[...]
+    cells = [cell_charges(line_ref, 0, step, sizes, w_charge, bias, n) for step in range(nz)]
+    charge_ref[...] = cells[0][1]
+    total = sum(q for _, q in cells)
+    lives = sum(pos[3:4, :] for pos, _ in cells)
+    base = jnp.sum(total, axis=1, keepdims=True) / jnp.sum(lives, axis=1, keepdims=True)
+    base = base.astype(BF16).astype(F32)
+    base_ref[...] = jnp.broadcast_to(base, base_ref.shape)
+    left, right = [], []
+    for step, (pos, q) in enumerate(cells):
+        places_ref[step] = pos
+        side, plane, level = charge_sides(pos, q, step, sizes, base)
+        planes_ref[step] = plane
+        levels_ref[step] = level
+        left.append(side)
+        right.append(plane)
+    sums_ref[...] = dot_nt(jnp.concatenate(left, axis=1), jnp.concatenate(right, axis=1))
+    own_cols = columns(cells[0][0], n)
+    for t, block in enumerate(line_blocks(sizes)):
+        step = (-block[2][0]) % nz
+
+        def store(row, value, t=t):
+            radial_scr[row : row + 32, t * n : (t + 1) * n] = value
+
+        block_radials(cells[step][0], block, own_cols, store, n)
+        lo = row_of(step, nz, n + 16, 0)
+        xcat_scr[t * n : (t + 1) * n, :] = line_ref[0, lo : lo + n, :]
+    gathered_ref[...] = dot(radial_scr[...], xcat_scr[...])
 
 
 def charge_kernel(
     sizes,
     group,
     near_ref,
+    line_sums_ref,
+    base_ref,
+    line_places_ref,
     w_charge_ref,
     bias_ref,
     sums_ref,
     part_ref,
     places_ref,
-    charge_ref,
-    *rest,
+    *kept,
 ):
-    *kept, charge_scr = rest
     charge_ch, channels = w_charge_ref.shape
     nz = sizes[2]
     n = places_ref.shape[2]
     wide = 2 * ORDERS * charge_ch
-    groups = near_ref.shape[0] // group
-    members = [(r, step) for r in range(group) for step in range(nz)]
     w_charge = w_charge_ref[...]
     bias = bias_ref[...]
-
-    def add_charges(g, carry):
-        total, live_total = carry
-        for r, step in members:
-            row = g * group + r
-            m = row * nz + step
-            pos = place_rows(near_ref, row, step, nz, n, charge_ch)
-            places_ref[m] = pos
-            live = pos[3:4, :]
-            lo = row_of(step, nz, n + 16, charge_ch + 16)
-            if step in full_steps(nz):
-                v = dot_nt(w_charge, near_ref[row, lo : lo + n, :]) + bias
-                q = v * sigmoid(v) * live
-            else:
-                q = near_ref[row, lo : lo + charge_ch, :].astype(F32)
-            charge_scr[m] = q
-            total = total + q
-            live_total = live_total + live
-        return total, live_total
-
-    start = (jnp.zeros((charge_ch, n), F32), jnp.zeros((1, n), F32))
-    if groups <= 4:
-        for g in range(groups):
-            start = add_charges(g, start)
-        total, live_total = start
-    else:
-        total, live_total = lax.fori_loop(0, groups, add_charges, start)
-    mean = jnp.sum(total, axis=1, keepdims=True) / jnp.sum(live_total, axis=1, keepdims=True)
-    mean = mean.astype(BF16).astype(F32)
-    charge_ref[...] = charge_scr[0]
-
-    def structure(g):
+    base = base_ref[...]
+    places_ref[0:nz] = line_places_ref[...]
+
+    def structure(row):
         left, right = [], []
-        for r, step in members:
-            m = (g * group + r) * nz + step
-            pos = places_ref[m]
-            tx, ty, tz = axis_tables(pos, place_of(m, 0, sizes), sizes)
-            live = pos[3:4, :]
-            living = jnp.concatenate([tz[0] * live, tz[1] * live], axis=0).astype(BF16)
-            plane = plane_table(tx, ty).astype(BF16)
-            if kept:
-                kept[0][m] = plane
-                kept[1][m] = jnp.concatenate(tz, axis=0)
-            left.append(
-                jnp.concatenate([spread((charge_scr[m] - mean) * live, tz), living], axis=0)
-            )
-            right.append(plane)
+        for r in range(group):
+            for step in range(nz):
+                pos, q = cell_charges(near_ref, row + r, step, sizes, w_charge, bias, n)
+                m = (row + r) * nz + step
+                places_ref[m] = pos
+                side, plane, level = charge_sides(pos, q, m, sizes, base)
+                if kept:
+                    kept[0][m - nz] = plane
+                    kept[1][m - nz] = level
+                left.append(side)
+                right.append(plane)
         return dot_nt(jnp.concatenate(left, axis=1), jnp.concatenate(right, axis=1))
 
-    add_groups(structure, groups, sums_ref)
+    add_groups(structure, near_ref.shape[0], group, sums_ref, line_sums_ref)
     part_ref[0 : wide + 16, :] = sums_ref[...].astype(BF16)
-    part_ref[wide + 16 : wide + 16 + charge_ch, :] = jnp.broadcast_to(mean, (charge_ch, 256)).astype(
-        BF16
-    )
+    part_ref[wide + 16 : wide + 16 + charge_ch, :] = jnp.concatenate([base, base], axis=1).astype(BF16)
 
 
 def message_kernel(
@@ -407,6 +456,7 @@
     far_ref,
     near_places_ref,
     mixed_ref,
+    line_gathered_ref,
     short_ref,
     far_places_ref,
     xcat_ref,
@@ -425,21 +475,22 @@
     lax.fori_loop(0, far_ref.shape[0], add_place, 0, unroll=min(4, far_ref.shape[0]))
     odd = lax.rem(lax.axis_index(AXES[0]), 2)
     own_cols = columns(near_places_ref[0], n)
+    done = 0
     for t, block in enumerate(blocks_of(sizes)):
         half, row, step = block_place(sizes, odd, block)
         lo = row_of(step, nz, n + 16, 0)
         xcat_ref[t * n : (t + 1) * n, :] = halves[half][row, lo : lo + n, :]
         pos = places[half][row * nz + step]
-        others = [pos[a : a + 1, :] for a in range(3)]
-        for first in range(0, n, 32):
-            cols = [c[first : first + 32, :] for c in own_cols]
-            u, decays = pair_terms(offsets(cols, others, block), block, first)
-            u2 = u * u
-            for b in range(len(GAMMAS)):
-                radial_scr[b * n + first : b * n + first + 32, t * n : (t + 1) * n] = (
-                    decays[b] * u2
-                ).astype(BF16)
-    gathered = dot(radial_scr[...], xcat_ref[...]).astype(BF16)
+        if block in line_blocks(sizes):
+            continue
+
+        def store(place, value, t=done):
+            radial_scr[place : place + 32, t * n : (t + 1) * n] = value
+
+        block_radials(pos, block, own_cols, store, n)
+        done += 1
+    rest = xcat_ref[len(line_blocks(sizes)) * n :, :]
+    gathered = (line_gathered_ref[...] + dot(radial_scr[...], rest)).astype(BF16)
     gathered = jnp.concatenate([gathered[b * n : (b + 1) * n, :] for b in range(len(GAMMAS))], axis=1)
     short_ref[...] = dot(gathered, mixed_ref[...])
 
@@ -460,7 +511,7 @@
     filt_ref,
     *rest,
 ):
-    *kept, grad_ref, pull_ref, refined_ref, field_ref, neutral_ref = rest
+    planes_ref, levels_ref, grad_ref, pull_ref, refined_ref, field_ref, neutral_ref = rest
     n, channels = features_ref.shape
     charge_ch = w_long_ref.shape[0]
     wide = 2 * ORDERS * charge_ch
@@ -488,12 +539,8 @@
 
     filtered(load, filt_ref, field_ref, charge_ch)
     neutral_ref[...] = (charge_ref[...] - mean) * live_row
-    if kept:
-        plane = kept[0][0]
-        tz = (kept[1][0, 0:8, :], kept[1][0, 8:16, :])
-    else:
-        tx, ty, tz = axis_tables(own, place_of(0, 0, sizes), sizes)
-        plane = plane_table(tx, ty).astype(BF16)
+    plane = planes_ref[0]
+    tz = (levels_ref[0, 0:8, :], levels_ref[0, 8:16, :])
     lifted = dot(field_ref[...], plane)
     potential = jnp.zeros((charge_ch, n), F32)
     for kind in range(2):
@@ -599,36 +646,54 @@
     force_ref[...] = jnp.concatenate([near[a] - slope[a] for a in range(3)], axis=0)
 
 
-def pull_kernel(sizes, group, near_ref, places_ref, w_long_ref, *rest):
+def pull_sides(ref, row, sizes, w_long, tables, n):
+    charge_ch = w_long.shape[0]
+    nz = sizes[2]
+    pulls = dot_nt(w_long, ref[row, 0 : len(full_steps(nz)) * n, :])
+    left, right = [], []
+    for step in range(nz):
+        lo = row_of(step, nz, n, charge_ch)
+        if step in full_steps(nz):
+            pull = pulls[:, lo : lo + n]
+        else:
+            pull = ref[row, lo : lo + charge_ch, :].astype(F32)
+        plane, tz = tables(row, step)
+        left.append(spread(pull, tz))
+        right.append(plane)
+    return left, right
+
+
+def line_pull_kernel(sizes, line_ref, planes_ref, levels_ref, w_long_ref, sums_ref):
+    n = levels_ref.shape[2]
+
+    def tables(row, step):
+        return planes_ref[step], (levels_ref[step, 0:8, :], levels_ref[step, 8:16, :])
+
+    left, right = pull_sides(line_ref, 0, sizes, w_long_ref[...], tables, n)
+    sums_ref[...] = dot_nt(jnp.concatenate(left, axis=1), jnp.concatenate(right, axis=1))
+
+
+def pull_kernel(sizes, group, near_ref, line_sums_ref, places_ref, w_long_ref, *rest):
     *kept, sums_ref, part_ref = rest
-    charge_ch = w_long_ref.shape[0]
+    nz = sizes[2]
     n = places_ref.shape[2]
-    nz = sizes[2]
-    whole = len(full_steps(nz)) * n
-    groups = near_ref.shape[0] // group
-
-    def structure(g):
+
+    def tables(row, step):
+        m = row * nz + step
+        if kept:
+            return kept[0][m - nz], (kept[1][m - nz, 0:8, :], kept[1][m - nz, 8:16, :])
+        tx, ty, tz = axis_tables(places_ref[m], place_of(m, 0, sizes), sizes)
+        return plane_table(tx, ty).astype(BF16), tz
+
+    def structure(row):
         left, right = [], []
-        rows = jnp.concatenate([near_ref[g * group + r, 0:whole, :] for r in range(group)], axis=0)
-        pulls = dot_nt(w_long_ref[...], rows)
         for r in range(group):
-            for step in range(nz):
-                m = (g * group + r) * nz + step
-                lo = row_of(step, nz, n, charge_ch)
-                if step in full_steps(nz):
-                    pull = pulls[:, r * whole + lo : r * whole + lo + n]
-                else:
-                    pull = near_ref[g * group + r, lo : lo + charge_ch, :].astype(F32)
-                if kept:
-                    tz = (kept[1][m, 0:8, :], kept[1][m, 8:16, :])
-                    right.append(kept[0][m])
-                else:
-                    tx, ty, tz = axis_tables(places_ref[m], place_of(m, 0, sizes), sizes)
-                    right.append(plane_table(tx, ty).astype(BF16))
-                left.append(spread(pull, tz))
+            sides = pull_sides(near_ref, row + r, sizes, w_long_ref[...], tables, n)
+            left += sides[0]
+            right += sides[1]
         return dot_nt(jnp.concatenate(left, axis=1), jnp.concatenate(right, axis=1))
 
-    add_groups(structure, groups, sums_ref)
+    add_groups(structure, near_ref.shape[0], group, sums_ref, line_sums_ref)
     part_ref[...] = sums_ref[...].astype(BF16)
 
 
@@ -766,7 +831,8 @@
     cells = sizes[0] * sizes[1] * sizes[2]
     half_cells = cells // 2
     lines = half_cells // sizes[2]
-    group = 2 if sizes[2] <= 4 and lines % 2 == 0 else 1
+    group = lines - 1 if cells <= 32 else 1
+    near_line = len(line_blocks(sizes))
     blocks = len(blocks_of(sizes))
     scale_long = 4.0 / math.sqrt(n * cells * waves)
     count = counts.reshape(1)
@@ -820,21 +886,47 @@
     )
     line = gather_line(packed, slim, sizes[2])
     line, filt, energy_row, mixed = lax.optimization_barrier((line, filt, energy_row, mixed))
-    (near,) = gather_cells(line, sizes, ())
+    line_sums, base, line_places, charge, line_gathered, line_planes, line_levels = run(
+        lambda *refs: line_kernel(sizes, *refs),
+        "line_sums",
+        [
+            held((wide + 16, 256), F32),
+            held((charge_ch, n), F32),
+            held((sizes[2], 8, n), F32),
+            held((charge_ch, n), F32),
+            held((bases * n, channels), F32),
+            held((sizes[2], 256, n), BF16),
+            held((sizes[2], 16, n), F32),
+        ],
+        [
+            pltpu.VMEM((bases * n, near_line * n), BF16),
+            pltpu.VMEM((near_line * n, channels), BF16),
+        ],
+        [line, w_charge, bias],
+        3,
+        1_000_000_000,
+    )
+    near, line_sums = gather_cells(line, sizes, (line_sums,))
     far = from_other_core(near)
-    sums, part, places, charge, *kept = run(
+    sums, part, places, *kept = run(
         lambda *refs: charge_kernel(sizes, group, *refs),
         "charge_sums",
         [
             held((wide + 16, 256), F32),
             held((wide + 16 + charge_ch, 256), BF16),
             held((half_cells, 8, n), F32),
-            held((charge_ch, n), F32),
         ]
-        + ([held((half_cells, 256, n), BF16), held((half_cells, 16, n), F32)] if fits else []),
-        [pltpu.VMEM((half_cells, charge_ch, n), F32)],
-        [near, w_charge, bias],
-        3,
+        + (
+            [
+                held((half_cells - sizes[2], 256, n), BF16),
+                held((half_cells - sizes[2], 16, n), F32),
+            ]
+            if fits
+            else []
+        ),
+        [],
+        [near, line_sums, base, line_places, w_charge, bias],
+        6,
         3_000_000_000,
     )
     far_part = from_other_core(part)
@@ -846,9 +938,9 @@
             held((half_cells, 8, n), F32),
             held((blocks * n, channels), BF16),
         ],
-        [pltpu.VMEM((bases * n, blocks * n), BF16)],
-        [near, far, places, mixed],
-        4,
+        [pltpu.VMEM((bases * n, (blocks - near_line) * n), BF16)],
+        [near, far, places, mixed, line_gathered],
+        5,
         3_000_000_000,
     )
     grad, pull, refined, field, neutral = run(
@@ -875,9 +967,10 @@
             w_long,
             energy_row,
             filt,
-            *kept,
+            line_planes,
+            line_levels,
         ],
-        12 + len(kept),
+        14,
         3_000_000_000,
     )
     grad_line, grad = lax.optimization_barrier((gather_line(grad, pull, sizes[2]), grad))
@@ -908,15 +1001,24 @@
         9,
         4_000_000_000,
     )
-    grad_near, force, lifted = gather_cells(grad_line, sizes, (force, lifted))
+    (line_back,) = run(
+        lambda *refs: line_pull_kernel(sizes, *refs),
+        "line_pulls",
+        [held((wide, 256), F32)],
+        [],
+        [grad_line, line_planes, line_levels, w_long],
+        4,
+        1_000_000_000,
+    )
+    grad_near, force, lifted, line_back = gather_cells(grad_line, sizes, (force, lifted, line_back))
     grad_far = from_other_core(grad_near)
     back, back_part = run(
         lambda *refs: pull_kernel(sizes, group, *refs),
         "pull_sums",
         [held((wide, 256), F32), held((wide, 256), BF16)],
         [],
-        [grad_near, places, w_long, *kept],
-        3 + len(kept),
+        [grad_near, line_back, places, w_long, *kept],
+        4 + len(kept),
         3_000_000_000,
     )
     far_back = from_other_core(back_part)

time: 48.2 us -> 47.3 us (0.981)
  waiting for transfers between devices: 13.1 us -> 11 us
  local copies, waits for them, and re-layouts: 0.01 us -> 0.72 us
  Pallas kernels: 14.9 us -> 15.4 us
    ppermute x6, waiting for transfers between devices: 6.63 us -> 4.38 us  [shifted(): return lax.ppermute(value, ('gx', 'gy'), moves)]
    unnamed x6, local copies, waits for them, and re-layouts: 0.01 us -> 0.72 us
    pallas_call x9 -> x11, Pallas kernels: 14.9 us -> 15.4 us  [call(): pl.pallas_call(kernel, name=name, out_shape=outs, in_specs=specs, out_spe...]
  transfers between devices with their start and end apart: 16 -> 16, of which waited for: 7 -> 8; matrix products, arithmetic and copies ran while one was open for 0% -> 0% of each run, Pallas kernels for 24% -> 25%
where the time goes in v7:
time: 47.3 us; the launch traced here: 47.1 us
  starting transfers between devices  18.3 us (39%)
  Pallas kernels  15.4 us (33%)
  waiting for transfers between devices  11 us (23%)
  between operations  1.42 us (3%)
  local copies, waits for them, and re-layouts  0.72 us (2%)
    pallas_call x11, Pallas kernels, call(): pl.pallas_call(kernel, name=name, out_shape=outs, in_specs=specs, out_spe...  15.4 us
    ppermute x6, starting transfers between devices, moved(): return lax.ppermute(rows, 'gz', [(i, (i + step) % nz) for i in range(nz)])  9.96 us
    ppermute x6, starting transfers between devices, shifted(): return lax.ppermute(value, ('gx', 'gy'), moves)  7.11 us
    ppermute x6, waiting for transfers between devices, moved(): return lax.ppermute(rows, 'gz', [(i, (i + step) % nz) for i in range(nz)])  6.36 us
    ppermute x6, waiting for transfers between devices, shifted(): return lax.ppermute(value, ('gx', 'gy'), moves)  4.38 us
    ppermute x4, starting transfers between devices, from_other_core(): lax.ppermute(value, 'gx', [(i, i ^ 1) for i in range(lax.axis_size('gx'))])  1.26 us
  transfers between devices with their start and end apart: 16, of which 8 were waited for; matrix products, arithmetic and copies ran while one was open for 0% of the time, Pallas kernels for 25%

profile of v7, /device:TPU:0, one launch (start us, length us, event | category | flops | bytes accessed | tf_op | source)
XLA Modules:
  0.0 47.1 jit_solution(17959619891745626920)
XLA Ops:
  1.3 1.0 %pack.1 = (bf16[144,128]{1,0:T(8,128)(2,1)S(1)}, bf16[80,128]{1,0:T(8,128)(2,1)S(1)}, f32[128,128]{1,0:T(8,128)S(1)}, f32[64,128]{1,0:T(8,128)S(1)}) custom-call(s32[1]{0:T(128)} %bitcast.15.count_ref, bf16[128,128]{1,0:T(8,128)(2,1)} %bitcast.16, f32[3,1,128]{2,1,0:T(1,128)} %bitcast.18, bf16[64,128]{1,0:T(8,128)(2,1)} %refs_4_.3, f32[1,64]{1,0:T(1,128)} %bitcast.19), custom_call_target="tpu_custom_call" | custom-call | flops 1000 | bytes 2000000 | tf_op jit(solution)/shard_map/pack/pallas_call | solution.py:800
  2.3 3.1 %collective-permute-start = (bf16[144,128]{1,0:T(8,128)(2,1)S(1)}, bf16[144,128]{1,0:T(8,128)(2,1)S(1)}, u32[]{:S(2)}, u32[]{:S(2)}) collective-permute-start(bf16[144,128]{1,0:T(8,128)(2,1)S(1)} %get-tuple-element.52), channel_id=1, source_target_pairs={{0,1},{1,2},{2,3},{3,0},{4,5},{5,6},{6,7},{7,4},{8,9},{9,10},{10,1... | collective-permute-start | bytes 110600 | tf_op jit(solution)/shard_map/ppermute | solution.py:752
  5.3 2.1 %collective-permute-start.1 = (bf16[144,128]{1,0:T(8,128)(2,1)S(1)}, bf16[144,128]{1,0:T(8,128)(2,1)S(1)}, u32[]{:S(2)}, u32[]{:S(2)}) collective-permute-start(bf16[144,128]{1,0:T(8,128)(2,1)S(1)} %get-tuple-element.52), channel_id=1, source_target_pairs={{0,3},{1,0},{2,1},{3,2},{4,7},{5,4},{6,5},{7,6},{8,11},{9,8},{10,9... | collective-permute-start | bytes 110600 | tf_op jit(solution)/shard_map/ppermute | solution.py:752
  7.4 0.9 %collective-permute-start.2 = (bf16[80,128]{1,0:T(8,128)(2,1)S(1)}, bf16[80,128]{1,0:T(8,128)(2,1)S(1)}, u32[]{:S(2)}, u32[]{:S(2)}) collective-permute-start(bf16[80,128]{1,0:T(8,128)(2,1)S(1)} %get-tuple-element.53), channel_id=1, source_target_pairs={{0,2},{1,3},{2,0},{3,1},{4,6},{5,7},{6,4},{7,5},{8,10},{9,11},{10,... | collective-permute-start | bytes 61448 | tf_op jit(solution)/shard_map/ppermute | solution.py:752
  8.4 2.0 %fold_filter.1 = (f32[7,256,128]{2,1,0:T(8,128)S(1)}, f32[1,128]{1,0:T(1,128)S(1)}, bf16[512,128]{1,0:T(8,128)(2,1)S(1)}) custom-call(f32[64,2048]{1,0:T(8,128)} %refs_0_.1, s32[3,2048]{1,0:T(4,128)} %refs_1_.2, f32[1,128]{1,0:T(1,128)} %bitcast.21, bf16[512,128]{1,0:T(8,128)(2,1)} %bitcast.20, bf16[128,128]{1,0:T(8,128)(2,1)} %refs_4_.2), custom_call_target="tpu_custom_call" | custom-call | flops 1000000000 | bytes 2000000 | tf_op jit(solution)/shard_map/fold_filter/pallas_call | solution.py:800
  10.4 1.7 %collective-permute-done.2 = bf16[80,128]{1,0:T(8,128)(2,1)S(1)} collective-permute-done((bf16[80,128]{1,0:T(8,128)(2,1)S(1)}, bf16[80,128]{1,0:T(8,128)(2,1)S(1)}, u32[]{:S(2)}, u32[]{:S(2)}) %collective-permute-start.2) | collective-permute-done | bytes 20512 | tf_op jit(solution)/shard_map/ppermute | solution.py:752
  12.1 1.7 %collective-permute-start.3 = (bf16[1,512,128]{2,1,0:T(8,128)(2,1)S(1)}, bf16[1,512,128]{2,1,0:T(8,128)(2,1)S(1)}, u32[]{:S(2)}, u32[]{:S(2)}) collective-permute-start(bf16[1,512,128]{2,1,0:T(8,128)(2,1)S(1)} %maximum_bitcast_fusion.refs_0_), channel_id=1, source_target_pairs={{0,4},{4,0},{8,12},{12,8},{16,20},{20,16},{24,28},{28,24},{1,5},{5... | collective-permute-start | bytes 393224 | tf_op jit(solution)/shard_map/ppermute | solution.py:767
  13.9 1.5 %collective-permute-start.4 = (bf16[1,512,128]{2,1,0:T(8,128)(2,1)S(1)}, bf16[1,512,128]{2,1,0:T(8,128)(2,1)S(1)}, u32[]{:S(2)}, u32[]{:S(2)}) collective-permute-start(bf16[1,512,128]{2,1,0:T(8,128)(2,1)S(1)} %maximum_bitcast_fusion.refs_0_), channel_id=1, source_target_pairs={{0,16},{4,20},{8,24},{12,28},{16,0},{20,4},{24,8},{28,12},{1,17},{... | collective-permute-start | bytes 393224 | tf_op jit(solution)/shard_map/ppermute | solution.py:767
  15.7 0.7 %copy-done.1 = bf16[64,128]{1,0:T(8,128)(2,1)S(1)} copy-done((bf16[64,128]{1,0:T(8,128)(2,1)S(1)}, bf16[64,128]{1,0:T(8,128)(2,1)}, u32[]{:S(2)}) %copy-start.1) | copy-done | bytes 16408
  16.4 1.0 %line_sums.1 = (f32[912,256]{1,0:T(8,128)S(1)}, f32[64,128]{1,0:T(8,128)S(1)}, f32[4,8,128]{2,1,0:T(8,128)S(1)}, f32[64,128]{1,0:T(8,128)S(1)}, f32[512,128]{1,0...) custom-call(bf16[1,512,128]{2,1,0:T(8,128)(2,1)S(1)} %maximum_bitcast_fusion.refs_0_, ...), custom_call_target="tpu_custom_call" | custom-call | flops 1000000000 | bytes 2000000 | tf_op jit(solution)/shard_map/line_sums/pallas_call | solution.py:800
  17.4 0.9 %collective-permute-done.3 = bf16[1,512,128]{2,1,0:T(8,128)(2,1)S(1)} collective-permute-done((bf16[1,512,128]{2,1,0:T(8,128)(2,1)S(1)}, bf16[1,512,128]{2,1,0:T(8,128)(2,1)S(1)}, u32[]{:S(2)}, u32[]{:S(2)}) %collective-permute-start.3) | collective-permute-done | bytes 131104 | tf_op jit(solution)/shard_map/ppermute | solution.py:767
  18.9 2.4 %collective-permute-done.5 = bf16[1,512,128]{2,1,0:T(8,128)(2,1)S(1)} collective-permute-done((bf16[1,512,128]{2,1,0:T(8,128)(2,1)S(1)}, bf16[1,512,128]{2,1,0:T(8,128)(2,1)S(1)}, u32[]{:S(2)}, u32[]{:S(2)}) %collective-permute-start.5) | collective-permute-done | bytes 131104 | tf_op jit(solution)/shard_map/ppermute | solution.py:767
  21.4 1.2 %charge_sums.1 = (f32[912,256]{1,0:T(8,128)S(1)}, bf16[976,256]{1,0:T(8,128)(2,1)S(1)}, f32[16,8,128]{2,1,0:T(8,128)S(1)}, bf16[12,256,128]{2,1,0:T(8,128)(2,1)S(1)}, f32[12,16,128]{2,1,0:T(8,128)S(1)}) custom-call(bf16[4,512,128]{2,1,0:T(8,128)(2,1)S(1)} %pad_maximum_fusion.refs_0_, f32[912,256]{1,0:T(8,128)S(1)} %get-tuple-element.61.refs_1_, ...), custom_call_target="tpu_custom_call" | custom-call | flops 3000000000 | bytes 2000000 | tf_op jit(solution)/shard_map/charge_sums/pallas_call | solution.py:800
  23.3 1.7 %message.1 = (f32[128,128]{1,0:T(8,128)S(1)}, f32[16,8,128]{2,1,0:T(8,128)S(1)}, bf16[2304,128]{1,0:T(8,128)(2,1)S(1)}) custom-call(bf16[4,512,128]{2,1,0:T(8,128)(2,1)S(1)} %pad_maximum_fusion.refs_0_, bf16[4,512,128]{2,1,0:T(8,128)(2,1)S(1)} %collective-permute-done.7.refs_1_, f32[16,8,128]{2,1,0:T(8,128)S(1)} %get-tuple-element.66.refs_2_.refs_4_, ...), custom_call_target="tpu_custom_call" | custom-call | flops 3000000000 | bytes 2000000 | tf_op jit(solution)/shard_map/message/pallas_call | solution.py:800
  25.0 1.2 %cotangents.1 = (bf16[128,128]{1,0:T(8,128)(2,1)S(1)}, bf16[64,128]{1,0:T(8,128)(2,1)S(1)}, f32[128,128]{1,0:T(8,128)S(1)}, bf16[896,256]{1,0:T(8,128)(2,1)S(1)}, f32[64,128]{1,0:T(8,128)S(1)}) custom-call(f32[128,128]{1,0:T(8,128)S(1)} %get-tuple-element.51.refs_0_, f32[912,256]{1,0:T(8,128)S(1)} %get-tuple-element.64.refs_1_, ...), custom_call_target="tpu_custom_call" | custom-call | flops 3000000000 | bytes 2000000 | tf_op jit(solution)/shard_map/cotangents/pallas_call | solution.py:800
  26.3 3.8 %collective-permute-start.9 = (bf16[128,128]{1,0:T(8,128)(2,1)S(1)}, bf16[128,128]{1,0:T(8,128)(2,1)S(1)}, u32[]{:S(2)}, u32[]{:S(2)}) collective-permute-start(bf16[128,128]{1,0:T(8,128)(2,1)S(1)} %get-tuple-element.78.refs_0_), channel_id=1, source_target_pairs={{0,3},{1,0},{2,1},{3,2},{4,7},{5,4},{6,5},{7,6},{8,11},{9,8},{10,9... | collective-permute-start | bytes 98312 | tf_op jit(solution)/shard_map/ppermute | solution.py:752
  30.1 4.6 %collective-permute-done.10 = bf16[64,128]{1,0:T(8,128)(2,1)S(1)} collective-permute-done((bf16[64,128]{1,0:T(8,128)(2,1)S(1)}, bf16[64,128]{1,0:T(8,128)(2,1)S(1)}, u32[]{:S(2)}, u32[]{:S(2)}) %collective-permute-start.10) | collective-permute-done | bytes 16416 | tf_op jit(solution)/shard_map/ppermute | solution.py:752
  34.8 0.6 %collective-permute-start.11 = (bf16[1,448,128]{2,1,0:T(8,128)(2,1)S(1)}, bf16[1,448,128]{2,1,0:T(8,128)(2,1)S(1)}, u32[]{:S(2)}, u32[]{:S(2)}) collective-permute-start(bf16[1,448,128]{2,1,0:T(8,128)(2,1)S(1)} %maximum_bitcast_fusion.1.refs_0_), channel_id=1, source_target_pairs={{0,4},{4,0},{8,12},{12,8},{16,20},{20,16},{24,28},{28,24},{1,5},{5... | collective-permute-start | bytes 344072 | tf_op jit(solution)/shard_map/ppermute | solution.py:767
  35.3 1.5 %collective-permute-start.12 = (bf16[1,448,128]{2,1,0:T(8,128)(2,1)S(1)}, bf16[1,448,128]{2,1,0:T(8,128)(2,1)S(1)}, u32[]{:S(2)}, u32[]{:S(2)}) collective-permute-start(bf16[1,448,128]{2,1,0:T(8,128)(2,1)S(1)} %maximum_bitcast_fusion.1.refs_0_), channel_id=1, source_target_pairs={{0,16},{4,20},{8,24},{12,28},{16,0},{20,4},{24,8},{28,12},{1,17},{... | collective-permute-start | bytes 344072 | tf_op jit(solution)/shard_map/ppermute | solution.py:767
  36.8 1.5 %collective-permute-start.13 = (bf16[1,448,128]{2,1,0:T(8,128)(2,1)S(1)}, bf16[1,448,128]{2,1,0:T(8,128)(2,1)S(1)}, u32[]{:S(2)}, u32[]{:S(2)}) collective-permute-start(bf16[1,448,128]{2,1,0:T(8,128)(2,1)S(1)} %maximum_bitcast_fusion.1.refs_0_), channel_id=1, source_target_pairs={{0,20},{4,16},{8,28},{12,24},{16,4},{20,0},{24,12},{28,8},{1,21},{... | collective-permute-start | bytes 344072 | tf_op jit(solution)/shard_map/ppermute | solution.py:767
  38.3 3.1 %own_terms.1 = (bf16[128,128]{1,0:T(8,128)(2,1)}, f32[1,128]{1,0:T(1,128)}, f32[3,128]{1,0:T(4,128)S(1)}, bf16[512,128]{1,0:T(8,128)(2,1)S(1)}, bf16[256,384]{1,...) custom-call(bf16[128,128]{1,0:T(8,128)(2,1)S(1)} %get-tuple-element.78.refs_0_, ...), custom_call_target="tpu_custom_call" | custom-call | flops 4000000000 | bytes 2000000 | tf_op jit(solution)/shard_map/own_terms/pallas_call | solution.py:800
  42.6 1.1 %pull_sums.1 = (f32[896,256]{1,0:T(8,128)S(1)}, bf16[896,256]{1,0:T(8,128)(2,1)S(1)}) custom-call(bf16[4,448,128]{2,1,0:T(8,128)(2,1)S(1)} %pad_maximum_fusion.1.refs_0_, f32[896,256]{1,0:T(8,128)S(1)} %line_pulls.1.refs_1_, f32[16,8,128]{2,1,0:T(8,128)S(1)} %get-tuple-element.66.refs_2_.refs_4_, bf16[64,128]{1,0:T(8,128)(2,1)S(1)} %copy-done.2, ...), custom_call_target="tpu_custom_call" | custom-call | flops 3000000000 | bytes 2000000 | tf_op jit(solution)/shard_map/pull_sums/pallas_call | solution.py:800
  44.4 1.3 %react.1.refs_5_ = f32[3,128]{1,0:T(4,128)S(1)} custom-call(bf16[4,448,128]{2,1,0:T(8,128)(2,1)S(1)} %pad_maximum_fusion.1.refs_0_, bf16[4,448,128]{2,1,0:T(8,128)(2,1)S(1)} %collective-permute-done.15.refs_1_, f32[16,8,128]{2,1,0:T(8,128)S(1)} %get-tuple-element.66.refs_2_.refs_4_, f32[16,8,128]{2,1,0:T(8,128)S(1)} %get-tuple-element.69.refs_5_.refs_3_, ...), custom_call_target="tpu_custom_call" | custom-call | flops 3000000000 | bytes 2000000 | tf_op jit(solution)/shard_map/react/pallas_call | solution.py:800
  45.8 1.3 %finish.1 = f32[3,1,128]{2,1,0:T(1,128)} custom-call(f32[896,256]{1,0:T(8,128)S(1)} %get-tuple-element.91.refs_0_, bf16[896,256]{1,0:T(8,128)(2,1)S(1)} %collective-permute-done.14.refs_1_, bf16[256,384]{1,0:T(8,128)(2,1)S(1)} %get-tuple-element.93.refs_2_, f32[16,128]{1,0:T(8,128)S(1)} %get-tuple-element.94.refs_3_, ...), custom_call_target="tpu_custom_call" | custom-call | flops 2000000000 | bytes 2000000 | tf_op jit(solution)/shard_map/finish/pallas_call | solution.py:800
  (29 shorter events, 3.6 us)
Async XLA Ops:
  2.3 9.9 %collective-permute-start = (bf16[144,128]{1,0:T(8,128)(2,1)S(1)}, bf16[144,128]{1,0:T(8,128)(2,1)S(1)}, u32[]{:S(2)}, u32[]{:S(2)}) collective-permute-start(bf16[144,128]{1,0:T(8,128)(2,1)S(1)} %get-tuple-element.52), channel_id=1, source_target_pairs={{0,1},{1,2},{2,3},{3,0},{4,5},{5,6},{6,7},{7,4},{8,9},{9,10},{10,1... | collective-permute-start | bytes 110600 | tf_op jit(solution)/shard_map/ppermute | solution.py:752
  5.3 6.8 %collective-permute-start.1 = (bf16[144,128]{1,0:T(8,128)(2,1)S(1)}, bf16[144,128]{1,0:T(8,128)(2,1)S(1)}, u32[]{:S(2)}, u32[]{:S(2)}) collective-permute-start(bf16[144,128]{1,0:T(8,128)(2,1)S(1)} %get-tuple-element.52), channel_id=1, source_target_pairs={{0,3},{1,0},{2,1},{3,2},{4,7},{5,4},{6,5},{7,6},{8,11},{9,8},{10,9... | collective-permute-start | bytes 110600 | tf_op jit(solution)/shard_map/ppermute | solution.py:752
  7.4 4.7 %collective-permute-start.2 = (bf16[80,128]{1,0:T(8,128)(2,1)S(1)}, bf16[80,128]{1,0:T(8,128)(2,1)S(1)}, u32[]{:S(2)}, u32[]{:S(2)}) collective-permute-start(bf16[80,128]{1,0:T(8,128)(2,1)S(1)} %get-tuple-element.53), channel_id=1, source_target_pairs={{0,2},{1,3},{2,0},{3,1},{4,6},{5,7},{6,4},{7,5},{8,10},{9,11},{10,... | collective-permute-start | bytes 61448 | tf_op jit(solution)/shard_map/ppermute | solution.py:752
  12.1 6.2 %collective-permute-start.3 = (bf16[1,512,128]{2,1,0:T(8,128)(2,1)S(1)}, bf16[1,512,128]{2,1,0:T(8,128)(2,1)S(1)}, u32[]{:S(2)}, u32[]{:S(2)}) collective-permute-start(bf16[1,512,128]{2,1,0:T(8,128)(2,1)S(1)} %maximum_bitcast_fusion.refs_0_), channel_id=1, source_target_pairs={{0,4},{4,0},{8,12},{12,8},{16,20},{20,16},{24,28},{28,24},{1,5},{5... | collective-permute-start | bytes 393224 | tf_op jit(solution)/shard_map/ppermute | solution.py:767
  13.9 5.0 %collective-permute-start.4 = (bf16[1,512,128]{2,1,0:T(8,128)(2,1)S(1)}, bf16[1,512,128]{2,1,0:T(8,128)(2,1)S(1)}, u32[]{:S(2)}, u32[]{:S(2)}) collective-permute-start(bf16[1,512,128]{2,1,0:T(8,128)(2,1)S(1)} %maximum_bitcast_fusion.refs_0_), channel_id=1, source_target_pairs={{0,16},{4,20},{8,24},{12,28},{16,0},{20,4},{24,8},{28,12},{1,17},{... | collective-permute-start | bytes 393224 | tf_op jit(solution)/shard_map/ppermute | solution.py:767
  15.4 5.9 %collective-permute-start.5 = (bf16[1,512,128]{2,1,0:T(8,128)(2,1)S(1)}, bf16[1,512,128]{2,1,0:T(8,128)(2,1)S(1)}, u32[]{:S(2)}, u32[]{:S(2)}) collective-permute-start(bf16[1,512,128]{2,1,0:T(8,128)(2,1)S(1)} %maximum_bitcast_fusion.refs_0_), channel_id=1, source_target_pairs={{0,20},{4,16},{8,28},{12,24},{16,4},{20,0},{24,12},{28,8},{1,21},{... | collective-permute-start | bytes 393224 | tf_op jit(solution)/shard_map/ppermute | solution.py:767
  15.7 0.7 %copy-start.1 = (bf16[64,128]{1,0:T(8,128)(2,1)S(1)}, bf16[64,128]{1,0:T(8,128)(2,1)}, u32[]{:S(2)}) copy-start(bf16[64,128]{1,0:T(8,128)(2,1)} %refs_4_.3) | copy-start | bytes 49156
  21.3 2.0 %collective-permute-start.7 = (bf16[4,512,128]{2,1,0:T(8,128)(2,1)S(1)}, bf16[4,512,128]{2,1,0:T(8,128)(2,1)S(1)}, u32[]{:S(2)}, u32[]{:S(2)}) collective-permute-start(bf16[4,512,128]{2,1,0:T(8,128)(2,1)S(1)} %pad_maximum_fusion.refs_0_), channel_id=1, source_target_pairs={{0,8},{8,0},{16,24},{24,16},{1,9},{9,1},{17,25},{25,17},{2,10},{10... | collective-permute-start | bytes 1572872 | tf_op jit(solution)/shard_map/ppermute | solution.py:782
  22.6 2.4 %collective-permute-start.6 = (bf16[976,256]{1,0:T(8,128)(2,1)S(1)}, bf16[976,256]{1,0:T(8,128)(2,1)S(1)}, u32[]{:S(2)}, u32[]{:S(2)}) collective-permute-start(bf16[976,256]{1,0:T(8,128)(2,1)S(1)} %get-tuple-element.65.refs_2_), channel_id=1, source_target_pairs={{0,8},{8,0},{16,24},{24,16},{1,9},{9,1},{17,25},{25,17},{2,10},{10... | collective-permute-start | bytes 1499144 | tf_op jit(solution)/shard_map/ppermute | solution.py:782
  23.3 1.7 %copy-start = (bf16[1,1,1,128,128]{4,3,2,1,0:T(8,128)(2,1)S(1)}, bf16[1,1,1,128,128]{4,3,2,1,0:T(8,128)(2,1)}, u32[]{:S(2)}) copy-start(bf16[1,1,1,128,128]{4,3,2,1,0:T(8,128)(2,1)} %param.11) | copy-start | bytes 98308
  23.3 1.7 %copy-start.2 = (bf16[64,128]{1,0:T(8,128)(2,1)S(1)}, bf16[64,128]{1,0:T(8,128)(2,1)}, u32[]{:S(2)}) copy-start(bf16[64,128]{1,0:T(8,128)(2,1)} %refs_3_.3) | copy-start | bytes 49156
  26.3 8.5 %collective-permute-start.8 = (bf16[128,128]{1,0:T(8,128)(2,1)S(1)}, bf16[128,128]{1,0:T(8,128)(2,1)S(1)}, u32[]{:S(2)}, u32[]{:S(2)}) collective-permute-start(bf16[128,128]{1,0:T(8,128)(2,1)S(1)} %get-tuple-element.78.refs_0_), channel_id=1, source_target_pairs={{0,1},{1,2},{2,3},{3,0},{4,5},{5,6},{6,7},{7,4},{8,9},{9,10},{10,1... | collective-permute-start | bytes 98312 | tf_op jit(solution)/shard_map/ppermute | solution.py:752
  26.3 8.5 %collective-permute-start.9 = (bf16[128,128]{1,0:T(8,128)(2,1)S(1)}, bf16[128,128]{1,0:T(8,128)(2,1)S(1)}, u32[]{:S(2)}, u32[]{:S(2)}) collective-permute-start(bf16[128,128]{1,0:T(8,128)(2,1)S(1)} %get-tuple-element.78.refs_0_), channel_id=1, source_target_pairs={{0,3},{1,0},{2,1},{3,2},{4,7},{5,4},{6,5},{7,6},{8,11},{9,8},{10,9... | collective-permute-start | bytes 98312 | tf_op jit(solution)/shard_map/ppermute | solution.py:752
  30.1 4.6 %collective-permute-start.10 = (bf16[64,128]{1,0:T(8,128)(2,1)S(1)}, bf16[64,128]{1,0:T(8,128)(2,1)S(1)}, u32[]{:S(2)}, u32[]{:S(2)}) collective-permute-start(bf16[64,128]{1,0:T(8,128)(2,1)S(1)} %get-tuple-element.77), channel_id=1, source_target_pairs={{0,2},{1,3},{2,0},{3,1},{4,6},{5,7},{6,4},{7,5},{8,10},{9,11},{10,... | collective-permute-start | bytes 49160 | tf_op jit(solution)/shard_map/ppermute | solution.py:752
  34.8 7.2 %collective-permute-start.11 = (bf16[1,448,128]{2,1,0:T(8,128)(2,1)S(1)}, bf16[1,448,128]{2,1,0:T(8,128)(2,1)S(1)}, u32[]{:S(2)}, u32[]{:S(2)}) collective-permute-start(bf16[1,448,128]{2,1,0:T(8,128)(2,1)S(1)} %maximum_bitcast_fusion.1.refs_0_), channel_id=1, source_target_pairs={{0,4},{4,0},{8,12},{12,8},{16,20},{20,16},{24,28},{28,24},{1,5},{5... | collective-permute-start | bytes 344072 | tf_op jit(solution)/shard_map/ppermute | solution.py:767
  35.3 6.6 %collective-permute-start.12 = (bf16[1,448,128]{2,1,0:T(8,128)(2,1)S(1)}, bf16[1,448,128]{2,1,0:T(8,128)(2,1)S(1)}, u32[]{:S(2)}, u32[]{:S(2)}) collective-permute-start(bf16[1,448,128]{2,1,0:T(8,128)(2,1)S(1)} %maximum_bitcast_fusion.1.refs_0_), channel_id=1, source_target_pairs={{0,16},{4,20},{8,24},{12,28},{16,0},{20,4},{24,8},{28,12},{1,17},{... | collective-permute-start | bytes 344072 | tf_op jit(solution)/shard_map/ppermute | solution.py:767
  36.8 5.7 %collective-permute-start.13 = (bf16[1,448,128]{2,1,0:T(8,128)(2,1)S(1)}, bf16[1,448,128]{2,1,0:T(8,128)(2,1)S(1)}, u32[]{:S(2)}, u32[]{:S(2)}) collective-permute-start(bf16[1,448,128]{2,1,0:T(8,128)(2,1)S(1)} %maximum_bitcast_fusion.1.refs_0_), channel_id=1, source_target_pairs={{0,20},{4,16},{8,28},{12,24},{16,4},{20,0},{24,12},{28,8},{1,21},{... | collective-permute-start | bytes 344072 | tf_op jit(solution)/shard_map/ppermute | solution.py:767
  42.5 1.9 %collective-permute-start.15 = (bf16[4,448,128]{2,1,0:T(8,128)(2,1)S(1)}, bf16[4,448,128]{2,1,0:T(8,128)(2,1)S(1)}, u32[]{:S(2)}, u32[]{:S(2)}) collective-permute-start(bf16[4,448,128]{2,1,0:T(8,128)(2,1)S(1)} %pad_maximum_fusion.1.refs_0_), channel_id=1, source_target_pairs={{0,8},{8,0},{16,24},{24,16},{1,9},{9,1},{17,25},{25,17},{2,10},{10... | collective-permute-start | bytes 1376264 | tf_op jit(solution)/shard_map/ppermute | solution.py:782
  43.7 2.0 %collective-permute-start.14 = (bf16[896,256]{1,0:T(8,128)(2,1)S(1)}, bf16[896,256]{1,0:T(8,128)(2,1)S(1)}, u32[]{:S(2)}, u32[]{:S(2)}) collective-permute-start(bf16[896,256]{1,0:T(8,128)(2,1)S(1)} %get-tuple-element.92), channel_id=1, source_target_pairs={{0,8},{8,0},{16,24},{24,16},{1,9},{9,1},{17,25},{25,17},{2,10},{10... | collective-permute-start | bytes 1376264 | tf_op jit(solution)/shard_map/ppermute | solution.py:782

commit v8 on v7

--- a/solution.py
+++ b/solution.py
@@ -143,7 +143,8 @@
     start = lax.axis_index(AXES[0]) if half == 0 else lax.axis_index(AXES[0]) + 1 - 2 * lax.rem(lax.axis_index(AXES[0]), 2)
     cx = lax.rem(start - 2 * dx + nx, nx)
     cy = lax.rem(lax.axis_index(AXES[1]) - dy + ny, ny)
-    cz = lax.rem(lax.axis_index(AXES[2]) - dz + nz, nz)
+    z = lax.axis_index(AXES[2])
+    cz = jnp.bitwise_xor(z, dz) if in_pairs(nz) else lax.rem(z - dz + nz, nz)
     return (cx.astype(F32), cy.astype(F32), cz.astype(F32))
 
 
@@ -286,8 +287,14 @@
     return sorted({0, 1 % nz, nz - 1})
 
 
+def in_pairs(nz):
+    return nz == 4
+
+
 def row_of(step, nz, full_rows, slim_rows):
     full = full_steps(nz)
+    if not isinstance(step, int):
+        return pl.multiple_of(lax.div(step + 1, 2) * full_rows, 16)
     if step in full:
         return full.index(step) * full_rows
     return len(full) * full_rows + (step - 2) * slim_rows
@@ -302,6 +309,8 @@
 def block_place(sizes, odd, block):
     nx, ny, nz = sizes
     dy, dz = (-block[1][0]) % ny, (-block[2][0]) % nz
+    if in_pairs(nz) and dz:
+        dz = 2 - block[2][0] * (1 - 2 * lax.rem(lax.axis_index(AXES[2]), 2))
     if block[0][0] == 0:
         return 0, dy, dz
     dx = odd * (nx // 2 - 1) if block[0][0] == 1 else (1 - odd) * (1 % (nx // 2))
@@ -395,14 +404,14 @@
     sums_ref[...] = dot_nt(jnp.concatenate(left, axis=1), jnp.concatenate(right, axis=1))
     own_cols = columns(cells[0][0], n)
     for t, block in enumerate(line_blocks(sizes)):
-        step = (-block[2][0]) % nz
+        step = block_place(sizes, 0, block)[2]
 
         def store(row, value, t=t):
             radial_scr[row : row + 32, t * n : (t + 1) * n] = value
 
-        block_radials(cells[step][0], block, own_cols, store, n)
+        block_radials(places_ref[step], block, own_cols, store, n)
         lo = row_of(step, nz, n + 16, 0)
-        xcat_scr[t * n : (t + 1) * n, :] = line_ref[0, lo : lo + n, :]
+        xcat_scr[t * n : (t + 1) * n, :] = line_ref[0, pl.ds(lo, n), :]
     gathered_ref[...] = dot(radial_scr[...], xcat_scr[...])
 
 
@@ -479,7 +488,7 @@
     for t, block in enumerate(blocks_of(sizes)):
         half, row, step = block_place(sizes, odd, block)
         lo = row_of(step, nz, n + 16, 0)
-        xcat_ref[t * n : (t + 1) * n, :] = halves[half][row, lo : lo + n, :]
+        xcat_ref[t * n : (t + 1) * n, :] = halves[half][row, pl.ds(lo, n), :]
         pos = places[half][row * nz + step]
         if block in line_blocks(sizes):
             continue
@@ -714,7 +723,7 @@
     for t, block in enumerate(blocks_of(sizes)):
         half, row, step = block_place(sizes, odd, block)
         lo = row_of(step, sizes[2], n, 0)
-        gcat_scr[t * n : (t + 1) * n, :] = halves[half][row, lo : lo + n, :]
+        gcat_scr[t * n : (t + 1) * n, :] = halves[half][row, pl.ds(lo, n), :]
     strength_scr[...] = dot_nt(lifted_ref[...], gcat_scr[...])
     places = (places_ref, far_places_ref)
     near = pair_force(sizes, places, strength_scr, n, None, slopes[0] if slopes else None)
@@ -749,7 +758,9 @@
 def gather_line(full, slim, nz):
     def moved(step):
         rows = full if step in full_steps(nz) else slim
-        return lax.ppermute(rows, "gz", [(i, (i + step) % nz) for i in range(nz)])
+        return lax.ppermute(
+            rows, "gz", [(i, i ^ step if in_pairs(nz) else (i + step) % nz) for i in range(nz)]
+        )
 
     steps = sorted(range(1, nz), key=lambda step: step not in full_steps(nz))
     return jnp.concatenate([full] + [moved(step) for step in steps], axis=0)[None]

time: 47.3 us -> 46.2 us (0.977)
  starting transfers between devices: 18.3 us -> 17.6 us
    ppermute x6, starting transfers between devices: 9.96 us -> 9.18 us  [moved(): lax.ppermute(rows, 'gz', [(i, i ^ step if in_pairs(nz) else (i + step) %...]
  transfers between devices with their start and end apart: 16 -> 16, of which waited for: 8 -> 8; matrix products, arithmetic and copies ran while one was open for 0% -> 0% of each run, Pallas kernels for 25% -> 26%
where the time goes in v8:
time: 46.2 us; the launch traced here: 45.9 us
  starting transfers between devices  17.6 us (38%)
  Pallas kernels  15.4 us (33%)
  waiting for transfers between devices  10.6 us (23%)
  between operations  1.43 us (3%)
  local copies, waits for them, and re-layouts  0.72 us (2%)
    pallas_call x11, Pallas kernels, call(): pl.pallas_call(kernel, name=name, out_shape=outs, in_specs=specs, out_spe...  15.4 us
    ppermute x6, starting transfers between devices, moved(): lax.ppermute(rows, 'gz', [(i, i ^ step if in_pairs(nz) else (i + step) %...  9.18 us
    ppermute x6, starting transfers between devices, shifted(): return lax.ppermute(value, ('gx', 'gy'), moves)  7.11 us
    ppermute x6, waiting for transfers between devices, moved(): lax.ppermute(rows, 'gz', [(i, i ^ step if in_pairs(nz) else (i + step) %...  5.91 us
    ppermute x6, waiting for transfers between devices, shifted(): return lax.ppermute(value, ('gx', 'gy'), moves)  4.46 us
    ppermute x4, starting transfers between devices, from_other_core(): lax.ppermute(value, 'gx', [(i, i ^ 1) for i in range(lax.axis_size('gx'))])  1.26 us
  transfers between devices with their start and end apart: 16, of which 8 were waited for; matrix products, arithmetic and copies ran while one was open for 0% of the time, Pallas kernels for 26%

profile of v8, /device:TPU:0, one launch (start us, length us, event | category | flops | bytes accessed | tf_op | source)
XLA Modules:
  0.0 45.9 jit_solution(2986548861255640550)
XLA Ops:
  1.3 1.0 %pack.1 = (bf16[144,128]{1,0:T(8,128)(2,1)S(1)}, bf16[80,128]{1,0:T(8,128)(2,1)S(1)}, f32[128,128]{1,0:T(8,128)S(1)}, f32[64,128]{1,0:T(8,128)S(1)}) custom-call(s32[1]{0:T(128)} %bitcast.15.count_ref, bf16[128,128]{1,0:T(8,128)(2,1)} %bitcast.16, f32[3,1,128]{2,1,0:T(1,128)} %bitcast.18, bf16[64,128]{1,0:T(8,128)(2,1)} %refs_4_.3, f32[1,64]{1,0:T(1,128)} %bitcast.19), custom_call_target="tpu_custom_call" | custom-call | flops 1000 | bytes 2000000 | tf_op jit(solution)/shard_map/pack/pallas_call | solution.py:811
  2.3 3.1 %collective-permute-start = (bf16[144,128]{1,0:T(8,128)(2,1)S(1)}, bf16[144,128]{1,0:T(8,128)(2,1)S(1)}, u32[]{:S(2)}, u32[]{:S(2)}) collective-permute-start(bf16[144,128]{1,0:T(8,128)(2,1)S(1)} %get-tuple-element.52), channel_id=1, source_target_pairs={{0,1},{1,0},{2,3},{3,2},{4,5},{5,4},{6,7},{7,6},{8,9},{9,8},{10,11... | collective-permute-start | bytes 110600 | tf_op jit(solution)/shard_map/ppermute | solution.py:761
  5.4 2.5 %collective-permute-start.1 = (bf16[144,128]{1,0:T(8,128)(2,1)S(1)}, bf16[144,128]{1,0:T(8,128)(2,1)S(1)}, u32[]{:S(2)}, u32[]{:S(2)}) collective-permute-start(bf16[144,128]{1,0:T(8,128)(2,1)S(1)} %get-tuple-element.52), channel_id=1, source_target_pairs={{0,3},{1,2},{2,1},{3,0},{4,7},{5,6},{6,5},{7,4},{8,11},{9,10},{10,... | collective-permute-start | bytes 110600 | tf_op jit(solution)/shard_map/ppermute | solution.py:761
  8.0 2.0 %fold_filter.1 = (f32[7,256,128]{2,1,0:T(8,128)S(1)}, f32[1,128]{1,0:T(1,128)S(1)}, bf16[512,128]{1,0:T(8,128)(2,1)S(1)}) custom-call(f32[64,2048]{1,0:T(8,128)} %refs_0_.1, s32[3,2048]{1,0:T(4,128)} %refs_1_.2, f32[1,128]{1,0:T(1,128)} %bitcast.21, bf16[512,128]{1,0:T(8,128)(2,1)} %bitcast.20, bf16[128,128]{1,0:T(8,128)(2,1)} %refs_4_.2), custom_call_target="tpu_custom_call" | custom-call | flops 1000000000 | bytes 2000000 | tf_op jit(solution)/shard_map/fold_filter/pallas_call | solution.py:811
  10.0 2.8 %collective-permute-done.2 = bf16[80,128]{1,0:T(8,128)(2,1)S(1)} collective-permute-done((bf16[80,128]{1,0:T(8,128)(2,1)S(1)}, bf16[80,128]{1,0:T(8,128)(2,1)S(1)}, u32[]{:S(2)}, u32[]{:S(2)}) %collective-permute-start.2) | collective-permute-done | bytes 20512 | tf_op jit(solution)/shard_map/ppermute | solution.py:761
  12.8 1.6 %collective-permute-start.3 = (bf16[1,512,128]{2,1,0:T(8,128)(2,1)S(1)}, bf16[1,512,128]{2,1,0:T(8,128)(2,1)S(1)}, u32[]{:S(2)}, u32[]{:S(2)}) collective-permute-start(bf16[1,512,128]{2,1,0:T(8,128)(2,1)S(1)} %maximum_bitcast_fusion.refs_0_), channel_id=1, source_target_pairs={{0,4},{4,0},{8,12},{12,8},{16,20},{20,16},{24,28},{28,24},{1,5},{5... | collective-permute-start | bytes 393224 | tf_op jit(solution)/shard_map/ppermute | solution.py:778
  14.3 1.5 %collective-permute-start.4 = (bf16[1,512,128]{2,1,0:T(8,128)(2,1)S(1)}, bf16[1,512,128]{2,1,0:T(8,128)(2,1)S(1)}, u32[]{:S(2)}, u32[]{:S(2)}) collective-permute-start(bf16[1,512,128]{2,1,0:T(8,128)(2,1)S(1)} %maximum_bitcast_fusion.refs_0_), channel_id=1, source_target_pairs={{0,16},{4,20},{8,24},{12,28},{16,0},{20,4},{24,8},{28,12},{1,17},{... | collective-permute-start | bytes 393224 | tf_op jit(solution)/shard_map/ppermute | solution.py:778
  17.0 1.0 %line_sums.1 = (f32[912,256]{1,0:T(8,128)S(1)}, f32[64,128]{1,0:T(8,128)S(1)}, f32[4,8,128]{2,1,0:T(8,128)S(1)}, f32[64,128]{1,0:T(8,128)S(1)}, f32[512,128]{1,0...) custom-call(bf16[1,512,128]{2,1,0:T(8,128)(2,1)S(1)} %maximum_bitcast_fusion.refs_0_, ...), custom_call_target="tpu_custom_call" | custom-call | flops 1000000000 | bytes 2000000 | tf_op jit(solution)/shard_map/line_sums/pallas_call | solution.py:811
  18.4 1.2 %collective-permute-done.4 = bf16[1,512,128]{2,1,0:T(8,128)(2,1)S(1)} collective-permute-done((bf16[1,512,128]{2,1,0:T(8,128)(2,1)S(1)}, bf16[1,512,128]{2,1,0:T(8,128)(2,1)S(1)}, u32[]{:S(2)}, u32[]{:S(2)}) %collective-permute-start.4) | collective-permute-done | bytes 131104 | tf_op jit(solution)/shard_map/ppermute | solution.py:778
  19.6 2.1 %collective-permute-done.5 = bf16[1,512,128]{2,1,0:T(8,128)(2,1)S(1)} collective-permute-done((bf16[1,512,128]{2,1,0:T(8,128)(2,1)S(1)}, bf16[1,512,128]{2,1,0:T(8,128)(2,1)S(1)}, u32[]{:S(2)}, u32[]{:S(2)}) %collective-permute-start.5) | collective-permute-done | bytes 131104 | tf_op jit(solution)/shard_map/ppermute | solution.py:778
  21.9 1.2 %charge_sums.1 = (f32[912,256]{1,0:T(8,128)S(1)}, bf16[976,256]{1,0:T(8,128)(2,1)S(1)}, f32[16,8,128]{2,1,0:T(8,128)S(1)}, bf16[12,256,128]{2,1,0:T(8,128)(2,1)S(1)}, f32[12,16,128]{2,1,0:T(8,128)S(1)}) custom-call(bf16[4,512,128]{2,1,0:T(8,128)(2,1)S(1)} %pad_maximum_fusion.refs_0_, f32[912,256]{1,0:T(8,128)S(1)} %get-tuple-element.61.refs_1_, ...), custom_call_target="tpu_custom_call" | custom-call | flops 3000000000 | bytes 2000000 | tf_op jit(solution)/shard_map/charge_sums/pallas_call | solution.py:811
  23.8 1.7 %message.1 = (f32[128,128]{1,0:T(8,128)S(1)}, f32[16,8,128]{2,1,0:T(8,128)S(1)}, bf16[2304,128]{1,0:T(8,128)(2,1)S(1)}) custom-call(bf16[4,512,128]{2,1,0:T(8,128)(2,1)S(1)} %pad_maximum_fusion.refs_0_, bf16[4,512,128]{2,1,0:T(8,128)(2,1)S(1)} %collective-permute-done.7.refs_1_, f32[16,8,128]{2,1,0:T(8,128)S(1)} %get-tuple-element.66.refs_2_.refs_4_, ...), custom_call_target="tpu_custom_call" | custom-call | flops 3000000000 | bytes 2000000 | tf_op jit(solution)/shard_map/message/pallas_call | solution.py:811
  25.5 1.2 %cotangents.1 = (bf16[128,128]{1,0:T(8,128)(2,1)S(1)}, bf16[64,128]{1,0:T(8,128)(2,1)S(1)}, f32[128,128]{1,0:T(8,128)S(1)}, bf16[896,256]{1,0:T(8,128)(2,1)S(1)}, f32[64,128]{1,0:T(8,128)S(1)}) custom-call(f32[128,128]{1,0:T(8,128)S(1)} %get-tuple-element.51.refs_0_, f32[912,256]{1,0:T(8,128)S(1)} %get-tuple-element.64.refs_1_, ...), custom_call_target="tpu_custom_call" | custom-call | flops 3000000000 | bytes 2000000 | tf_op jit(solution)/shard_map/cotangents/pallas_call | solution.py:811
  27.3 1.2 %collective-permute-start.9 = (bf16[128,128]{1,0:T(8,128)(2,1)S(1)}, bf16[128,128]{1,0:T(8,128)(2,1)S(1)}, u32[]{:S(2)}, u32[]{:S(2)}) collective-permute-start(bf16[128,128]{1,0:T(8,128)(2,1)S(1)} %get-tuple-element.78.refs_0_), channel_id=1, source_target_pairs={{0,3},{1,2},{2,1},{3,0},{4,7},{5,6},{6,5},{7,4},{8,11},{9,10},{10,... | collective-permute-start | bytes 98312 | tf_op jit(solution)/shard_map/ppermute | solution.py:761
  28.5 1.7 %collective-permute-start.10 = (bf16[64,128]{1,0:T(8,128)(2,1)S(1)}, bf16[64,128]{1,0:T(8,128)(2,1)S(1)}, u32[]{:S(2)}, u32[]{:S(2)}) collective-permute-start(bf16[64,128]{1,0:T(8,128)(2,1)S(1)} %get-tuple-element.77), channel_id=1, source_target_pairs={{0,2},{1,3},{2,0},{3,1},{4,6},{5,7},{6,4},{7,5},{8,10},{9,11},{10,... | collective-permute-start | bytes 49160 | tf_op jit(solution)/shard_map/ppermute | solution.py:761
  30.2 3.1 %collective-permute-done.10 = bf16[64,128]{1,0:T(8,128)(2,1)S(1)} collective-permute-done((bf16[64,128]{1,0:T(8,128)(2,1)S(1)}, bf16[64,128]{1,0:T(8,128)(2,1)S(1)}, u32[]{:S(2)}, u32[]{:S(2)}) %collective-permute-start.10) | collective-permute-done | bytes 16416 | tf_op jit(solution)/shard_map/ppermute | solution.py:761
  33.4 0.8 %collective-permute-start.11 = (bf16[1,448,128]{2,1,0:T(8,128)(2,1)S(1)}, bf16[1,448,128]{2,1,0:T(8,128)(2,1)S(1)}, u32[]{:S(2)}, u32[]{:S(2)}) collective-permute-start(bf16[1,448,128]{2,1,0:T(8,128)(2,1)S(1)} %maximum_bitcast_fusion.1.refs_0_), channel_id=1, source_target_pairs={{0,4},{4,0},{8,12},{12,8},{16,20},{20,16},{24,28},{28,24},{1,5},{5... | collective-permute-start | bytes 344072 | tf_op jit(solution)/shard_map/ppermute | solution.py:778
  34.1 1.5 %collective-permute-start.12 = (bf16[1,448,128]{2,1,0:T(8,128)(2,1)S(1)}, bf16[1,448,128]{2,1,0:T(8,128)(2,1)S(1)}, u32[]{:S(2)}, u32[]{:S(2)}) collective-permute-start(bf16[1,448,128]{2,1,0:T(8,128)(2,1)S(1)} %maximum_bitcast_fusion.1.refs_0_), channel_id=1, source_target_pairs={{0,16},{4,20},{8,24},{12,28},{16,0},{20,4},{24,8},{28,12},{1,17},{... | collective-permute-start | bytes 344072 | tf_op jit(solution)/shard_map/ppermute | solution.py:778
  35.6 1.3 %collective-permute-start.13 = (bf16[1,448,128]{2,1,0:T(8,128)(2,1)S(1)}, bf16[1,448,128]{2,1,0:T(8,128)(2,1)S(1)}, u32[]{:S(2)}, u32[]{:S(2)}) collective-permute-start(bf16[1,448,128]{2,1,0:T(8,128)(2,1)S(1)} %maximum_bitcast_fusion.1.refs_0_), channel_id=1, source_target_pairs={{0,20},{4,16},{8,28},{12,24},{16,4},{20,0},{24,12},{28,8},{1,21},{... | collective-permute-start | bytes 344072 | tf_op jit(solution)/shard_map/ppermute | solution.py:778
  36.9 3.1 %own_terms.1 = (bf16[128,128]{1,0:T(8,128)(2,1)}, f32[1,128]{1,0:T(1,128)}, f32[3,128]{1,0:T(4,128)S(1)}, bf16[512,128]{1,0:T(8,128)(2,1)S(1)}, bf16[256,384]{1,...) custom-call(bf16[128,128]{1,0:T(8,128)(2,1)S(1)} %get-tuple-element.78.refs_0_, ...), custom_call_target="tpu_custom_call" | custom-call | flops 4000000000 | bytes 2000000 | tf_op jit(solution)/shard_map/own_terms/pallas_call | solution.py:811
  40.6 0.7 %collective-permute-done.13 = bf16[1,448,128]{2,1,0:T(8,128)(2,1)S(1)} collective-permute-done((bf16[1,448,128]{2,1,0:T(8,128)(2,1)S(1)}, bf16[1,448,128]{2,1,0:T(8,128)(2,1)S(1)}, u32[]{:S(2)}, u32[]{:S(2)}) %collective-permute-start.13) | collective-permute-done | bytes 114720 | tf_op jit(solution)/shard_map/ppermute | solution.py:778
  41.5 1.1 %pull_sums.1 = (f32[896,256]{1,0:T(8,128)S(1)}, bf16[896,256]{1,0:T(8,128)(2,1)S(1)}) custom-call(bf16[4,448,128]{2,1,0:T(8,128)(2,1)S(1)} %pad_maximum_fusion.1.refs_0_, f32[896,256]{1,0:T(8,128)S(1)} %line_pulls.1.refs_1_, f32[16,8,128]{2,1,0:T(8,128)S(1)} %get-tuple-element.66.refs_2_.refs_4_, bf16[64,128]{1,0:T(8,128)(2,1)S(1)} %copy-done.2, ...), custom_call_target="tpu_custom_call" | custom-call | flops 3000000000 | bytes 2000000 | tf_op jit(solution)/shard_map/pull_sums/pallas_call | solution.py:811
  43.3 1.3 %react.1.refs_5_ = f32[3,128]{1,0:T(4,128)S(1)} custom-call(bf16[4,448,128]{2,1,0:T(8,128)(2,1)S(1)} %pad_maximum_fusion.1.refs_0_, bf16[4,448,128]{2,1,0:T(8,128)(2,1)S(1)} %collective-permute-done.15.refs_1_, f32[16,8,128]{2,1,0:T(8,128)S(1)} %get-tuple-element.66.refs_2_.refs_4_, f32[16,8,128]{2,1,0:T(8,128)S(1)} %get-tuple-element.69.refs_5_.refs_3_, ...), custom_call_target="tpu_custom_call" | custom-call | flops 3000000000 | bytes 2000000 | tf_op jit(solution)/shard_map/react/pallas_call | solution.py:811
  44.6 1.3 %finish.1 = f32[3,1,128]{2,1,0:T(1,128)} custom-call(f32[896,256]{1,0:T(8,128)S(1)} %get-tuple-element.91.refs_0_, bf16[896,256]{1,0:T(8,128)(2,1)S(1)} %collective-permute-done.14.refs_1_, bf16[256,384]{1,0:T(8,128)(2,1)S(1)} %get-tuple-element.93.refs_2_, f32[16,128]{1,0:T(8,128)S(1)} %get-tuple-element.94.refs_3_, ...), custom_call_target="tpu_custom_call" | custom-call | flops 2000000000 | bytes 2000000 | tf_op jit(solution)/shard_map/finish/pallas_call | solution.py:811
  (29 shorter events, 4.5 us)
Async XLA Ops:
  2.3 10.5 %collective-permute-start = (bf16[144,128]{1,0:T(8,128)(2,1)S(1)}, bf16[144,128]{1,0:T(8,128)(2,1)S(1)}, u32[]{:S(2)}, u32[]{:S(2)}) collective-permute-start(bf16[144,128]{1,0:T(8,128)(2,1)S(1)} %get-tuple-element.52), channel_id=1, source_target_pairs={{0,1},{1,0},{2,3},{3,2},{4,5},{5,4},{6,7},{7,6},{8,9},{9,8},{10,11... | collective-permute-start | bytes 110600 | tf_op jit(solution)/shard_map/ppermute | solution.py:761
  5.4 7.4 %collective-permute-start.1 = (bf16[144,128]{1,0:T(8,128)(2,1)S(1)}, bf16[144,128]{1,0:T(8,128)(2,1)S(1)}, u32[]{:S(2)}, u32[]{:S(2)}) collective-permute-start(bf16[144,128]{1,0:T(8,128)(2,1)S(1)} %get-tuple-element.52), channel_id=1, source_target_pairs={{0,3},{1,2},{2,1},{3,0},{4,7},{5,6},{6,5},{7,4},{8,11},{9,10},{10,... | collective-permute-start | bytes 110600 | tf_op jit(solution)/shard_map/ppermute | solution.py:761
  7.8 4.9 %collective-permute-start.2 = (bf16[80,128]{1,0:T(8,128)(2,1)S(1)}, bf16[80,128]{1,0:T(8,128)(2,1)S(1)}, u32[]{:S(2)}, u32[]{:S(2)}) collective-permute-start(bf16[80,128]{1,0:T(8,128)(2,1)S(1)} %get-tuple-element.53), channel_id=1, source_target_pairs={{0,2},{1,3},{2,0},{3,1},{4,6},{5,7},{6,4},{7,5},{8,10},{9,11},{10,... | collective-permute-start | bytes 61448 | tf_op jit(solution)/shard_map/ppermute | solution.py:761
  12.8 5.6 %collective-permute-start.3 = (bf16[1,512,128]{2,1,0:T(8,128)(2,1)S(1)}, bf16[1,512,128]{2,1,0:T(8,128)(2,1)S(1)}, u32[]{:S(2)}, u32[]{:S(2)}) collective-permute-start(bf16[1,512,128]{2,1,0:T(8,128)(2,1)S(1)} %maximum_bitcast_fusion.refs_0_), channel_id=1, source_target_pairs={{0,4},{4,0},{8,12},{12,8},{16,20},{20,16},{24,28},{28,24},{1,5},{5... | collective-permute-start | bytes 393224 | tf_op jit(solution)/shard_map/ppermute | solution.py:778
  14.3 5.3 %collective-permute-start.4 = (bf16[1,512,128]{2,1,0:T(8,128)(2,1)S(1)}, bf16[1,512,128]{2,1,0:T(8,128)(2,1)S(1)}, u32[]{:S(2)}, u32[]{:S(2)}) collective-permute-start(bf16[1,512,128]{2,1,0:T(8,128)(2,1)S(1)} %maximum_bitcast_fusion.refs_0_), channel_id=1, source_target_pairs={{0,16},{4,20},{8,24},{12,28},{16,0},{20,4},{24,8},{28,12},{1,17},{... | collective-permute-start | bytes 393224 | tf_op jit(solution)/shard_map/ppermute | solution.py:778
  15.8 5.9 %collective-permute-start.5 = (bf16[1,512,128]{2,1,0:T(8,128)(2,1)S(1)}, bf16[1,512,128]{2,1,0:T(8,128)(2,1)S(1)}, u32[]{:S(2)}, u32[]{:S(2)}) collective-permute-start(bf16[1,512,128]{2,1,0:T(8,128)(2,1)S(1)} %maximum_bitcast_fusion.refs_0_), channel_id=1, source_target_pairs={{0,20},{4,16},{8,28},{12,24},{16,4},{20,0},{24,12},{28,8},{1,21},{... | collective-permute-start | bytes 393224 | tf_op jit(solution)/shard_map/ppermute | solution.py:778
  16.3 0.7 %copy-start.1 = (bf16[64,128]{1,0:T(8,128)(2,1)S(1)}, bf16[64,128]{1,0:T(8,128)(2,1)}, u32[]{:S(2)}) copy-start(bf16[64,128]{1,0:T(8,128)(2,1)} %refs_4_.3) | copy-start | bytes 49156
  21.8 2.0 %collective-permute-start.7 = (bf16[4,512,128]{2,1,0:T(8,128)(2,1)S(1)}, bf16[4,512,128]{2,1,0:T(8,128)(2,1)S(1)}, u32[]{:S(2)}, u32[]{:S(2)}) collective-permute-start(bf16[4,512,128]{2,1,0:T(8,128)(2,1)S(1)} %pad_maximum_fusion.refs_0_), channel_id=1, source_target_pairs={{0,8},{8,0},{16,24},{24,16},{1,9},{9,1},{17,25},{25,17},{2,10},{10... | collective-permute-start | bytes 1572872 | tf_op jit(solution)/shard_map/ppermute | solution.py:793
  23.1 2.4 %collective-permute-start.6 = (bf16[976,256]{1,0:T(8,128)(2,1)S(1)}, bf16[976,256]{1,0:T(8,128)(2,1)S(1)}, u32[]{:S(2)}, u32[]{:S(2)}) collective-permute-start(bf16[976,256]{1,0:T(8,128)(2,1)S(1)} %get-tuple-element.65.refs_2_), channel_id=1, source_target_pairs={{0,8},{8,0},{16,24},{24,16},{1,9},{9,1},{17,25},{25,17},{2,10},{10... | collective-permute-start | bytes 1499144 | tf_op jit(solution)/shard_map/ppermute | solution.py:793
  23.8 1.7 %copy-start = (bf16[1,1,1,128,128]{4,3,2,1,0:T(8,128)(2,1)S(1)}, bf16[1,1,1,128,128]{4,3,2,1,0:T(8,128)(2,1)}, u32[]{:S(2)}) copy-start(bf16[1,1,1,128,128]{4,3,2,1,0:T(8,128)(2,1)} %param.11) | copy-start | bytes 98308
  23.8 1.7 %copy-start.2 = (bf16[64,128]{1,0:T(8,128)(2,1)S(1)}, bf16[64,128]{1,0:T(8,128)(2,1)}, u32[]{:S(2)}) copy-start(bf16[64,128]{1,0:T(8,128)(2,1)} %refs_3_.3) | copy-start | bytes 49156
  26.7 6.6 %collective-permute-start.8 = (bf16[128,128]{1,0:T(8,128)(2,1)S(1)}, bf16[128,128]{1,0:T(8,128)(2,1)S(1)}, u32[]{:S(2)}, u32[]{:S(2)}) collective-permute-start(bf16[128,128]{1,0:T(8,128)(2,1)S(1)} %get-tuple-element.78.refs_0_), channel_id=1, source_target_pairs={{0,1},{1,0},{2,3},{3,2},{4,5},{5,4},{6,7},{7,6},{8,9},{9,8},{10,11... | collective-permute-start | bytes 98312 | tf_op jit(solution)/shard_map/ppermute | solution.py:761
  27.3 6.1 %collective-permute-start.9 = (bf16[128,128]{1,0:T(8,128)(2,1)S(1)}, bf16[128,128]{1,0:T(8,128)(2,1)S(1)}, u32[]{:S(2)}, u32[]{:S(2)}) collective-permute-start(bf16[128,128]{1,0:T(8,128)(2,1)S(1)} %get-tuple-element.78.refs_0_), channel_id=1, source_target_pairs={{0,3},{1,2},{2,1},{3,0},{4,7},{5,6},{6,5},{7,4},{8,11},{9,10},{10,... | collective-permute-start | bytes 98312 | tf_op jit(solution)/shard_map/ppermute | solution.py:761
  28.5 4.8 %collective-permute-start.10 = (bf16[64,128]{1,0:T(8,128)(2,1)S(1)}, bf16[64,128]{1,0:T(8,128)(2,1)S(1)}, u32[]{:S(2)}, u32[]{:S(2)}) collective-permute-start(bf16[64,128]{1,0:T(8,128)(2,1)S(1)} %get-tuple-element.77), channel_id=1, source_target_pairs={{0,2},{1,3},{2,0},{3,1},{4,6},{5,7},{6,4},{7,5},{8,10},{9,11},{10,... | collective-permute-start | bytes 49160 | tf_op jit(solution)/shard_map/ppermute | solution.py:761
  33.4 7.2 %collective-permute-start.11 = (bf16[1,448,128]{2,1,0:T(8,128)(2,1)S(1)}, bf16[1,448,128]{2,1,0:T(8,128)(2,1)S(1)}, u32[]{:S(2)}, u32[]{:S(2)}) collective-permute-start(bf16[1,448,128]{2,1,0:T(8,128)(2,1)S(1)} %maximum_bitcast_fusion.1.refs_0_), channel_id=1, source_target_pairs={{0,4},{4,0},{8,12},{12,8},{16,20},{20,16},{24,28},{28,24},{1,5},{5... | collective-permute-start | bytes 344072 | tf_op jit(solution)/shard_map/ppermute | solution.py:778
  34.1 6.4 %collective-permute-start.12 = (bf16[1,448,128]{2,1,0:T(8,128)(2,1)S(1)}, bf16[1,448,128]{2,1,0:T(8,128)(2,1)S(1)}, u32[]{:S(2)}, u32[]{:S(2)}) collective-permute-start(bf16[1,448,128]{2,1,0:T(8,128)(2,1)S(1)} %maximum_bitcast_fusion.1.refs_0_), channel_id=1, source_target_pairs={{0,16},{4,20},{8,24},{12,28},{16,0},{20,4},{24,8},{28,12},{1,17},{... | collective-permute-start | bytes 344072 | tf_op jit(solution)/shard_map/ppermute | solution.py:778
  35.6 5.7 %collective-permute-start.13 = (bf16[1,448,128]{2,1,0:T(8,128)(2,1)S(1)}, bf16[1,448,128]{2,1,0:T(8,128)(2,1)S(1)}, u32[]{:S(2)}, u32[]{:S(2)}) collective-permute-start(bf16[1,448,128]{2,1,0:T(8,128)(2,1)S(1)} %maximum_bitcast_fusion.1.refs_0_), channel_id=1, source_target_pairs={{0,20},{4,16},{8,28},{12,24},{16,4},{20,0},{24,12},{28,8},{1,21},{... | collective-permute-start | bytes 344072 | tf_op jit(solution)/shard_map/ppermute | solution.py:778
  41.4 1.9 %collective-permute-start.15 = (bf16[4,448,128]{2,1,0:T(8,128)(2,1)S(1)}, bf16[4,448,128]{2,1,0:T(8,128)(2,1)S(1)}, u32[]{:S(2)}, u32[]{:S(2)}) collective-permute-start(bf16[4,448,128]{2,1,0:T(8,128)(2,1)S(1)} %pad_maximum_fusion.1.refs_0_), channel_id=1, source_target_pairs={{0,8},{8,0},{16,24},{24,16},{1,9},{9,1},{17,25},{25,17},{2,10},{10... | collective-permute-start | bytes 1376264 | tf_op jit(solution)/shard_map/ppermute | solution.py:793
  42.6 2.1 %collective-permute-start.14 = (bf16[896,256]{1,0:T(8,128)(2,1)S(1)}, bf16[896,256]{1,0:T(8,128)(2,1)S(1)}, u32[]{:S(2)}, u32[]{:S(2)}) collective-permute-start(bf16[896,256]{1,0:T(8,128)(2,1)S(1)} %get-tuple-element.92), channel_id=1, source_target_pairs={{0,8},{8,0},{16,24},{24,16},{1,9},{9,1},{17,25},{25,17},{2,10},{10... | collective-permute-start | bytes 1376264 | tf_op jit(solution)/shard_map/ppermute | solution.py:793
